TPU v7x, 32 devices: a whole 2x2x4 slice. The times are simulated.
32 devices in a mesh: dp: 8 (over z, y), head: 4 (over x, core).
Axes of the slice: x: 2, y: 2, z: 4, core: 2. Of those that a mesh axis runs over, the one named last changes fastest.
Arguments:
- ids: int32 [16, 512], P('dp'), may hold values from 0 to 31999
- targets: int32 [16, 512], P('dp'), may hold values from 0 to 31999
- target_mask: int32 [16, 512], P('dp'), may hold values from 0 to 1, as said below
- memory: bfloat16 [16, 512, 1024], P('dp'), may hold values from -6 to 6
- old_states: bfloat16 [16, 1536, 1024], P('dp'), may hold values from -6 to 6
- mem_fill: int32 [16], P('dp'), may hold values from 0 to 512, as said below
- comp_fill: int32 [16], P('dp'), may hold values from 0 to 512, as said below
- table: float32 [32000, 1024], P('head', 'dp'), may hold values from -0.5625 to 0.5625
- qkv: float32 [3, 1024, 1024], P(None, 'dp', 'head'), may hold values from -0.1875 to 0.1875
- wout: float32 [1024, 1024], P('head', 'dp'), may hold values from -1.5 to 1.5
- wconv: float32 [8, 384, 128], P('head', None, 'dp'), may hold values from -0.3125 to 0.3125
- wup: float32 [1024, 4096], P('dp', 'head'), may hold values from -0.1875 to 0.1875
- wdown: float32 [4096, 1024], P('head', 'dp'), may hold values from -0.09375 to 0.09375
- gains: float32 [3, 1024], P(None, 'dp'), may hold values from 0.5 to 1.5
- table_rows: float32 [32000], P('head'), may hold values from 3.0517577e-09 to 1.1444092e-08
- table_cols: float32 [1024], P('dp'), may hold values from 3.0517577e-09 to 1.1444092e-08
- qkv_rows: float32 [3, 1024], P(None, 'dp'), may hold values from 9.536743e-08 to 3.5762787e-07
- qkv_cols: float32 [1024], P('head'), may hold values from 9.536743e-08 to 3.5762787e-07
- out_rows: float32 [1024], P('head'), may hold values from 9.536743e-08 to 3.5762787e-07
- out_cols: float32 [1024], P('dp'), may hold values from 9.536743e-08 to 3.5762787e-07
- conv_rows: float32 [8, 384], P('head'), may hold values from 9.536743e-08 to 3.5762787e-07
- conv_cols: float32 [128], P('dp'), may hold values from 9.536743e-08 to 3.5762787e-07
- up_rows: float32 [1024], P('dp'), may hold values from 9.536743e-08 to 3.5762787e-07
- up_cols: float32 [4096], P('head'), may hold values from 9.536743e-08 to 3.5762787e-07
- down_rows: float32 [4096], P('head'), may hold values from 9.536743e-08 to 3.5762787e-07
- down_cols: float32 [1024], P('dp'), may hold values from 9.536743e-08 to 3.5762787e-07
- gains_second: float32 [3, 1024], P(None, 'dp'), may hold values from 3.8146973e-07 to 1.4305115e-06
Outputs:
- loss_sum: float32 [], replicated
- token_count: float32 [], replicated
- new_table: float32 [32000, 1024], P('head', 'dp')
- table_grad: float32 [32000, 1024], P('head', 'dp')
- new_table_rows: float32 [32000], P('head')
- new_table_cols: float32 [1024], P('dp')
- new_qkv: float32 [3, 1024, 1024], P(None, 'dp', 'head')
- qkv_grad: float32 [3, 1024, 1024], P(None, 'dp', 'head')
- new_qkv_rows: float32 [3, 1024], P(None, 'dp')
- new_qkv_cols: float32 [1024], P('head')
- new_wout: float32 [1024, 1024], P('head', 'dp')
- wout_grad: float32 [1024, 1024], P('head', 'dp')
- new_out_rows: float32 [1024], P('head')
- new_out_cols: float32 [1024], P('dp')
- new_wconv: float32 [8, 384, 128], P('head', None, 'dp')
- wconv_grad: float32 [8, 384, 128], P('head', None, 'dp')
- new_conv_rows: float32 [8, 384], P('head')
- new_conv_cols: float32 [128], P('dp')
- new_wup: float32 [1024, 4096], P('dp', 'head')
- wup_grad: float32 [1024, 4096], P('dp', 'head')
- new_up_rows: float32 [1024], P('dp')
- new_up_cols: float32 [4096], P('head')
- new_wdown: float32 [4096, 1024], P('head', 'dp')
- wdown_grad: float32 [4096, 1024], P('head', 'dp')
- new_down_rows: float32 [4096], P('head')
- new_down_cols: float32 [1024], P('dp')
- new_gains: float32 [3, 1024], P(None, 'dp')
- gains_grad: float32 [3, 1024], P(None, 'dp')
- new_gains_second: float32 [3, 1024], P(None, 'dp')
Inputs may be any that keep to these rules, and one draw needn't show every extreme that they name: `target_mask`: position 0 of every stream counts. `mem_fill`: some stream has a full memory and some an empty one. `comp_fill`: some stream has a full compressed memory and some an empty one.
All inputs are finite; a program needn't handle non-finite values.
Results may differ from a plain program's by a relative error of at most 0.013.
The roundings to bfloat16 on the way count: a program that leaves them out, or rounds other values in their place, can miss the bound.
Values may be sent and summed in bfloat16 or wider, within the bound.
No kernel may reach another device: no remote copies, remote signals or barrier semaphores. Data moves between devices by JAX's collectives and lax.ppermute only.
A program may use at most 320 MiB of HBM per device.

v0:
```python
import math

import jax
import jax.numpy as jnp
from jax import lax
from jax.sharding import PartitionSpec as P

D = 1024
H = 8
DH = 128
MEM = 512
CMEM = 512
RATE = 3
STEP = 10


TINY_NORM = 1e-06
TINY_SQUARE = 1e-30
LEARN_RATE = 0.5
CLIP_LEVEL = 1.0


def merged(value, axis, combine):
    everything = jax.tree.map(lambda part: lax.all_gather(part, axis), value)
    first = jax.tree.map(lambda part: part[0], everything)

    def turn(k, so_far):
        return combine(so_far, jax.tree.map(lambda part: part[k], everything))

    return lax.fori_loop(1, lax.axis_size(axis), turn, first)


def rms_norm(values, gain):
    return values * lax.rsqrt(jnp.mean(values * values, axis=-1, keepdims=True) + TINY_NORM) * gain


def norm_back(values, gain, upstream):
    return jax.vjp(rms_norm, values, gain)[1](upstream)


def gain_only(values, gain, upstream):
    return jax.vjp(lambda scaled: rms_norm(values, scaled), gain)[1](upstream)[0]


def visible_keys(mem_fill, comp_fill, seg_len):
    slots = jnp.arange(CMEM + MEM + seg_len, dtype=jnp.int32)[None, None, :]
    position = jnp.arange(seg_len, dtype=jnp.int32)[None, :, None]
    mem_count = mem_fill[:, None, None]
    comp_count = comp_fill[:, None, None]
    comp_ok = (slots < CMEM) & (slots >= CMEM - comp_count)
    mem_ok = (slots >= CMEM) & (slots < CMEM + MEM) & (slots >= CMEM + MEM - mem_count)
    own_ok = (slots >= CMEM + MEM) & (slots - CMEM - MEM <= position)
    return comp_ok | mem_ok | own_ok


def project(inputs, weight):
    return jnp.einsum("...d,de->...e", inputs, weight, preferred_element_type=jnp.float32)


def local(
    ids,
    targets,
    target_mask,
    memory,
    old_states,
    mem_fill,
    comp_fill,
    table,
    qkv,
    wout,
    wconv,
    wup,
    wdown,
    gains,
    table_rows,
    table_cols,
    qkv_rows,
    qkv_cols,
    out_rows,
    out_cols,
    conv_rows,
    conv_cols,
    up_rows,
    up_cols,
    down_rows,
    down_cols,
    gains_second,
):
    lowp = jnp.bfloat16
    single = jnp.float32
    axis_info = {
        "dp": (lax.axis_size("dp"), lax.axis_index("dp")),
        "head": (lax.axis_size("head"), lax.axis_index("head")),
    }
    heads_here, head_index = axis_info["head"]
    streams = ids.shape[0]
    seg_len = ids.shape[1]
    rows_here = streams * seg_len
    local_heads = H // heads_here
    width = local_heads * DH
    keys_total = CMEM + MEM + seg_len
    scale = DH ** (-0.5)
    full_table, full_qkv, full_out, full_conv, full_up, full_down, full_gains = (
        lax.all_gather(table.astype(lowp), "dp", axis=1, tiled=True),
        lax.all_gather(qkv.astype(lowp), "dp", axis=1, tiled=True),
        lax.all_gather(wout.astype(lowp), "dp", axis=1, tiled=True),
        lax.all_gather(wconv.astype(lowp), "dp", axis=2, tiled=True),
        lax.all_gather(wup.astype(lowp), "dp", axis=0, tiled=True),
        lax.all_gather(wdown.astype(lowp), "dp", axis=1, tiled=True),
        lax.all_gather(gains.astype(lowp), "dp", axis=1, tiled=True),
    )
    gain_vals = full_gains.astype(single)
    gain_one = gain_vals[0]
    vocab_here = full_table.shape[0]
    first_word = head_index * vocab_here
    local_ids = ids.reshape(-1) - first_word
    inside = (local_ids >= 0) & (local_ids < vocab_here)
    safe_ids = jnp.clip(local_ids, 0, vocab_here - 1)
    looked = jnp.where(inside[:, None], jnp.take(full_table, safe_ids, axis=0), jnp.zeros((), lowp))
    embedded = lax.psum(looked.astype(single).astype(jnp.bfloat16), "head").astype(jnp.float32)
    mem_float = memory.astype(single)
    old_float = old_states.astype(single)
    normed = rms_norm(embedded, gain_one).astype(lowp)
    mem_normed = rms_norm(mem_float, gain_one).astype(lowp)
    old_normed = rms_norm(old_float, gain_one).astype(lowp)
    queries = project(normed, full_qkv[0]).astype(lowp)
    conv_blocks = full_conv.reshape(local_heads, RATE, DH, DH)

    def old_blocks(raw):
        return raw.reshape(streams, CMEM, RATE, local_heads, DH)

    def squeeze(raw):
        folded = jnp.einsum(
            "scjhd,hjde->sche", old_blocks(raw), conv_blocks, preferred_element_type=single
        )
        return folded.reshape(streams, CMEM, width).astype(lowp)

    def stacked(which):
        seg_part = project(normed, full_qkv[which]).astype(lowp)
        mem_part = project(mem_normed, full_qkv[which]).astype(lowp)
        old_part = project(old_normed, full_qkv[which]).astype(lowp)
        joined = jnp.concatenate(
            [squeeze(old_part), mem_part, seg_part.reshape(streams, seg_len, width)], axis=1
        )
        return (joined.reshape(streams, keys_total, local_heads, DH), old_part)

    all_keys, old_keys = stacked(1)
    all_values, old_values = stacked(2)
    query_heads = queries.reshape(streams, seg_len, local_heads, DH)
    allowed = visible_keys(mem_fill, comp_fill, seg_len)[:, None]

    def attention_weights():
        scores = (
            jnp.einsum("sqhd,skhd->shqk", query_heads, all_keys, preferred_element_type=single)
            * scale
        )
        return jax.nn.softmax(jnp.where(allowed, scores, -1e30), axis=-1)

    probs = attention_weights()
    mixed = (
        jnp.einsum("shqk,skhd->sqhd", probs.astype(lowp), all_values, preferred_element_type=single)
        .reshape(rows_here, width)
        .astype(lowp)
    )
    attn_part = jnp.dot(mixed, full_out, preferred_element_type=single)
    after_attn = embedded + lax.psum(attn_part, "head")
    ffn_in = rms_norm(after_attn, gain_vals[1]).astype(lowp)
    hidden_pre = jnp.dot(ffn_in, full_up, preferred_element_type=single)
    hidden_act = jax.nn.gelu(hidden_pre).astype(lowp)
    ffn_part = jnp.dot(hidden_act, full_down, preferred_element_type=single)
    after_ffn = after_attn + lax.psum(ffn_part, "head")
    final_in = rms_norm(after_ffn, gain_vals[2]).astype(lowp)
    block_rows = math.gcd(rows_here, 512)
    blocks = rows_here // block_rows
    target_local = targets - first_word
    word_index = jnp.arange(vocab_here, dtype=jnp.int32)

    def logit_block(packed):
        inputs, wanted = packed
        logits = jnp.einsum("rd,vd->rv", inputs, full_table, preferred_element_type=single)
        highest = jnp.max(logits, axis=-1)
        summed = jnp.sum(jnp.exp(logits - highest[:, None]), axis=-1)
        hit = jnp.sum(jnp.where(wanted[:, None] == word_index[None, :], logits, 0.0), axis=-1)
        return (logits, highest, summed, hit)

    logits, highest, summed, hit = lax.map(
        logit_block, (final_in.reshape(blocks, block_rows, D), target_local)
    )

    def combine(first, second):
        upper = jnp.maximum(first[0], second[0])
        return (
            upper,
            first[1] * jnp.exp(first[0] - upper) + second[1] * jnp.exp(second[0] - upper),
            first[2] + second[2],
        )

    high_all, sum_all, hit_all = merged((highest, summed, hit), "head", combine)
    log_total = high_all + jnp.log(sum_all)
    counted = target_mask.astype(single)
    loss_local = jnp.sum(counted * (log_total - hit_all))
    count_local = jnp.sum(counted)
    onehot = (target_local[..., None] == word_index).astype(single)
    dlogits = ((jnp.exp(logits - log_total[..., None]) - onehot) * counted[..., None]).astype(lowp)
    dlog_flat = dlogits.reshape(rows_here, vocab_here)
    final_part = jnp.dot(dlog_flat, full_table, preferred_element_type=single)
    table_grad = jnp.einsum("rv,rd->vd", dlog_flat, final_in, preferred_element_type=single)
    final_grad = lax.psum(final_part, "head")
    grad_after_ffn, gain_three = norm_back(after_ffn, gain_vals[2], final_grad)
    down_in = grad_after_ffn.astype(lowp)
    act_grad = jnp.einsum("rd,fd->rf", down_in, full_down, preferred_element_type=single)
    down_grad = jnp.einsum("rf,rd->fd", hidden_act, down_in, preferred_element_type=single)
    pre_grad = jax.vjp(jax.nn.gelu, hidden_pre)[1](act_grad)[0].astype(lowp)
    up_grad = jnp.einsum("rd,rf->df", ffn_in, pre_grad, preferred_element_type=single)
    ffn_in_part = jnp.einsum("rf,df->rd", pre_grad, full_up, preferred_element_type=single)
    ffn_in_grad = lax.psum(ffn_in_part, "head")
    grad_mid, gain_two = norm_back(after_attn, gain_vals[1], ffn_in_grad)
    grad_after_attn = grad_after_ffn + grad_mid
    attn_in = grad_after_attn.astype(lowp)
    out_grad = jnp.einsum("rw,rd->wd", mixed, attn_in, preferred_element_type=single)
    mixed_grad = (
        jnp.einsum("rd,wd->rw", attn_in, full_out, preferred_element_type=single)
        .astype(lowp)
        .reshape(streams, seg_len, local_heads, DH)
    )
    probs = attention_weights()
    prob_grad = jnp.einsum("sqhd,skhd->shqk", mixed_grad, all_values, preferred_element_type=single)
    score_grad = (probs * (prob_grad - jnp.sum(probs * prob_grad, axis=-1, keepdims=True))).astype(
        lowp
    )
    query_grad = (
        (jnp.einsum("shqk,skhd->sqhd", score_grad, all_keys, preferred_element_type=single) * scale)
        .reshape(rows_here, width)
        .astype(lowp)
    )
    key_grad = (
        jnp.einsum("shqk,sqhd->skhd", score_grad, query_heads, preferred_element_type=single)
        * scale
    ).astype(lowp)
    value_grad = jnp.einsum(
        "shqk,sqhd->skhd", probs.astype(lowp), mixed_grad, preferred_element_type=single
    ).astype(lowp)

    def unsqueeze(grad_heads):
        spread = jnp.einsum(
            "sche,hjde->scjhd", grad_heads, conv_blocks, preferred_element_type=single
        )
        return spread.reshape(streams, RATE * CMEM, width).astype(lowp)

    comp_kg = key_grad[:, :CMEM]
    comp_vg = value_grad[:, :CMEM]
    conv_grad = (
        jnp.einsum("scjhd,sche->hjde", old_blocks(old_keys), comp_kg, preferred_element_type=single)
        + jnp.einsum(
            "scjhd,sche->hjde", old_blocks(old_values), comp_vg, preferred_element_type=single
        )
    ).reshape(local_heads, RATE * DH, DH)
    old_kg = unsqueeze(comp_kg)
    old_vg = unsqueeze(comp_vg)
    mem_kg = key_grad[:, CMEM : CMEM + MEM].reshape(streams, MEM, width)
    mem_vg = value_grad[:, CMEM : CMEM + MEM].reshape(streams, MEM, width)
    seg_kg = key_grad[:, CMEM + MEM :].reshape(rows_here, width)
    seg_vg = value_grad[:, CMEM + MEM :].reshape(rows_here, width)

    def weight_part(inputs, mem_in, old_in, seg_g, mem_g, old_g):
        return (
            jnp.einsum("rd,re->de", inputs, seg_g, preferred_element_type=single)
            + jnp.einsum("smd,sme->de", mem_in, mem_g, preferred_element_type=single)
            + jnp.einsum("smd,sme->de", old_in, old_g, preferred_element_type=single)
        )

    qkv_grad = jnp.stack(
        [
            jnp.einsum("rd,re->de", normed, query_grad, preferred_element_type=single),
            weight_part(normed, mem_normed, old_normed, seg_kg, mem_kg, old_kg),
            weight_part(normed, mem_normed, old_normed, seg_vg, mem_vg, old_vg),
        ]
    )

    def back_in(key_g, value_g):
        return jnp.einsum(
            "...e,de->...d", key_g, full_qkv[1], preferred_element_type=single
        ) + jnp.einsum("...e,de->...d", value_g, full_qkv[2], preferred_element_type=single)

    seg_in_part = back_in(seg_kg, seg_vg) + jnp.einsum(
        "re,de->rd", query_grad, full_qkv[0], preferred_element_type=single
    )
    side_part = gain_only(mem_float, gain_one, back_in(mem_kg, mem_vg)) + gain_only(
        old_float, gain_one, back_in(old_kg, old_vg)
    )
    seg_in_grad, side_gain = lax.psum((seg_in_part, side_part), "head")
    grad_embed_norm, gain_first = norm_back(embedded, gain_one, seg_in_grad)
    embed_grad = grad_after_attn + grad_embed_norm
    table_grad = table_grad + jax.ops.segment_sum(
        jnp.where(inside[:, None], embed_grad, 0.0), safe_ids, num_segments=vocab_here
    )
    gains_grad = jnp.stack([gain_first + side_gain, gain_two, gain_three])
    grads = (
        lax.psum_scatter(table_grad, "dp", scatter_dimension=1, tiled=True),
        lax.psum_scatter(qkv_grad, "dp", scatter_dimension=1, tiled=True),
        lax.psum_scatter(out_grad, "dp", scatter_dimension=1, tiled=True),
        lax.psum_scatter(conv_grad, "dp", scatter_dimension=2, tiled=True),
        lax.psum_scatter(up_grad, "dp", scatter_dimension=0, tiled=True),
        lax.psum_scatter(down_grad, "dp", scatter_dimension=1, tiled=True),
        lax.psum_scatter(gains_grad, "dp", scatter_dimension=1, tiled=True),
    )
    weights_now = (table, qkv, wout, wconv, wup, wdown)
    rows_old = (table_rows, qkv_rows, out_rows, conv_rows, up_rows, down_rows)
    cols_old = (table_cols, qkv_cols, out_cols, conv_cols, up_cols, down_cols)
    row_axes = ("head", "dp", "head", "head", "dp", "head")
    col_axes = ("dp", "head", "dp", "dp", "head", "dp")
    row_part = []
    col_part = []
    scalar_list = []
    for index in range(6):
        square = grads[index] * grads[index]
        row_part.append(jnp.sum(square, axis=-1))
        col_part.append(jnp.sum(square, axis=tuple(range(square.ndim - 1))))
        scalar_list.append(jnp.sum(square))
        scalar_list.append(jnp.sum(rows_old[index]) / axis_info[col_axes[index]][0])
    scalar_list.append(loss_local / heads_here)
    scalar_list.append(count_local / heads_here)
    scalar_part = jnp.stack(scalar_list)
    row_e, row_o, row_c, row_d, col_q, col_u = lax.psum(
        (row_part[0], row_part[2], row_part[3], row_part[5], col_part[1], col_part[4]), "dp"
    )
    row_q, row_u, col_e, col_o, col_c, col_d = lax.psum(
        (row_part[1], row_part[4], col_part[0], col_part[2], col_part[3], col_part[5]), "head"
    )
    scalars = lax.psum(scalar_part, ("dp", "head"))
    row_sums = [row_e, row_q, row_o, row_c, row_u, row_d]
    col_sums = [col_e, col_q, col_o, col_c, col_u, col_d]
    loss_all = scalars[12]
    count_all = scalars[13]
    inverse = 1.0 / count_all
    decay = 1.0 - STEP ** (-0.8)
    updates = []
    stats_new = []
    scaled = []
    counts = []
    update_sq = []
    weight_sq = []
    for index in range(6):
        rows_total = rows_old[index].size * axis_info[row_axes[index]][0]
        cols_total = cols_old[index].size * axis_info[col_axes[index]][0]
        grad_scaled = grads[index] * inverse
        rows_new = decay * rows_old[index] + (1.0 - decay) * (
            row_sums[index] * inverse * inverse / cols_total + TINY_SQUARE
        )
        cols_new = decay * cols_old[index] + (1.0 - decay) * (
            col_sums[index] * inverse * inverse / rows_total + TINY_SQUARE
        )
        mean_row = decay * scalars[2 * index + 1] / rows_total + (1.0 - decay) * (
            scalars[2 * index] * inverse * inverse / (rows_total * cols_total) + TINY_SQUARE
        )
        second = rows_new[..., None] * cols_new / mean_row
        direction = grad_scaled * lax.rsqrt(second)
        updates.append(direction)
        stats_new.append((rows_new, cols_new))
        scaled.append(grad_scaled)
        counts.append(rows_total * cols_total)
        update_sq.append(jnp.sum(direction * direction))
        weight_sq.append(jnp.sum(weights_now[index] * weights_now[index]))
    gain_scaled = grads[6] * inverse
    second_new = decay * gains_second + (1.0 - decay) * (gain_scaled * gain_scaled + TINY_SQUARE)
    gain_dir = gain_scaled * lax.rsqrt(second_new)
    for which in range(3):
        update_sq.append(jnp.sum(gain_dir[which] * gain_dir[which]) / heads_here)
        weight_sq.append(jnp.sum(gains[which] * gains[which]) / heads_here)
    update_total, weight_total = lax.psum(
        (jnp.stack(update_sq), jnp.stack(weight_sq)), ("dp", "head")
    )
    results = [loss_all, count_all]
    for index in range(6):
        factor = jnp.maximum(0.001, jnp.sqrt(weight_total[index] / counts[index]))
        denom = jnp.maximum(1.0, jnp.sqrt(update_total[index] / counts[index]) / CLIP_LEVEL)
        new_weight = weights_now[index] - LEARN_RATE * factor * updates[index] / denom
        results += [new_weight, scaled[index], stats_new[index][0], stats_new[index][1]]
    gain_factor = jnp.maximum(0.001, jnp.sqrt(weight_total[6:] / D))[:, None]
    gain_denom = jnp.maximum(1.0, jnp.sqrt(update_total[6:] / D) / CLIP_LEVEL)[:, None]
    results += [gains - LEARN_RATE * gain_factor * gain_dir / gain_denom, gain_scaled, second_new]
    return tuple(results)


def solution(mesh):
    in_specs = (
        P("dp", None),
        P("dp", None),
        P("dp", None),
        P("dp", None, None),
        P("dp", None, None),
        P("dp"),
        P("dp"),
        P("head", "dp"),
        P(None, "dp", "head"),
        P("head", "dp"),
        P("head", None, "dp"),
        P("dp", "head"),
        P("head", "dp"),
        P(None, "dp"),
        P("head"),
        P("dp"),
        P(None, "dp"),
        P("head"),
        P("head"),
        P("dp"),
        P("head", None),
        P("dp"),
        P("dp"),
        P("head"),
        P("head"),
        P("dp"),
        P(None, "dp"),
    )
    out_specs = (
        P(),
        P(),
        P("head", "dp"),
        P("head", "dp"),
        P("head"),
        P("dp"),
        P(None, "dp", "head"),
        P(None, "dp", "head"),
        P(None, "dp"),
        P("head"),
        P("head", "dp"),
        P("head", "dp"),
        P("head"),
        P("dp"),
        P("head", None, "dp"),
        P("head", None, "dp"),
        P("head", None),
        P("dp"),
        P("dp", "head"),
        P("dp", "head"),
        P("dp"),
        P("head"),
        P("head", "dp"),
        P("head", "dp"),
        P("head"),
        P("dp"),
        P(None, "dp"),
        P(None, "dp"),
        P(None, "dp"),
    )
    return jax.shard_map(local, mesh=mesh, in_specs=in_specs, out_specs=out_specs, check_vma=False)
```

profile of v0, /device:TPU:0, one launch (start us, length us, event | category | flops | bytes accessed | tf_op | source)
XLA Modules:
  0.0 2285.7 jit_solution(13200575617768252451)
XLA Ops:
  17.0 32.8 %all_gather.42 = bf16[2,384,128]{1,2,0:T(8,128)(2,1)S(1)} all-gather(bf16[2,384,16]{1,2,0:T(8,128)(2,1)S(1)} %get-tuple-element.403), channel_id=1, replica_groups=mesh['dp'=8,'head'=4] {'dp'}, dimensions={2}, use_global_device_ids=true | all-gather | bytes 221184 | tf_op jit(solution)/shard_map/all_gather | solution.py:107
  50.1 20.5 all_gather.40
  71.9 36.4 %all_gather.43 = bf16[256,1024]{1,0:T(8,128)(2,1)} all-gather(bf16[256,128]{1,0:T(8,128)(2,1)S(1)} %get-tuple-element.401), channel_id=1, replica_groups=mesh['dp'=8,'head'=4] {'dp'}, dimensions={1}, use_global_device_ids=true | all-gather | bytes 589824 | tf_op jit(solution)/shard_map/all_gather | solution.py:106
  127.8 162.4 %all-gather.11.cloned.1.call-done = bf16[8000,1024]{1,0:T(8,128)(2,1)} async-done(((bf16[8000,128]{1,0:T(8,128)(2,1)}), bf16[8000,1024]{1,0:T(8,128)(2,1)}) %all-gather.11.cloned.1.call-update) | async-done | bytes 16384016 | tf_op jit(solution)/shard_map/all_gather | solution.py:104
  290.2 13.8 gather_fusion
  323.6 33.2 %all-reduce.10.cloned.1.call-done = bf16[1024,1024]{1,0:T(8,128)(2,1)} async-done(((bf16[1024,1024]{1,0:T(8,128)(2,1)}), bf16[1024,1024]{1,0:T(8,128)(2,1)}) %all-reduce.10.cloned.1.call-update) | async-done | bytes 2097168 | tf_op jit(solution)/shard_map/psum | solution.py:120
  378.4 16.5 fusion.213
  409.0 82.8 %all-reduce.12.cloned.1.call-done = f32[1024,1024]{1,0:T(8,128)} async-done(((f32[1024,1024]{1,0:T(8,128)}), f32[1024,1024]{1,0:T(8,128)}) %all-reduce.12.cloned.1.call-update) | async-done | bytes 4194320 | tf_op jit(solution)/shard_map/psum | solution.py:166
  496.6 47.2 %all-gather.15.cloned.1.call-done = bf16[1024,1024]{1,0:T(8,128)(2,1)} async-done(((bf16[128,1024]{1,0:T(8,128)(2,1)}), bf16[1024,1024]{1,0:T(8,128)(2,1)}) %all-gather.15.cloned.1.call-update) | async-done | bytes 2097168 | tf_op jit(solution)/shard_map/all_gather | solution.py:108
  551.0 44.8 %all-gather.17.cloned.1.call-done = bf16[1024,1024]{1,0:T(8,128)(2,1)} async-done(((bf16[1024,128]{1,0:T(8,128)(2,1)}), bf16[1024,1024]{1,0:T(8,128)(2,1)}) %all-gather.17.cloned.1.call-update) | async-done | bytes 2097168 | tf_op jit(solution)/shard_map/all_gather | solution.py:109
  604.7 82.6 %all-reduce.14.cloned.1.call-done = f32[1024,1024]{1,0:T(8,128)} async-done(((f32[1024,1024]{1,0:T(8,128)}), f32[1024,1024]{1,0:T(8,128)}) %all-reduce.14.cloned.1.call-update) | async-done | bytes 4194320 | tf_op jit(solution)/shard_map/psum | solution.py:171
  693.7 71.8 %while.37 = (s32[]{:T(128)}, f32[2,512,8000]{1,2,0:T(8,128)}, f32[2,512]{1,0:T(2,128)S(1)}, f32[2,512]{1,0:T(2,128)S(1)}, f32[2,512]{1,0:T(2,128)S(1)}, /*index=...) while((s32[]{:T(128)}, f32[2,512,8000]{1,2,0:T(8,128)}, ...), condition=%wide.region_14.15_spmd.clone, body=%wide.region_10.14_spmd.clone.sunk | while | flops 8413182464 | bytes 82996352 | solution.py:186
  693.9 20.9 bitcast_dynamic-update-slice_fusion.2
  729.7 20.9 bitcast_dynamic-update-slice_fusion.2
  757.4 8.0 select_reduce_fusion.2
  782.2 20.5 multiply_convert_fusion
  802.7 20.7 copy.136
  823.4 23.6 %fusion.215 = f32[1024,1024]{1,0:T(8,128)} fusion(bf16[1024,8000]{1,0:T(8,128)(2,1)} %bitcast.300, bf16[8000,1024]{1,0:T(8,128)(2,1)} %get-tuple-element.633), kind=kOutput, calls=%fused_computation.334 | convolution fusion | flops 16777216000 | bytes 36962304 | tf_op jit(solution)/shard_map/dot_general | solution.py:206
  847.1 85.7 %all-reduce.16.cloned.1.call-done = f32[1024,1024]{1,0:T(8,128)} async-done(((f32[1024,1024]{1,0:T(8,128)}), f32[1024,1024]{1,0:T(8,128)}) %all-reduce.16.cloned.1.call-update) | async-done | bytes 4194320 | tf_op jit(solution)/shard_map/psum | solution.py:208
  952.3 85.5 %all-reduce.18.cloned.1.call-done = f32[1024,1024]{1,0:T(8,128)} async-done(((f32[1024,1024]{1,0:T(8,128)}), f32[1024,1024]{1,0:T(8,128)}) %all-reduce.18.cloned.1.call-update) | async-done | bytes 4194320 | tf_op jit(solution)/shard_map/psum | solution.py:216
  1050.0 10.4 multiply_reduce_fusion
  1142.0 8.3 fusion.139
  1150.5 25.8 %fusion.214 = f32[8000,1024]{1,0:T(8,128)} fusion(bf16[1024,8000]{1,0:T(8,128)(2,1)} %bitcast.301, bf16[1024,1024]{1,0:T(8,128)(2,1)} %bitcast.311), kind=kOutput, calls=%fused_computation.333 | convolution fusion | flops 16777216000 | bytes 51249152 | tf_op jit(solution)/shard_map/rv,rd->vd/dot_general | solution.py:207
  1180.0 33.2 %scatter_custom_fusion = f32[8000,1024]{1,0:T(8,128)} fusion(f32[8000,1024]{1,0:T(8,128)} %fusion.214, s32[1024]{0:T(1024)} %bitcast.353, f32[1024,1024]{1,0:T(8,128)} %copy-done.2, f32[]{:T(128)} %constant.261.clone.1, bf16[1024,1024]{1,0:T(8,128)(2,1)S(1)} %copy-done.6, f32[1024]{0:T(1024)S(1)} %multiply_multiply_fusion.4, ...), kind=kCustom, calls=%fused_computation.68 | custom fusion | flops 9437184 | bytes 43267584 | tf_op jit(solution)/shard_map/scatter-add | solution.py:294
  1241.6 62.2 %reduce-scatter.14.cloned.1.call-done = f32[256,128]{1,0:T(8,128)} async-done(((f32[256,1024]{1,0:T(8,128)}), f32[256,128]{1,0:T(8,128)}) %reduce-scatter.14.cloned.1.call-update) | async-done | bytes 131088 | tf_op jit(solution)/shard_map/reduce_scatter | solution.py:301
  1305.3 76.8 %reduce-scatter.12.cloned.1.call-done = f32[3,128,256]{2,1,0:T(8,128)} async-done(((f32[3,1024,256]{2,1,0:T(8,128)}), f32[3,128,256]{2,1,0:T(8,128)}) %reduce-scatter.12.cloned.1.call-update) | async-done | bytes 393232 | tf_op jit(solution)/shard_map/reduce_scatter | solution.py:300
  1383.9 89.3 %reduce-scatter.18.cloned.1.call-done = f32[128,1024]{1,0:T(8,128)} async-done(((f32[1024,1024]{1,0:T(8,128)}), f32[128,1024]{1,0:T(8,128)}) %reduce-scatter.18.cloned.1.call-update) | async-done | bytes 524304 | tf_op jit(solution)/shard_map/reduce_scatter | solution.py:303
  1475.0 89.9 %reduce-scatter.20.cloned.1.call-done = f32[1024,128]{1,0:T(8,128)} async-done(((f32[1024,1024]{1,0:T(8,128)}), f32[1024,128]{1,0:T(8,128)}) %reduce-scatter.20.cloned.1.call-update) | async-done | bytes 524304 | tf_op jit(solution)/shard_map/reduce_scatter | solution.py:304
  1566.8 533.1 %reduce-scatter.10.cloned.1.call-done = f32[8000,128]{1,0:T(8,128)} async-done(((f32[8000,1024]{1,0:T(8,128)}), f32[8000,128]{1,0:T(8,128)}) %reduce-scatter.10.cloned.1.call-update) | async-done | bytes 4096016 | tf_op jit(solution)/shard_map/reduce_scatter | solution.py:299
  2116.0 38.3 %psum.160 = f32[14]{0:T(128)S(1)} all-reduce(f32[14]{0:T(128)S(1)} %stack.143), channel_id=1, replica_groups=mesh['dp'=8,'head'=4] {'dp','head'}, use_global_device_ids=true, to_apply=%region_45.46 | all-reduce | flops 14 | bytes 112 | tf_op jit(solution)/shard_map/psum | solution.py:330
  2155.7 37.6 %all-reduce.1 = (f32[8000]{0:T(1024)S(1)}, f32[256]{0:T(256)S(1)}, f32[256]{0:T(256)S(1)}, f32[2,384]{1,0:T(2,128)S(1)}, f32[1024]{0:T(1024)S(1)}, /*index=5*/f32[1024]{0:T(1024)S(1)}) all-reduce(f32[8000]{0:T(1024)S(1)} %get-tuple-element.290, f32[256]{0:T(256)S(1)} %get-tuple-element.300, ...), channel_id=1, replica_groups=mesh['dp'=8,'head'=4] {'dp'}, use_global_device_ids=true, to_apply=%region_57.58 | all-reduce | flops 11328 | bytes 90624 | tf_op jit(solution)/shard_map/psum | solution.py:324
  2220.9 36.8 %all-reduce = (f32[9]{0:T(128)S(1)}, f32[9]{0:T(128)S(1)}) all-reduce(f32[9]{0:T(128)S(1)} %stack.165, f32[9]{0:T(128)S(1)} %stack.153), channel_id=1, replica_groups=mesh['dp'=8,'head'=4] {'dp','head'}, use_global_device_ids=true, to_apply=%region_96.97 | all-reduce | flops 18 | bytes 144 | tf_op jit(solution)/shard_map/psum | solution.py:370
  (527 shorter events, 343.3 us)
Async XLA Ops:
  7.2 107.8 %all-gather.13.cloned.1.call-start = ((), (), s32[]{:S(2)}) async-start(), calls=%async_computation.9 | async-start | bytes 1769472 | tf_op jit(solution)/shard_map/all_gather | solution.py:105
  9.7 280.4 %all-gather.11.cloned.1.call-start = ((), (), s32[]{:S(2)}) async-start(), calls=%async_computation.7 | async-start | bytes 18432000 | tf_op jit(solution)/shard_map/all_gather | solution.py:104
  16.2 340.5 %all-reduce.10.cloned.1.call-start = ((), (), s32[]{:S(2)}) async-start(), calls=%async_computation.8 | async-start | bytes 4194304 | tf_op jit(solution)/shard_map/psum | solution.py:120
  71.2 287.6 %copy-start.80 = (f32[1,1024]{1,0:T(1,128)}, f32[1,1024]{1,0:T(1,128)S(1)}, u32[]{:S(2)}) copy-start(f32[1,1024]{1,0:T(1,128)S(1)} %get-tuple-element.406) | copy-start | bytes 12292
  71.2 472.5 %copy-start.86 = (f32[1,1024]{1,0:T(1,128)}, f32[1,1024]{1,0:T(1,128)S(1)}, u32[]{:S(2)}) copy-start(f32[1,1024]{1,0:T(1,128)S(1)} %get-tuple-element.405) | copy-start | bytes 12292
  71.3 620.0 %copy-start.76 = (f32[1,1024]{1,0:T(1,128)}, f32[1,1024]{1,0:T(1,128)S(1)}, u32[]{:S(2)}) copy-start(f32[1,1024]{1,0:T(1,128)S(1)} %get-tuple-element.404) | copy-start | bytes 12292
  307.1 184.7 %all-reduce.12.cloned.1.call-start = ((), (), s32[]{:S(2)}) async-start(), calls=%async_computation.10 | async-start | bytes 8388608 | tf_op jit(solution)/shard_map/psum | solution.py:166
  406.0 137.7 %all-gather.15.cloned.1.call-start = ((), (), s32[]{:S(2)}) async-start(), calls=%async_computation.11 | async-start | bytes 2359296 | tf_op jit(solution)/shard_map/all_gather | solution.py:108
  407.5 188.4 %all-gather.17.cloned.1.call-start = ((), (), s32[]{:S(2)}) async-start(), calls=%async_computation.12 | async-start | bytes 2359296 | tf_op jit(solution)/shard_map/all_gather | solution.py:109
  408.9 278.3 %all-reduce.14.cloned.1.call-start = ((), (), s32[]{:S(2)}) async-start(), calls=%async_computation.13 | async-start | bytes 8388608 | tf_op jit(solution)/shard_map/psum | solution.py:171
  603.4 329.4 %all-reduce.16.cloned.1.call-start = ((), (), s32[]{:S(2)}) async-start(), calls=%async_computation.14 | async-start | bytes 8388608 | tf_op jit(solution)/shard_map/psum | solution.py:208
  847.0 190.8 %all-reduce.18.cloned.1.call-start = ((), (), s32[]{:S(2)}) async-start(), calls=%async_computation.15 | async-start | bytes 8388608 | tf_op jit(solution)/shard_map/psum | solution.py:216
  952.1 224.3 %all-reduce.20.cloned.1.call-start = ((), (), s32[]{:S(2)}) async-start(), calls=%async_computation.16 | async-start | bytes 8388608 | tf_op jit(solution)/shard_map/psum | solution.py:291
  1086.2 153.9 %reduce-scatter.16.cloned.1.call-start = ((), (), s32[]{:S(2)}) async-start(), calls=%async_computation.20 | async-start | bytes 442368 | tf_op jit(solution)/shard_map/reduce_scatter | solution.py:302
  1109.4 194.3 %reduce-scatter.14.cloned.1.call-start = ((), (), s32[]{:S(2)}) async-start(), calls=%async_computation.19 | async-start | bytes 1179648 | tf_op jit(solution)/shard_map/reduce_scatter | solution.py:301
  1115.9 266.3 %reduce-scatter.12.cloned.1.call-start = ((), (), s32[]{:S(2)}) async-start(), calls=%async_computation.18 | async-start | bytes 3538944 | tf_op jit(solution)/shard_map/reduce_scatter | solution.py:300
  1134.2 338.9 %reduce-scatter.18.cloned.1.call-start = ((), (), s32[]{:S(2)}) async-start(), calls=%async_computation.21 | async-start | bytes 4718592 | tf_op jit(solution)/shard_map/reduce_scatter | solution.py:303
  1142.0 422.9 %reduce-scatter.20.cloned.1.call-start = ((), (), s32[]{:S(2)}) async-start(), calls=%async_computation.22 | async-start | bytes 4718592 | tf_op jit(solution)/shard_map/reduce_scatter | solution.py:304
  1150.3 949.6 %reduce-scatter.10.cloned.1.call-start = ((), (), s32[]{:S(2)}) async-start(), calls=%async_computation.17 | async-start | bytes 36864000 | tf_op jit(solution)/shard_map/reduce_scatter | solution.py:299
  1213.3 999.5 %reduce-scatter.22.cloned.1.call-start = ((), (), s32[]{:S(2)}) async-start(), calls=%async_computation.23 | async-start | bytes 589824
  1240.0 871.0 %copy-start.98 = (f32[1024]{0:T(1024)S(1)}, f32[1024]{0:T(1024)}, u32[]{:S(2)}) copy-start(f32[1024]{0:T(1024)} %get-tuple-element.286) | copy-start | bytes 12292
  1240.0 871.0 %copy-start.99 = (f32[1024]{0:T(1024)S(1)}, f32[1024]{0:T(1024)}, u32[]{:S(2)}) copy-start(f32[1024]{0:T(1024)} %get-tuple-element.284) | copy-start | bytes 12292
  1240.0 959.9 %copy-start.129 = (f32[128]{0:T(128)S(1)}, f32[128]{0:T(128)}, u32[]{:S(2)}) copy-start(f32[128]{0:T(128)} %param.56) | copy-start | bytes 1540
  1240.0 960.6 %copy-start.121 = (f32[1024]{0:T(1024)S(1)}, f32[1024]{0:T(1024)}, u32[]{:S(2)}) copy-start(f32[1024]{0:T(1024)} %param.54) | copy-start | bytes 12292
  1240.0 960.6 %copy-start.130 = (f32[16]{0:T(128)S(1)}, f32[16]{0:T(128)}, u32[]{:S(2)}) copy-start(f32[16]{0:T(128)} %param.52) | copy-start | bytes 196
  1240.1 960.6 %copy-start.131 = (f32[128]{0:T(128)S(1)}, f32[128]{0:T(128)}, u32[]{:S(2)}) copy-start(f32[128]{0:T(128)} %param.50) | copy-start | bytes 1540
  1240.1 960.7 %copy-start.125 = (f32[256]{0:T(256)S(1)}, f32[256]{0:T(256)}, u32[]{:S(2)}) copy-start(f32[256]{0:T(256)} %param.48) | copy-start | bytes 3076
  1240.1 960.7 %copy-start.132 = (f32[128]{0:T(128)S(1)}, f32[128]{0:T(128)}, u32[]{:S(2)}) copy-start(f32[128]{0:T(128)} %param.46) | copy-start | bytes 1540
  1473.2 729.1 %copy-start.39 = (f32[128,1024]{1,0:T(8,128)S(1)}, f32[128,1024]{1,0:T(8,128)}, u32[]{:S(2)}) copy-start(f32[128,1024]{1,0:T(8,128)} %reduce-scatter.18.cloned.1.call-done) | copy-start | bytes 1572868
  1475.0 728.2 %copy-start.65 = (f32[256,128]{1,0:T(8,128)S(1)}, f32[256,128]{1,0:T(8,128)}, u32[]{:S(2)}) copy-start(f32[256,128]{1,0:T(8,128)} %reduce-scatter.14.cloned.1.call-done) | copy-start | bytes 393220
  1475.0 728.9 %copy-start.50 = (f32[3,128,256]{2,1,0:T(8,128)S(1)}, f32[3,128,256]{2,1,0:T(8,128)}, u32[]{:S(2)}) copy-start(f32[3,128,256]{2,1,0:T(8,128)} %reduce-scatter.12.cloned.1.call-done) | copy-start | bytes 1179652
  1564.9 636.6 %copy-start.40 = (f32[1024,128]{1,0:T(8,128)S(1)}, f32[1024,128]{1,0:T(8,128)}, u32[]{:S(2)}) copy-start(f32[1024,128]{1,0:T(8,128)} %reduce-scatter.20.cloned.1.call-done) | copy-start | bytes 1572868
  (132 other events, 4075.5 us)
Sparse Core Ops, SparseCore 0:
  10.8 47.5 all-gather.12
  61.0 229.1 all-gather.10
  307.2 49.5 all-reduce.9
  406.1 85.5 all-reduce.11
  494.3 49.4 all-gather.14
  546.2 49.5 all-gather.16
  603.5 83.6 all-reduce.13
  847.1 85.6 all-reduce.15
  952.2 85.6 all-reduce.17
  1086.4 85.6 all-reduce.19
  1175.9 61.5 reduce-scatter.15
  1240.7 62.9 reduce-scatter.13
  1308.3 73.7 reduce-scatter.11
  1386.0 87.0 reduce-scatter.17
  1476.6 88.2 reduce-scatter.19
  1569.2 530.6 reduce-scatter.9
  2116.2 60.4 reduce-scatter.21
where the time goes:
time: 2290 us
  waiting for transfers between devices  1480 us (65%)
  matrix products  238 us (10%)
  blocking collectives  225 us (10%)
  other arithmetic  204 us (9%)
  local copies, waits for them, and re-layouts  98.3 us (4%)
  between operations  42 us (2%)
    reduce_scatter x1, waiting for transfers between devices, local(): lax.psum_scatter(table_grad, 'dp', scatter_dimension=1, tiled=True)  533 us
    all_gather x1, waiting for transfers between devices, local(): lax.all_gather(table.astype(lowp), 'dp', axis=1, tiled=True)  162 us
    reduce_scatter x1, waiting for transfers between devices, local(): lax.psum_scatter(down_grad, 'dp', scatter_dimension=1, tiled=True)  89.9 us
    reduce_scatter x1, waiting for transfers between devices, local(): lax.psum_scatter(up_grad, 'dp', scatter_dimension=0, tiled=True)  89.3 us
    psum x1, waiting for transfers between devices, local(): final_grad = lax.psum(final_part, 'head')  85.7 us
    psum x1, waiting for transfers between devices, local(): ffn_in_grad = lax.psum(ffn_in_part, 'head')  85.5 us
    psum x1, waiting for transfers between devices, local(): after_attn = embedded + lax.psum(attn_part, 'head')  82.8 us
    psum x1, waiting for transfers between devices, local(): after_ffn = after_attn + lax.psum(ffn_part, 'head')  82.6 us
  transfers between devices with their start and end apart: 17, of which 13 were waited for; matrix products, arithmetic and copies ran while one was open for 10% of the time, Pallas kernels for 0%

commit v1 on v0

--- a/solution.py
+++ b/solution.py
@@ -28,6 +28,31 @@
         return combine(so_far, jax.tree.map(lambda part: part[k], everything))
 
     return lax.fori_loop(1, lax.axis_size(axis), turn, first)
+
+
+def swap(value, axis, mask):
+    size = lax.axis_size(axis)
+    return lax.ppermute(value, axis, [(i, i ^ mask) for i in range(size)])
+
+
+def head_sum(part):
+    rows, cols = part.shape
+    low_bit = lax.axis_index("head") % 2
+    high_bit = lax.axis_index("head") // 2
+    cut = part.astype(jnp.bfloat16).reshape(2, 2, rows // 4, cols)
+    kept = lax.dynamic_index_in_dim(cut, low_bit, 1, keepdims=False)
+    gone = lax.dynamic_index_in_dim(cut, 1 - low_bit, 1, keepdims=False)
+    half = kept.astype(jnp.float32) + swap(gone, "head", 1).astype(jnp.float32)
+    half = half.astype(jnp.bfloat16)
+    mine = lax.dynamic_index_in_dim(half, high_bit, 0, keepdims=False)
+    other = lax.dynamic_index_in_dim(half, 1 - high_bit, 0, keepdims=False)
+    own = mine.astype(jnp.float32) + swap(other, "head", 2).astype(jnp.float32)
+    own = own.astype(jnp.bfloat16)
+    far = swap(own, "head", 2)
+    pair = jnp.where(high_bit == 0, jnp.stack([own, far]), jnp.stack([far, own]))
+    near = swap(pair, "head", 1)
+    both = jnp.where(low_bit == 0, jnp.stack([pair, near], 1), jnp.stack([near, pair], 1))
+    return both.reshape(rows, cols).astype(jnp.float32)
 
 
 def rms_norm(values, gain):
@@ -117,7 +142,7 @@
     inside = (local_ids >= 0) & (local_ids < vocab_here)
     safe_ids = jnp.clip(local_ids, 0, vocab_here - 1)
     looked = jnp.where(inside[:, None], jnp.take(full_table, safe_ids, axis=0), jnp.zeros((), lowp))
-    embedded = lax.psum(looked.astype(single).astype(jnp.bfloat16), "head").astype(jnp.float32)
+    embedded = head_sum(looked)
     mem_float = memory.astype(single)
     old_float = old_states.astype(single)
     normed = rms_norm(embedded, gain_one).astype(lowp)
@@ -163,12 +188,12 @@
         .astype(lowp)
     )
     attn_part = jnp.dot(mixed, full_out, preferred_element_type=single)
-    after_attn = embedded + lax.psum(attn_part, "head")
+    after_attn = embedded + head_sum(attn_part)
     ffn_in = rms_norm(after_attn, gain_vals[1]).astype(lowp)
     hidden_pre = jnp.dot(ffn_in, full_up, preferred_element_type=single)
     hidden_act = jax.nn.gelu(hidden_pre).astype(lowp)
     ffn_part = jnp.dot(hidden_act, full_down, preferred_element_type=single)
-    after_ffn = after_attn + lax.psum(ffn_part, "head")
+    after_ffn = after_attn + head_sum(ffn_part)
     final_in = rms_norm(after_ffn, gain_vals[2]).astype(lowp)
     block_rows = math.gcd(rows_here, 512)
     blocks = rows_here // block_rows
@@ -205,7 +230,7 @@
     dlog_flat = dlogits.reshape(rows_here, vocab_here)
     final_part = jnp.dot(dlog_flat, full_table, preferred_element_type=single)
     table_grad = jnp.einsum("rv,rd->vd", dlog_flat, final_in, preferred_element_type=single)
-    final_grad = lax.psum(final_part, "head")
+    final_grad = head_sum(final_part)
     grad_after_ffn, gain_three = norm_back(after_ffn, gain_vals[2], final_grad)
     down_in = grad_after_ffn.astype(lowp)
     act_grad = jnp.einsum("rd,fd->rf", down_in, full_down, preferred_element_type=single)
@@ -213,7 +238,7 @@
     pre_grad = jax.vjp(jax.nn.gelu, hidden_pre)[1](act_grad)[0].astype(lowp)
     up_grad = jnp.einsum("rd,rf->df", ffn_in, pre_grad, preferred_element_type=single)
     ffn_in_part = jnp.einsum("rf,df->rd", pre_grad, full_up, preferred_element_type=single)
-    ffn_in_grad = lax.psum(ffn_in_part, "head")
+    ffn_in_grad = head_sum(ffn_in_part)
     grad_mid, gain_two = norm_back(after_attn, gain_vals[1], ffn_in_grad)
     grad_after_attn = grad_after_ffn + grad_mid
     attn_in = grad_after_attn.astype(lowp)
@@ -288,7 +313,7 @@
     side_part = gain_only(mem_float, gain_one, back_in(mem_kg, mem_vg)) + gain_only(
         old_float, gain_one, back_in(old_kg, old_vg)
     )
-    seg_in_grad, side_gain = lax.psum((seg_in_part, side_part), "head")
+    seg_in_grad, side_gain = head_sum(seg_in_part), lax.psum(side_part, "head")
     grad_embed_norm, gain_first = norm_back(embedded, gain_one, seg_in_grad)
     embed_grad = grad_after_attn + grad_embed_norm
     table_grad = table_grad + jax.ops.segment_sum(
@@ -296,12 +321,12 @@
     )
     gains_grad = jnp.stack([gain_first + side_gain, gain_two, gain_three])
     grads = (
-        lax.psum_scatter(table_grad, "dp", scatter_dimension=1, tiled=True),
-        lax.psum_scatter(qkv_grad, "dp", scatter_dimension=1, tiled=True),
-        lax.psum_scatter(out_grad, "dp", scatter_dimension=1, tiled=True),
+        lax.psum_scatter(table_grad.astype(lowp), "dp", scatter_dimension=1, tiled=True).astype(single),
+        lax.psum_scatter(qkv_grad.astype(lowp), "dp", scatter_dimension=1, tiled=True).astype(single),
+        lax.psum_scatter(out_grad.astype(lowp), "dp", scatter_dimension=1, tiled=True).astype(single),
         lax.psum_scatter(conv_grad, "dp", scatter_dimension=2, tiled=True),
-        lax.psum_scatter(up_grad, "dp", scatter_dimension=0, tiled=True),
-        lax.psum_scatter(down_grad, "dp", scatter_dimension=1, tiled=True),
+        lax.psum_scatter(up_grad.astype(lowp), "dp", scatter_dimension=0, tiled=True).astype(single),
+        lax.psum_scatter(down_grad.astype(lowp), "dp", scatter_dimension=1, tiled=True).astype(single),
         lax.psum_scatter(gains_grad, "dp", scatter_dimension=1, tiled=True),
     )
     weights_now = (table, qkv, wout, wconv, wup, wdown)

time: 2290 us -> 1590 us (0.69)
  waiting for transfers between devices: 1480 us -> 671 us
  local copies, waits for them, and re-layouts: 98.3 us -> 146 us
  other arithmetic: 204 us -> 242 us
    reduce_scatter x5 -> x2, waiting for transfers between devices: 851 us -> 17.8 us  [the longest x1 17.8 us: local(): lax.psum_scatter(qkv_grad.astype(lowp), 'dp', scatter_dimension=1, tiled=...]
    psum x6 -> x0, waiting for transfers between devices: 370 us -> none  [the longest x1 85.7 us: local(): final_grad = lax.psum(final_part, 'head')]
    unnamed x18 -> x15, waiting for transfers between devices: 0.28 us -> 340 us
    ppermute x0 -> x24, waiting for transfers between devices: none -> 143 us  [swap(): return lax.ppermute(value, axis, [(i, i ^ mask) for i in range(size)])]
    all_gather x1, waiting for transfers between devices: 47.2 us -> 0.01 us  [local(): lax.all_gather(wup.astype(lowp), 'dp', axis=0, tiled=True)]
    convert_element_type x0 -> x17, other arithmetic: none -> 43.5 us  [the longest x1 17.3 us: local(): table_grad.astype(lowp)]
    all_gather x1, waiting for transfers between devices: 44.8 us -> 6.79 us  [local(): lax.all_gather(wdown.astype(lowp), 'dp', axis=1, tiled=True)]
    unnamed x298 -> x365, local copies, waits for them, and re-layouts: 17.9 us -> 48.2 us
  transfers between devices with their start and end apart: 17 -> 35, of which waited for: 13 -> 25; matrix products, arithmetic and copies ran while one was open for 10% -> 23% of each run, Pallas kernels for 0% -> 0%
where the time goes in v1:
time: 1590 us; the launch traced here: 1580 us
  waiting for transfers between devices  671 us (42%)
  other arithmetic  242 us (15%)
  blocking collectives  228 us (14%)
  matrix products  227 us (14%)
  local copies, waits for them, and re-layouts  146 us (9%)
  between operations  42.3 us (3%)
  starting transfers between devices  20.2 us (1%)
    unnamed x15, waiting for transfers between devices  340 us
    all_gather x1, waiting for transfers between devices, local(): lax.all_gather(table.astype(lowp), 'dp', axis=1, tiled=True)  163 us
    ppermute x24, waiting for transfers between devices, swap(): return lax.ppermute(value, axis, [(i, i ^ mask) for i in range(size)])  143 us
    unnamed x365, local copies, waits for them, and re-layouts  48.2 us
    dot_general x2, matrix products, logit_block(): jnp.einsum('rd,vd->rv', inputs, full_table, preferred_element_type=single)  41.8 us
    all_gather x1, blocking collectives, local(): lax.all_gather(wout.astype(lowp), 'dp', axis=1, tiled=True)  38.8 us
    psum x1, blocking collectives, local(): scalars = lax.psum(scalar_part, ('dp', 'head'))  38.5 us
    psum x1, blocking collectives, local(): lax.psum((row_part[0], row_part[2], row_part[3], row_part[5], col_part[1]...  37.4 us
  transfers between devices with their start and end apart: 35, of which 25 were waited for; matrix products, arithmetic and copies ran while one was open for 23% of the time, Pallas kernels for 0%

profile of v1, /device:TPU:0, one launch (start us, length us, event | category | flops | bytes accessed | tf_op | source)
XLA Modules:
  0.0 1577.1 jit_solution(1562348526240942041)
XLA Ops:
  16.7 22.4 %all_gather.40 = bf16[3,1024]{1,0:T(4,128)(2,1)S(1)} all-gather(bf16[3,128]{1,0:T(4,128)(2,1)S(1)} %convert_element_type.577), channel_id=1, replica_groups=mesh['dp'=8,'head'=4] {'dp'}, dimensions={1}, use_global_device_ids=true | all-gather | bytes 6912 | tf_op jit(solution)/shard_map/all_gather | solution.py:135
  45.3 38.8 %all_gather.43 = bf16[256,1024]{1,0:T(8,128)(2,1)} all-gather(bf16[256,128]{1,0:T(8,128)(2,1)S(1)} %get-tuple-element.405), channel_id=1, replica_groups=mesh['dp'=8,'head'=4] {'dp'}, dimensions={1}, use_global_device_ids=true | all-gather | bytes 589824 | tf_op jit(solution)/shard_map/all_gather | solution.py:131
  84.7 163.4 %all-gather.11.cloned.1.call-done = bf16[8000,1024]{1,0:T(8,128)(2,1)} async-done(((bf16[8000,128]{1,0:T(8,128)(2,1)}), bf16[8000,1024]{1,0:T(8,128)(2,1)}) %all-gather.11.cloned.1.call-update) | async-done | bytes 16384016 | tf_op jit(solution)/shard_map/all_gather | solution.py:129
  248.2 12.7 gather_fusion
  263.8 31.7 %all_gather.42 = bf16[2,384,128]{1,2,0:T(8,128)(2,1)S(1)} all-gather(bf16[2,384,16]{1,2,0:T(8,128)(2,1)S(1)} %get-tuple-element.407), channel_id=1, replica_groups=mesh['dp'=8,'head'=4] {'dp'}, dimensions={2}, use_global_device_ids=true | all-gather | bytes 221184 | tf_op jit(solution)/shard_map/all_gather | solution.py:132
  368.4 16.9 %fusion.262 = (f32[2,2,512]{2,1,0:T(2,128)S(1)}, f32[2,2,512,1536]{3,2,1,0:T(8,128)}) fusion(f32[2,2,512,1536]{3,2,1,0:T(8,128)} %fusion.97, pred[2,512,1536]{2,1,0:T(8,128)(4,1)S(1)} %copy-done.82), kind=kOutput, calls=%fused_computation.431 | output fusion | flops 18875904 | bytes 26746880 | tf_op jit(solution)/shard_map/sub | solution.py:182
  403.0 11.7 collective-permute-done.5
  417.2 12.2 collective-permute-done.6
  462.1 12.5 collective-permute-done.9
  476.4 11.7 collective-permute-done.10
  499.2 71.8 %while.37 = (s32[]{:T(128)}, f32[2,512,8000]{1,2,0:T(8,128)}, f32[2,512]{1,0:T(2,128)S(1)}, f32[2,512]{1,0:T(2,128)S(1)}, f32[2,512]{1,0:T(2,128)S(1)}, /*index=...) while((s32[]{:T(128)}, f32[2,512,8000]{1,2,0:T(8,128)}, ...), condition=%wide.region_11.12_spmd.clone, body=%wide.region_7.11_spmd.clone.sunk | while | flops 8413182464 | bytes 82996352 | solution.py:211
  499.4 20.9 %bitcast_dynamic-update-slice_fusion.2 = (f32[2,512,8000]{1,2,0:T(8,128)}, f32[512,8000]{0,1:T(8,128)}) fusion(f32[2,512,8000]{1,2,0:T(8,128)} %get-tuple-element.575, s32[]{:T(128)} %get-tuple-element.574, bf16[8000,1024]{1,0:T(8,128)(2,1)} %get-tuple-element.591, bf16[2,512,1024]{2,1,0:T(8,128)(2,1)S(1)} %get-tuple-element.590), kind=kOutput, calls=%fused_computation.10.clone.1 | convolution fusion | flops 8388608000 | bytes 50201600 | tf_op jit(solution)/shard_map/while/body/eval_jaxpr/rd,vd->rv/dot_general | solution.py:205
  535.2 20.9 %bitcast_dynamic-update-slice_fusion.2 = (f32[2,512,8000]{1,2,0:T(8,128)}, f32[512,8000]{0,1:T(8,128)}) fusion(f32[2,512,8000]{1,2,0:T(8,128)} %get-tuple-element.575, s32[]{:T(128)} %get-tuple-element.574, bf16[8000,1024]{1,0:T(8,128)(2,1)} %get-tuple-element.591, bf16[2,512,1024]{2,1,0:T(8,128)(2,1)S(1)} %get-tuple-element.590), kind=kOutput, calls=%fused_computation.10.clone.1 | convolution fusion | flops 8388608000 | bytes 50201600 | tf_op jit(solution)/shard_map/while/body/eval_jaxpr/rd,vd->rv/dot_general | solution.py:205
  587.7 20.5 %multiply_convert_fusion = bf16[2,512,8000]{1,2,0:T(8,128)(2,1)} fusion(f32[2,512,8000]{1,2,0:T(8,128)} %get-tuple-element.257, f32[2,512]{1,0:T(2,128)S(1)} %copy-done.138, s32[2,512]{1,0:T(2,128)S(1)} %get-tuple-element.703, f32[2,512]{1,0:T(2,128)S(1)} %get-tuple-element.376), kind=kLoop, calls=%fused_computation.19 | loop fusion | flops 49152000 | bytes 49164288 | tf_op jit(solution)/shard_map/convert_element_type | solution.py:229
  608.3 20.6 %copy.207 = bf16[2,512,8000]{2,1,0:T(8,128)(2,1)} copy(bf16[2,512,8000]{1,2,0:T(8,128)(2,1)} %multiply_convert_fusion) | data formatting | bytes 32768000 | tf_op jit(solution)/shard_map/convert_element_type | solution.py:229
  628.8 21.9 %convolution_convert_fusion.2 = bf16[1024,1024]{1,0:T(8,128)(2,1)S(1)} fusion(bf16[1024,8000]{1,0:T(8,128)(2,1)} %bitcast.538, bf16[8000,1024]{1,0:T(8,128)(2,1)} %get-tuple-element.641), kind=kOutput, calls=%fused_computation.147 | convolution fusion | flops 16778264576 | bytes 34865152 | tf_op jit(solution)/shard_map/dot_general | solution.py:231
  655.5 12.7 collective-permute-done.13
  670.0 11.9 collective-permute-done.14
  703.0 12.7 collective-permute-done.17
  717.4 11.9 collective-permute-done.18
  745.4 12.4 multiply_reduce_fusion
  880.2 11.7 fusion.252
  893.8 25.8 %fusion.264 = f32[8000,1024]{1,0:T(8,128)} fusion(bf16[1024,8000]{1,0:T(8,128)(2,1)} %bitcast.539, bf16[1024,1024]{1,0:T(8,128)(2,1)} %bitcast.599), kind=kOutput, calls=%fused_computation.433 | convolution fusion | flops 16777216000 | bytes 51249152 | tf_op jit(solution)/shard_map/rv,rd->vd/dot_general | solution.py:232
  925.7 33.7 %scatter_custom_fusion = f32[8000,1024]{1,0:T(8,128)} fusion(f32[8000,1024]{1,0:T(8,128)} %fusion.264, s32[1024]{0:T(1024)S(1)} %bitcast.655, f32[1024,1024]{1,0:T(8,128)} %copy-done.8, f32[1024,1024]{1,0:T(8,128)} %bitcast_multiply_fusion.5, f32[1024,1024]{1,0:T(8,128)} %fusion.40, f32[]{:T(128)} %constant.355.clone.1, pred[1024]{0:T(1024)(128)(4,1)S(1)} %and.102), kind=kCustom, calls=%fused_computation.66 | custom fusion | flops 5242880 | bytes 45352448 | tf_op jit(solution)/shard_map/scatter-add | solution.py:319
  959.4 17.3 %convert_element_type.686 = bf16[8000,1024]{1,0:T(8,128)(2,1)} convert(f32[8000,1024]{1,0:T(8,128)} %scatter_custom_fusion) | non-fusion elementwise | flops 8192000 | bytes 49152000 | tf_op jit(solution)/shard_map/convert_element_type | solution.py:324
  976.7 20.6 %copy.277 = bf16[8000,1024]{0,1:T(8,128)(2,1)} copy(bf16[8000,1024]{1,0:T(8,128)(2,1)} %convert_element_type.686) | data formatting | bytes 32768000
  1029.4 17.8 %reduce-scatter.16.cloned.1.call-done = bf16[3,128,256]{2,1,0:T(8,128)(2,1)} async-done(((bf16[3,1024,256]{2,1,0:T(8,128)(2,1)}), bf16[3,128,256]{2,1,0:T(8,128)(2,1)}) %reduce-scatter.16.cloned.1.call-update) | async-done | bytes 196624 | tf_op jit(solution)/shard_map/reduce_scatter | solution.py:325
  1051.2 61.1 %reduce-scatter.24.cloned.1.call-done = bf16[128,256]{1,0:T(8,128)(2,1)} async-done(((bf16[1024,256]{1,0:T(8,128)(2,1)}), bf16[128,256]{1,0:T(8,128)(2,1)}) %reduce-scatter.24.cloned.1.call-update) | async-done | bytes 65552
  1114.0 278.8 %reduce-scatter.22.cloned.1.call-done = bf16[128,8000]{1,0:T(8,128)(2,1)} async-done(((bf16[1024,8000]{1,0:T(8,128)(2,1)}), bf16[128,8000]{1,0:T(8,128)(2,1)}) %reduce-scatter.22.cloned.1.call-update) | async-done | bytes 2048016
  1409.9 38.5 %psum.112 = f32[14]{0:T(128)S(1)} all-reduce(f32[14]{0:T(128)S(1)} %stack.417), channel_id=1, replica_groups=mesh['dp'=8,'head'=4] {'dp','head'}, use_global_device_ids=true, to_apply=%region_39.40 | all-reduce | flops 14 | bytes 112 | tf_op jit(solution)/shard_map/psum | solution.py:355
  1449.7 37.4 %all-reduce.1 = (f32[8000]{0:T(1024)S(1)}, f32[256]{0:T(256)S(1)}, f32[256]{0:T(256)S(1)}, f32[2,384]{1,0:T(2,128)S(1)}, f32[1024]{0:T(1024)S(1)}, /*index=5*/f32[1024]{0:T(1024)S(1)}) all-reduce(f32[8000]{0:T(1024)S(1)} %get-tuple-element.288, f32[256]{0:T(256)S(1)} %get-tuple-element.298, ...), channel_id=1, replica_groups=mesh['dp'=8,'head'=4] {'dp'}, use_global_device_ids=true, to_apply=%region_51.52 | all-reduce | flops 11328 | bytes 90624 | tf_op jit(solution)/shard_map/psum | solution.py:349
  1512.4 36.8 %all-reduce = (f32[9]{0:T(128)S(1)}, f32[9]{0:T(128)S(1)}) all-reduce(f32[9]{0:T(128)S(1)} %stack.439, f32[9]{0:T(128)S(1)} %stack.427), channel_id=1, replica_groups=mesh['dp'=8,'head'=4] {'dp','head'}, use_global_device_ids=true, to_apply=%region_90.91 | all-reduce | flops 18 | bytes 144 | tf_op jit(solution)/shard_map/psum | solution.py:395
  (672 shorter events, 454.9 us)
Async XLA Ops:
  7.2 240.9 %all-gather.11.cloned.1.call-start = ((), (), s32[]{:S(2)}) async-start(), calls=%async_computation.7 | async-start | bytes 18432000 | tf_op jit(solution)/shard_map/all_gather | solution.py:129
  13.6 287.8 %all-gather.13.cloned.1.call-start = ((), (), s32[]{:S(2)}) async-start(), calls=%async_computation.8 | async-start | bytes 1769472 | tf_op jit(solution)/shard_map/all_gather | solution.py:130
  15.0 423.5 %all-gather.15.cloned.1.call-start = ((), (), s32[]{:S(2)}) async-start(), calls=%async_computation.9 | async-start | bytes 2359296 | tf_op jit(solution)/shard_map/all_gather | solution.py:133
  16.5 435.3 %all-gather.17.cloned.1.call-start = ((), (), s32[]{:S(2)}) async-start(), calls=%async_computation.10 | async-start | bytes 2359296 | tf_op jit(solution)/shard_map/all_gather | solution.py:134
  263.8 33.8 %collective-permute-start = (bf16[2,256,1024]{2,1,0:T(8,128)(2,1)}, bf16[2,256,1024]{2,1,0:T(8,128)(2,1)}, u32[]{:S(2)}, u32[]{:S(2)}) collective-permute-start(bf16[2,256,1024]{2,1,0:T(8,128)(2,1)} %dynamic-slice_bitcast_fusion.5), channel_id=1, source_target_pairs={{0,1},{1,0},{2,3},{3,2},{4,5},{5,4},{6,7},{7,6},{8,9},{9,8},{10,11... | collective-permute-start | bytes 3145736 | tf_op jit(solution)/shard_map/ppermute | solution.py:35
  300.0 12.6 collective-permute-start.1
  313.9 9.2 collective-permute-start.2
  324.3 20.4 %collective-permute-start.3 = (bf16[2,256,1024]{2,1,0:T(8,128)(2,1)}, bf16[2,256,1024]{2,1,0:T(8,128)(2,1)S(1)}, u32[]{:S(2)}, u32[]{:S(2)}) collective-permute-start(bf16[2,256,1024]{2,1,0:T(8,128)(2,1)} %maximum_select_fusion.6), channel_id=1, source_target_pairs={{0,1},{1,0},{2,3},{3,2},{4,5},{5,4},{6,7},{7,6},{8,9},{9,8},{10,11... | collective-permute-start | bytes 3145736 | tf_op jit(solution)/shard_map/ppermute | solution.py:35
  395.8 2.9 collective-permute-start.4
  400.3 14.4 collective-permute-start.5
  402.9 621.5 %reduce-scatter.18.cloned.1.call-start = ((), (), s32[]{:S(2)}) async-start(), calls=%async_computation.12 | async-start | bytes 442368 | tf_op jit(solution)/shard_map/reduce_scatter | solution.py:327
  415.9 13.6 collective-permute-start.6
  429.6 2.7 collective-permute-start.7
  457.4 2.7 collective-permute-start.8
  460.6 14.0 collective-permute-start.9
  474.9 13.2 collective-permute-start.10
  489.3 3.0 collective-permute-start.11
  650.8 2.7 collective-permute-start.12
  654.0 14.2 collective-permute-start.13
  668.4 13.4 collective-permute-start.14
  701.4 14.2 collective-permute-start.17
  715.9 13.4 collective-permute-start.18
  778.0 247.8 %reduce-scatter.26.cloned.1.call-start = ((), (), s32[]{:S(2)}) async-start(), calls=%async_computation.16 | async-start | bytes 2359296
  789.6 238.1 %reduce-scatter.20.cloned.1.call-start = ((), (), s32[]{:S(2)}) async-start(), calls=%async_computation.13 | async-start | bytes 2359296 | tf_op jit(solution)/shard_map/reduce_scatter | solution.py:328
  795.6 251.6 %reduce-scatter.16.cloned.1.call-start = ((), (), s32[]{:S(2)}) async-start(), calls=%async_computation.11 | async-start | bytes 1769472 | tf_op jit(solution)/shard_map/reduce_scatter | solution.py:325
  818.3 27.7 %collective-permute-start.20 = (bf16[2,256,1024]{2,1,0:T(8,128)(2,1)}, bf16[2,256,1024]{2,1,0:T(8,128)(2,1)}, u32[]{:S(2)}, u32[]{:S(2)}) collective-permute-start(bf16[2,256,1024]{2,1,0:T(8,128)(2,1)} %dynamic-slice_bitcast_fusion), channel_id=1, source_target_pairs={{0,1},{1,0},{2,3},{3,2},{4,5},{5,4},{6,7},{7,6},{8,9},{9,8},{10,11... | collective-permute-start | bytes 3145736 | tf_op jit(solution)/shard_map/ppermute | solution.py:35
  847.7 14.2 collective-permute-start.21
  862.2 13.5 collective-permute-start.22
  876.9 3.3 collective-permute-start.23
  878.2 234.1 %reduce-scatter.24.cloned.1.call-start = ((), (), s32[]{:S(2)}) async-start(), calls=%async_computation.15 | async-start | bytes 589824
  893.7 499.1 %reduce-scatter.22.cloned.1.call-start = ((), (), s32[]{:S(2)}) async-start(), calls=%async_computation.14 | async-start | bytes 18579456
  997.4 507.0 %reduce-scatter.28.cloned.1.call-start = ((), (), s32[]{:S(2)}) async-start(), calls=%async_computation.17 | async-start | bytes 589824
  (177 other events, 6080.7 us)
Sparse Core Ops, SparseCore 0:
  13.8 234.3 all-gather.10
  250.9 43.9 all-gather.12
  297.6 48.2 all-gather.14
  403.0 48.7 all-gather.16
  778.1 59.5 reduce-scatter.17
  841.1 66.7 reduce-scatter.25
  911.5 66.9 reduce-scatter.19
  982.5 64.5 reduce-scatter.15
  1051.4 60.8 reduce-scatter.23
  1116.2 276.5 reduce-scatter.21
  1410.0 59.9 reduce-scatter.27

commit v2 on v0

v2 whole, which is shorter than its diff:
```python
import functools

import jax
import jax.numpy as jnp
from jax import lax
from jax.experimental import pallas as pl
from jax.experimental.pallas import tpu as pltpu
from jax.sharding import PartitionSpec as P

D = 1024
H = 8
DH = 128
MEM = 512
CMEM = 512
RATE = 3
STEP = 10


TINY_NORM = 1e-06
TINY_SQUARE = 1e-30
LEARN_RATE = 0.5
CLIP_LEVEL = 1.0

lowp = jnp.bfloat16
single = jnp.float32
NT = (((1,), (1,)), ((), ()))
TN = (((0,), (0,)), ((), ()))
NN = (((1,), (0,)), ((), ()))
MIB = 1024 * 1024


def mm(left, right, dims=NN):
    return lax.dot_general(left, right, dims, preferred_element_type=single)


def swap(value, axis, mask):
    size = lax.axis_size(axis)
    return lax.ppermute(value, axis, [(i, i ^ mask) for i in range(size)])


def after(value, dep):
    return lax.optimization_barrier((value, dep))[0]


def block_order(size):
    return list(range(0, size, 2)) + list(range(1, size, 2))


def gather_blocks(piece, axis):
    size = lax.axis_size("dp")
    near = jnp.concatenate([piece] + [swap(piece, "dp", m) for m in range(2, size, 2)], axis=axis)
    return jnp.concatenate([near, swap(near, "dp", 1)], axis=axis)


def split(value, axis, parts):
    width = value.shape[axis] // parts
    return [lax.slice_in_dim(value, i * width, (i + 1) * width, axis=axis) for i in range(parts)]


def reduce_blocks(own, far, axis):
    size = lax.axis_size("dp")
    total = own + swap(far.astype(lowp), "head", 2).astype(single)
    keep, send = split(total, axis, 2)
    keep = keep + swap(send.astype(lowp), "dp", 1).astype(single)
    pieces = split(keep, axis, size // 2)
    result = pieces[0]
    for i in range(1, size // 2):
        result = result + swap(pieces[i].astype(lowp), "dp", 2 * i).astype(single)
    return result


def reorder(value, mask):
    if mask == 0:
        return value
    order = block_order(lax.axis_size("dp"))
    cols = split(value, 1, len(order))
    return jnp.concatenate([cols[order.index(j ^ mask)] for j in order], axis=1)


def relative(value, x, c):
    value = jnp.where(x == 1, jnp.flip(value, -3), value)
    value = jnp.where(c == 1, jnp.flip(value, -2), value)
    return jnp.swapaxes(value, -3, -2)


def rms(values, gain):
    inv = lax.rsqrt(jnp.mean(values * values, axis=-1, keepdims=True) + TINY_NORM)
    return (values * inv * gain).astype(lowp), inv


def rms_back(values, inv, gain, upstream):
    scaled = gain * upstream
    inner = jnp.sum(scaled * values, axis=-1, keepdims=True) / D
    return scaled * inv - values * (inner * inv * inv * inv)


def vmem(shape=None, index=None):
    if shape is None:
        return pl.BlockSpec(memory_space=pltpu.VMEM)
    return pl.BlockSpec(shape, index)


def smem():
    return pl.BlockSpec(memory_space=pltpu.SMEM)


def params(mib):
    return pltpu.CompilerParams(vmem_limit_bytes=mib * MIB)


def lookup_kernel(first_ref, ids_ref, table_ref, out_ref, tok_ref, row_ref, count_ref, held):
    total = ids_ref.shape[0]
    vocab = table_ref.shape[0]
    first = first_ref[0]

    def group(g, count):
        for j in range(8):
            t = g * 8 + j
            word = ids_ref[t] - first
            inside = jnp.logical_and(word >= 0, word < vocab)
            safe = jnp.where(inside, word, 0)
            flag = jnp.where(inside, 1, 0)
            held[pl.ds(t, 1), :] = table_ref[pl.ds(safe, 1), :] * flag.astype(single)
            tok_ref[count] = t
            row_ref[count] = safe
            count = count + flag
        return count

    count = lax.fori_loop(0, total // 8, group, jnp.int32(0))
    for j in range(8):
        tok_ref[count + j] = total
        row_ref[count + j] = 0
    count_ref[0] = count

    @pl.loop(0, total // 512)
    def _(i):
        rows = pl.ds(pl.multiple_of(i * 512, 512), 512)
        out_ref[rows, :] = held[rows, :].astype(lowp)


def lookup(first, ids, table):
    total = ids.shape[0]
    width = table.shape[1]
    return pl.pallas_call(
        lookup_kernel,
        out_shape=(
            jax.ShapeDtypeStruct((total, width), lowp),
            jax.ShapeDtypeStruct((total + 8,), jnp.int32),
            jax.ShapeDtypeStruct((total + 8,), jnp.int32),
            jax.ShapeDtypeStruct((1,), jnp.int32),
        ),
        in_specs=[smem(), smem(), vmem()],
        out_specs=(vmem(), smem(), smem(), smem()),
        scratch_shapes=[pltpu.VMEM((total, width), single)],
        compiler_params=params(40),
    )(first, ids, table)


def scatter_kernel(count_ref, tok_ref, row_ref, base_ref, grad_ref, out_ref, rows):
    total = grad_ref.shape[0]
    vocab = base_ref.shape[0]

    @pl.loop(0, total // 512)
    def _(i):
        here = pl.ds(pl.multiple_of(i * 512, 512), 512)
        rows[here, :] = grad_ref[here, :].astype(single)

    rows[pl.ds(total, 8), :] = jnp.zeros((8, rows.shape[1]), single)

    @pl.loop(0, vocab // 400)
    def _(i):
        here = pl.ds(pl.multiple_of(i * 400, 400), 400)
        out_ref[here, :] = base_ref[here, :]

    def group(g, carry):
        for j in range(8):
            token = tok_ref[g * 8 + j]
            row = row_ref[g * 8 + j]
            out_ref[pl.ds(row, 1), :] = out_ref[pl.ds(row, 1), :] + rows[pl.ds(token, 1), :]
        return carry

    lax.fori_loop(0, (count_ref[0] + 7) // 8, group, jnp.int32(0))


def scatter(count, tok, row, base, grad):
    total, width = grad.shape
    return pl.pallas_call(
        scatter_kernel,
        out_shape=jax.ShapeDtypeStruct(base.shape, single),
        in_specs=[smem(), smem(), smem(), vmem(), vmem()],
        out_specs=vmem(),
        scratch_shapes=[pltpu.VMEM((total + 8, width), single)],
        compiler_params=params(48),
    )(count, tok, row, base, grad)


def state_kernel(order, width, place_ref, gain_ref, in_ref, out_ref, held):
    rows = in_ref.shape[1]
    values = in_ref[0].astype(single)
    inv = lax.rsqrt(jnp.mean(values * values, axis=-1, keepdims=True) + TINY_NORM)
    for p, j in enumerate(order):
        start = pl.multiple_of((place_ref[1] ^ j) * width, width)
        block = in_ref[0, :, pl.ds(start, width)].astype(single)
        held[p] = block * inv * gain_ref[:, p * width : (p + 1) * width]
    groups = out_ref.shape[0]
    for p in range(len(order)):
        cols = slice(p * width, (p + 1) * width)
        if groups == 1:
            out_ref[0, :, cols] = held[p].astype(lowp)
        else:
            for j in range(groups):
                part = held[p, pl.ds(j, rows // groups, stride=groups), :]
                out_ref[j, :, cols] = part.astype(lowp)


def state_norm(place, gain, states, groups):
    size = lax.axis_size("dp")
    order = block_order(size)
    width = D // size
    count = states.shape[1] // groups
    if width % 128:
        values = lax.dynamic_index_in_dim(states, place[0], 0, keepdims=False).astype(single)
        inv = lax.rsqrt(jnp.mean(values * values, axis=-1, keepdims=True) + TINY_NORM)
        lanes = jnp.arange(D, dtype=jnp.int32)
        blocks = jnp.asarray(order, jnp.int32)[lanes // width] ^ place[1]
        source = blocks * width + lanes % width
        shuffle = (lanes[:, None] == source[None, :]).astype(single)
        moved = jnp.dot(values * inv, shuffle, precision=lax.Precision.HIGHEST)
        out = (moved * gain).astype(lowp)
        return jnp.swapaxes(out.reshape(count, groups, D), 0, 1)
    tile = 128
    return pl.pallas_call(
        functools.partial(state_kernel, order, width),
        out_shape=jax.ShapeDtypeStruct((groups, count, D), lowp),
        grid_spec=pltpu.PrefetchScalarGridSpec(
            num_scalar_prefetch=1,
            grid=(count // tile,),
            in_specs=[
                pl.BlockSpec((1, D), lambda i, s: (0, 0)),
                pl.BlockSpec((1, tile * groups, D), lambda i, s: (s[0], i, 0)),
            ],
            out_specs=pl.BlockSpec((groups, tile, D), lambda i, s: (0, i, 0)),
            scratch_shapes=[pltpu.VMEM((len(order), tile * groups, width), single)],
        ),
        compiler_params=params(24),
    )(place, gain, states)


def compress_kernel(old_ref, weight_ref, conv_ref, comp_ref, raw_ref):
    heads = conv_ref.shape[0]
    sums = [None] * (2 * heads)
    for j in range(RATE):
        raw = mm(old_ref[j], weight_ref[...]).astype(lowp)
        raw_ref[j] = raw
        for n in range(2 * heads):
            piece = raw[:, n * DH : (n + 1) * DH]
            term = mm(piece, conv_ref[n % heads, j * DH : (j + 1) * DH, :])
            sums[n] = term if j == 0 else sums[n] + term
    for n in range(2 * heads):
        comp_ref[:, n * DH : (n + 1) * DH] = sums[n].astype(lowp)


def compress(old3, weight, conv):
    rows = old3.shape[1]
    wide = weight.shape[1]
    tile = 256
    return pl.pallas_call(
        compress_kernel,
        grid=(rows // tile,),
        out_shape=(
            jax.ShapeDtypeStruct((rows, wide), lowp),
            jax.ShapeDtypeStruct((RATE, rows, wide), lowp),
        ),
        in_specs=[
            pl.BlockSpec((RATE, tile, D), lambda i: (0, i, 0)),
            pl.BlockSpec(weight.shape, lambda i: (0, 0)),
            pl.BlockSpec(conv.shape, lambda i: (0, 0, 0)),
        ],
        out_specs=(
            pl.BlockSpec((tile, wide), lambda i: (i, 0)),
            pl.BlockSpec((RATE, tile, wide), lambda i: (0, i, 0)),
        ),
        compiler_params=params(40),
    )(old3, weight, conv)


def expand_kernel(grad_ref, raw_ref, conv_ref, out_ref, conv_out_ref):
    heads = conv_ref.shape[0]
    for h in range(heads):
        for j in range(RATE):
            rows = slice(j * DH, (j + 1) * DH)
            taps = conv_ref[h, rows, :]
            total = None
            for n in (h, heads + h):
                cols = slice(n * DH, (n + 1) * DH)
                grad = grad_ref[:, cols]
                out_ref[j, :, cols] = mm(grad, taps, NT).astype(lowp)
                term = mm(raw_ref[j, :, cols], grad, TN)
                total = term if total is None else total + term
            conv_out_ref[h, rows, :] = total


def expand(grad, raw, conv):
    return pl.pallas_call(
        expand_kernel,
        out_shape=(
            jax.ShapeDtypeStruct(raw.shape, lowp),
            jax.ShapeDtypeStruct(conv.shape, single),
        ),
        in_specs=[vmem()] * 3,
        out_specs=(vmem(), vmem()),
        compiler_params=params(40),
    )(grad, raw, conv)


def masked_scores(info_ref, query, keys):
    rows = query.shape[0]
    scale = DH ** (-0.5)
    result = []
    for which, key in enumerate(keys):
        slots = key.shape[0]
        col = lax.broadcasted_iota(jnp.int32, (rows, slots), 1)
        if which < 2:
            seen = col >= slots - info_ref[which]
        else:
            row = lax.broadcasted_iota(jnp.int32, (rows, slots), 0)
            shift = info_ref[2]
            row = row + shift
            col = col + shift
            row = jnp.where(row >= slots, row - slots, row)
            col = jnp.where(col >= slots, col - slots, col)
            seen = col <= row
        result.append(jnp.where(seen, mm(query, key, NT) * scale, -1e30))
    return result


def attend_kernel(info_ref, q_ref, ks_ref, vs_ref, kc_ref, vc_ref, km_ref, vm_ref, out_ref, lse_ref):
    query = q_ref[...]
    scores = masked_scores(info_ref, query, [kc_ref[...], km_ref[...], ks_ref[...]])
    top = functools.reduce(jnp.maximum, [jnp.max(s, axis=-1, keepdims=True) for s in scores])
    total = 0.0
    mixed = 0.0
    for score, value in zip(scores, (vc_ref, vm_ref, vs_ref)):
        weight = jnp.exp(score - top)
        total = total + jnp.sum(weight, axis=-1, keepdims=True)
        mixed = mixed + mm(weight.astype(lowp), value[...])
    out_ref[...] = (mixed / total).astype(lowp)
    lse_ref[0] = top + jnp.log(total)


def attend_back_kernel(
    info_ref, q_ref, ks_ref, vs_ref, kc_ref, vc_ref, km_ref, vm_ref, lse_ref, up_ref,
    seg_ref, comp_ref, mem_ref,
):
    head = pl.program_id(0)
    wide = pl.num_programs(0) * DH
    scale = DH ** (-0.5)
    query = q_ref[...]
    upstream = up_ref[...]
    keys = [kc_ref[...], km_ref[...], ks_ref[...]]
    scores = masked_scores(info_ref, query, keys)
    probs = [jnp.exp(s - lse_ref[0]) for s in scores]
    prob_grads = [mm(upstream, v[...], NT) for v in (vc_ref, vm_ref, vs_ref)]
    inner = 0.0
    for p, g in zip(probs, prob_grads):
        inner = inner + jnp.sum(p * g, axis=-1, keepdims=True)
    here = pl.ds(pl.multiple_of(head * DH, DH), DH)
    second = pl.ds(pl.multiple_of(wide + head * DH, DH), DH)
    third = pl.ds(pl.multiple_of(2 * wide + head * DH, DH), DH)
    query_grad = 0.0
    places = ((comp_ref, here, second), (mem_ref, here, second), (seg_ref, second, third))
    for p, g, key, (ref, key_at, value_at) in zip(probs, prob_grads, keys, places):
        score_grad = (p * (g - inner)).astype(lowp)
        query_grad = query_grad + mm(score_grad, key)
        ref[:, key_at] = (mm(score_grad, query, TN) * scale).astype(lowp)
        ref[:, value_at] = mm(p.astype(lowp), upstream, TN).astype(lowp)
    seg_ref[:, here] = (query_grad * scale).astype(lowp)


def head_specs(seg, comp, mem, heads):
    def cols(array, first):
        return pl.BlockSpec((array.shape[0], DH), lambda h: (0, first + h))

    return [
        smem(),
        cols(seg, 0),
        cols(seg, heads),
        cols(seg, 2 * heads),
        cols(comp, 0),
        cols(comp, heads),
        cols(mem, 0),
        cols(mem, heads),
    ]


def attend(info, seg, comp, mem):
    rows = seg.shape[0]
    heads = comp.shape[1] // (2 * DH)
    return pl.pallas_call(
        attend_kernel,
        grid=(heads,),
        out_shape=(
            jax.ShapeDtypeStruct((rows, heads * DH), lowp),
            jax.ShapeDtypeStruct((heads, rows, 1), single),
        ),
        in_specs=head_specs(seg, comp, mem, heads),
        out_specs=(
            pl.BlockSpec((rows, DH), lambda h: (0, h)),
            pl.BlockSpec((1, rows, 1), lambda h: (h, 0, 0)),
        ),
        compiler_params=params(48),
    )(info, seg, seg, seg, comp, comp, mem, mem)


def attend_back(info, seg, comp, mem, lse, upstream):
    rows = seg.shape[0]
    heads = comp.shape[1] // (2 * DH)
    whole = lambda h: (0, 0)
    return pl.pallas_call(
        attend_back_kernel,
        grid=(heads,),
        out_shape=(
            jax.ShapeDtypeStruct(seg.shape, lowp),
            jax.ShapeDtypeStruct(comp.shape, lowp),
            jax.ShapeDtypeStruct(mem.shape, lowp),
        ),
        in_specs=head_specs(seg, comp, mem, heads)
        + [
            pl.BlockSpec((1, rows, 1), lambda h: (h, 0, 0)),
            pl.BlockSpec((rows, DH), lambda h: (0, h)),
        ],
        out_specs=(
            pl.BlockSpec(seg.shape, whole),
            pl.BlockSpec(comp.shape, whole),
            pl.BlockSpec(mem.shape, whole),
        ),
        compiler_params=params(56),
    )(info, seg, seg, seg, comp, comp, mem, mem, lse, upstream)


def columns_of(rows):
    tall = jnp.concatenate([rows, jnp.zeros((120, rows.shape[1]), single)], axis=0)
    return jnp.transpose(tall)


def logits_kernel(words, info_ref, in_ref, table_ref, out_ref, stat_ref):
    logits = mm(in_ref[...], table_ref[...], NT)
    wanted = columns_of(info_ref[...])[:, 0:1].astype(jnp.int32)
    col = lax.broadcasted_iota(jnp.int32, logits.shape, 1)
    hit = jnp.sum(jnp.where(col == wanted, logits, 0.0), axis=-1, keepdims=True)
    logits = jnp.where(col < words, logits, -1e30)
    top = jnp.max(logits, axis=-1, keepdims=True)
    raised = jnp.exp(logits - top)
    total = jnp.sum(raised, axis=-1, keepdims=True)
    out_ref[...] = raised.astype(lowp)
    lane = lax.broadcasted_iota(jnp.int32, (logits.shape[0], 128), 1)
    packed = jnp.where(lane == 0, top, jnp.where(lane == 1, total, jnp.where(lane == 2, hit, 0.0)))
    stat_ref[...] = jnp.transpose(packed)[:8]


def logits_part(words, info, inputs, table):
    rows = inputs.shape[0]
    slots = table.shape[0]
    tile = 256
    return pl.pallas_call(
        functools.partial(logits_kernel, words),
        grid=(rows // tile,),
        out_shape=(
            jax.ShapeDtypeStruct((rows, slots), lowp),
            jax.ShapeDtypeStruct((8, rows), single),
        ),
        in_specs=[
            pl.BlockSpec((8, tile), lambda i: (0, i)),
            pl.BlockSpec((tile, D), lambda i: (i, 0)),
            pl.BlockSpec(table.shape, lambda i: (0, 0)),
        ],
        out_specs=(
            pl.BlockSpec((tile, slots), lambda i: (i, 0)),
            pl.BlockSpec((8, tile), lambda i: (0, i)),
        ),
        compiler_params=params(40),
    )(info, inputs, table)


def logits_back_kernel(info_ref, in_ref, table_ref, out_ref, grad_ref):
    info = columns_of(info_ref[...])
    wanted = info[:, 0:1].astype(jnp.int32)
    counted = info[:, 1:2]
    factor = info[:, 2:3]
    raised = in_ref[...].astype(single)
    col = lax.broadcasted_iota(jnp.int32, raised.shape, 1)
    grads = (raised * factor - jnp.where(col == wanted, counted, 0.0)).astype(lowp)
    out_ref[...] = grads
    grad_ref[...] = mm(grads, table_ref[...]).astype(lowp)


def logits_back(info, raised, table):
    rows, slots = raised.shape
    tile = 256
    return pl.pallas_call(
        logits_back_kernel,
        grid=(rows // tile,),
        out_shape=(
            jax.ShapeDtypeStruct((rows, slots), lowp),
            jax.ShapeDtypeStruct((rows, D), lowp),
        ),
        in_specs=[
            pl.BlockSpec((8, tile), lambda i: (0, i)),
            pl.BlockSpec((tile, slots), lambda i: (i, 0)),
            pl.BlockSpec(table.shape, lambda i: (0, 0)),
        ],
        out_specs=(
            pl.BlockSpec((tile, slots), lambda i: (i, 0)),
            pl.BlockSpec((tile, D), lambda i: (i, 0)),
        ),
        compiler_params=params(40),
    )(info, raised, table)


def table_grad_kernel(count, *refs):
    grads = refs[:count]
    inputs = refs[count : 2 * count]
    keep_ref, send_ref = refs[2 * count :]
    total = mm(grads[0][...], inputs[0][...], TN)
    for i in range(1, count):
        total = total + mm(grads[i][...], inputs[i][...], TN)
    half = keep_ref.shape[1]
    keep_ref[...] = total[:, :half]
    send_ref[...] = total[:, half:].astype(send_ref.dtype)


def table_grad_part(grads, inputs):
    count = len(grads)
    rows, slots = grads[0].shape
    block = min(256, slots)
    return pl.pallas_call(
        functools.partial(table_grad_kernel, count),
        grid=(slots // block,),
        out_shape=(
            jax.ShapeDtypeStruct((slots, D // 2), single),
            jax.ShapeDtypeStruct((slots, D // 2), lowp),
        ),
        in_specs=[pl.BlockSpec((rows, block), lambda i: (0, i))] * count
        + [pl.BlockSpec((rows, D), lambda i: (0, 0))] * count,
        out_specs=(
            pl.BlockSpec((block, D // 2), lambda i: (i, 0)),
            pl.BlockSpec((block, D // 2), lambda i: (i, 0)),
        ),
        compiler_params=params(56),
    )(*grads, *inputs)


def local(
    ids,
    targets,
    target_mask,
    memory,
    old_states,
    mem_fill,
    comp_fill,
    table,
    qkv,
    wout,
    wconv,
    wup,
    wdown,
    gains,
    table_rows,
    table_cols,
    qkv_rows,
    qkv_cols,
    out_rows,
    out_cols,
    conv_rows,
    conv_cols,
    up_rows,
    up_cols,
    down_rows,
    down_cols,
    gains_second,
):
    dp_size, head_size = lax.axis_size("dp"), lax.axis_size("head")
    d, h = lax.axis_index("dp"), lax.axis_index("head")
    x, c = h // 2, h % 2
    order = block_order(dp_size)
    reach = dp_size // 2
    streams, seg_len = ids.shape
    half = seg_len // 2
    per_group = streams * seg_len
    vocab, width = table.shape
    assert head_size == 4 and streams == 2

    flat = jnp.concatenate(
        [
            ids.astype(single).reshape(-1),
            targets.astype(single).reshape(-1),
            target_mask.astype(single).reshape(-1),
            gains.astype(lowp).astype(single).reshape(-1),
        ]
    )
    room = -flat.shape[0] % 1024
    flat = jnp.concatenate([flat, jnp.zeros((room,), single)]).reshape(1, -1, 128)
    small = gather_blocks(flat, 0).reshape(dp_size, -1)

    def field(i):
        raw = small[:, i * per_group : (i + 1) * per_group]
        return relative(raw.reshape(dp_size, 2, 2, half), x, c)

    ids_all = jnp.transpose(field(0), (1, 2, 0, 3)).reshape(-1).astype(jnp.int32)
    targets_all = field(1)
    mask_all = field(2)
    gain_blocks = small[:, 3 * per_group : 3 * per_group + 3 * width].reshape(dp_size, 3, width)
    gain_vals = jnp.swapaxes(gain_blocks, 0, 1).reshape(3, 1, D)
    count_all = jnp.sum(small[:, 2 * per_group : 3 * per_group])

    low_qkv = qkv.astype(lowp)
    own_qkv = gather_blocks(low_qkv, 1)
    full_qkv = jnp.concatenate([own_qkv, swap(own_qkv, "head", 2)], axis=2)
    low_conv = wconv.astype(lowp)
    near_conv = gather_blocks(low_conv, 2)
    conv_lanes = jnp.arange(DH, dtype=jnp.int32)
    conv_width = DH // dp_size
    conv_natural = (jnp.asarray(order, jnp.int32)[conv_lanes // conv_width] ^ d) * conv_width
    conv_natural = conv_natural + conv_lanes % conv_width
    conv_shuffle = (conv_natural[:, None] == conv_lanes[None, :]).astype(lowp)
    near_conv = mm(near_conv.reshape(-1, DH), conv_shuffle).astype(lowp).reshape(near_conv.shape)
    full_conv = jnp.concatenate([near_conv, swap(near_conv, "head", 2)], axis=0)

    low_out = after(wout.astype(lowp), own_qkv)
    own_out = gather_blocks(low_out, 1)
    full_out = jnp.concatenate([own_out, swap(own_out, "head", 2)], axis=0)
    low_up = after(wup.astype(lowp), own_out)
    own_up = gather_blocks(low_up, 0)
    full_up = jnp.concatenate([own_up, swap(own_up, "head", 2)], axis=1)
    low_down = after(wdown.astype(lowp), own_up)
    own_down = gather_blocks(low_down, 1)
    full_down = jnp.concatenate([own_down, swap(own_down, "head", 2)], axis=0)

    words = vocab // reach
    z = d // 2
    low_table = after(table.astype(lowp), own_down)
    near_table = []
    for m in range(0, dp_size, 2):
        part = lax.dynamic_slice_in_dim(low_table, (z ^ (m // 2)) * words, words, 0)
        near_table.append(part if m == 0 else swap(part, "dp", m))
    near_table = jnp.concatenate(near_table, axis=1)
    loss_table = jnp.concatenate([near_table, swap(near_table, "dp", 1)], axis=1)
    slots = -(-words // 256) * 256
    loss_table = jnp.concatenate([loss_table, jnp.zeros((slots - words, D), lowp)], axis=0)

    first_word = h * vocab
    looked, tok_list, row_list, list_count = lookup(first_word.reshape(1), ids_all, table)
    looked = looked.reshape(2, -1, width)
    looked = looked[0] + swap(looked[1], "head", 1)
    looked = looked.reshape(2, -1, width)
    looked = looked[0] + swap(looked[1], "head", 2)
    looked = looked.reshape(dp_size, half, width)
    pieces = [looked[p] if p == 0 else swap(looked[p], "dp", m) for p, m in enumerate(order)]
    embedded = jnp.concatenate(pieces, axis=1).astype(single)
    normed, inv_first = rms(embedded, gain_vals[0])
    normed = jnp.concatenate([normed, swap(normed, "head", 1)], axis=0)

    place = jnp.stack([x, d])
    mem_normed = state_norm(place, gain_vals[0], memory, 1)[0]
    old_normed = state_norm(place, gain_vals[0], old_states, RATE)
    key_value = jnp.concatenate([full_qkv[1], full_qkv[2]], axis=1)
    all_three = jnp.concatenate([full_qkv[0], key_value], axis=1)
    comp, old_raw = compress(old_normed, key_value, full_conv)
    mem = mm(mem_normed, key_value).astype(lowp)
    seg = mm(normed, all_three).astype(lowp)
    info = jnp.stack(
        [
            lax.dynamic_index_in_dim(comp_fill, x, 0, keepdims=False),
            lax.dynamic_index_in_dim(mem_fill, x, 0, keepdims=False),
            c * half,
        ]
    ).astype(jnp.int32)
    mixed, lse = attend(info, seg, comp, mem)

    def core_sum(part):
        return part[:half] + swap(part[half:].astype(lowp), "head", 1).astype(single)

    def core_both(part):
        return jnp.concatenate([part, swap(part, "head", 1)], axis=0)

    after_attn = embedded + core_sum(mm(mixed, full_out))
    ffn_in, inv_second = rms(after_attn, gain_vals[1])
    ffn_in = core_both(ffn_in)
    hidden_pre = mm(ffn_in, full_up)
    hidden_act = jax.nn.gelu(hidden_pre).astype(lowp)
    after_ffn = after_attn + core_sum(mm(hidden_act, full_down))
    final_in, inv_third = rms(after_ffn, gain_vals[2])

    word_start = first_word + z * words
    chunks = []
    infos = []
    for m in range(0, dp_size, 2):
        piece = final_in if m == 0 else swap(reorder(final_in, m), "dp", m)
        pair = jnp.concatenate([piece, swap(piece, "head", 2)], axis=0)
        chunks.append(core_both(pair))
        wanted = targets_all[m // 2].reshape(-1) - word_start.astype(single)
        wanted = jnp.where((wanted >= 0) & (wanted < words), wanted, -1.0)
        counted = mask_all[m // 2].reshape(-1)
        infos.append((wanted, counted))
    blank = jnp.zeros((per_group,), single)
    raised = []
    stats = []
    for chunk, (wanted, counted) in zip(chunks, infos):
        packed = jnp.stack([wanted] + [blank] * 7)
        out, stat = logits_part(words, packed, chunk, loss_table)
        raised.append(out)
        stats.append(stat)
    own_stats = jnp.stack([stat[:3] for stat in stats], axis=1)

    def combine(first, second):
        top = jnp.maximum(first[0], second[0])
        total = first[1] * jnp.exp(first[0] - top) + second[1] * jnp.exp(second[0] - top)
        return jnp.stack([top, total, first[2] + second[2]])

    grid4 = own_stats.reshape(3, reach, 2, 2, half)
    other = swap(grid4, "head", 1)
    grid4 = combine(grid4, jnp.flip(other, 2))
    other = swap(grid4, "head", 2)
    grid4 = combine(grid4, jnp.flip(other, 3))
    step = 1
    while step < reach:
        other = swap(grid4, "dp", 2 * step)
        index = [i ^ step for i in range(reach)]
        other = jnp.stack([other[:, i] for i in index], axis=1)
        grid4 = combine(grid4, other)
        step *= 2
    merged = grid4.reshape(3, reach, per_group)
    log_total = merged[0] + jnp.log(merged[1])
    own_loss = infos[0][1][:half] * (log_total[0, :half] - merged[2, 0, :half])
    loss_local = jnp.sum(own_loss)

    dlogits = [None] * reach
    final_grad = None
    for i in list(range(1, reach)) + [0]:
        wanted, counted = infos[i]
        factor = jnp.exp(own_stats[0, i] - log_total[i]) * counted
        packed = jnp.stack([wanted, counted, factor] + [blank] * 5)
        dlogits[i], part = logits_back(packed, raised[i], loss_table)
        rows = per_group // 2
        part = part[:rows].astype(single) + swap(part[rows:], "head", 1).astype(single)
        rows = rows // 2
        part = part[:rows] + swap(part[rows:].astype(lowp), "head", 2).astype(single)
        if i:
            part = reorder(swap(part.astype(lowp), "dp", 2 * i), 2 * i).astype(single)
        final_grad = part if final_grad is None else final_grad + part

    keep, send = table_grad_part(dlogits[:4], chunks[:4])
    for start in range(4, reach, 4):
        more = table_grad_part(dlogits[start : start + 4], chunks[start : start + 4])
        keep = keep + more[0]
        send = (send.astype(single) + more[1].astype(single)).astype(lowp)
    keep = keep + swap(send.astype(lowp), "dp", 1).astype(single)
    table_base = jnp.zeros((vocab, width), single)
    for i, part in enumerate(split(keep[:words], 1, reach)):
        part = part if i == 0 else swap(part.astype(lowp), "dp", 2 * i).astype(single)
        table_base = lax.dynamic_update_slice_in_dim(table_base, part, (z ^ i) * words, 0)

    grad_after_ffn = rms_back(after_ffn, inv_third, gain_vals[2], final_grad)
    down_in = core_both(grad_after_ffn.astype(lowp))
    act_grad = mm(down_in, full_down, NT)
    pre_grad = jax.vjp(jax.nn.gelu, hidden_pre)[1](act_grad)[0].astype(lowp)
    ffn_in_grad = core_sum(mm(pre_grad, full_up, NT))
    grad_after_attn = grad_after_ffn + rms_back(after_attn, inv_second, gain_vals[1], ffn_in_grad)
    attn_in = core_both(grad_after_attn.astype(lowp))

    mixed_grad = mm(attn_in, full_out, NT).astype(lowp)
    seg_grad, comp_grad, mem_grad = attend_back(info, seg, comp, mem, lse, mixed_grad)
    seg_in_grad = core_sum(mm(seg_grad, all_three, NT))
    embed_grad = grad_after_attn + rms_back(embedded, inv_first, gain_vals[0], seg_in_grad)
    pieces = [
        part if m == 0 else swap(part, "dp", m)
        for part, m in zip(split(embed_grad.astype(lowp), 1, dp_size), order)
    ]
    rows_grad = jnp.stack(pieces)
    rows_grad = jnp.stack([rows_grad, swap(rows_grad, "head", 2)])
    rows_grad = jnp.stack([rows_grad, swap(rows_grad, "head", 1)]).reshape(-1, width)

    old_grad, conv_sum = expand(comp_grad, old_raw, full_conv)
    seg_sum = mm(normed, seg_grad, TN)
    side_sum = mm(mem_normed, mem_grad, TN) + mm(
        old_normed.reshape(-1, D), old_grad.reshape(-1, old_grad.shape[-1]), TN
    )
    wide = seg_sum.shape[1] // 3
    own = wide // 2

    def three(first):
        def cols(array, base):
            return array[:, base + first : base + first + own]

        return jnp.stack(
            [
                cols(seg_sum, 0),
                cols(seg_sum, wide) + cols(side_sum, 0),
                cols(seg_sum, 2 * wide) + cols(side_sum, wide),
            ]
        )

    def in_order(value):
        moved = mm(value.astype(lowp).reshape(-1, DH), conv_shuffle, NT)
        return moved.reshape(value.shape)

    heads_own = wconv.shape[0]
    hidden_own = wup.shape[1]
    down_sum = mm(hidden_act, down_in, TN)
    up_sum = mm(ffn_in, pre_grad, TN)
    out_sum = mm(mixed, attn_in, TN)
    down_grad = reduce_blocks(down_sum[:hidden_own], down_sum[hidden_own:], 1)
    up_grad = reduce_blocks(up_sum[:, :hidden_own], up_sum[:, hidden_own:], 0)
    out_grad = reduce_blocks(out_sum[: wout.shape[0]], out_sum[wout.shape[0] :], 1)
    qkv_grad = reduce_blocks(three(0), three(own), 1)
    conv_grad = reduce_blocks(in_order(conv_sum[:heads_own]), in_order(conv_sum[heads_own:]), 2)
    table_grad = scatter(list_count, tok_list, row_list, table_base, rows_grad)

    gains_low = gains.astype(lowp).astype(single)
    gain_part = jnp.stack(
        [
            jnp.sum(low_qkv.astype(single) * qkv_grad, axis=(0, 2)),
            jnp.sum(wup.astype(lowp).astype(single) * up_grad, axis=1),
            jnp.sum(table.astype(lowp).astype(single) * table_base, axis=0),
        ]
    )

    grads = (table_grad, qkv_grad, out_grad, conv_grad, up_grad, down_grad)
    weights_now = (table, qkv, wout, wconv, wup, wdown)
    rows_old = (table_rows, qkv_rows, out_rows, conv_rows, up_rows, down_rows)
    cols_old = (table_cols, qkv_cols, out_cols, conv_cols, up_cols, down_cols)
    sizes = {"dp": dp_size, "head": head_size}
    row_axes = ("head", "dp", "head", "head", "dp", "head")
    col_axes = ("dp", "head", "dp", "dp", "head", "dp")

    def pack(arrays):
        joined = jnp.concatenate([a.reshape(-1) for a in arrays])
        return jnp.concatenate([joined, jnp.zeros((-joined.shape[0] % 1024,), single)])

    def unpack(joined, arrays):
        result = []
        start = 0
        for a in arrays:
            result.append(joined[start : start + a.size].reshape(a.shape))
            start += a.size
        return result

    def sum_over(arrays, axis):
        joined = pack(arrays)
        mask = 1
        while mask < sizes[axis]:
            joined = joined + swap(joined, axis, mask)
            mask *= 2
        return unpack(joined, arrays)

    row_part = []
    col_part = []
    scalar_list = []
    for index in range(6):
        square = grads[index] * grads[index]
        row_part.append(jnp.sum(square, axis=-1))
        col_part.append(jnp.sum(square, axis=tuple(range(square.ndim - 1))))
        scalar_list.append(jnp.sum(square))
        scalar_list.append(jnp.sum(rows_old[index]) / sizes[col_axes[index]])
    for weight in weights_now:
        scalar_list.append(jnp.sum(weight * weight))
    for which in range(3):
        scalar_list.append(jnp.sum(gains[which] * gains[which]) / head_size)
    scalar_list.append(loss_local)
    scalars = jnp.stack(scalar_list)
    row_q, row_u, col_e, col_o, col_c, col_d, gain_raw, scalars = sum_over(
        [row_part[1], row_part[4], col_part[0], col_part[2], col_part[3], col_part[5], gain_part, scalars],
        "head",
    )
    row_e, row_o, row_c, row_d, col_q, col_u, scalars = sum_over(
        [row_part[0], row_part[2], row_part[3], row_part[5], col_part[1], col_part[4], scalars], "dp"
    )
    row_sums = [row_e, row_q, row_o, row_c, row_u, row_d]
    col_sums = [col_e, col_q, col_o, col_c, col_u, col_d]
    weight_total = scalars[12:21]
    loss_all = scalars[21]
    inverse = 1.0 / count_all
    decay = 1.0 - STEP ** (-0.8)
    updates = []
    stats_new = []
    scaled = []
    counts = []
    update_sq = []
    for index in range(6):
        rows_total = rows_old[index].size * sizes[row_axes[index]]
        cols_total = cols_old[index].size * sizes[col_axes[index]]
        grad_scaled = grads[index] * inverse
        rows_new = decay * rows_old[index] + (1.0 - decay) * (
            row_sums[index] * inverse * inverse / cols_total + TINY_SQUARE
        )
        cols_new = decay * cols_old[index] + (1.0 - decay) * (
            col_sums[index] * inverse * inverse / rows_total + TINY_SQUARE
        )
        mean_row = decay * scalars[2 * index + 1] / rows_total + (1.0 - decay) * (
            scalars[2 * index] * inverse * inverse / (rows_total * cols_total) + TINY_SQUARE
        )
        second = rows_new[..., None] * cols_new / mean_row
        direction = grad_scaled * lax.rsqrt(second)
        updates.append(direction)
        stats_new.append((rows_new, cols_new))
        scaled.append(grad_scaled)
        counts.append(rows_total * cols_total)
        update_sq.append(jnp.sum(direction * direction))
    gain_scaled = gain_raw / gains_low * inverse
    second_new = decay * gains_second + (1.0 - decay) * (gain_scaled * gain_scaled + TINY_SQUARE)
    gain_dir = gain_scaled * lax.rsqrt(second_new)
    for which in range(3):
        update_sq.append(jnp.sum(gain_dir[which] * gain_dir[which]) / head_size)
    update_total = sum_over(sum_over([jnp.stack(update_sq)], "head"), "dp")[0]
    results = [loss_all, count_all]
    for index in range(6):
        factor = jnp.maximum(0.001, jnp.sqrt(weight_total[index] / counts[index]))
        denom = jnp.maximum(1.0, jnp.sqrt(update_total[index] / counts[index]) / CLIP_LEVEL)
        new_weight = weights_now[index] - LEARN_RATE * factor * updates[index] / denom
        results += [new_weight, scaled[index], stats_new[index][0], stats_new[index][1]]
    gain_factor = jnp.maximum(0.001, jnp.sqrt(weight_total[6:] / D))[:, None]
    gain_denom = jnp.maximum(1.0, jnp.sqrt(update_total[6:] / D) / CLIP_LEVEL)[:, None]
    results += [gains - LEARN_RATE * gain_factor * gain_dir / gain_denom, gain_scaled, second_new]
    return tuple(results)


def solution(mesh):
    in_specs = (
        P("dp", None),
        P("dp", None),
        P("dp", None),
        P("dp", None, None),
        P("dp", None, None),
        P("dp"),
        P("dp"),
        P("head", "dp"),
        P(None, "dp", "head"),
        P("head", "dp"),
        P("head", None, "dp"),
        P("dp", "head"),
        P("head", "dp"),
        P(None, "dp"),
        P("head"),
        P("dp"),
        P(None, "dp"),
        P("head"),
        P("head"),
        P("dp"),
        P("head", None),
        P("dp"),
        P("dp"),
        P("head"),
        P("head"),
        P("dp"),
        P(None, "dp"),
    )
    out_specs = (
        P(),
        P(),
        P("head", "dp"),
        P("head", "dp"),
        P("head"),
        P("dp"),
        P(None, "dp", "head"),
        P(None, "dp", "head"),
        P(None, "dp"),
        P("head"),
        P("head", "dp"),
        P("head", "dp"),
        P("head"),
        P("dp"),
        P("head", None, "dp"),
        P("head", None, "dp"),
        P("head", None),
        P("dp"),
        P("dp", "head"),
        P("dp", "head"),
        P("dp"),
        P("head"),
        P("head", "dp"),
        P("head", "dp"),
        P("head"),
        P("dp"),
        P(None, "dp"),
        P(None, "dp"),
        P(None, "dp"),
    )
    return jax.shard_map(local, mesh=mesh, in_specs=in_specs, out_specs=out_specs, check_vma=False)
```

time: 2290 us -> 1160 us (0.51)
  waiting for transfers between devices: 1480 us -> 453 us
  blocking collectives: 225 us -> 0 us
  matrix products: 238 us -> 34.6 us
  starting transfers between devices: 2.41 us -> 190 us
  Pallas kernels: 0 us -> 181 us
  other arithmetic: 204 us -> 114 us
  local copies, waits for them, and re-layouts: 98.3 us -> 146 us
    reduce_scatter x6 -> x0, waiting for transfers between devices: 851 us -> none  [the longest x1 533 us: local(): lax.psum_scatter(table_grad, 'dp', scatter_dimension=1, tiled=True)]
    ppermute x0 -> x124, waiting for transfers between devices: none -> 453 us  [swap(): return lax.ppermute(value, axis, [(i, i ^ mask) for i in range(size)])]
    psum x6 -> x0, waiting for transfers between devices: 370 us -> none  [the longest x1 85.7 us: local(): final_grad = lax.psum(final_part, 'head')]
    all_gather x4 -> x0, waiting for transfers between devices: 254 us -> none  [the longest x1 162 us: local(): lax.all_gather(table.astype(lowp), 'dp', axis=1, tiled=True)]
    dot_general x46 -> x18, matrix products: 238 us -> 34.6 us  [mm(): return lax.dot_general(left, right, dims, preferred_element_type=single)]
    ppermute x0 -> x124, starting transfers between devices: none -> 190 us  [swap(): return lax.ppermute(value, axis, [(i, i ^ mask) for i in range(size)])]
    pallas_call x0 -> x17, Pallas kernels: none -> 181 us  [the longest x1 45 us: lookup(): pl.pallas_call(lookup_kernel, out_shape=(jax.ShapeDtypeStruct((total, wid...]
    psum x4 -> x0, blocking collectives: 120 us -> none  [the longest x1 38.3 us: local(): scalars = lax.psum(scalar_part, ('dp', 'head'))]
  transfers between devices with their start and end apart: 17 -> 124, of which waited for: 13 -> 59; matrix products, arithmetic and copies ran while one was open for 10% -> 15% of each run, Pallas kernels for 0% -> 14%
where the time goes in v2:
time: 1160 us; the launch traced here: 1150 us
  waiting for transfers between devices  453 us (39%)
  starting transfers between devices  190 us (16%)
  Pallas kernels  181 us (16%)
  local copies, waits for them, and re-layouts  146 us (13%)
  other arithmetic  114 us (10%)
  matrix products  34.6 us (3%)
  between operations  28.8 us (2%)
    ppermute x124, waiting for transfers between devices, swap(): return lax.ppermute(value, axis, [(i, i ^ mask) for i in range(size)])  453 us
    ppermute x124, starting transfers between devices, swap(): return lax.ppermute(value, axis, [(i, i ^ mask) for i in range(size)])  190 us
    unnamed x515, local copies, waits for them, and re-layouts  79.1 us
    pallas_call x1, Pallas kernels, lookup(): pl.pallas_call(lookup_kernel, out_shape=(jax.ShapeDtypeStruct((total, wid...  45 us
    dot_general x18, matrix products, mm(): return lax.dot_general(left, right, dims, preferred_element_type=single)  34.6 us
    pallas_call x4, Pallas kernels, logits_back(): pl.pallas_call(logits_back_kernel, grid=(rows // tile,), out_shape=(jax.S...  33.5 us
    pallas_call x4, Pallas kernels, logits_part(): pl.pallas_call(functools.partial(logits_kernel, words), grid=(rows // til...  29.6 us
    pallas_call x1, Pallas kernels, table_grad_part(): pl.pallas_call(functools.partial(table_grad_kernel, count), grid=(slots /...  24.5 us
  transfers between devices with their start and end apart: 124, of which 59 were waited for; matrix products, arithmetic and copies ran while one was open for 15% of the time, Pallas kernels for 14%

profile of v2, /device:TPU:0, one launch (start us, length us, event | category | flops | bytes accessed | tf_op | source)
XLA Modules:
  0.0 1148.9 jit_solution(11823788133442942189)
XLA Ops:
  40.1 12.2 %collective-permute-done.20 = bf16[2,384,16]{2,1,0:T(8,128)(2,1)S(1)} collective-permute-done((bf16[2,384,16]{2,1,0:T(8,128)(2,1)S(1)}, bf16[2,384,16]{2,1,0:T(8,128)(2,1)S(1)}, u32[]{:S(2)}, u32[]{:S(2)}) %collective-permute-start.20) | collective-permute-done | bytes 24608 | tf_op jit(solution)/shard_map/ppermute | solution.py:38
  60.7 45.0 %shard_map.491 = (bf16[8192,128]{1,0:T(8,128)(2,1)S(1)}, s32[8200]{0:T(1024)S(1)}, s32[8200]{0:T(1024)S(1)}, s32[1]{0:T(128)}) custom-call(s32[1]{0:T(128)} %bitcast.first_ref, s32[8192]{0:T(1024)S(1)} %bitcast.220, f32[8000,128]{1,0:T(8,128)S(1)} %copy-done.5), custom_call_target="tpu_custom_call" | custom-call | tf_op jit(solution)/shard_map/pallas_call | solution.py:144
  122.2 10.3 collective-permute-done.17
  196.9 8.0 collective-permute-start.11
  239.0 10.5 shard_map.495
  271.5 16.3 %collective-permute-done.44 = bf16[2000,128]{1,0:T(8,128)(2,1)S(1)} collective-permute-done((bf16[2000,128]{1,0:T(8,128)(2,1)S(1)}, bf16[2000,128]{1,0:T(8,128)(2,1)S(1)}, u32[]{:S(2)}, u32[]{:S(2)}) %collective-permute-start.44) | collective-permute-done | bytes 512032 | tf_op jit(solution)/shard_map/ppermute | solution.py:38
  288.5 17.8 %collective-permute-done.45 = bf16[2000,128]{1,0:T(8,128)(2,1)S(1)} collective-permute-done((bf16[2000,128]{1,0:T(8,128)(2,1)S(1)}, bf16[2000,128]{1,0:T(8,128)(2,1)S(1)}, u32[]{:S(2)}, u32[]{:S(2)}) %collective-permute-start.45) | collective-permute-done | bytes 512032 | tf_op jit(solution)/shard_map/ppermute | solution.py:38
  310.6 33.4 %collective-permute-done.40 = bf16[1024,1024]{1,0:T(8,128)(2,1)S(1)} collective-permute-done((bf16[1024,1024]{1,0:T(8,128)(2,1)S(1)}, bf16[1024,1024]{1,0:T(8,128)(2,1)S(1)}, u32[]{:S(2)}, u32[]{:S(2)}) %collective-permute-start.40) | collective-permute-done | bytes 2097184 | tf_op jit(solution)/shard_map/ppermute | solution.py:38
  359.5 19.5 %collective-permute-done.48 = bf16[256,1024]{1,0:T(8,128)(2,1)S(1)} collective-permute-done((bf16[256,1024]{1,0:T(8,128)(2,1)S(1)}, bf16[256,1024]{1,0:T(8,128)(2,1)S(1)}, u32[]{:S(2)}, u32[]{:S(2)}) %collective-permute-start.48) | collective-permute-done | bytes 524320 | tf_op jit(solution)/shard_map/ppermute | solution.py:38
  380.3 14.8 %collective-permute-done.51 = bf16[256,1024]{1,0:T(8,128)(2,1)S(1)} collective-permute-done((bf16[256,1024]{1,0:T(8,128)(2,1)S(1)}, bf16[256,1024]{1,0:T(8,128)(2,1)S(1)}, u32[]{:S(2)}, u32[]{:S(2)}) %collective-permute-start.51) | collective-permute-done | bytes 524320 | tf_op jit(solution)/shard_map/ppermute | solution.py:38
  398.8 10.8 collective-permute-done.52
  501.6 8.4 shard_map.501
  522.6 8.4 shard_map.502
  545.4 8.4 shard_map.503
  584.6 8.4 shard_map.500
  597.8 24.5 %shard_map.504 = (f32[2048,512]{1,0:T(8,128)}, bf16[2048,512]{1,0:T(8,128)(2,1)}) custom-call(bf16[1024,2048]{1,0:T(8,128)(2,1)} %copy-done.32, bf16[1024,2048]{1,0:T(8,128)(2,1)} %copy-done.29, bf16[1024,2048]{1,0:T(8,128)(2,1)} %copy-done.30, bf16[1024,2048]{1,0:T(8,128)(2,1)} %copy-done.31, bf16[1024,1024]{1,0:T(8,128)(2,1)} %copy-done.7, ...), custom_call_target="tpu_custom_call" | custom-call | tf_op jit(solution)/shard_map/pallas_call | solution.py:536
  645.8 9.0 collective-permute-done.69
  657.9 8.1 collective-permute-done.72
  668.8 11.3 collective-permute-done.73
  680.4 11.0 collective-permute-done.70
  696.5 10.8 collective-permute-start.62
  710.8 15.0 %collective-permute-done.62 = bf16[2000,128]{1,0:T(8,128)(2,1)S(1)} collective-permute-done((bf16[2000,128]{1,0:T(8,128)(2,1)S(1)}, bf16[2000,128]{1,0:T(8,128)(2,1)S(1)}, u32[]{:S(2)}, u32[]{:S(2)}) %collective-permute-start.62) | collective-permute-done | bytes 512032 | tf_op jit(solution)/shard_map/ppermute | solution.py:38
  725.9 19.1 %collective-permute-done.63 = bf16[2000,128]{1,0:T(8,128)(2,1)S(1)} collective-permute-done((bf16[2000,128]{1,0:T(8,128)(2,1)S(1)}, bf16[2000,128]{1,0:T(8,128)(2,1)S(1)}, u32[]{:S(2)}, u32[]{:S(2)}) %collective-permute-start.63) | collective-permute-done | bytes 512032 | tf_op jit(solution)/shard_map/ppermute | solution.py:38
  770.3 15.1 %shard_map.505 = (bf16[512,1536]{1,0:T(8,128)(2,1)}, bf16[512,1024]{1,0:T(8,128)(2,1)}, bf16[512,1024]{1,0:T(8,128)(2,1)}) custom-call(s32[3]{0:T(128)} %copy-done.59, bf16[512,1536]{1,0:T(8,128)(2,1)} %copy-done.4, bf16[512,1536]{1,0:T(8,128)(2,1)} %copy-done.4, bf16[512,1536]{1,0:T(8,128)(2,1)} %copy-done.4, bf16[512,1024]{1,0:T(8,128)(2,1)} %copy-done.8, ...), custom_call_target="tpu_custom_call" | custom-call | tf_op jit(solution)/shard_map/pallas_call | solution.py:419
  799.9 10.8 collective-permute-done.94
  815.7 11.1 collective-permute-start.96
  836.9 84.3 %collective-permute-done.89 = bf16[256,1024]{1,0:T(8,128)(2,1)S(1)} collective-permute-done((bf16[256,1024]{1,0:T(8,128)(2,1)S(1)}, bf16[256,1024]{1,0:T(8,128)(2,1)S(1)}, u32[]{:S(2)}, u32[]{:S(2)}) %collective-permute-start.89) | collective-permute-done | bytes 524320 | tf_op jit(solution)/shard_map/ppermute | solution.py:38
  978.9 13.4 %collective-permute-done.110 = bf16[512,1024]{1,0:T(8,128)(2,1)S(1)} collective-permute-done((bf16[512,1024]{1,0:T(8,128)(2,1)S(1)}, bf16[512,1024]{1,0:T(8,128)(2,1)S(1)}, u32[]{:S(2)}, u32[]{:S(2)}) %collective-permute-start.110) | collective-permute-done | bytes 1048608 | tf_op jit(solution)/shard_map/ppermute | solution.py:38
  995.8 14.7 %collective-permute-done.100 = bf16[1024,512]{1,0:T(8,128)(2,1)S(1)} collective-permute-done((bf16[1024,512]{1,0:T(8,128)(2,1)S(1)}, bf16[1024,512]{1,0:T(8,128)(2,1)S(1)}, u32[]{:S(2)}, u32[]{:S(2)}) %collective-permute-start.100) | collective-permute-done | bytes 1048608 | tf_op jit(solution)/shard_map/ppermute | solution.py:38
  1014.1 12.1 %shard_map.506 = f32[8000,128]{1,0:T(8,128)} custom-call(s32[1]{0:T(128)} %get-tuple-element.64.count_ref, s32[8200]{0:T(1024)S(1)} %copy-done.52, s32[8200]{0:T(1024)S(1)} %copy-done.54, f32[8000,128]{1,0:T(8,128)} %copy-done.60, bf16[8192,128]{1,0:T(8,128)(2,1)S(1)} %bitcast.219), custom_call_target="tpu_custom_call" | custom-call | tf_op jit(solution)/shard_map/pallas_call | solution.py:187
  1040.4 8.4 collective-permute-done.102
  1054.5 8.7 concatenate.212
  (1048 shorter events, 600.7 us)
Async XLA Ops:
  10.9 99.3 %collective-permute-start.14 = (bf16[3,128,256]{2,1,0:T(8,128)(2,1)S(1)}, bf16[3,128,256]{2,1,0:T(8,128)(2,1)}, u32[]{:S(2)}, u32[]{:S(2)}) collective-permute-start(bf16[3,128,256]{2,1,0:T(8,128)(2,1)S(1)} %get-tuple-element.177), channel_id=1, source_target_pairs={{0,8},{4,12},{8,0},{12,4},{16,24},{20,28},{24,16},{28,20},{1,9},{5... | collective-permute-start | bytes 589832 | tf_op jit(solution)/shard_map/ppermute | solution.py:38
  11.7 98.4 %collective-permute-start.15 = (bf16[3,128,256]{2,1,0:T(8,128)(2,1)S(1)}, bf16[3,128,256]{2,1,0:T(8,128)(2,1)}, u32[]{:S(2)}, u32[]{:S(2)}) collective-permute-start(bf16[3,128,256]{2,1,0:T(8,128)(2,1)S(1)} %get-tuple-element.177), channel_id=1, source_target_pairs={{0,16},{4,20},{8,24},{12,28},{16,0},{20,4},{24,8},{28,12},{1,17},{... | collective-permute-start | bytes 589832 | tf_op jit(solution)/shard_map/ppermute | solution.py:38
  40.1 70.1 %collective-permute-start.16 = (bf16[3,128,256]{2,1,0:T(8,128)(2,1)S(1)}, bf16[3,128,256]{2,1,0:T(8,128)(2,1)S(1)}, u32[]{:S(2)}, u32[]{:S(2)}) collective-permute-start(bf16[3,128,256]{2,1,0:T(8,128)(2,1)S(1)} %get-tuple-element.177), channel_id=1, source_target_pairs={{0,24},{4,28},{8,16},{12,20},{16,8},{20,12},{24,0},{28,4},{1,25},{... | collective-permute-start | bytes 589832 | tf_op jit(solution)/shard_map/ppermute | solution.py:38
  54.7 59.6 %collective-permute-start.22 = (bf16[2,384,64]{2,1,0:T(8,128)(2,1)}, bf16[2,384,64]{2,1,0:T(8,128)(2,1)}, u32[]{:S(2)}, u32[]{:S(2)}) collective-permute-start(bf16[2,384,64]{2,1,0:T(8,128)(2,1)} %pad_maximum_fusion.43), channel_id=1, source_target_pairs={{0,4},{4,0},{8,12},{12,8},{16,20},{20,16},{24,28},{28,24},{1,5},{5... | collective-permute-start | bytes 294920 | tf_op jit(solution)/shard_map/ppermute | solution.py:38
  108.0 37.7 %collective-permute-start.4 = (bf16[4096,128]{1,0:T(8,128)(2,1)}, bf16[4096,128]{1,0:T(8,128)(2,1)}, u32[]{:S(2)}, u32[]{:S(2)}) collective-permute-start(bf16[4096,128]{1,0:T(8,128)(2,1)} %slice.882), channel_id=1, source_target_pairs={{0,1},{1,0},{2,3},{3,2},{4,5},{5,4},{6,7},{7,6},{8,9},{9,8},{10,11... | collective-permute-start | bytes 3145736 | tf_op jit(solution)/shard_map/ppermute | solution.py:38
  116.8 48.8 %collective-permute-start.23 = (bf16[2,384,128]{2,1,0:T(8,128)(2,1)}, bf16[2,384,128]{2,1,0:T(8,128)(2,1)}, u32[]{:S(2)}, u32[]{:S(2)}) collective-permute-start(bf16[2,384,128]{2,1,0:T(8,128)(2,1)} %bitcast.23), channel_id=1, source_target_pairs={{0,2},{1,3},{2,0},{3,1},{4,6},{5,7},{6,4},{7,5},{8,10},{9,11},{10,... | collective-permute-start | bytes 589832 | tf_op jit(solution)/shard_map/ppermute | solution.py:38
  166.8 46.5 %collective-permute-start.18 = (bf16[3,1024,256]{2,1,0:T(8,128)(2,1)}, bf16[3,1024,256]{2,1,0:T(8,128)(2,1)S(1)}, u32[]{:S(2)}, u32[]{:S(2)}) collective-permute-start(bf16[3,1024,256]{2,1,0:T(8,128)(2,1)} %constant_dynamic-update-slice_fusion.9), channel_id=1, source_target_pairs={{0,2},{1,3},{2,0},{3,1},{4,6},{5,7},{6,4},{7,5},{8,10},{9,11},{10,... | collective-permute-start | bytes 4718600 | tf_op jit(solution)/shard_map/ppermute | solution.py:38
  168.3 81.2 %collective-permute-start.28 = (bf16[256,1024]{1,0:T(8,128)(2,1)}, bf16[256,1024]{1,0:T(8,128)(2,1)S(1)}, u32[]{:S(2)}, u32[]{:S(2)}) collective-permute-start(bf16[256,1024]{1,0:T(8,128)(2,1)} %copy-done.102), channel_id=1, source_target_pairs={{0,2},{1,3},{2,0},{3,1},{4,6},{5,7},{6,4},{7,5},{8,10},{9,11},{10,... | collective-permute-start | bytes 1572872 | tf_op jit(solution)/shard_map/ppermute | solution.py:38
  175.6 37.9 %collective-permute-start.34 = (bf16[512,1024]{1,0:T(8,128)(2,1)S(1)}, bf16[512,1024]{1,0:T(8,128)(2,1)S(1)}, u32[]{:S(2)}, u32[]{:S(2)}) collective-permute-start(bf16[512,1024]{1,0:T(8,128)(2,1)S(1)} %pad_maximum_fusion.20), channel_id=1, source_target_pairs={{0,4},{4,0},{8,12},{12,8},{16,20},{20,16},{24,28},{28,24},{1,5},{5... | collective-permute-start | bytes 3145736 | tf_op jit(solution)/shard_map/ppermute | solution.py:38
  251.0 57.1 %collective-permute-start.35 = (bf16[1024,1024]{1,0:T(8,128)(2,1)S(1)}, bf16[1024,1024]{1,0:T(8,128)(2,1)S(1)}, u32[]{:S(2)}, u32[]{:S(2)}) collective-permute-start(bf16[1024,1024]{1,0:T(8,128)(2,1)S(1)} %constant_dynamic-update-slice_fusion.19), channel_id=1, source_target_pairs={{0,2},{1,3},{2,0},{3,1},{4,6},{5,7},{6,4},{7,5},{8,10},{9,11},{10,... | collective-permute-start | bytes 6291464 | tf_op jit(solution)/shard_map/ppermute | solution.py:38
  260.3 83.7 %collective-permute-start.40 = (bf16[1024,1024]{1,0:T(8,128)(2,1)S(1)}, bf16[1024,1024]{1,0:T(8,128)(2,1)S(1)}, u32[]{:S(2)}, u32[]{:S(2)}) collective-permute-start(bf16[1024,1024]{1,0:T(8,128)(2,1)S(1)} %constant_dynamic-update-slice_fusion.24), channel_id=1, source_target_pairs={{0,2},{1,3},{2,0},{3,1},{4,6},{5,7},{6,4},{7,5},{8,10},{9,11},{10,... | collective-permute-start | bytes 6291464 | tf_op jit(solution)/shard_map/ppermute | solution.py:38
  306.6 72.9 %collective-permute-start.47 = (bf16[2000,512]{1,0:T(8,128)(2,1)S(1)}, bf16[2000,512]{1,0:T(8,128)(2,1)S(1)}, u32[]{:S(2)}, u32[]{:S(2)}) collective-permute-start(bf16[2000,512]{1,0:T(8,128)(2,1)S(1)} %pad_maximum_fusion.10), channel_id=1, source_target_pairs={{0,4},{4,0},{8,12},{12,8},{16,20},{20,16},{24,28},{28,24},{1,5},{5... | collective-permute-start | bytes 6144008 | tf_op jit(solution)/shard_map/ppermute | solution.py:38
  349.2 46.5 %collective-permute-start.42 = (bf16[256,1024]{1,0:T(8,128)(2,1)S(1)}, bf16[256,1024]{1,0:T(8,128)(2,1)S(1)}, u32[]{:S(2)}, u32[]{:S(2)}) collective-permute-start(bf16[256,1024]{1,0:T(8,128)(2,1)S(1)} %multiply_convert_fusion.1), channel_id=1, source_target_pairs={{0,2},{1,3},{2,0},{3,1},{4,6},{5,7},{6,4},{7,5},{8,10},{9,11},{10,... | collective-permute-start | bytes 1572872 | tf_op jit(solution)/shard_map/ppermute | solution.py:38
  356.8 38.3 %collective-permute-start.51 = (bf16[256,1024]{1,0:T(8,128)(2,1)S(1)}, bf16[256,1024]{1,0:T(8,128)(2,1)S(1)}, u32[]{:S(2)}, u32[]{:S(2)}) collective-permute-start(bf16[256,1024]{1,0:T(8,128)(2,1)S(1)} %pad_maximum_fusion.40), channel_id=1, source_target_pairs={{0,16},{4,20},{8,24},{12,28},{16,0},{20,4},{24,8},{28,12},{1,17},{... | collective-permute-start | bytes 1572872 | tf_op jit(solution)/shard_map/ppermute | solution.py:38
  358.0 37.9 %collective-permute-start.54 = (bf16[256,1024]{1,0:T(8,128)(2,1)S(1)}, bf16[256,1024]{1,0:T(8,128)(2,1)S(1)}, u32[]{:S(2)}, u32[]{:S(2)}) collective-permute-start(bf16[256,1024]{1,0:T(8,128)(2,1)S(1)} %constant_dynamic-update-slice_fusion.48), channel_id=1, source_target_pairs={{0,24},{4,28},{8,16},{12,20},{16,8},{20,12},{24,0},{28,4},{1,25},{... | collective-permute-start | bytes 1572872 | tf_op jit(solution)/shard_map/ppermute | solution.py:38
  416.7 47.1 %collective-permute-start.56 = (bf16[512,1024]{1,0:T(8,128)(2,1)}, bf16[512,1024]{1,0:T(8,128)(2,1)}, u32[]{:S(2)}, u32[]{:S(2)}) collective-permute-start(bf16[512,1024]{1,0:T(8,128)(2,1)} %pad_maximum_fusion.25), channel_id=1, source_target_pairs={{0,1},{1,0},{2,3},{3,2},{4,5},{5,4},{6,7},{7,6},{8,9},{9,8},{10,11... | collective-permute-start | bytes 3145736 | tf_op jit(solution)/shard_map/ppermute | solution.py:38
  513.0 113.8 %collective-permute-start.65 = (bf16[512,1024]{1,0:T(8,128)(2,1)}, bf16[512,1024]{1,0:T(8,128)(2,1)}, u32[]{:S(2)}, u32[]{:S(2)}) collective-permute-start(bf16[512,1024]{1,0:T(8,128)(2,1)} %slice.969), channel_id=1, source_target_pairs={{0,1},{1,0},{2,3},{3,2},{4,5},{5,4},{6,7},{7,6},{8,9},{9,8},{10,11... | collective-permute-start | bytes 3145736 | tf_op jit(solution)/shard_map/ppermute | solution.py:38
  535.4 93.9 %collective-permute-start.68 = (bf16[512,1024]{1,0:T(8,128)(2,1)}, bf16[512,1024]{1,0:T(8,128)(2,1)}, u32[]{:S(2)}, u32[]{:S(2)}) collective-permute-start(bf16[512,1024]{1,0:T(8,128)(2,1)} %slice.981), channel_id=1, source_target_pairs={{0,1},{1,0},{2,3},{3,2},{4,5},{5,4},{6,7},{7,6},{8,9},{9,8},{10,11... | collective-permute-start | bytes 3145736 | tf_op jit(solution)/shard_map/ppermute | solution.py:38
  558.1 74.3 %collective-permute-start.71 = (bf16[512,1024]{1,0:T(8,128)(2,1)}, bf16[512,1024]{1,0:T(8,128)(2,1)}, u32[]{:S(2)}, u32[]{:S(2)}) collective-permute-start(bf16[512,1024]{1,0:T(8,128)(2,1)} %slice.989), channel_id=1, source_target_pairs={{0,1},{1,0},{2,3},{3,2},{4,5},{5,4},{6,7},{7,6},{8,9},{9,8},{10,11... | collective-permute-start | bytes 3145736 | tf_op jit(solution)/shard_map/ppermute | solution.py:38
  622.3 69.9 %collective-permute-start.61 = (bf16[2048,512]{1,0:T(8,128)(2,1)}, bf16[2048,512]{1,0:T(8,128)(2,1)}, u32[]{:S(2)}, u32[]{:S(2)}) collective-permute-start(bf16[2048,512]{1,0:T(8,128)(2,1)} %get-tuple-element.87), channel_id=1, source_target_pairs={{0,4},{4,0},{8,12},{12,8},{16,20},{20,16},{24,28},{28,24},{1,5},{5... | collective-permute-start | bytes 6291464 | tf_op jit(solution)/shard_map/ppermute | solution.py:38
  636.5 55.0 %collective-permute-start.75 = (bf16[256,1024]{1,0:T(8,128)(2,1)S(1)}, bf16[256,1024]{1,0:T(8,128)(2,1)S(1)}, u32[]{:S(2)}, u32[]{:S(2)}) collective-permute-start(bf16[256,1024]{1,0:T(8,128)(2,1)S(1)} %slice.1699), channel_id=1, source_target_pairs={{0,2},{1,3},{2,0},{3,1},{4,6},{5,7},{6,4},{7,5},{8,10},{9,11},{10,... | collective-permute-start | bytes 1572872 | tf_op jit(solution)/shard_map/ppermute | solution.py:38
  707.5 37.7 %collective-permute-start.76 = (bf16[256,1024]{1,0:T(8,128)(2,1)S(1)}, bf16[256,1024]{1,0:T(8,128)(2,1)S(1)}, u32[]{:S(2)}, u32[]{:S(2)}) collective-permute-start(bf16[256,1024]{1,0:T(8,128)(2,1)S(1)} %fusion.58), channel_id=1, source_target_pairs={{0,1},{1,0},{2,3},{3,2},{4,5},{5,4},{6,7},{7,6},{8,9},{9,8},{10,11... | collective-permute-start | bytes 1572872 | tf_op jit(solution)/shard_map/ppermute | solution.py:38
  758.3 204.7 %collective-permute-start.109 = (bf16[1024,1024]{1,0:T(8,128)(2,1)}, bf16[1024,1024]{1,0:T(8,128)(2,1)S(1)}, u32[]{:S(2)}, u32[]{:S(2)}) collective-permute-start(bf16[1024,1024]{1,0:T(8,128)(2,1)} %slice.1691), channel_id=1, source_target_pairs={{0,2},{1,3},{2,0},{3,1},{4,6},{5,7},{6,4},{7,5},{8,10},{9,11},{10,... | collective-permute-start | bytes 6291464 | tf_op jit(solution)/shard_map/ppermute | solution.py:38
  793.7 41.2 %collective-permute-start.79 = (bf16[256,1024]{1,0:T(8,128)(2,1)}, bf16[256,1024]{1,0:T(8,128)(2,1)S(1)}, u32[]{:S(2)}, u32[]{:S(2)}) collective-permute-start(bf16[256,1024]{1,0:T(8,128)(2,1)} %slice.1697), channel_id=1, source_target_pairs={{0,1},{1,0},{2,3},{3,2},{4,5},{5,4},{6,7},{7,6},{8,9},{9,8},{10,11... | collective-permute-start | bytes 1572872 | tf_op jit(solution)/shard_map/ppermute | solution.py:38
  830.7 139.7 %collective-permute-start.99 = (bf16[1024,1024]{1,0:T(8,128)(2,1)S(1)}, bf16[1024,1024]{1,0:T(8,128)(2,1)S(1)}, u32[]{:S(2)}, u32[]{:S(2)}) collective-permute-start(bf16[1024,1024]{1,0:T(8,128)(2,1)S(1)} %copy-done.83), channel_id=1, source_target_pairs={{0,2},{1,3},{2,0},{3,1},{4,6},{5,7},{6,4},{7,5},{8,10},{9,11},{10,... | collective-permute-start | bytes 6291464 | tf_op jit(solution)/shard_map/ppermute | solution.py:38
  831.5 144.8 %collective-permute-start.104 = (bf16[3,1024,256]{2,1,0:T(8,128)(2,1)}, bf16[3,1024,256]{2,1,0:T(8,128)(2,1)}, u32[]{:S(2)}, u32[]{:S(2)}) collective-permute-start(bf16[3,1024,256]{2,1,0:T(8,128)(2,1)} %pad_maximum_fusion.13), channel_id=1, source_target_pairs={{0,2},{1,3},{2,0},{3,1},{4,6},{5,7},{6,4},{7,5},{8,10},{9,11},{10,... | collective-permute-start | bytes 4718600 | tf_op jit(solution)/shard_map/ppermute | solution.py:38
  833.1 88.1 %collective-permute-start.89 = (bf16[256,1024]{1,0:T(8,128)(2,1)S(1)}, bf16[256,1024]{1,0:T(8,128)(2,1)S(1)}, u32[]{:S(2)}, u32[]{:S(2)}) collective-permute-start(bf16[256,1024]{1,0:T(8,128)(2,1)S(1)} %slice.1696), channel_id=1, source_target_pairs={{0,2},{1,3},{2,0},{3,1},{4,6},{5,7},{6,4},{7,5},{8,10},{9,11},{10,... | collective-permute-start | bytes 1572872 | tf_op jit(solution)/shard_map/ppermute | solution.py:38
  836.1 87.5 %collective-permute-start.80 = (bf16[256,128]{1,0:T(8,128)(2,1)S(1)}, bf16[256,128]{1,0:T(8,128)(2,1)S(1)}, u32[]{:S(2)}, u32[]{:S(2)}) collective-permute-start(bf16[256,128]{1,0:T(8,128)(2,1)S(1)} %get-tuple-element.217), channel_id=1, source_target_pairs={{0,8},{4,12},{8,0},{12,4},{16,24},{20,28},{24,16},{28,20},{1,9},{5... | collective-permute-start | bytes 196616 | tf_op jit(solution)/shard_map/ppermute | solution.py:38
  922.0 37.7 %collective-permute-start.90 = (bf16[256,512]{1,0:T(8,128)(2,1)S(1)}, bf16[256,512]{1,0:T(8,128)(2,1)S(1)}, u32[]{:S(2)}, u32[]{:S(2)}) collective-permute-start(bf16[256,512]{1,0:T(8,128)(2,1)S(1)} %slice.1705), channel_id=1, source_target_pairs={{0,4},{4,0},{8,12},{12,8},{16,20},{20,16},{24,28},{28,24},{1,5},{5... | collective-permute-start | bytes 786440 | tf_op jit(solution)/shard_map/ppermute | solution.py:38
  971.6 38.9 %collective-permute-start.100 = (bf16[1024,512]{1,0:T(8,128)(2,1)S(1)}, bf16[1024,512]{1,0:T(8,128)(2,1)S(1)}, u32[]{:S(2)}, u32[]{:S(2)}) collective-permute-start(bf16[1024,512]{1,0:T(8,128)(2,1)S(1)} %slice.1694), channel_id=1, source_target_pairs={{0,4},{4,0},{8,12},{12,8},{16,20},{20,16},{24,28},{28,24},{1,5},{5... | collective-permute-start | bytes 3145736 | tf_op jit(solution)/shard_map/ppermute | solution.py:38
  978.1 57.3 %collective-permute-start.105 = (bf16[3,512,256]{2,1,0:T(8,128)(2,1)S(1)}, bf16[3,512,256]{2,1,0:T(8,128)(2,1)S(1)}, u32[]{:S(2)}, u32[]{:S(2)}) collective-permute-start(bf16[3,512,256]{2,1,0:T(8,128)(2,1)S(1)} %slice.1695), channel_id=1, source_target_pairs={{0,4},{4,0},{8,12},{12,8},{16,20},{20,16},{24,28},{28,24},{1,5},{5... | collective-permute-start | bytes 2359304 | tf_op jit(solution)/shard_map/ppermute | solution.py:38
  993.9 38.5 %collective-permute-start.112 = (bf16[128,1024]{1,0:T(8,128)(2,1)S(1)}, bf16[128,1024]{1,0:T(8,128)(2,1)S(1)}, u32[]{:S(2)}, u32[]{:S(2)}) collective-permute-start(bf16[128,1024]{1,0:T(8,128)(2,1)S(1)} %get-tuple-element.198), channel_id=1, source_target_pairs={{0,16},{4,20},{8,24},{12,28},{16,0},{20,4},{24,8},{28,12},{1,17},{... | collective-permute-start | bytes 786440 | tf_op jit(solution)/shard_map/ppermute | solution.py:38
  (313 other events, 5652.5 us)

commit v3 on v2

--- a/solution.py
+++ b/solution.py
@@ -43,13 +43,20 @@
 
 
 def block_order(size):
-    return list(range(0, size, 2)) + list(range(1, size, 2))
+    order = [0]
+    step = size // 2
+    while step:
+        order = order + [j + step for j in order]
+        step //= 2
+    return order
 
 
 def gather_blocks(piece, axis):
-    size = lax.axis_size("dp")
-    near = jnp.concatenate([piece] + [swap(piece, "dp", m) for m in range(2, size, 2)], axis=axis)
-    return jnp.concatenate([near, swap(near, "dp", 1)], axis=axis)
+    mask = lax.axis_size("dp") // 2
+    while mask:
+        piece = jnp.concatenate([piece, swap(piece, "dp", mask)], axis=axis)
+        mask //= 2
+    return piece
 
 
 def split(value, axis, parts):
@@ -57,21 +64,15 @@
     return [lax.slice_in_dim(value, i * width, (i + 1) * width, axis=axis) for i in range(parts)]
 
 
-def reduce_blocks(own, far, axis):
-    size = lax.axis_size("dp")
-    total = own + swap(far.astype(lowp), "head", 2).astype(single)
-    keep, send = split(total, axis, 2)
-    keep = keep + swap(send.astype(lowp), "dp", 1).astype(single)
-    pieces = split(keep, axis, size // 2)
-    result = pieces[0]
-    for i in range(1, size // 2):
-        result = result + swap(pieces[i].astype(lowp), "dp", 2 * i).astype(single)
-    return result
+def reduce_blocks(keep, send, mask=1):
+    total = keep + swap(send.astype(lowp), "dp", mask).astype(single)
+    mask *= 2
+    if mask == lax.axis_size("dp"):
+        return total
+    return reduce_blocks(*split(total, 1, 2), mask)
 
 
 def reorder(value, mask):
-    if mask == 0:
-        return value
     order = block_order(lax.axis_size("dp"))
     cols = split(value, 1, len(order))
     return jnp.concatenate([cols[order.index(j ^ mask)] for j in order], axis=1)
@@ -108,29 +109,23 @@
     return pltpu.CompilerParams(vmem_limit_bytes=mib * MIB)
 
 
-def lookup_kernel(first_ref, ids_ref, table_ref, out_ref, tok_ref, row_ref, count_ref, held):
-    total = ids_ref.shape[0]
+def cost(flops, size, exps=0):
+    return pl.CostEstimate(flops=flops, bytes_accessed=size, transcendentals=exps)
+
+
+def lookup_kernel(row_ref, table_ref, out_ref, tab, held, sem):
+    total = row_ref.shape[0]
     vocab = table_ref.shape[0]
-    first = first_ref[0]
-
-    def group(g, count):
-        for j in range(8):
-            t = g * 8 + j
-            word = ids_ref[t] - first
-            inside = jnp.logical_and(word >= 0, word < vocab)
-            safe = jnp.where(inside, word, 0)
-            flag = jnp.where(inside, 1, 0)
-            held[pl.ds(t, 1), :] = table_ref[pl.ds(safe, 1), :] * flag.astype(single)
-            tok_ref[count] = t
-            row_ref[count] = safe
-            count = count + flag
-        return count
-
-    count = lax.fori_loop(0, total // 8, group, jnp.int32(0))
-    for j in range(8):
-        tok_ref[count + j] = total
-        row_ref[count + j] = 0
-    count_ref[0] = count
+    copy = pltpu.make_async_copy(table_ref, tab.at[pl.ds(0, vocab)], sem)
+    copy.start()
+    tab[pl.ds(vocab, 8), :] = jnp.zeros((8, tab.shape[1]), single)
+    copy.wait()
+
+    @pl.loop(0, total // 16)
+    def _(g):
+        for j in range(16):
+            t = g * 16 + j
+            held[pl.ds(t, 1), :] = tab[pl.ds(row_ref[t], 1), :]
 
     @pl.loop(0, total // 512)
     def _(i):
@@ -138,22 +133,105 @@
         out_ref[rows, :] = held[rows, :].astype(lowp)
 
 
-def lookup(first, ids, table):
-    total = ids.shape[0]
-    width = table.shape[1]
+def lookup(rows, table):
+    total = rows.shape[0]
+    vocab, width = table.shape
     return pl.pallas_call(
         lookup_kernel,
+        out_shape=jax.ShapeDtypeStruct((total, width), lowp),
+        in_specs=[smem(), pl.BlockSpec(memory_space=pl.ANY)],
+        out_specs=vmem(),
+        scratch_shapes=[
+            pltpu.VMEM((vocab + 8, width), single),
+            pltpu.VMEM((total, width), single),
+            pltpu.SemaphoreType.DMA(()),
+        ],
+        compiler_params=params(60),
+        cost_estimate=cost(0, 30 * MIB),
+    )(rows, table)
+
+
+def list_kernel(vocab, row_ref, tok_ref, out_ref, count_ref):
+    total = row_ref.shape[0]
+
+    def group(g, count):
+        for j in range(8):
+            t = g * 8 + j
+            row = row_ref[t]
+            tok_ref[count] = t
+            out_ref[count] = row
+            count = count + jnp.where(row < vocab, 1, 0)
+        return count
+
+    count = lax.fori_loop(0, total // 8, group, jnp.int32(0))
+    for j in range(8):
+        tok_ref[count + j] = total
+        out_ref[count + j] = 0
+    count_ref[0] = count
+
+
+def own_list(rows, vocab):
+    total = rows.shape[0]
+    return pl.pallas_call(
+        functools.partial(list_kernel, vocab),
         out_shape=(
-            jax.ShapeDtypeStruct((total, width), lowp),
             jax.ShapeDtypeStruct((total + 8,), jnp.int32),
             jax.ShapeDtypeStruct((total + 8,), jnp.int32),
             jax.ShapeDtypeStruct((1,), jnp.int32),
         ),
-        in_specs=[smem(), smem(), vmem()],
-        out_specs=(vmem(), smem(), smem(), smem()),
-        scratch_shapes=[pltpu.VMEM((total, width), single)],
-        compiler_params=params(40),
-    )(first, ids, table)
+        in_specs=[smem()],
+        out_specs=(smem(), smem(), smem()),
+        cost_estimate=cost(0, 40 * MIB),
+    )(rows)
+
+
+def place_kernel(order, place_ref, in_ref, gain_ref, out_ref, norm_ref, held):
+    width = in_ref.shape[2]
+    for p, j in enumerate(order):
+        block = in_ref[pl.ds(place_ref[1] ^ j, 1)][0]
+        out_ref[:, p * width : (p + 1) * width] = block
+        held[:, p * width : (p + 1) * width] = block.astype(single)
+    values = held[...]
+    inv = lax.rsqrt(jnp.mean(values * values, axis=-1, keepdims=True) + TINY_NORM)
+    norm_ref[...] = (values * inv * gain_ref[...]).astype(lowp)
+
+
+def place_embedding(place, blocks, gain):
+    rows = blocks.shape[1]
+    return pl.pallas_call(
+        functools.partial(place_kernel, block_order(blocks.shape[0])),
+        out_shape=(jax.ShapeDtypeStruct((rows, D), lowp), jax.ShapeDtypeStruct((rows, D), lowp)),
+        in_specs=[smem(), vmem(), vmem()],
+        out_specs=(vmem(), vmem()),
+        scratch_shapes=[pltpu.VMEM((rows, D), single)],
+        compiler_params=params(60),
+        cost_estimate=cost(0, 3 * MIB),
+    )(place, blocks, gain)
+
+
+def embed_back_kernel(order, place_ref, in_ref, gain_ref, keep_ref, more_ref, grad_ref, out_ref, held):
+    values = in_ref[...].astype(single)
+    inv = lax.rsqrt(jnp.mean(values * values, axis=-1, keepdims=True) + TINY_NORM)
+    upstream = keep_ref[...] + more_ref[...].astype(single)
+    held[...] = grad_ref[...] + rms_back(values, inv, gain_ref[...], upstream)
+    width = out_ref.shape[2]
+    for p, j in enumerate(order):
+        block = held[:, p * width : (p + 1) * width].astype(lowp)
+        out_ref[pl.ds(place_ref[1] ^ j, 1)] = block[None]
+
+
+def embed_back(place, values, gain, keep, more, grad):
+    rows = values.shape[0]
+    size = lax.axis_size("dp")
+    return pl.pallas_call(
+        functools.partial(embed_back_kernel, block_order(size)),
+        out_shape=jax.ShapeDtypeStruct((size, rows, D // size), lowp),
+        in_specs=[smem()] + [vmem()] * 5,
+        out_specs=vmem(),
+        scratch_shapes=[pltpu.VMEM((rows, D), single)],
+        compiler_params=params(60),
+        cost_estimate=cost(0, 4 * MIB),
+    )(place, values, gain, keep, more, grad)
 
 
 def scatter_kernel(count_ref, tok_ref, row_ref, base_ref, grad_ref, out_ref, rows):
@@ -190,7 +268,8 @@
         in_specs=[smem(), smem(), smem(), vmem(), vmem()],
         out_specs=vmem(),
         scratch_shapes=[pltpu.VMEM((total + 8, width), single)],
-        compiler_params=params(48),
+        compiler_params=params(60),
+        cost_estimate=cost(0, 30 * MIB),
     )(count, tok, row, base, grad)
 
 
@@ -242,7 +321,8 @@
             out_specs=pl.BlockSpec((groups, tile, D), lambda i, s: (0, i, 0)),
             scratch_shapes=[pltpu.VMEM((len(order), tile * groups, width), single)],
         ),
-        compiler_params=params(24),
+        compiler_params=params(60),
+        cost_estimate=cost(0, 4 * count * groups * D),
     )(place, gain, states)
 
 
@@ -250,7 +330,7 @@
     heads = conv_ref.shape[0]
     sums = [None] * (2 * heads)
     for j in range(RATE):
-        raw = mm(old_ref[j], weight_ref[...]).astype(lowp)
+        raw = mm(old_ref[j], weight_ref[...], NT).astype(lowp)
         raw_ref[j] = raw
         for n in range(2 * heads):
             piece = raw[:, n * DH : (n + 1) * DH]
@@ -262,7 +342,7 @@
 
 def compress(old3, weight, conv):
     rows = old3.shape[1]
-    wide = weight.shape[1]
+    wide = weight.shape[0]
     tile = 256
     return pl.pallas_call(
         compress_kernel,
@@ -280,7 +360,8 @@
             pl.BlockSpec((tile, wide), lambda i: (i, 0)),
             pl.BlockSpec((RATE, tile, wide), lambda i: (0, i, 0)),
         ),
-        compiler_params=params(40),
+        compiler_params=params(60),
+        cost_estimate=cost(4 * RATE * rows * D * D, 12 * MIB),
     )(old3, weight, conv)
 
 
@@ -309,7 +390,8 @@
         ),
         in_specs=[vmem()] * 3,
         out_specs=(vmem(), vmem()),
-        compiler_params=params(40),
+        compiler_params=params(60),
+        cost_estimate=cost(2000 * MIB, 10 * MIB),
     )(grad, raw, conv)
 
 
@@ -377,15 +459,15 @@
     seg_ref[:, here] = (query_grad * scale).astype(lowp)
 
 
-def head_specs(seg, comp, mem, heads):
+def head_specs(query, seg, comp, mem, heads):
     def cols(array, first):
         return pl.BlockSpec((array.shape[0], DH), lambda h: (0, first + h))
 
     return [
         smem(),
+        cols(query, 0),
         cols(seg, 0),
         cols(seg, heads),
-        cols(seg, 2 * heads),
         cols(comp, 0),
         cols(comp, heads),
         cols(mem, 0),
@@ -393,7 +475,7 @@
     ]
 
 
-def attend(info, seg, comp, mem):
+def attend(info, query, seg, comp, mem):
     rows = seg.shape[0]
     heads = comp.shape[1] // (2 * DH)
     return pl.pallas_call(
@@ -403,16 +485,17 @@
             jax.ShapeDtypeStruct((rows, heads * DH), lowp),
             jax.ShapeDtypeStruct((heads, rows, 1), single),
         ),
-        in_specs=head_specs(seg, comp, mem, heads),
+        in_specs=head_specs(query, seg, comp, mem, heads),
         out_specs=(
             pl.BlockSpec((rows, DH), lambda h: (0, h)),
             pl.BlockSpec((1, rows, 1), lambda h: (h, 0, 0)),
         ),
-        compiler_params=params(48),
-    )(info, seg, seg, seg, comp, comp, mem, mem)
-
-
-def attend_back(info, seg, comp, mem, lse, upstream):
+        compiler_params=params(60),
+        cost_estimate=cost(7000 * MIB, 6 * MIB),
+    )(info, query, seg, seg, comp, comp, mem, mem)
+
+
+def attend_back(info, query, seg, comp, mem, lse, upstream):
     rows = seg.shape[0]
     heads = comp.shape[1] // (2 * DH)
     whole = lambda h: (0, 0)
@@ -420,22 +503,23 @@
         attend_back_kernel,
         grid=(heads,),
         out_shape=(
-            jax.ShapeDtypeStruct(seg.shape, lowp),
+            jax.ShapeDtypeStruct((rows, 3 * heads * DH), lowp),
             jax.ShapeDtypeStruct(comp.shape, lowp),
             jax.ShapeDtypeStruct(mem.shape, lowp),
         ),
-        in_specs=head_specs(seg, comp, mem, heads)
+        in_specs=head_specs(query, seg, comp, mem, heads)
         + [
             pl.BlockSpec((1, rows, 1), lambda h: (h, 0, 0)),
             pl.BlockSpec((rows, DH), lambda h: (0, h)),
         ],
         out_specs=(
-            pl.BlockSpec(seg.shape, whole),
+            pl.BlockSpec((rows, 3 * heads * DH), whole),
             pl.BlockSpec(comp.shape, whole),
             pl.BlockSpec(mem.shape, whole),
         ),
-        compiler_params=params(56),
-    )(info, seg, seg, seg, comp, comp, mem, mem, lse, upstream)
+        compiler_params=params(60),
+        cost_estimate=cost(11000 * MIB, 9 * MIB),
+    )(info, query, seg, seg, comp, comp, mem, mem, lse, upstream)
 
 
 def columns_of(rows):
@@ -478,15 +562,16 @@
             pl.BlockSpec((tile, slots), lambda i: (i, 0)),
             pl.BlockSpec((8, tile), lambda i: (0, i)),
         ),
-        compiler_params=params(40),
+        compiler_params=params(60),
+        cost_estimate=cost(4 * rows * slots * D, 10 * MIB),
     )(info, inputs, table)
 
 
-def logits_back_kernel(info_ref, in_ref, table_ref, out_ref, grad_ref):
+def logits_back_kernel(info_ref, factor_ref, in_ref, table_ref, out_ref, grad_ref):
     info = columns_of(info_ref[...])
     wanted = info[:, 0:1].astype(jnp.int32)
     counted = info[:, 1:2]
-    factor = info[:, 2:3]
+    factor = columns_of(factor_ref[...])[:, 0:1]
     raised = in_ref[...].astype(single)
     col = lax.broadcasted_iota(jnp.int32, raised.shape, 1)
     grads = (raised * factor - jnp.where(col == wanted, counted, 0.0)).astype(lowp)
@@ -494,7 +579,7 @@
     grad_ref[...] = mm(grads, table_ref[...]).astype(lowp)
 
 
-def logits_back(info, raised, table):
+def logits_back(info, factor, raised, table):
     rows, slots = raised.shape
     tile = 256
     return pl.pallas_call(
@@ -505,6 +590,7 @@
             jax.ShapeDtypeStruct((rows, D), lowp),
         ),
         in_specs=[
+            pl.BlockSpec((8, tile), lambda i: (0, i)),
             pl.BlockSpec((8, tile), lambda i: (0, i)),
             pl.BlockSpec((tile, slots), lambda i: (i, 0)),
             pl.BlockSpec(table.shape, lambda i: (0, 0)),
@@ -513,26 +599,35 @@
             pl.BlockSpec((tile, slots), lambda i: (i, 0)),
             pl.BlockSpec((tile, D), lambda i: (i, 0)),
         ),
-        compiler_params=params(40),
-    )(info, raised, table)
+        compiler_params=params(60),
+        cost_estimate=cost(4 * rows * slots * D, 12 * MIB),
+    )(info, factor, raised, table)
+
+
+def halves(total, keep_ref, send_ref):
+    half = keep_ref.shape[1]
+    keep_ref[...] = total[:, :half]
+    send_ref[...] = total[:, half:].astype(send_ref.dtype)
 
 
 def table_grad_kernel(count, *refs):
     grads = refs[:count]
     inputs = refs[count : 2 * count]
-    keep_ref, send_ref = refs[2 * count :]
     total = mm(grads[0][...], inputs[0][...], TN)
     for i in range(1, count):
         total = total + mm(grads[i][...], inputs[i][...], TN)
-    half = keep_ref.shape[1]
-    keep_ref[...] = total[:, :half]
-    send_ref[...] = total[:, half:].astype(send_ref.dtype)
+    halves(total, *refs[2 * count :])
 
 
 def table_grad_part(grads, inputs):
     count = len(grads)
-    rows, slots = grads[0].shape
-    block = min(256, slots)
+    rows = sum(g.shape[0] for g in grads)
+    slots = grads[0].shape[1]
+    block = 256
+    if rows > 4096:
+        total = sum(mm(g, v, TN) for g, v in zip(grads, inputs))
+        keep, send = split(total, 1, 2)
+        return keep, send.astype(lowp)
     return pl.pallas_call(
         functools.partial(table_grad_kernel, count),
         grid=(slots // block,),
@@ -540,14 +635,124 @@
             jax.ShapeDtypeStruct((slots, D // 2), single),
             jax.ShapeDtypeStruct((slots, D // 2), lowp),
         ),
-        in_specs=[pl.BlockSpec((rows, block), lambda i: (0, i))] * count
-        + [pl.BlockSpec((rows, D), lambda i: (0, 0))] * count,
+        in_specs=[pl.BlockSpec((g.shape[0], block), lambda i: (0, i)) for g in grads]
+        + [pl.BlockSpec(v.shape, lambda i: (0, 0)) for v in inputs],
         out_specs=(
             pl.BlockSpec((block, D // 2), lambda i: (i, 0)),
             pl.BlockSpec((block, D // 2), lambda i: (i, 0)),
         ),
-        compiler_params=params(56),
+        compiler_params=params(60),
+        cost_estimate=cost(3 * rows * slots * D, 30 * MIB),
     )(*grads, *inputs)
+
+
+def hidden_grad_kernel(blocks, pre_ref, act_ref, in_ref, down_ref, keep_ref, send_ref):
+    step = pl.program_id(0)
+
+    @pl.when(step < blocks)
+    def _():
+        halves(mm(pre_ref[...], in_ref[...], TN), keep_ref, send_ref)
+
+    @pl.when(step >= blocks)
+    def _():
+        halves(mm(act_ref[...], down_ref[...], TN), keep_ref, send_ref)
+
+
+def hidden_grads(pre_grad, hidden_act, ffn_in, down_in):
+    rows, hidden = pre_grad.shape
+    block = 256
+    blocks = hidden // block
+    return pl.pallas_call(
+        functools.partial(hidden_grad_kernel, blocks),
+        grid=(2 * blocks,),
+        out_shape=(
+            jax.ShapeDtypeStruct((2 * hidden, D // 2), single),
+            jax.ShapeDtypeStruct((2 * hidden, D // 2), lowp),
+        ),
+        in_specs=[
+            pl.BlockSpec((rows, block), lambda i: (0, jnp.minimum(i, blocks - 1))),
+            pl.BlockSpec((rows, block), lambda i: (0, jnp.maximum(i - blocks, 0))),
+            pl.BlockSpec((rows, D), lambda i: (0, 0)),
+            pl.BlockSpec((rows, D), lambda i: (0, 0)),
+        ],
+        out_specs=(
+            pl.BlockSpec((block, D // 2), lambda i: (i, 0)),
+            pl.BlockSpec((block, D // 2), lambda i: (i, 0)),
+        ),
+        compiler_params=params(60),
+        cost_estimate=cost(6 * rows * hidden * D, 16 * MIB),
+    )(pre_grad, hidden_act, ffn_in, down_in)
+
+
+def attn_grad_kernel(
+    seg_ref, mixed_ref, mem_ref, old_ref, normed_ref, up_ref, mem_in_ref, old_in_ref, far_ref, own_ref
+):
+    step = pl.program_id(0)
+    which = step % 4
+
+    def give(total):
+        @pl.when(step < 4)
+        def _():
+            far_ref[...] = total.astype(lowp)
+
+        @pl.when(step >= 4)
+        def _():
+            own_ref[...] = total
+
+    @pl.when(which == 0)
+    def _():
+        give(mm(seg_ref[...], normed_ref[...], TN))
+
+    @pl.when(which == 3)
+    def _():
+        give(mm(mixed_ref[...], up_ref[...], TN))
+
+    @pl.when(jnp.logical_and(which > 0, which < 3))
+    def _():
+        total = mm(seg_ref[...], normed_ref[...], TN)
+        total = total + mm(mem_ref[...], mem_in_ref[...], TN)
+        give(total + mm(old_ref[...], old_in_ref[...], TN))
+
+
+def attn_grads(seg_grad, mixed, mem_grad, old_grad, normed, attn_in, mem_in, old_in):
+    block = mixed.shape[1] // 2
+
+    def side(i):
+        return 1 - i // 4
+
+    def whole(array):
+        return pl.BlockSpec(array.shape, lambda i: (0, 0))
+
+    return pl.pallas_call(
+        attn_grad_kernel,
+        grid=(8,),
+        out_shape=(
+            jax.ShapeDtypeStruct((4 * block, D), lowp),
+            jax.ShapeDtypeStruct((4 * block, D), single),
+        ),
+        in_specs=[
+            pl.BlockSpec(
+                (seg_grad.shape[0], block), lambda i: (0, jnp.minimum(i % 4, 2) * 2 + side(i))
+            ),
+            pl.BlockSpec((mixed.shape[0], block), lambda i: (0, side(i))),
+            pl.BlockSpec(
+                (mem_grad.shape[0], block), lambda i: (0, jnp.clip(i % 4 - 1, 0, 1) * 2 + side(i))
+            ),
+            pl.BlockSpec(
+                (old_grad.shape[0], block), lambda i: (0, jnp.clip(i % 4 - 1, 0, 1) * 2 + side(i))
+            ),
+            whole(normed),
+            whole(attn_in),
+            whole(mem_in),
+            whole(old_in),
+        ],
+        out_specs=(
+            pl.BlockSpec((block, D), lambda i: (jnp.minimum(i, 3), 0)),
+            pl.BlockSpec((block, D), lambda i: (jnp.maximum(i - 4, 0), 0)),
+        ),
+        compiler_params=params(60),
+        cost_estimate=cost(9000 * MIB, 20 * MIB),
+    )(seg_grad, mixed, mem_grad, old_grad, normed, attn_in, mem_in, old_in)
 
 
 def local(
@@ -601,46 +806,76 @@
     room = -flat.shape[0] % 1024
     flat = jnp.concatenate([flat, jnp.zeros((room,), single)]).reshape(1, -1, 128)
     small = gather_blocks(flat, 0).reshape(dp_size, -1)
-
-    def field(i):
-        raw = small[:, i * per_group : (i + 1) * per_group]
-        return relative(raw.reshape(dp_size, 2, 2, half), x, c)
-
-    ids_all = jnp.transpose(field(0), (1, 2, 0, 3)).reshape(-1).astype(jnp.int32)
-    targets_all = field(1)
-    mask_all = field(2)
+    place = jnp.stack([x, d])
+
+    def field(raw):
+        return relative(raw.reshape(-1, 2, 2, half), x, c)
+
+    ids_all = small[:, :per_group]
+    position = [order.index(j) for j in range(dp_size)]
+    ids_all = jnp.take(ids_all, jnp.asarray(position, jnp.int32)[jnp.arange(dp_size) ^ d], axis=0)
+    ids_all = jnp.transpose(field(ids_all), (1, 2, 0, 3)).reshape(-1).astype(jnp.int32)
+    table_rows_all = ids_all - h * vocab
+    inside = (table_rows_all >= 0) & (table_rows_all < vocab)
+    table_rows_all = jnp.where(inside, table_rows_all, vocab)
+    targets_all = field(small[:reach, per_group : 2 * per_group])
+    mask_all = field(small[:reach, 2 * per_group : 3 * per_group])
     gain_blocks = small[:, 3 * per_group : 3 * per_group + 3 * width].reshape(dp_size, 3, width)
     gain_vals = jnp.swapaxes(gain_blocks, 0, 1).reshape(3, 1, D)
     count_all = jnp.sum(small[:, 2 * per_group : 3 * per_group])
 
+    heads_own = wconv.shape[0]
+    wide = qkv.shape[2]
+    conv_rows_own = wconv.size // width
     low_qkv = qkv.astype(lowp)
-    own_qkv = gather_blocks(low_qkv, 1)
-    full_qkv = jnp.concatenate([own_qkv, swap(own_qkv, "head", 2)], axis=2)
-    low_conv = wconv.astype(lowp)
-    near_conv = gather_blocks(low_conv, 2)
+    pack_one = jnp.concatenate(
+        [
+            jnp.swapaxes(low_qkv, 1, 2).reshape(3 * wide, width),
+            wout.astype(lowp),
+            wconv.astype(lowp).reshape(conv_rows_own, width),
+        ]
+    )
+    own_one = gather_blocks(after(pack_one, small), 1)
+    far_one = swap(own_one, "head", 2)
+    near_rows = split(own_one[: 4 * wide], 0, 4)
+    far_rows = split(far_one[: 4 * wide], 0, 4)
+    query_weight = jnp.concatenate([near_rows[0], far_rows[0]])
+    pair_weight = jnp.concatenate([near_rows[1], far_rows[1], near_rows[2], far_rows[2]])
+    full_out = jnp.concatenate([near_rows[3], far_rows[3]])
+
     conv_lanes = jnp.arange(DH, dtype=jnp.int32)
     conv_width = DH // dp_size
     conv_natural = (jnp.asarray(order, jnp.int32)[conv_lanes // conv_width] ^ d) * conv_width
     conv_natural = conv_natural + conv_lanes % conv_width
     conv_shuffle = (conv_natural[:, None] == conv_lanes[None, :]).astype(lowp)
-    near_conv = mm(near_conv.reshape(-1, DH), conv_shuffle).astype(lowp).reshape(near_conv.shape)
-    full_conv = jnp.concatenate([near_conv, swap(near_conv, "head", 2)], axis=0)
-
-    low_out = after(wout.astype(lowp), own_qkv)
-    own_out = gather_blocks(low_out, 1)
-    full_out = jnp.concatenate([own_out, swap(own_out, "head", 2)], axis=0)
-    low_up = after(wup.astype(lowp), own_out)
-    own_up = gather_blocks(low_up, 0)
-    full_up = jnp.concatenate([own_up, swap(own_up, "head", 2)], axis=1)
-    low_down = after(wdown.astype(lowp), own_up)
-    own_down = gather_blocks(low_down, 1)
-    full_down = jnp.concatenate([own_down, swap(own_down, "head", 2)], axis=0)
+    taps = heads_own * RATE * DH
+
+    def conv_natural_order(rows):
+        value = jnp.swapaxes(rows.reshape(conv_rows_own, dp_size, width), 0, 1)
+        value = jnp.swapaxes(value.reshape(dp_size, taps, conv_width), 0, 1)
+        moved = mm(value.reshape(taps, DH), conv_shuffle).astype(lowp)
+        return moved.reshape(heads_own, RATE * DH, DH)
+
+    def conv_block_order(value):
+        moved = mm(value.astype(lowp).reshape(taps, DH), conv_shuffle, NT).astype(lowp)
+        moved = jnp.swapaxes(moved.reshape(taps, dp_size, conv_width), 0, 1)
+        moved = jnp.swapaxes(moved.reshape(dp_size, conv_rows_own, width), 0, 1)
+        return moved.reshape(conv_rows_own, D)
+
+    full_conv = jnp.concatenate(
+        [conv_natural_order(own_one[4 * wide :]), conv_natural_order(far_one[4 * wide :])]
+    )
+
+    hidden_own = wup.shape[1]
+    pack_two = jnp.concatenate([wup.astype(lowp).T, wdown.astype(lowp)])
+    own_two = gather_blocks(after(pack_two, own_one), 1)
+    full_up, full_down = split(own_two, 0, 2)
 
     words = vocab // reach
     z = d // 2
-    low_table = after(table.astype(lowp), own_down)
+    low_table = after(table.astype(lowp), own_two)
     near_table = []
-    for m in range(0, dp_size, 2):
+    for m in order[:reach]:
         part = lax.dynamic_slice_in_dim(low_table, (z ^ (m // 2)) * words, words, 0)
         near_table.append(part if m == 0 else swap(part, "dp", m))
     near_table = jnp.concatenate(near_table, axis=1)
@@ -648,26 +883,21 @@
     slots = -(-words // 256) * 256
     loss_table = jnp.concatenate([loss_table, jnp.zeros((slots - words, D), lowp)], axis=0)
 
-    first_word = h * vocab
-    looked, tok_list, row_list, list_count = lookup(first_word.reshape(1), ids_all, table)
-    looked = looked.reshape(2, -1, width)
-    looked = looked[0] + swap(looked[1], "head", 1)
-    looked = looked.reshape(2, -1, width)
+    own_half, far_half = split(table_rows_all, 0, 2)
+    looked_far = swap(lookup(far_half, table), "head", 1)
+    looked = (lookup(own_half, table) + looked_far).reshape(2, -1, width)
     looked = looked[0] + swap(looked[1], "head", 2)
-    looked = looked.reshape(dp_size, half, width)
-    pieces = [looked[p] if p == 0 else swap(looked[p], "dp", m) for p, m in enumerate(order)]
-    embedded = jnp.concatenate(pieces, axis=1).astype(single)
-    normed, inv_first = rms(embedded, gain_vals[0])
+    looked = lax.all_to_all(looked.reshape(dp_size, half, width), "dp", 0, 0)
+    embedded_low, normed = place_embedding(place, looked, gain_vals[0])
+    embedded = embedded_low.astype(single)
     normed = jnp.concatenate([normed, swap(normed, "head", 1)], axis=0)
 
-    place = jnp.stack([x, d])
     mem_normed = state_norm(place, gain_vals[0], memory, 1)[0]
     old_normed = state_norm(place, gain_vals[0], old_states, RATE)
-    key_value = jnp.concatenate([full_qkv[1], full_qkv[2]], axis=1)
-    all_three = jnp.concatenate([full_qkv[0], key_value], axis=1)
-    comp, old_raw = compress(old_normed, key_value, full_conv)
-    mem = mm(mem_normed, key_value).astype(lowp)
-    seg = mm(normed, all_three).astype(lowp)
+    comp, old_raw = compress(old_normed, pair_weight, full_conv)
+    mem = mm(mem_normed, pair_weight, NT).astype(lowp)
+    query = mm(normed, query_weight, NT).astype(lowp)
+    seg = mm(normed, pair_weight, NT).astype(lowp)
     info = jnp.stack(
         [
             lax.dynamic_index_in_dim(comp_fill, x, 0, keepdims=False),
@@ -675,145 +905,148 @@
             c * half,
         ]
     ).astype(jnp.int32)
-    mixed, lse = attend(info, seg, comp, mem)
+    mixed, lse = attend(info, query, seg, comp, mem)
 
     def core_sum(part):
-        return part[:half] + swap(part[half:].astype(lowp), "head", 1).astype(single)
+        rows = part.shape[0] // 2
+        return part[:rows] + swap(part[rows:].astype(lowp), "head", 1).astype(single)
 
     def core_both(part):
         return jnp.concatenate([part, swap(part, "head", 1)], axis=0)
 
+    def group_sum(part):
+        part = core_sum(part)
+        rows = part.shape[0] // 2
+        return part[:rows] + swap(part[rows:].astype(lowp), "head", 2).astype(single)
+
+    def group_both(part):
+        return core_both(jnp.concatenate([part, swap(part, "head", 2)], axis=0))
+
     after_attn = embedded + core_sum(mm(mixed, full_out))
     ffn_in, inv_second = rms(after_attn, gain_vals[1])
-    ffn_in = core_both(ffn_in)
-    hidden_pre = mm(ffn_in, full_up)
+    ffn_in = group_both(ffn_in)
+    hidden_pre = mm(ffn_in, full_up, NT)
     hidden_act = jax.nn.gelu(hidden_pre).astype(lowp)
-    after_ffn = after_attn + core_sum(mm(hidden_act, full_down))
+    after_ffn = after_attn + group_sum(mm(hidden_act, full_down))
     final_in, inv_third = rms(after_ffn, gain_vals[2])
 
-    word_start = first_word + z * words
+    word_start = (h * vocab + z * words).astype(single)
+    wanted_all = targets_all - word_start
+    wanted_all = jnp.where((wanted_all >= 0) & (wanted_all < words), wanted_all, -1.0)
+    groups = [(0, 1)]
+    pieces = [final_in]
+    mask = dp_size // 2
+    while mask > 1:
+        joined = jnp.concatenate(pieces) if len(pieces) > 1 else pieces[0]
+        pieces.append(swap(reorder(joined, mask), "dp", mask))
+        groups.append((groups[-1][1], 2 * groups[-1][1]))
+        mask //= 2
+    info_all = jnp.stack([wanted_all, mask_all] + [jnp.zeros_like(mask_all)] * 6)
     chunks = []
     infos = []
-    for m in range(0, dp_size, 2):
-        piece = final_in if m == 0 else swap(reorder(final_in, m), "dp", m)
-        pair = jnp.concatenate([piece, swap(piece, "head", 2)], axis=0)
-        chunks.append(core_both(pair))
-        wanted = targets_all[m // 2].reshape(-1) - word_start.astype(single)
-        wanted = jnp.where((wanted >= 0) & (wanted < words), wanted, -1.0)
-        counted = mask_all[m // 2].reshape(-1)
-        infos.append((wanted, counted))
-    blank = jnp.zeros((per_group,), single)
     raised = []
     stats = []
-    for chunk, (wanted, counted) in zip(chunks, infos):
-        packed = jnp.stack([wanted] + [blank] * 7)
+    for (first, last), piece in zip(groups, pieces):
+        chunk = group_both(piece)
+        packed = jnp.transpose(info_all[:, first:last], (0, 2, 3, 1, 4)).reshape(8, -1)
         out, stat = logits_part(words, packed, chunk, loss_table)
+        chunks.append(chunk)
+        infos.append(packed)
         raised.append(out)
-        stats.append(stat)
-    own_stats = jnp.stack([stat[:3] for stat in stats], axis=1)
+        stats.append(stat[:3].reshape(3, 2, 2, last - first, half))
+    own_stats = jnp.concatenate(stats, axis=3)
 
     def combine(first, second):
         top = jnp.maximum(first[0], second[0])
         total = first[1] * jnp.exp(first[0] - top) + second[1] * jnp.exp(second[0] - top)
         return jnp.stack([top, total, first[2] + second[2]])
 
-    grid4 = own_stats.reshape(3, reach, 2, 2, half)
-    other = swap(grid4, "head", 1)
-    grid4 = combine(grid4, jnp.flip(other, 2))
-    other = swap(grid4, "head", 2)
-    grid4 = combine(grid4, jnp.flip(other, 3))
-    step = 1
-    while step < reach:
-        other = swap(grid4, "dp", 2 * step)
-        index = [i ^ step for i in range(reach)]
-        other = jnp.stack([other[:, i] for i in index], axis=1)
-        grid4 = combine(grid4, other)
-        step *= 2
-    merged = grid4.reshape(3, reach, per_group)
+    merged = own_stats
+    merged = combine(merged, jnp.flip(swap(merged, "head", 1), 1))
+    merged = combine(merged, jnp.flip(swap(merged, "head", 2), 2))
+    mask = 2
+    while mask < dp_size:
+        other = split(swap(merged, "dp", mask), 3, reach)
+        other = [other[order.index(j ^ mask)] for j in order[:reach]]
+        merged = combine(merged, jnp.concatenate(other, axis=3))
+        mask *= 2
     log_total = merged[0] + jnp.log(merged[1])
-    own_loss = infos[0][1][:half] * (log_total[0, :half] - merged[2, 0, :half])
-    loss_local = jnp.sum(own_loss)
-
-    dlogits = [None] * reach
-    final_grad = None
-    for i in list(range(1, reach)) + [0]:
-        wanted, counted = infos[i]
-        factor = jnp.exp(own_stats[0, i] - log_total[i]) * counted
-        packed = jnp.stack([wanted, counted, factor] + [blank] * 5)
-        dlogits[i], part = logits_back(packed, raised[i], loss_table)
-        rows = per_group // 2
-        part = part[:rows].astype(single) + swap(part[rows:], "head", 1).astype(single)
-        rows = rows // 2
-        part = part[:rows] + swap(part[rows:].astype(lowp), "head", 2).astype(single)
-        if i:
-            part = reorder(swap(part.astype(lowp), "dp", 2 * i), 2 * i).astype(single)
-        final_grad = part if final_grad is None else final_grad + part
-
-    keep, send = table_grad_part(dlogits[:4], chunks[:4])
-    for start in range(4, reach, 4):
-        more = table_grad_part(dlogits[start : start + 4], chunks[start : start + 4])
-        keep = keep + more[0]
-        send = (send.astype(single) + more[1].astype(single)).astype(lowp)
-    keep = keep + swap(send.astype(lowp), "dp", 1).astype(single)
+    loss_local = jnp.sum(mask_all[0, 0, 0] * (log_total[0, 0, 0] - merged[2, 0, 0, 0]))
+    factor_all = jnp.exp(own_stats[0] - log_total)
+
+    dlogits = [None] * len(groups)
+    parts = []
+    for i in reversed(range(len(groups))):
+        first, last = groups[i]
+        factor = factor_all[:, :, first:last].reshape(1, -1) * infos[i][1:2]
+        factor = jnp.broadcast_to(factor, infos[i].shape)
+        dlogits[i], part = logits_back(infos[i], factor, raised[i], loss_table)
+        parts.append(group_sum(part.astype(single)))
+    mask = 2
+    total = jnp.zeros(())
+    for i in range(len(groups) - 1):
+        moved = swap(reorder(parts[0].astype(lowp), mask), "dp", mask).astype(single)
+        rest = []
+        start = 0
+        for part in reversed(parts[1:]):
+            rest.append(part + moved[start : start + part.shape[0]])
+            start += part.shape[0]
+        parts = rest[::-1]
+        mask *= 2
+    final_grad = parts[0]
+
+    keep, send = table_grad_part(dlogits, chunks)
+    keep = keep + swap(send, "dp", 1).astype(single)
     table_base = jnp.zeros((vocab, width), single)
-    for i, part in enumerate(split(keep[:words], 1, reach)):
-        part = part if i == 0 else swap(part.astype(lowp), "dp", 2 * i).astype(single)
-        table_base = lax.dynamic_update_slice_in_dim(table_base, part, (z ^ i) * words, 0)
+    for m, part in zip(order[:reach], split(keep[:words], 1, reach)):
+        part = part if m == 0 else swap(part.astype(lowp), "dp", m).astype(single)
+        table_base = lax.dynamic_update_slice_in_dim(table_base, part, (z ^ (m // 2)) * words, 0)
 
     grad_after_ffn = rms_back(after_ffn, inv_third, gain_vals[2], final_grad)
-    down_in = core_both(grad_after_ffn.astype(lowp))
+    down_in = group_both(grad_after_ffn.astype(lowp))
     act_grad = mm(down_in, full_down, NT)
     pre_grad = jax.vjp(jax.nn.gelu, hidden_pre)[1](act_grad)[0].astype(lowp)
-    ffn_in_grad = core_sum(mm(pre_grad, full_up, NT))
+    ffn_in_grad = group_sum(mm(pre_grad, full_up))
     grad_after_attn = grad_after_ffn + rms_back(after_attn, inv_second, gain_vals[1], ffn_in_grad)
     attn_in = core_both(grad_after_attn.astype(lowp))
 
     mixed_grad = mm(attn_in, full_out, NT).astype(lowp)
-    seg_grad, comp_grad, mem_grad = attend_back(info, seg, comp, mem, lse, mixed_grad)
-    seg_in_grad = core_sum(mm(seg_grad, all_three, NT))
-    embed_grad = grad_after_attn + rms_back(embedded, inv_first, gain_vals[0], seg_in_grad)
-    pieces = [
-        part if m == 0 else swap(part, "dp", m)
-        for part, m in zip(split(embed_grad.astype(lowp), 1, dp_size), order)
-    ]
-    rows_grad = jnp.stack(pieces)
+    seg_grad, comp_grad, mem_grad = attend_back(info, query, seg, comp, mem, lse, mixed_grad)
+    seg_in = mm(seg_grad, jnp.concatenate([query_weight, pair_weight]))
+    rows_grad = embed_back(
+        place,
+        embedded_low,
+        gain_vals[0],
+        seg_in[:half],
+        swap(seg_in[half:].astype(lowp), "head", 1),
+        grad_after_attn,
+    )
+    rows_grad = lax.all_to_all(rows_grad, "dp", 0, 0)
     rows_grad = jnp.stack([rows_grad, swap(rows_grad, "head", 2)])
     rows_grad = jnp.stack([rows_grad, swap(rows_grad, "head", 1)]).reshape(-1, width)
 
+    two = reduce_blocks(*hidden_grads(pre_grad, hidden_act, ffn_in, down_in))
+    up_grad = two[:hidden_own].T
+    down_grad = two[hidden_own:]
     old_grad, conv_sum = expand(comp_grad, old_raw, full_conv)
-    seg_sum = mm(normed, seg_grad, TN)
-    side_sum = mm(mem_normed, mem_grad, TN) + mm(
-        old_normed.reshape(-1, D), old_grad.reshape(-1, old_grad.shape[-1]), TN
+    far_sum, own_sum = attn_grads(
+        seg_grad,
+        mixed,
+        mem_grad,
+        old_grad.reshape(-1, old_grad.shape[-1]),
+        normed,
+        attn_in,
+        mem_normed,
+        old_normed.reshape(-1, D),
     )
-    wide = seg_sum.shape[1] // 3
-    own = wide // 2
-
-    def three(first):
-        def cols(array, base):
-            return array[:, base + first : base + first + own]
-
-        return jnp.stack(
-            [
-                cols(seg_sum, 0),
-                cols(seg_sum, wide) + cols(side_sum, 0),
-                cols(seg_sum, 2 * wide) + cols(side_sum, wide),
-            ]
-        )
-
-    def in_order(value):
-        moved = mm(value.astype(lowp).reshape(-1, DH), conv_shuffle, NT)
-        return moved.reshape(value.shape)
-
-    heads_own = wconv.shape[0]
-    hidden_own = wup.shape[1]
-    down_sum = mm(hidden_act, down_in, TN)
-    up_sum = mm(ffn_in, pre_grad, TN)
-    out_sum = mm(mixed, attn_in, TN)
-    down_grad = reduce_blocks(down_sum[:hidden_own], down_sum[hidden_own:], 1)
-    up_grad = reduce_blocks(up_sum[:, :hidden_own], up_sum[:, hidden_own:], 0)
-    out_grad = reduce_blocks(out_sum[: wout.shape[0]], out_sum[wout.shape[0] :], 1)
-    qkv_grad = reduce_blocks(three(0), three(own), 1)
-    conv_grad = reduce_blocks(in_order(conv_sum[:heads_own]), in_order(conv_sum[heads_own:]), 2)
+    far_sum = jnp.concatenate([far_sum, conv_block_order(conv_sum[heads_own:])])
+    own_sum = jnp.concatenate([own_sum, conv_block_order(conv_sum[:heads_own]).astype(single)])
+    one = own_sum + swap(far_sum, "head", 2).astype(single)
+    one = reduce_blocks(*split(one, 1, 2))
+    qkv_grad = jnp.swapaxes(one[: 3 * wide].reshape(3, wide, width), 1, 2)
+    out_grad = one[3 * wide : 4 * wide]
+    conv_grad = one[4 * wide :].reshape(wconv.shape)
+    tok_list, row_list, list_count = own_list(after(table_rows_all, final_in), vocab)
     table_grad = scatter(list_count, tok_list, row_list, table_base, rows_grad)
 
     gains_low = gains.astype(lowp).astype(single)
@@ -833,25 +1066,12 @@
     row_axes = ("head", "dp", "head", "head", "dp", "head")
     col_axes = ("dp", "head", "dp", "dp", "head", "dp")
 
-    def pack(arrays):
-        joined = jnp.concatenate([a.reshape(-1) for a in arrays])
-        return jnp.concatenate([joined, jnp.zeros((-joined.shape[0] % 1024,), single)])
-
-    def unpack(joined, arrays):
-        result = []
-        start = 0
-        for a in arrays:
-            result.append(joined[start : start + a.size].reshape(a.shape))
-            start += a.size
-        return result
-
-    def sum_over(arrays, axis):
-        joined = pack(arrays)
+    def sum_over_dp(joined):
         mask = 1
-        while mask < sizes[axis]:
-            joined = joined + swap(joined, axis, mask)
+        while mask < dp_size:
+            joined = joined + swap(joined, "dp", mask)
             mask *= 2
-        return unpack(joined, arrays)
+        return joined
 
     row_part = []
     col_part = []
@@ -867,14 +1087,28 @@
     for which in range(3):
         scalar_list.append(jnp.sum(gains[which] * gains[which]) / head_size)
     scalar_list.append(loss_local)
-    scalars = jnp.stack(scalar_list)
-    row_q, row_u, col_e, col_o, col_c, col_d, gain_raw, scalars = sum_over(
-        [row_part[1], row_part[4], col_part[0], col_part[2], col_part[3], col_part[5], gain_part, scalars],
+    row_q, row_u, col_e, col_o, col_c, col_d, gain_raw, scalars = lax.psum(
+        (
+            row_part[1],
+            row_part[4],
+            col_part[0],
+            col_part[2],
+            col_part[3],
+            col_part[5],
+            gain_part,
+            jnp.stack(scalar_list),
+        ),
         "head",
     )
-    row_e, row_o, row_c, row_d, col_q, col_u, scalars = sum_over(
-        [row_part[0], row_part[2], row_part[3], row_part[5], col_part[1], col_part[4], scalars], "dp"
-    )
+    members = [col_part[4], row_part[5], row_part[3], row_part[2], col_part[1], scalars, row_part[0]]
+    joined = jnp.concatenate([m.reshape(-1) for m in members])
+    joined = sum_over_dp(jnp.concatenate([joined, jnp.zeros((-joined.shape[0] % 1024,), single)]))
+    sums = []
+    start = 0
+    for member in members:
+        sums.append(joined[start : start + member.size].reshape(member.shape))
+        start += member.size
+    col_u, row_d, row_c, row_o, col_q, scalars, row_e = sums
     row_sums = [row_e, row_q, row_o, row_c, row_u, row_d]
     col_sums = [col_e, col_q, col_o, col_c, col_u, col_d]
     weight_total = scalars[12:21]
@@ -911,7 +1145,8 @@
     gain_dir = gain_scaled * lax.rsqrt(second_new)
     for which in range(3):
         update_sq.append(jnp.sum(gain_dir[which] * gain_dir[which]) / head_size)
-    update_total = sum_over(sum_over([jnp.stack(update_sq)], "head"), "dp")[0]
+    update_total = jnp.concatenate([jnp.stack(update_sq), jnp.zeros((1024 - 9,), single)])
+    update_total = sum_over_dp(lax.psum(update_total, "head"))[:9]
     results = [loss_all, count_all]
     for index in range(6):
         factor = jnp.maximum(0.001, jnp.sqrt(weight_total[index] / counts[index]))

time: 1160 us -> 958 us (0.83)
  waiting for transfers between devices: 453 us -> 309 us
  starting transfers between devices: 190 us -> 86.1 us
  Pallas kernels: 181 us -> 241 us
  local copies, waits for them, and re-layouts: 146 us -> 106 us
  other arithmetic: 114 us -> 133 us
  blocking collectives: 0 us -> 12.6 us
    ppermute x124 -> x67, waiting for transfers between devices: 453 us -> 309 us  [swap(): return lax.ppermute(value, axis, [(i, i ^ mask) for i in range(size)])]
    ppermute x124 -> x67, starting transfers between devices: 190 us -> 77.3 us  [swap(): return lax.ppermute(value, axis, [(i, i ^ mask) for i in range(size)])]
    unnamed x515 -> x266, local copies, waits for them, and re-layouts: 79.1 us -> 38 us
    pallas_call x1 -> x7, Pallas kernels: 45 us -> 77.1 us  [the longest x1 28.3 us: own_list(): pl.pallas_call(functools.partial(list_kernel, vocab), out_shape=(jax.Shap...]
    psum x0 -> x2, blocking collectives: none -> 12.6 us  [the longest x1 6.8 us: local(): lax.psum((row_part[1], row_part[4], col_part[0], col_part[2], col_part[3]...]
    pallas_call x4 -> x3, Pallas kernels: 29.6 us -> 38.6 us  [logits_part(): pl.pallas_call(functools.partial(logits_kernel, words), grid=(rows // til...]
    pallas_call x4 -> x3, Pallas kernels: 33.5 us -> 37.8 us  [logits_back(): pl.pallas_call(logits_back_kernel, grid=(rows // tile,), out_shape=(jax.S...]
    dot_general x18 -> x14, matrix products: 34.6 us -> 35.2 us  [mm(): return lax.dot_general(left, right, dims, preferred_element_type=single)]
  transfers between devices with their start and end apart: 124 -> 69, of which waited for: 59 -> 34; matrix products, arithmetic and copies ran while one was open for 15% -> 21% of each run, Pallas kernels for 14% -> 22%
where the time goes in v3:
time: 958 us; the launch traced here: 951 us
  waiting for transfers between devices  309 us (32%)
  Pallas kernels  241 us (25%)
  other arithmetic  133 us (14%)
  local copies, waits for them, and re-layouts  106 us (11%)
  starting transfers between devices  86.1 us (9%)
  matrix products  35.2 us (4%)
  between operations  27.8 us (3%)
  blocking collectives  12.6 us (1%)
    ppermute x67, waiting for transfers between devices, swap(): return lax.ppermute(value, axis, [(i, i ^ mask) for i in range(size)])  309 us
    ppermute x67, starting transfers between devices, swap(): return lax.ppermute(value, axis, [(i, i ^ mask) for i in range(size)])  77.3 us
    pallas_call x3, Pallas kernels, logits_part(): pl.pallas_call(functools.partial(logits_kernel, words), grid=(rows // til...  38.6 us
    unnamed x266, local copies, waits for them, and re-layouts  38 us
    pallas_call x3, Pallas kernels, logits_back(): pl.pallas_call(logits_back_kernel, grid=(rows // tile,), out_shape=(jax.S...  37.8 us
    dot_general x14, matrix products, mm(): return lax.dot_general(left, right, dims, preferred_element_type=single)  35.2 us
    pallas_call x1, Pallas kernels, own_list(): pl.pallas_call(functools.partial(list_kernel, vocab), out_shape=(jax.Shap...  28.3 us
    pallas_call x1, Pallas kernels, table_grad_part(): pl.pallas_call(functools.partial(table_grad_kernel, count), grid=(slots /...  24.1 us
  transfers between devices with their start and end apart: 69, of which 34 were waited for; matrix products, arithmetic and copies ran while one was open for 21% of the time, Pallas kernels for 22%

profile of v3, /device:TPU:0, one launch (start us, length us, event | category | flops | bytes accessed | tf_op | source)
XLA Modules:
  0.0 950.6 jit_solution(13008118455551304216)
XLA Ops:
  24.6 12.4 %collective-permute-done.6 = bf16[1120,128]{1,0:T(8,128)(2,1)S(1)} collective-permute-done((bf16[1120,128]{1,0:T(8,128)(2,1)S(1)}, bf16[1120,128]{1,0:T(8,128)(2,1)S(1)}, u32[]{:S(2)}, u32[]{:S(2)}) %collective-permute-start.6) | collective-permute-done | bytes 286752 | tf_op jit(solution)/shard_map/ppermute | solution.py:38
  37.9 8.6 shard_map.501
  53.7 8.6 shard_map.500
  68.8 8.7 collective-permute-done.8
  112.4 11.1 %collective-permute-done.13 = bf16[2048,128]{1,0:T(8,128)(2,1)S(1)} collective-permute-done((bf16[2048,128]{1,0:T(8,128)(2,1)S(1)}, bf16[2048,128]{1,0:T(8,128)(2,1)S(1)}, u32[]{:S(2)}, u32[]{:S(2)}) %collective-permute-start.13) | collective-permute-done | bytes 524320 | tf_op jit(solution)/shard_map/ppermute | solution.py:38
  153.6 8.1 shard_map.504
  161.6 10.9 %shard_map.506 = (bf16[512,512]{1,0:T(8,128)(2,1)}, f32[4,512,1]{2,1,0:T(8,128)}) custom-call(s32[3]{0:T(128)} %pad_add_fusion.1.info_ref, bf16[512,512]{1,0:T(8,128)(2,1)} %convolution_convert_fusion.3.q_ref, bf16[512,1024]{1,0:T(8,128)(2,1)} %convolution_convert_fusion.1.ks_ref.vs_ref, bf16[512,1024]{1,0:T(8,128)(2,1)} %convolution_convert_fusion.1.ks_ref.vs_ref, ...), custom_call_target="tpu_custom_call" | custom-call | flops 7340032000 | bytes 6291456 | tf_op jit(solution)/shard_map/pallas_call | solution.py:481
  179.6 12.5 %collective-permute-done.11 = bf16[256,1024]{1,0:T(8,128)(2,1)S(1)} collective-permute-done((bf16[256,1024]{1,0:T(8,128)(2,1)S(1)}, bf16[256,1024]{1,0:T(8,128)(2,1)S(1)}, u32[]{:S(2)}, u32[]{:S(2)}) %collective-permute-start.11) | collective-permute-done | bytes 524320 | tf_op jit(solution)/shard_map/ppermute | solution.py:38
  194.0 30.0 %collective-permute-done.15 = bf16[2048,512]{1,0:T(8,128)(2,1)S(1)} collective-permute-done((bf16[2048,512]{1,0:T(8,128)(2,1)S(1)}, bf16[2048,512]{1,0:T(8,128)(2,1)S(1)}, u32[]{:S(2)}, u32[]{:S(2)}) %collective-permute-start.15) | collective-permute-done | bytes 2097184 | tf_op jit(solution)/shard_map/ppermute | solution.py:38
  261.5 39.1 %collective-permute-done.24 = bf16[256,1024]{1,0:T(8,128)(2,1)S(1)} collective-permute-done((bf16[256,1024]{1,0:T(8,128)(2,1)S(1)}, bf16[256,1024]{1,0:T(8,128)(2,1)S(1)}, u32[]{:S(2)}, u32[]{:S(2)}) %collective-permute-start.24) | collective-permute-done | bytes 524320 | tf_op jit(solution)/shard_map/ppermute | solution.py:38
  301.8 9.9 %collective-permute-done.20 = bf16[2000,128]{1,0:T(8,128)(2,1)} collective-permute-done((bf16[2000,128]{1,0:T(8,128)(2,1)}, bf16[2000,128]{1,0:T(8,128)(2,1)}, u32[]{:S(2)}, u32[]{:S(2)}) %collective-permute-start.20) | collective-permute-done | bytes 512032 | tf_op jit(solution)/shard_map/ppermute | solution.py:38
  320.5 11.1 %collective-permute-start.27 = (bf16[512,1024]{1,0:T(8,128)(2,1)}, bf16[512,1024]{1,0:T(8,128)(2,1)}, u32[]{:S(2)}, u32[]{:S(2)}) collective-permute-start(bf16[512,1024]{1,0:T(8,128)(2,1)} %get-tuple-element.264), channel_id=1, source_target_pairs={{0,8},{4,12},{8,0},{12,4},{16,24},{20,28},{24,16},{28,20},{1,9},{5... | collective-permute-start | bytes 3145736 | tf_op jit(solution)/shard_map/ppermute | solution.py:38
  334.0 20.7 %collective-permute-done.27 = bf16[512,1024]{1,0:T(8,128)(2,1)} collective-permute-done((bf16[512,1024]{1,0:T(8,128)(2,1)}, bf16[512,1024]{1,0:T(8,128)(2,1)}, u32[]{:S(2)}, u32[]{:S(2)}) %collective-permute-start.27) | collective-permute-done | bytes 1048608 | tf_op jit(solution)/shard_map/ppermute | solution.py:38
  383.4 10.5 %shard_map.508 = (bf16[1024,2048]{1,0:T(8,128)(2,1)}, f32[8,1024]{1,0:T(8,128)}) custom-call(f32[8,1024]{1,0:T(8,128)} %reshape_transpose.7.info_ref, bf16[1024,1024]{1,0:T(8,128)(2,1)} %constant_dynamic-update-slice_fusion.24.in_ref.refs_4_, bf16[2048,1024]{1,0:T(8,128)(2,1)} %concatenate.189.table_ref), custom_call_target="tpu_custom_call" | custom-call | flops 8589934592 | bytes 10485760 | tf_op jit(solution)/shard_map/pallas_call | solution.py:549
  397.5 10.5 %shard_map.507 = (bf16[1024,2048]{1,0:T(8,128)(2,1)}, f32[8,1024]{1,0:T(8,128)}) custom-call(f32[8,1024]{1,0:T(8,128)} %reshape_transpose.6.info_ref, bf16[1024,1024]{1,0:T(8,128)(2,1)} %pad_maximum_fusion.4.in_ref.refs_3_, bf16[2048,1024]{1,0:T(8,128)(2,1)} %concatenate.189.table_ref), custom_call_target="tpu_custom_call" | custom-call | flops 8589934592 | bytes 10485760 | tf_op jit(solution)/shard_map/pallas_call | solution.py:549
  415.4 17.7 %shard_map.509 = (bf16[2048,2048]{1,0:T(8,128)(2,1)}, f32[8,2048]{1,0:T(8,128)}) custom-call(f32[8,2048]{1,0:T(8,128)} %reshape.520.info_ref, bf16[2048,1024]{1,0:T(8,128)(2,1)} %constant_dynamic-update-slice_fusion.27.in_ref.refs_5_, bf16[2048,1024]{1,0:T(8,128)(2,1)} %concatenate.189.table_ref), custom_call_target="tpu_custom_call" | custom-call | flops 17179869184 | bytes 10485760 | tf_op jit(solution)/shard_map/pallas_call | solution.py:549
  452.5 17.0 %shard_map.511 = (bf16[2048,2048]{1,0:T(8,128)(2,1)}, bf16[2048,1024]{1,0:T(8,128)(2,1)}) custom-call(f32[8,2048]{1,0:T(8,128)} %reshape.520.info_ref, f32[8,2048]{1,0:T(8,128)} %broadcast_in_dim.35.factor_ref, bf16[2048,2048]{1,0:T(8,128)(2,1)} %get-tuple-element.77.in_ref, bf16[2048,1024]{1,0:T(8,128)(2,1)} %concatenate.189.table_ref), custom_call_target="tpu_custom_call" | custom-call | flops 17179869184 | bytes 12582912 | tf_op jit(solution)/shard_map/pallas_call | solution.py:585
  479.4 10.6 %shard_map.512 = (bf16[1024,2048]{1,0:T(8,128)(2,1)}, bf16[1024,1024]{1,0:T(8,128)(2,1)}) custom-call(f32[8,1024]{1,0:T(8,128)} %reshape_transpose.7.info_ref, f32[8,1024]{1,0:T(8,128)} %broadcast_in_dim.36.factor_ref, bf16[1024,2048]{1,0:T(8,128)(2,1)} %get-tuple-element.79.in_ref, bf16[2048,1024]{1,0:T(8,128)(2,1)} %concatenate.189.table_ref), custom_call_target="tpu_custom_call" | custom-call | flops 8589934592 | bytes 12582912 | tf_op jit(solution)/shard_map/pallas_call | solution.py:585
  493.0 10.2 %shard_map.510 = (bf16[1024,2048]{1,0:T(8,128)(2,1)}, bf16[1024,1024]{1,0:T(8,128)(2,1)}) custom-call(f32[8,1024]{1,0:T(8,128)} %reshape_transpose.6.info_ref, f32[8,1024]{1,0:T(8,128)} %broadcast_in_dim.34.factor_ref, bf16[1024,2048]{1,0:T(8,128)(2,1)} %get-tuple-element.75.in_ref, bf16[2048,1024]{1,0:T(8,128)(2,1)} %concatenate.189.table_ref), custom_call_target="tpu_custom_call" | custom-call | flops 8589934592 | bytes 12582912 | tf_op jit(solution)/shard_map/pallas_call | solution.py:585
  513.4 19.3 %collective-permute-done.38 = bf16[512,1024]{1,0:T(8,128)(2,1)S(1)} collective-permute-done((bf16[512,1024]{1,0:T(8,128)(2,1)S(1)}, bf16[512,1024]{1,0:T(8,128)(2,1)S(1)}, u32[]{:S(2)}, u32[]{:S(2)}) %collective-permute-start.38) | collective-permute-done | bytes 1048608 | tf_op jit(solution)/shard_map/ppermute | solution.py:38
  535.9 22.9 %collective-permute-done.41 = bf16[256,1024]{1,0:T(8,128)(2,1)S(1)} collective-permute-done((bf16[256,1024]{1,0:T(8,128)(2,1)S(1)}, bf16[256,1024]{1,0:T(8,128)(2,1)S(1)}, u32[]{:S(2)}, u32[]{:S(2)}) %collective-permute-start.41) | collective-permute-done | bytes 524320 | tf_op jit(solution)/shard_map/ppermute | solution.py:38
  575.9 24.1 %shard_map.518 = (f32[2048,512]{1,0:T(8,128)}, bf16[2048,512]{1,0:T(8,128)(2,1)}) custom-call(bf16[1024,2048]{1,0:T(8,128)(2,1)} %get-tuple-element.96.refs_0_, bf16[1024,2048]{1,0:T(8,128)(2,1)} %get-tuple-element.97.refs_1_, bf16[2048,2048]{1,0:T(8,128)(2,1)} %get-tuple-element.98.refs_2_, bf16[1024,1024]{1,0:T(8,128)(2,1)} %pad_maximum_fusion.4.in_ref.refs_3_, ...), custom_call_target="tpu_custom_call" | custom-call | flops 25769803776 | bytes 31457280 | tf_op jit(solution)/shard_map/pallas_call | solution.py:631
  603.1 28.3 %shard_map.517 = (s32[8200]{0:T(1024)}, s32[8200]{0:T(1024)}, s32[1]{0:T(128)}) custom-call(s32[8192]{0:T(1024)} %copy-done.44), custom_call_target="tpu_custom_call" | custom-call | bytes 41943040 | tf_op jit(solution)/shard_map/pallas_call | solution.py:175
  632.1 7.9 fusion.6.pre_ref
  671.3 11.4 %shard_map.513 = (f32[2048,512]{1,0:T(8,128)}, bf16[2048,512]{1,0:T(8,128)(2,1)}) custom-call(bf16[1024,1024]{1,0:T(8,128)(2,1)} %copy-done.107, bf16[1024,1024]{1,0:T(8,128)(2,1)} %copy-done.106, bf16[1024,1024]{1,0:T(8,128)(2,1)} %pad_maximum_fusion.2.in_ref, bf16[1024,1024]{1,0:T(8,128)(2,1)} %pad_maximum_fusion.6.down_ref), custom_call_target="tpu_custom_call" | custom-call | flops 6442450944 | bytes 16777216 | tf_op jit(solution)/shard_map/pallas_call | solution.py:665
  684.7 15.1 %shard_map.514 = (bf16[512,1536]{1,0:T(8,128)(2,1)}, bf16[512,1024]{1,0:T(8,128)(2,1)}, bf16[512,1024]{1,0:T(8,128)(2,1)}) custom-call(s32[3]{0:T(128)} %pad_add_fusion.1.info_ref, bf16[512,512]{1,0:T(8,128)(2,1)} %convolution_convert_fusion.3.q_ref, bf16[512,1024]{1,0:T(8,128)(2,1)} %convolution_convert_fusion.1.ks_ref.vs_ref, ...), custom_call_target="tpu_custom_call" | custom-call | flops 11534336000 | bytes 9437184 | tf_op jit(solution)/shard_map/pallas_call | solution.py:502
  708.1 14.8 %shard_map.516 = (bf16[1024,1024]{1,0:T(8,128)(2,1)}, f32[1024,1024]{1,0:T(8,128)}) custom-call(bf16[512,1536]{1,0:T(8,128)(2,1)} %get-tuple-element.84.seg_ref, bf16[512,512]{1,0:T(8,128)(2,1)} %get-tuple-element.69.mixed_ref, bf16[512,1024]{1,0:T(8,128)(2,1)} %get-tuple-element.85.mem_ref, bf16[1536,1024]{1,0:T(8,128)(2,1)} %bitcast.426, ...), custom_call_target="tpu_custom_call" | custom-call | flops 9437184000 | bytes 20971520 | tf_op jit(solution)/shard_map/pallas_call | solution.py:726
  752.2 28.3 %collective-permute-done.50 = bf16[1120,1024]{1,0:T(8,128)(2,1)} collective-permute-done((bf16[1120,1024]{1,0:T(8,128)(2,1)}, bf16[1120,1024]{1,0:T(8,128)(2,1)}, u32[]{:S(2)}, u32[]{:S(2)}) %collective-permute-start.50) | collective-permute-done | bytes 2293792 | tf_op jit(solution)/shard_map/ppermute | solution.py:38
  797.5 9.3 collective-permute-done.59
  824.5 13.4 %shard_map.520 = f32[8000,128]{1,0:T(8,128)} custom-call(s32[1]{0:T(128)} %get-tuple-element.93.count_ref, s32[8200]{0:T(1024)} %get-tuple-element.94.tok_ref, s32[8200]{0:T(1024)} %get-tuple-element.95.row_ref, f32[8000,128]{1,0:T(8,128)} %convert_dynamic-update-slice_fusion.base_ref, bf16[8192,128]{1,0:T(8,128)(2,1)} %bitcast.371), custom_call_target="tpu_custom_call" | custom-call | bytes 31457280 | tf_op jit(solution)/shard_map/pallas_call | solution.py:265
  843.5 8.9 collective-permute-done.53
  855.1 8.5 stack.218
  (668 shorter events, 442.5 us)
Async XLA Ops:
  52.1 25.4 %collective-permute-start.8 = (bf16[1120,512]{1,0:T(8,128)(2,1)}, bf16[1120,512]{1,0:T(8,128)(2,1)S(1)}, u32[]{:S(2)}, u32[]{:S(2)}) collective-permute-start(bf16[1120,512]{1,0:T(8,128)(2,1)} %pad_maximum_fusion.10), channel_id=1, source_target_pairs={{0,4},{4,0},{8,12},{12,8},{16,20},{20,16},{24,28},{28,24},{1,5},{5... | collective-permute-start | bytes 3440648 | tf_op jit(solution)/shard_map/ppermute | solution.py:38
  78.6 49.2 %collective-permute-start.9 = (bf16[1120,1024]{1,0:T(8,128)(2,1)}, bf16[1120,1024]{1,0:T(8,128)(2,1)}, u32[]{:S(2)}, u32[]{:S(2)}) collective-permute-start(bf16[1120,1024]{1,0:T(8,128)(2,1)} %constant_dynamic-update-slice_fusion.3), channel_id=1, source_target_pairs={{0,2},{1,3},{2,0},{3,1},{4,6},{5,7},{6,4},{7,5},{8,10},{9,11},{10,... | collective-permute-start | bytes 6881288 | tf_op jit(solution)/shard_map/ppermute | solution.py:38
  100.1 23.4 %collective-permute-start.13 = (bf16[2048,128]{1,0:T(8,128)(2,1)S(1)}, bf16[2048,128]{1,0:T(8,128)(2,1)S(1)}, u32[]{:S(2)}, u32[]{:S(2)}) collective-permute-start(bf16[2048,128]{1,0:T(8,128)(2,1)S(1)} %pad_maximum_fusion.22), channel_id=1, source_target_pairs={{0,16},{4,20},{8,24},{12,28},{16,0},{20,4},{24,8},{28,12},{1,17},{... | collective-permute-start | bytes 1572872 | tf_op jit(solution)/shard_map/ppermute | solution.py:38
  124.7 49.8 %collective-permute-start.14 = (bf16[2048,256]{1,0:T(8,128)(2,1)}, bf16[2048,256]{1,0:T(8,128)(2,1)}, u32[]{:S(2)}, u32[]{:S(2)}) collective-permute-start(bf16[2048,256]{1,0:T(8,128)(2,1)} %pad_maximum_fusion.13), channel_id=1, source_target_pairs={{0,8},{4,12},{8,0},{12,4},{16,24},{20,28},{24,16},{28,20},{1,9},{5... | collective-permute-start | bytes 3145736 | tf_op jit(solution)/shard_map/ppermute | solution.py:38
  176.0 48.0 %collective-permute-start.15 = (bf16[2048,512]{1,0:T(8,128)(2,1)S(1)}, bf16[2048,512]{1,0:T(8,128)(2,1)S(1)}, u32[]{:S(2)}, u32[]{:S(2)}) collective-permute-start(bf16[2048,512]{1,0:T(8,128)(2,1)S(1)} %pad_maximum_fusion.3), channel_id=1, source_target_pairs={{0,4},{4,0},{8,12},{12,8},{16,20},{20,16},{24,28},{28,24},{1,5},{5... | collective-permute-start | bytes 6291464 | tf_op jit(solution)/shard_map/ppermute | solution.py:38
  192.2 32.1 %collective-permute-start.12 = (bf16[512,1024]{1,0:T(8,128)(2,1)S(1)}, bf16[512,1024]{1,0:T(8,128)(2,1)S(1)}, u32[]{:S(2)}, u32[]{:S(2)}) collective-permute-start(bf16[512,1024]{1,0:T(8,128)(2,1)S(1)} %pad_maximum_fusion.12), channel_id=1, source_target_pairs={{0,1},{1,0},{2,3},{3,2},{4,5},{5,4},{6,7},{7,6},{8,9},{9,8},{10,11... | collective-permute-start | bytes 3145736 | tf_op jit(solution)/shard_map/ppermute | solution.py:38
  252.3 48.3 %collective-permute-start.24 = (bf16[256,1024]{1,0:T(8,128)(2,1)S(1)}, bf16[256,1024]{1,0:T(8,128)(2,1)S(1)}, u32[]{:S(2)}, u32[]{:S(2)}) collective-permute-start(bf16[256,1024]{1,0:T(8,128)(2,1)S(1)} %constant_dynamic-update-slice_fusion.16), channel_id=1, source_target_pairs={{0,16},{4,20},{8,24},{12,28},{16,0},{20,4},{24,8},{28,12},{1,17},{... | collective-permute-start | bytes 1572872 | tf_op jit(solution)/shard_map/ppermute | solution.py:38
  256.8 54.8 %collective-permute-start.20 = (bf16[2000,128]{1,0:T(8,128)(2,1)}, bf16[2000,128]{1,0:T(8,128)(2,1)}, u32[]{:S(2)}, u32[]{:S(2)}) collective-permute-start(bf16[2000,128]{1,0:T(8,128)(2,1)} %get-tuple-element.247), channel_id=1, source_target_pairs={{0,16},{4,20},{8,24},{12,28},{16,0},{20,4},{24,8},{28,12},{1,17},{... | collective-permute-start | bytes 1536008 | tf_op jit(solution)/shard_map/ppermute | solution.py:38
  256.9 54.8 %collective-permute-start.21 = (bf16[2000,128]{1,0:T(8,128)(2,1)}, bf16[2000,128]{1,0:T(8,128)(2,1)}, u32[]{:S(2)}, u32[]{:S(2)}) collective-permute-start(bf16[2000,128]{1,0:T(8,128)(2,1)} %get-tuple-element.246), channel_id=1, source_target_pairs={{0,8},{4,12},{8,0},{12,4},{16,24},{20,28},{24,16},{28,20},{1,9},{5... | collective-permute-start | bytes 1536008 | tf_op jit(solution)/shard_map/ppermute | solution.py:38
  258.0 53.7 %collective-permute-start.22 = (bf16[2000,128]{1,0:T(8,128)(2,1)}, bf16[2000,128]{1,0:T(8,128)(2,1)}, u32[]{:S(2)}, u32[]{:S(2)}) collective-permute-start(bf16[2000,128]{1,0:T(8,128)(2,1)} %get-tuple-element.245), channel_id=1, source_target_pairs={{0,24},{4,28},{8,16},{12,20},{16,8},{20,12},{24,0},{28,4},{1,25},{... | collective-permute-start | bytes 1536008 | tf_op jit(solution)/shard_map/ppermute | solution.py:38
  261.2 54.5 %collective-permute-start.18 = (bf16[256,1024]{1,0:T(8,128)(2,1)S(1)}, bf16[256,1024]{1,0:T(8,128)(2,1)}, u32[]{:S(2)}, u32[]{:S(2)}) collective-permute-start(bf16[256,1024]{1,0:T(8,128)(2,1)S(1)} %multiply_convert_fusion.1), channel_id=1, source_target_pairs={{0,2},{1,3},{2,0},{3,1},{4,6},{5,7},{6,4},{7,5},{8,10},{9,11},{10,... | collective-permute-start | bytes 1572872 | tf_op jit(solution)/shard_map/ppermute | solution.py:38
  314.7 47.0 %collective-permute-start.23 = (bf16[2000,512]{1,0:T(8,128)(2,1)}, bf16[2000,512]{1,0:T(8,128)(2,1)}, u32[]{:S(2)}, u32[]{:S(2)}) collective-permute-start(bf16[2000,512]{1,0:T(8,128)(2,1)} %pad_maximum_fusion.8), channel_id=1, source_target_pairs={{0,4},{4,0},{8,12},{12,8},{16,20},{20,16},{24,28},{28,24},{1,5},{5... | collective-permute-start | bytes 6144008 | tf_op jit(solution)/shard_map/ppermute | solution.py:38
  320.5 34.2 %collective-permute-start.27 = (bf16[512,1024]{1,0:T(8,128)(2,1)}, bf16[512,1024]{1,0:T(8,128)(2,1)}, u32[]{:S(2)}, u32[]{:S(2)}) collective-permute-start(bf16[512,1024]{1,0:T(8,128)(2,1)} %get-tuple-element.264), channel_id=1, source_target_pairs={{0,8},{4,12},{8,0},{12,4},{16,24},{20,28},{24,16},{28,20},{1,9},{5... | collective-permute-start | bytes 3145736 | tf_op jit(solution)/shard_map/ppermute | solution.py:38
  354.6 24.0 %collective-permute-start.28 = (bf16[512,1024]{1,0:T(8,128)(2,1)}, bf16[512,1024]{1,0:T(8,128)(2,1)S(1)}, u32[]{:S(2)}, u32[]{:S(2)}) collective-permute-start(bf16[512,1024]{1,0:T(8,128)(2,1)} %collective-permute-done.27), channel_id=1, source_target_pairs={{0,2},{1,3},{2,0},{3,1},{4,6},{5,7},{6,4},{7,5},{8,10},{9,11},{10,... | collective-permute-start | bytes 3145736 | tf_op jit(solution)/shard_map/ppermute | solution.py:38
  358.0 24.4 %collective-permute-start.26 = (bf16[512,1024]{1,0:T(8,128)(2,1)}, bf16[512,1024]{1,0:T(8,128)(2,1)S(1)}, u32[]{:S(2)}, u32[]{:S(2)}) collective-permute-start(bf16[512,1024]{1,0:T(8,128)(2,1)} %get-tuple-element.265), channel_id=1, source_target_pairs={{0,1},{1,0},{2,3},{3,2},{4,5},{5,4},{6,7},{7,6},{8,9},{9,8},{10,11... | collective-permute-start | bytes 3145736 | tf_op jit(solution)/shard_map/ppermute | solution.py:38
  370.3 24.4 %collective-permute-start.19 = (bf16[512,1024]{1,0:T(8,128)(2,1)}, bf16[512,1024]{1,0:T(8,128)(2,1)}, u32[]{:S(2)}, u32[]{:S(2)}) collective-permute-start(bf16[512,1024]{1,0:T(8,128)(2,1)} %get-tuple-element.263), channel_id=1, source_target_pairs={{0,1},{1,0},{2,3},{3,2},{4,5},{5,4},{6,7},{7,6},{8,9},{9,8},{10,11... | collective-permute-start | bytes 3145736 | tf_op jit(solution)/shard_map/ppermute | solution.py:38
  382.4 29.8 %collective-permute-start.29 = (bf16[1024,1024]{1,0:T(8,128)(2,1)}, bf16[1024,1024]{1,0:T(8,128)(2,1)}, u32[]{:S(2)}, u32[]{:S(2)}) collective-permute-start(bf16[1024,1024]{1,0:T(8,128)(2,1)} %pad_maximum_fusion.5), channel_id=1, source_target_pairs={{0,1},{1,0},{2,3},{3,2},{4,5},{5,4},{6,7},{7,6},{8,9},{9,8},{10,11... | collective-permute-start | bytes 6291464 | tf_op jit(solution)/shard_map/ppermute | solution.py:38
  478.7 26.3 %collective-permute-start.37 = (bf16[512,1024]{1,0:T(8,128)(2,1)S(1)}, bf16[512,1024]{1,0:T(8,128)(2,1)}, u32[]{:S(2)}, u32[]{:S(2)}) collective-permute-start(bf16[512,1024]{1,0:T(8,128)(2,1)S(1)} %slice.1304), channel_id=1, source_target_pairs={{0,2},{1,3},{2,0},{3,1},{4,6},{5,7},{6,4},{7,5},{8,10},{9,11},{10,... | collective-permute-start | bytes 3145736 | tf_op jit(solution)/shard_map/ppermute | solution.py:38
  507.4 25.3 %collective-permute-start.38 = (bf16[512,1024]{1,0:T(8,128)(2,1)S(1)}, bf16[512,1024]{1,0:T(8,128)(2,1)S(1)}, u32[]{:S(2)}, u32[]{:S(2)}) collective-permute-start(bf16[512,1024]{1,0:T(8,128)(2,1)S(1)} %pad_maximum_fusion.15), channel_id=1, source_target_pairs={{0,8},{4,12},{8,0},{12,4},{16,24},{20,28},{24,16},{28,20},{1,9},{5... | collective-permute-start | bytes 3145736 | tf_op jit(solution)/shard_map/ppermute | solution.py:38
  513.0 22.9 %collective-permute-start.35 = (bf16[256,1024]{1,0:T(8,128)(2,1)S(1)}, bf16[256,1024]{1,0:T(8,128)(2,1)S(1)}, u32[]{:S(2)}, u32[]{:S(2)}) collective-permute-start(bf16[256,1024]{1,0:T(8,128)(2,1)S(1)} %slice.1311), channel_id=1, source_target_pairs={{0,2},{1,3},{2,0},{3,1},{4,6},{5,7},{6,4},{7,5},{8,10},{9,11},{10,... | collective-permute-start | bytes 1572872 | tf_op jit(solution)/shard_map/ppermute | solution.py:38
  533.5 25.3 %collective-permute-start.41 = (bf16[256,1024]{1,0:T(8,128)(2,1)S(1)}, bf16[256,1024]{1,0:T(8,128)(2,1)S(1)}, u32[]{:S(2)}, u32[]{:S(2)}) collective-permute-start(bf16[256,1024]{1,0:T(8,128)(2,1)S(1)} %constant_dynamic-update-slice_fusion.30), channel_id=1, source_target_pairs={{0,16},{4,20},{8,24},{12,28},{16,0},{20,4},{24,8},{28,12},{1,17},{... | collective-permute-start | bytes 1572872 | tf_op jit(solution)/shard_map/ppermute | solution.py:38
  575.9 56.2 %collective-permute-start.43 = (bf16[512,1024]{1,0:T(8,128)(2,1)}, bf16[512,1024]{1,0:T(8,128)(2,1)}, u32[]{:S(2)}, u32[]{:S(2)}) collective-permute-start(bf16[512,1024]{1,0:T(8,128)(2,1)} %pad_maximum_fusion.16), channel_id=1, source_target_pairs={{0,1},{1,0},{2,3},{3,2},{4,5},{5,4},{6,7},{7,6},{8,9},{9,8},{10,11... | collective-permute-start | bytes 3145736 | tf_op jit(solution)/shard_map/ppermute | solution.py:38
  600.0 48.3 %collective-permute-start.54 = (bf16[2048,512]{1,0:T(8,128)(2,1)}, bf16[2048,512]{1,0:T(8,128)(2,1)}, u32[]{:S(2)}, u32[]{:S(2)}) collective-permute-start(bf16[2048,512]{1,0:T(8,128)(2,1)} %get-tuple-element.100), channel_id=1, source_target_pairs={{0,4},{4,0},{8,12},{12,8},{16,20},{20,16},{24,28},{28,24},{1,5},{5... | collective-permute-start | bytes 6291464 | tf_op jit(solution)/shard_map/ppermute | solution.py:38
  652.1 77.7 %collective-permute-start.55 = (bf16[2000,128]{1,0:T(8,128)(2,1)}, bf16[2000,128]{1,0:T(8,128)(2,1)}, u32[]{:S(2)}, u32[]{:S(2)}) collective-permute-start(bf16[2000,128]{1,0:T(8,128)(2,1)} %get-tuple-element.244), channel_id=1, source_target_pairs={{0,16},{4,20},{8,24},{12,28},{16,0},{20,4},{24,8},{28,12},{1,17},{... | collective-permute-start | bytes 1536008 | tf_op jit(solution)/shard_map/ppermute | solution.py:38
  652.1 79.7 %collective-permute-start.56 = (bf16[2000,128]{1,0:T(8,128)(2,1)}, bf16[2000,128]{1,0:T(8,128)(2,1)S(1)}, u32[]{:S(2)}, u32[]{:S(2)}) collective-permute-start(bf16[2000,128]{1,0:T(8,128)(2,1)} %get-tuple-element.243), channel_id=1, source_target_pairs={{0,8},{4,12},{8,0},{12,4},{16,24},{20,28},{24,16},{28,20},{1,9},{5... | collective-permute-start | bytes 1536008 | tf_op jit(solution)/shard_map/ppermute | solution.py:38
  655.3 132.9 %collective-permute-start.57 = (bf16[2000,128]{1,0:T(8,128)(2,1)}, bf16[2000,128]{1,0:T(8,128)(2,1)}, u32[]{:S(2)}, u32[]{:S(2)}) collective-permute-start(bf16[2000,128]{1,0:T(8,128)(2,1)} %get-tuple-element.242), channel_id=1, source_target_pairs={{0,24},{4,28},{8,16},{12,20},{16,8},{20,12},{24,0},{28,4},{1,25},{... | collective-permute-start | bytes 1536008 | tf_op jit(solution)/shard_map/ppermute | solution.py:38
  682.7 54.9 %collective-permute-start.44 = (bf16[2048,512]{1,0:T(8,128)(2,1)}, bf16[2048,512]{1,0:T(8,128)(2,1)}, u32[]{:S(2)}, u32[]{:S(2)}) collective-permute-start(bf16[2048,512]{1,0:T(8,128)(2,1)} %get-tuple-element.82), channel_id=1, source_target_pairs={{0,4},{4,0},{8,12},{12,8},{16,20},{20,16},{24,28},{28,24},{1,5},{5... | collective-permute-start | bytes 6291464 | tf_op jit(solution)/shard_map/ppermute | solution.py:38
  728.2 52.2 %collective-permute-start.50 = (bf16[1120,1024]{1,0:T(8,128)(2,1)}, bf16[1120,1024]{1,0:T(8,128)(2,1)}, u32[]{:S(2)}, u32[]{:S(2)}) collective-permute-start(bf16[1120,1024]{1,0:T(8,128)(2,1)} %pad_maximum_fusion), channel_id=1, source_target_pairs={{0,2},{1,3},{2,0},{3,1},{4,6},{5,7},{6,4},{7,5},{8,10},{9,11},{10,... | collective-permute-start | bytes 6881288 | tf_op jit(solution)/shard_map/ppermute | solution.py:38
  741.2 54.1 %collective-permute-start.45 = (bf16[2048,256]{1,0:T(8,128)(2,1)}, bf16[2048,256]{1,0:T(8,128)(2,1)}, u32[]{:S(2)}, u32[]{:S(2)}) collective-permute-start(bf16[2048,256]{1,0:T(8,128)(2,1)} %slice.1303), channel_id=1, source_target_pairs={{0,8},{4,12},{8,0},{12,4},{16,24},{20,28},{24,16},{28,20},{1,9},{5... | collective-permute-start | bytes 3145736 | tf_op jit(solution)/shard_map/ppermute | solution.py:38
  748.1 45.8 %all-to-all-start.1 = ((bf16[8,256,128]{2,1,0:T(8,128)(2,1)}), bf16[8,256,128]{2,1,0:T(8,128)(2,1)S(1)}, u32[]{:S(2)}, u32[]{:S(2)}) async-start(bf16[8,256,128]{2,1,0:T(8,128)(2,1)} %shard_map.519), calls=%async_computation.1 | async-start | bytes 1048576 | tf_op jit(solution)/shard_map/all_to_all | solution.py:1024
  786.5 26.6 %collective-permute-start.51 = (bf16[1120,512]{1,0:T(8,128)(2,1)S(1)}, bf16[1120,512]{1,0:T(8,128)(2,1)S(1)}, u32[]{:S(2)}, u32[]{:S(2)}) collective-permute-start(bf16[1120,512]{1,0:T(8,128)(2,1)S(1)} %slice.1301), channel_id=1, source_target_pairs={{0,4},{4,0},{8,12},{12,8},{16,20},{20,16},{24,28},{28,24},{1,5},{5... | collective-permute-start | bytes 3440648 | tf_op jit(solution)/shard_map/ppermute | solution.py:38
  797.4 24.0 %collective-permute-start.46 = (bf16[2048,128]{1,0:T(8,128)(2,1)S(1)}, bf16[2048,128]{1,0:T(8,128)(2,1)S(1)}, u32[]{:S(2)}, u32[]{:S(2)}) collective-permute-start(bf16[2048,128]{1,0:T(8,128)(2,1)S(1)} %slice.1309), channel_id=1, source_target_pairs={{0,16},{4,20},{8,24},{12,28},{16,0},{20,4},{24,8},{28,12},{1,17},{... | collective-permute-start | bytes 1572872 | tf_op jit(solution)/shard_map/ppermute | solution.py:38
  (145 other events, 2062.7 us)

commit v4 on v3

--- a/solution.py
+++ b/solution.py
@@ -38,8 +38,12 @@
     return lax.ppermute(value, axis, [(i, i ^ mask) for i in range(size)])
 
 
-def after(value, dep):
-    return lax.optimization_barrier((value, dep))[0]
+def after(value, *deps):
+    return lax.optimization_barrier((value, *deps))[0]
+
+
+def together(*values):
+    return lax.optimization_barrier(values)
 
 
 def block_order(size):
@@ -51,12 +55,14 @@
     return order
 
 
-def gather_blocks(piece, axis):
+def gather_blocks(piece, axis, start=None):
+    steps = []
     mask = lax.axis_size("dp") // 2
     while mask:
         piece = jnp.concatenate([piece, swap(piece, "dp", mask)], axis=axis)
+        steps.append(piece)
         mask //= 2
-    return piece
+    return piece, steps
 
 
 def split(value, axis, parts):
@@ -110,7 +116,9 @@
 
 
 def cost(flops, size, exps=0):
-    return pl.CostEstimate(flops=flops, bytes_accessed=size, transcendentals=exps)
+    return pl.CostEstimate(
+        flops=int(0.4 * flops), bytes_accessed=int(0.4 * size), transcendentals=exps
+    )
 
 
 def lookup_kernel(row_ref, table_ref, out_ref, tab, held, sem):
@@ -138,6 +146,7 @@
     vocab, width = table.shape
     return pl.pallas_call(
         lookup_kernel,
+        name="lookup",
         out_shape=jax.ShapeDtypeStruct((total, width), lowp),
         in_specs=[smem(), pl.BlockSpec(memory_space=pl.ANY)],
         out_specs=vmem(),
@@ -151,38 +160,32 @@
     )(rows, table)
 
 
-def list_kernel(vocab, row_ref, tok_ref, out_ref, count_ref):
-    total = row_ref.shape[0]
+def list_kernel(code_ref, out_ref, count_ref):
+    total = code_ref.shape[0]
 
     def group(g, count):
-        for j in range(8):
-            t = g * 8 + j
-            row = row_ref[t]
-            tok_ref[count] = t
-            out_ref[count] = row
-            count = count + jnp.where(row < vocab, 1, 0)
+        for j in range(16):
+            code = code_ref[g * 16 + j]
+            out_ref[count] = code
+            count = count + jnp.where(code >= 0, 1, 0)
         return count
 
-    count = lax.fori_loop(0, total // 8, group, jnp.int32(0))
-    for j in range(8):
-        tok_ref[count + j] = total
-        out_ref[count + j] = 0
-    count_ref[0] = count
-
-
-def own_list(rows, vocab):
-    total = rows.shape[0]
-    return pl.pallas_call(
-        functools.partial(list_kernel, vocab),
+    count_ref[0] = lax.fori_loop(0, total // 16, group, jnp.int32(0))
+
+
+def own_list(codes):
+    total = codes.shape[0]
+    return pl.pallas_call(
+        list_kernel,
+        name="own_list",
         out_shape=(
             jax.ShapeDtypeStruct((total + 8,), jnp.int32),
-            jax.ShapeDtypeStruct((total + 8,), jnp.int32),
             jax.ShapeDtypeStruct((1,), jnp.int32),
         ),
         in_specs=[smem()],
-        out_specs=(smem(), smem(), smem()),
-        cost_estimate=cost(0, 40 * MIB),
-    )(rows)
+        out_specs=(smem(), smem()),
+        cost_estimate=cost(0, 60 * MIB),
+    )(codes)
 
 
 def place_kernel(order, place_ref, in_ref, gain_ref, out_ref, norm_ref, held):
@@ -200,6 +203,7 @@
     rows = blocks.shape[1]
     return pl.pallas_call(
         functools.partial(place_kernel, block_order(blocks.shape[0])),
+        name="place_embedding",
         out_shape=(jax.ShapeDtypeStruct((rows, D), lowp), jax.ShapeDtypeStruct((rows, D), lowp)),
         in_specs=[smem(), vmem(), vmem()],
         out_specs=(vmem(), vmem()),
@@ -225,6 +229,7 @@
     size = lax.axis_size("dp")
     return pl.pallas_call(
         functools.partial(embed_back_kernel, block_order(size)),
+        name="embed_back",
         out_shape=jax.ShapeDtypeStruct((size, rows, D // size), lowp),
         in_specs=[smem()] + [vmem()] * 5,
         out_specs=vmem(),
@@ -234,7 +239,7 @@
     )(place, values, gain, keep, more, grad)
 
 
-def scatter_kernel(count_ref, tok_ref, row_ref, base_ref, grad_ref, out_ref, rows):
+def scatter_kernel(bits, count_ref, code_ref, base_ref, grad_ref, out_ref, rows):
     total = grad_ref.shape[0]
     vocab = base_ref.shape[0]
 
@@ -250,27 +255,32 @@
         here = pl.ds(pl.multiple_of(i * 400, 400), 400)
         out_ref[here, :] = base_ref[here, :]
 
+    count = count_ref[0]
+
     def group(g, carry):
         for j in range(8):
-            token = tok_ref[g * 8 + j]
-            row = row_ref[g * 8 + j]
+            index = g * 8 + j
+            code = jnp.where(index < count, code_ref[index], total << bits)
+            token = lax.shift_right_logical(code, bits)
+            row = code & ((1 << bits) - 1)
             out_ref[pl.ds(row, 1), :] = out_ref[pl.ds(row, 1), :] + rows[pl.ds(token, 1), :]
         return carry
 
-    lax.fori_loop(0, (count_ref[0] + 7) // 8, group, jnp.int32(0))
-
-
-def scatter(count, tok, row, base, grad):
+    lax.fori_loop(0, (count + 7) // 8, group, jnp.int32(0))
+
+
+def scatter(bits, count, codes, base, grad):
     total, width = grad.shape
     return pl.pallas_call(
-        scatter_kernel,
+        functools.partial(scatter_kernel, bits),
+        name="scatter",
         out_shape=jax.ShapeDtypeStruct(base.shape, single),
-        in_specs=[smem(), smem(), smem(), vmem(), vmem()],
+        in_specs=[smem(), smem(), vmem(), vmem()],
         out_specs=vmem(),
         scratch_shapes=[pltpu.VMEM((total + 8, width), single)],
         compiler_params=params(60),
         cost_estimate=cost(0, 30 * MIB),
-    )(count, tok, row, base, grad)
+    )(count, codes, base, grad)
 
 
 def state_kernel(order, width, place_ref, gain_ref, in_ref, out_ref, held):
@@ -296,9 +306,10 @@
     size = lax.axis_size("dp")
     order = block_order(size)
     width = D // size
+    streams = states.shape[0]
     count = states.shape[1] // groups
     if width % 128:
-        values = lax.dynamic_index_in_dim(states, place[0], 0, keepdims=False).astype(single)
+        values = jnp.where(place[0] == 1, jnp.flip(states, 0), states).astype(single).reshape(-1, D)
         inv = lax.rsqrt(jnp.mean(values * values, axis=-1, keepdims=True) + TINY_NORM)
         lanes = jnp.arange(D, dtype=jnp.int32)
         blocks = jnp.asarray(order, jnp.int32)[lanes // width] ^ place[1]
@@ -306,63 +317,71 @@
         shuffle = (lanes[:, None] == source[None, :]).astype(single)
         moved = jnp.dot(values * inv, shuffle, precision=lax.Precision.HIGHEST)
         out = (moved * gain).astype(lowp)
-        return jnp.swapaxes(out.reshape(count, groups, D), 0, 1)
+        return jnp.swapaxes(out.reshape(streams * count, groups, D), 0, 1)
     tile = 128
     return pl.pallas_call(
         functools.partial(state_kernel, order, width),
-        out_shape=jax.ShapeDtypeStruct((groups, count, D), lowp),
+        name="state_norm",
+        out_shape=jax.ShapeDtypeStruct((groups, streams * count, D), lowp),
         grid_spec=pltpu.PrefetchScalarGridSpec(
             num_scalar_prefetch=1,
-            grid=(count // tile,),
+            grid=(streams, count // tile),
             in_specs=[
-                pl.BlockSpec((1, D), lambda i, s: (0, 0)),
-                pl.BlockSpec((1, tile * groups, D), lambda i, s: (s[0], i, 0)),
+                pl.BlockSpec((1, D), lambda n, i, s: (0, 0)),
+                pl.BlockSpec((1, tile * groups, D), lambda n, i, s: (s[0] ^ n, i, 0)),
             ],
-            out_specs=pl.BlockSpec((groups, tile, D), lambda i, s: (0, i, 0)),
+            out_specs=pl.BlockSpec(
+                (groups, tile, D), lambda n, i, s: (0, n * (count // tile) + i, 0)
+            ),
             scratch_shapes=[pltpu.VMEM((len(order), tile * groups, width), single)],
         ),
         compiler_params=params(60),
-        cost_estimate=cost(0, 4 * count * groups * D),
+        cost_estimate=cost(0, 4 * streams * count * groups * D),
     )(place, gain, states)
 
 
-def compress_kernel(old_ref, weight_ref, conv_ref, comp_ref, raw_ref):
+def compress_kernel(old_ref, key_ref, value_ref, conv_ref, comp_ref, raw_ref):
     heads = conv_ref.shape[0]
-    sums = [None] * (2 * heads)
-    for j in range(RATE):
-        raw = mm(old_ref[j], weight_ref[...], NT).astype(lowp)
-        raw_ref[j] = raw
-        for n in range(2 * heads):
-            piece = raw[:, n * DH : (n + 1) * DH]
-            term = mm(piece, conv_ref[n % heads, j * DH : (j + 1) * DH, :])
-            sums[n] = term if j == 0 else sums[n] + term
-    for n in range(2 * heads):
-        comp_ref[:, n * DH : (n + 1) * DH] = sums[n].astype(lowp)
-
-
-def compress(old3, weight, conv):
+    wide = heads * DH
+    for part, weight_ref in enumerate((key_ref, value_ref)):
+        sums = [None] * heads
+        for j in range(RATE):
+            raw = mm(old_ref[j], weight_ref[...], NT).astype(lowp)
+            raw_ref[j, :, part * wide : (part + 1) * wide] = raw
+            for n in range(heads):
+                piece = raw[:, n * DH : (n + 1) * DH]
+                term = mm(piece, conv_ref[n, j * DH : (j + 1) * DH, :])
+                sums[n] = term if j == 0 else sums[n] + term
+        for n in range(heads):
+            first = part * wide + n * DH
+            comp_ref[:, first : first + DH] = sums[n].astype(lowp)
+
+
+def compress(old3, weights, conv):
     rows = old3.shape[1]
-    wide = weight.shape[0]
+    wide = conv.shape[0] * DH
     tile = 256
     return pl.pallas_call(
         compress_kernel,
+        name="compress",
         grid=(rows // tile,),
         out_shape=(
-            jax.ShapeDtypeStruct((rows, wide), lowp),
-            jax.ShapeDtypeStruct((RATE, rows, wide), lowp),
+            jax.ShapeDtypeStruct((rows, 2 * wide), lowp),
+            jax.ShapeDtypeStruct((RATE, rows, 2 * wide), lowp),
         ),
         in_specs=[
             pl.BlockSpec((RATE, tile, D), lambda i: (0, i, 0)),
-            pl.BlockSpec(weight.shape, lambda i: (0, 0)),
+            pl.BlockSpec((wide, D), lambda i: (1, 0)),
+            pl.BlockSpec((wide, D), lambda i: (2, 0)),
             pl.BlockSpec(conv.shape, lambda i: (0, 0, 0)),
         ],
         out_specs=(
-            pl.BlockSpec((tile, wide), lambda i: (i, 0)),
-            pl.BlockSpec((RATE, tile, wide), lambda i: (0, i, 0)),
-        ),
-        compiler_params=params(60),
-        cost_estimate=cost(4 * RATE * rows * D * D, 12 * MIB),
-    )(old3, weight, conv)
+            pl.BlockSpec((tile, 2 * wide), lambda i: (i, 0)),
+            pl.BlockSpec((RATE, tile, 2 * wide), lambda i: (0, i, 0)),
+        ),
+        compiler_params=params(60),
+        cost_estimate=cost(4 * RATE * rows * wide * D, 12 * MIB),
+    )(old3, weights, weights, conv)
 
 
 def expand_kernel(grad_ref, raw_ref, conv_ref, out_ref, conv_out_ref):
@@ -384,6 +403,7 @@
 def expand(grad, raw, conv):
     return pl.pallas_call(
         expand_kernel,
+        name="expand",
         out_shape=(
             jax.ShapeDtypeStruct(raw.shape, lowp),
             jax.ShapeDtypeStruct(conv.shape, single),
@@ -391,7 +411,7 @@
         in_specs=[vmem()] * 3,
         out_specs=(vmem(), vmem()),
         compiler_params=params(60),
-        cost_estimate=cost(2000 * MIB, 10 * MIB),
+        cost_estimate=cost(2000 * MIB, 12 * MIB),
     )(grad, raw, conv)
 
 
@@ -403,10 +423,10 @@
         slots = key.shape[0]
         col = lax.broadcasted_iota(jnp.int32, (rows, slots), 1)
         if which < 2:
-            seen = col >= slots - info_ref[which]
+            seen = col >= slots - info_ref[2 * pl.program_id(0) + which]
         else:
             row = lax.broadcasted_iota(jnp.int32, (rows, slots), 0)
-            shift = info_ref[2]
+            shift = info_ref[4]
             row = row + shift
             col = col + shift
             row = jnp.where(row >= slots, row - slots, row)
@@ -416,33 +436,39 @@
     return result
 
 
+def rows_of(ref):
+    return ref[...].reshape(-1, ref.shape[-1])
+
+
 def attend_kernel(info_ref, q_ref, ks_ref, vs_ref, kc_ref, vc_ref, km_ref, vm_ref, out_ref, lse_ref):
-    query = q_ref[...]
-    scores = masked_scores(info_ref, query, [kc_ref[...], km_ref[...], ks_ref[...]])
+    query = rows_of(q_ref)
+    scores = masked_scores(info_ref, query, [kc_ref[...], km_ref[...], rows_of(ks_ref)])
     top = functools.reduce(jnp.maximum, [jnp.max(s, axis=-1, keepdims=True) for s in scores])
     total = 0.0
     mixed = 0.0
-    for score, value in zip(scores, (vc_ref, vm_ref, vs_ref)):
+    for score, value in zip(scores, (vc_ref[...], vm_ref[...], rows_of(vs_ref))):
         weight = jnp.exp(score - top)
         total = total + jnp.sum(weight, axis=-1, keepdims=True)
-        mixed = mixed + mm(weight.astype(lowp), value[...])
-    out_ref[...] = (mixed / total).astype(lowp)
-    lse_ref[0] = top + jnp.log(total)
+        mixed = mixed + mm(weight.astype(lowp), value)
+    out_ref[...] = (mixed / total).astype(lowp).reshape(out_ref.shape)
+    lse_ref[0, 0] = top + jnp.log(total)
 
 
 def attend_back_kernel(
     info_ref, q_ref, ks_ref, vs_ref, kc_ref, vc_ref, km_ref, vm_ref, lse_ref, up_ref,
     seg_ref, comp_ref, mem_ref,
 ):
-    head = pl.program_id(0)
-    wide = pl.num_programs(0) * DH
+    head = pl.program_id(1)
+    wide = pl.num_programs(1) * DH
     scale = DH ** (-0.5)
-    query = q_ref[...]
-    upstream = up_ref[...]
-    keys = [kc_ref[...], km_ref[...], ks_ref[...]]
+    query = rows_of(q_ref)
+    upstream = rows_of(up_ref)
+    keys = [kc_ref[...], km_ref[...], rows_of(ks_ref)]
     scores = masked_scores(info_ref, query, keys)
-    probs = [jnp.exp(s - lse_ref[0]) for s in scores]
-    prob_grads = [mm(upstream, v[...], NT) for v in (vc_ref, vm_ref, vs_ref)]
+    probs = [jnp.exp(s - lse_ref[0, 0]) for s in scores]
+    prob_grads = [
+        mm(upstream, v, NT) for v in (vc_ref[...], vm_ref[...], rows_of(vs_ref))
+    ]
     inner = 0.0
     for p, g in zip(probs, prob_grads):
         inner = inner + jnp.sum(p * g, axis=-1, keepdims=True)
@@ -454,20 +480,29 @@
     for p, g, key, (ref, key_at, value_at) in zip(probs, prob_grads, keys, places):
         score_grad = (p * (g - inner)).astype(lowp)
         query_grad = query_grad + mm(score_grad, key)
-        ref[:, key_at] = (mm(score_grad, query, TN) * scale).astype(lowp)
-        ref[:, value_at] = mm(p.astype(lowp), upstream, TN).astype(lowp)
-    seg_ref[:, here] = (query_grad * scale).astype(lowp)
-
-
-def head_specs(query, seg, comp, mem, heads):
+        shape = ref.shape[:-1] + (DH,)
+        key_grad = (mm(score_grad, query, TN) * scale).astype(lowp)
+        value_grad = mm(p.astype(lowp), upstream, TN).astype(lowp)
+        ref[..., key_at] = key_grad.reshape(shape)
+        ref[..., value_at] = value_grad.reshape(shape)
+    shape = seg_ref.shape[:-1] + (DH,)
+    seg_ref[..., here] = (query_grad * scale).astype(lowp).reshape(shape)
+
+
+def head_specs(seg, comp, mem, heads):
+    streams = seg.shape[1]
+
+    def of_seg(first):
+        return pl.BlockSpec((2, 1, seg.shape[2], DH), lambda n, h: (0, n, 0, first + h))
+
     def cols(array, first):
-        return pl.BlockSpec((array.shape[0], DH), lambda h: (0, first + h))
+        return pl.BlockSpec((array.shape[0] // streams, DH), lambda n, h: (n, first + h))
 
     return [
         smem(),
-        cols(query, 0),
-        cols(seg, 0),
-        cols(seg, heads),
+        of_seg(0),
+        of_seg(heads),
+        of_seg(2 * heads),
         cols(comp, 0),
         cols(comp, heads),
         cols(mem, 0),
@@ -475,51 +510,54 @@
     ]
 
 
-def attend(info, query, seg, comp, mem):
-    rows = seg.shape[0]
+def attend(info, seg, comp, mem):
+    _, streams, half, _ = seg.shape
     heads = comp.shape[1] // (2 * DH)
     return pl.pallas_call(
         attend_kernel,
-        grid=(heads,),
+        name="attend",
+        grid=(streams, heads),
         out_shape=(
-            jax.ShapeDtypeStruct((rows, heads * DH), lowp),
-            jax.ShapeDtypeStruct((heads, rows, 1), single),
-        ),
-        in_specs=head_specs(query, seg, comp, mem, heads),
+            jax.ShapeDtypeStruct((2, streams, half, heads * DH), lowp),
+            jax.ShapeDtypeStruct((streams, heads, 2 * half, 1), single),
+        ),
+        in_specs=head_specs(seg, comp, mem, heads),
         out_specs=(
-            pl.BlockSpec((rows, DH), lambda h: (0, h)),
-            pl.BlockSpec((1, rows, 1), lambda h: (h, 0, 0)),
+            pl.BlockSpec((2, 1, half, DH), lambda n, h: (0, n, 0, h)),
+            pl.BlockSpec((1, 1, 2 * half, 1), lambda n, h: (n, h, 0, 0)),
         ),
         compiler_params=params(60),
         cost_estimate=cost(7000 * MIB, 6 * MIB),
-    )(info, query, seg, seg, comp, comp, mem, mem)
-
-
-def attend_back(info, query, seg, comp, mem, lse, upstream):
-    rows = seg.shape[0]
+    )(info, seg, seg, seg, comp, comp, mem, mem)
+
+
+def attend_back(info, seg, comp, mem, lse, upstream):
+    _, streams, half, wide = seg.shape
     heads = comp.shape[1] // (2 * DH)
-    whole = lambda h: (0, 0)
+    slots = comp.shape[0] // streams
+    kept = mem.shape[0] // streams
     return pl.pallas_call(
         attend_back_kernel,
-        grid=(heads,),
+        name="attend_back",
+        grid=(streams, heads),
         out_shape=(
-            jax.ShapeDtypeStruct((rows, 3 * heads * DH), lowp),
+            jax.ShapeDtypeStruct(seg.shape, lowp),
             jax.ShapeDtypeStruct(comp.shape, lowp),
             jax.ShapeDtypeStruct(mem.shape, lowp),
         ),
-        in_specs=head_specs(query, seg, comp, mem, heads)
+        in_specs=head_specs(seg, comp, mem, heads)
         + [
-            pl.BlockSpec((1, rows, 1), lambda h: (h, 0, 0)),
-            pl.BlockSpec((rows, DH), lambda h: (0, h)),
+            pl.BlockSpec((1, 1, 2 * half, 1), lambda n, h: (n, h, 0, 0)),
+            pl.BlockSpec((2, 1, half, DH), lambda n, h: (0, n, 0, h)),
         ],
         out_specs=(
-            pl.BlockSpec((rows, 3 * heads * DH), whole),
-            pl.BlockSpec(comp.shape, whole),
-            pl.BlockSpec(mem.shape, whole),
+            pl.BlockSpec((2, 1, half, wide), lambda n, h: (0, n, 0, 0)),
+            pl.BlockSpec((slots, comp.shape[1]), lambda n, h: (n, 0)),
+            pl.BlockSpec((kept, mem.shape[1]), lambda n, h: (n, 0)),
         ),
         compiler_params=params(60),
         cost_estimate=cost(11000 * MIB, 9 * MIB),
-    )(info, query, seg, seg, comp, comp, mem, mem, lse, upstream)
+    )(info, seg, seg, seg, comp, comp, mem, mem, lse, upstream)
 
 
 def columns_of(rows):
@@ -548,6 +586,7 @@
     tile = 256
     return pl.pallas_call(
         functools.partial(logits_kernel, words),
+        name="logits_part",
         grid=(rows // tile,),
         out_shape=(
             jax.ShapeDtypeStruct((rows, slots), lowp),
@@ -584,6 +623,7 @@
     tile = 256
     return pl.pallas_call(
         logits_back_kernel,
+        name="logits_back",
         grid=(rows // tile,),
         out_shape=(
             jax.ShapeDtypeStruct((rows, slots), lowp),
@@ -630,6 +670,7 @@
         return keep, send.astype(lowp)
     return pl.pallas_call(
         functools.partial(table_grad_kernel, count),
+        name="table_grad_part",
         grid=(slots // block,),
         out_shape=(
             jax.ShapeDtypeStruct((slots, D // 2), single),
@@ -664,6 +705,7 @@
     blocks = hidden // block
     return pl.pallas_call(
         functools.partial(hidden_grad_kernel, blocks),
+        name="hidden_grads",
         grid=(2 * blocks,),
         out_shape=(
             jax.ShapeDtypeStruct((2 * hidden, D // 2), single),
@@ -685,74 +727,65 @@
 
 
 def attn_grad_kernel(
-    seg_ref, mixed_ref, mem_ref, old_ref, normed_ref, up_ref, mem_in_ref, old_in_ref, far_ref, own_ref
+    seg_ref, mixed_ref, mem_ref, old_ref, normed_ref, up_ref, mem_in_ref, old_in_ref, keep_ref, send_ref
 ):
-    step = pl.program_id(0)
-    which = step % 4
-
-    def give(total):
-        @pl.when(step < 4)
-        def _():
-            far_ref[...] = total.astype(lowp)
-
-        @pl.when(step >= 4)
-        def _():
-            own_ref[...] = total
+    which = pl.program_id(0)
 
     @pl.when(which == 0)
     def _():
-        give(mm(seg_ref[...], normed_ref[...], TN))
+        halves(mm(seg_ref[...], normed_ref[...], TN), keep_ref, send_ref)
 
     @pl.when(which == 3)
     def _():
-        give(mm(mixed_ref[...], up_ref[...], TN))
+        halves(mm(mixed_ref[...], up_ref[...], TN), keep_ref, send_ref)
 
     @pl.when(jnp.logical_and(which > 0, which < 3))
     def _():
         total = mm(seg_ref[...], normed_ref[...], TN)
         total = total + mm(mem_ref[...], mem_in_ref[...], TN)
-        give(total + mm(old_ref[...], old_in_ref[...], TN))
+        total = total + mm(old_ref[...], old_in_ref[...], TN)
+        halves(total, keep_ref, send_ref)
 
 
 def attn_grads(seg_grad, mixed, mem_grad, old_grad, normed, attn_in, mem_in, old_in):
-    block = mixed.shape[1] // 2
-
-    def side(i):
-        return 1 - i // 4
+    block = mixed.shape[1]
 
     def whole(array):
         return pl.BlockSpec(array.shape, lambda i: (0, 0))
 
     return pl.pallas_call(
         attn_grad_kernel,
-        grid=(8,),
+        name="attn_grads",
+        grid=(4,),
         out_shape=(
-            jax.ShapeDtypeStruct((4 * block, D), lowp),
-            jax.ShapeDtypeStruct((4 * block, D), single),
+            jax.ShapeDtypeStruct((4 * block, D // 2), single),
+            jax.ShapeDtypeStruct((4 * block, D // 2), lowp),
         ),
         in_specs=[
-            pl.BlockSpec(
-                (seg_grad.shape[0], block), lambda i: (0, jnp.minimum(i % 4, 2) * 2 + side(i))
-            ),
-            pl.BlockSpec((mixed.shape[0], block), lambda i: (0, side(i))),
-            pl.BlockSpec(
-                (mem_grad.shape[0], block), lambda i: (0, jnp.clip(i % 4 - 1, 0, 1) * 2 + side(i))
-            ),
-            pl.BlockSpec(
-                (old_grad.shape[0], block), lambda i: (0, jnp.clip(i % 4 - 1, 0, 1) * 2 + side(i))
-            ),
+            pl.BlockSpec((seg_grad.shape[0], block), lambda i: (0, jnp.minimum(i, 2))),
+            whole(mixed),
+            pl.BlockSpec((mem_grad.shape[0], block), lambda i: (0, jnp.clip(i - 1, 0, 1))),
+            pl.BlockSpec((old_grad.shape[0], block), lambda i: (0, jnp.clip(i - 1, 0, 1))),
             whole(normed),
             whole(attn_in),
             whole(mem_in),
             whole(old_in),
         ],
         out_specs=(
-            pl.BlockSpec((block, D), lambda i: (jnp.minimum(i, 3), 0)),
-            pl.BlockSpec((block, D), lambda i: (jnp.maximum(i - 4, 0), 0)),
-        ),
-        compiler_params=params(60),
-        cost_estimate=cost(9000 * MIB, 20 * MIB),
+            pl.BlockSpec((block, D // 2), lambda i: (i, 0)),
+            pl.BlockSpec((block, D // 2), lambda i: (i, 0)),
+        ),
+        compiler_params=params(60),
+        cost_estimate=cost(9000 * MIB, 24 * MIB),
     )(seg_grad, mixed, mem_grad, old_grad, normed, attn_in, mem_in, old_in)
+
+
+def scalar_row(values, length=128):
+    lane = jnp.arange(length, dtype=jnp.int32)
+    row = jnp.zeros((length,), single)
+    for i, value in enumerate(values):
+        row = jnp.where(lane == i, value, row)
+    return row
 
 
 def local(
@@ -795,6 +828,17 @@
     vocab, width = table.shape
     assert head_size == 4 and streams == 2
 
+    weights_now = (table, qkv, wout, wconv, wup, wdown)
+    rows_old = (table_rows, qkv_rows, out_rows, conv_rows, up_rows, down_rows)
+    cols_old = (table_cols, qkv_cols, out_cols, conv_cols, up_cols, down_cols)
+    sizes = {"dp": dp_size, "head": head_size}
+    row_axes = ("head", "dp", "head", "head", "dp", "head")
+    col_axes = ("dp", "head", "dp", "dp", "head", "dp")
+    early = [jnp.sum(old) / sizes[axis] for old, axis in zip(rows_old, col_axes)]
+    early += [jnp.sum(weight * weight) for weight in weights_now]
+    gain_sums = jnp.sum(gains * gains, axis=1) / head_size
+    early = scalar_row(early + [gain_sums[0], gain_sums[1], gain_sums[2]])
+
     flat = jnp.concatenate(
         [
             ids.astype(single).reshape(-1),
@@ -805,7 +849,8 @@
     )
     room = -flat.shape[0] % 1024
     flat = jnp.concatenate([flat, jnp.zeros((room,), single)]).reshape(1, -1, 128)
-    small = gather_blocks(flat, 0).reshape(dp_size, -1)
+    small, small_steps = gather_blocks(flat, 0)
+    small = small.reshape(dp_size, -1)
     place = jnp.stack([x, d])
 
     def field(raw):
@@ -817,6 +862,9 @@
     ids_all = jnp.transpose(field(ids_all), (1, 2, 0, 3)).reshape(-1).astype(jnp.int32)
     table_rows_all = ids_all - h * vocab
     inside = (table_rows_all >= 0) & (table_rows_all < vocab)
+    bits = vocab.bit_length()
+    token_codes = (jnp.arange(ids_all.shape[0], dtype=jnp.int32) << bits) | table_rows_all
+    token_codes = jnp.where(inside, token_codes, -1)
     table_rows_all = jnp.where(inside, table_rows_all, vocab)
     targets_all = field(small[:reach, per_group : 2 * per_group])
     mask_all = field(small[:reach, 2 * per_group : 3 * per_group])
@@ -835,14 +883,7 @@
             wconv.astype(lowp).reshape(conv_rows_own, width),
         ]
     )
-    own_one = gather_blocks(after(pack_one, small), 1)
-    far_one = swap(own_one, "head", 2)
-    near_rows = split(own_one[: 4 * wide], 0, 4)
-    far_rows = split(far_one[: 4 * wide], 0, 4)
-    query_weight = jnp.concatenate([near_rows[0], far_rows[0]])
-    pair_weight = jnp.concatenate([near_rows[1], far_rows[1], near_rows[2], far_rows[2]])
-    full_out = jnp.concatenate([near_rows[3], far_rows[3]])
-
+    own_one, steps_one = gather_blocks(after(pack_one, small_steps[0]), 1)
     conv_lanes = jnp.arange(DH, dtype=jnp.int32)
     conv_width = DH // dp_size
     conv_natural = (jnp.asarray(order, jnp.int32)[conv_lanes // conv_width] ^ d) * conv_width
@@ -862,99 +903,118 @@
         moved = jnp.swapaxes(moved.reshape(dp_size, conv_rows_own, width), 0, 1)
         return moved.reshape(conv_rows_own, D)
 
-    full_conv = jnp.concatenate(
-        [conv_natural_order(own_one[4 * wide :]), conv_natural_order(far_one[4 * wide :])]
-    )
+    full_conv = conv_natural_order(own_one[4 * wide :])
 
     hidden_own = wup.shape[1]
     pack_two = jnp.concatenate([wup.astype(lowp).T, wdown.astype(lowp)])
-    own_two = gather_blocks(after(pack_two, own_one), 1)
-    full_up, full_down = split(own_two, 0, 2)
+    own_two, steps_two = gather_blocks(after(pack_two, steps_one[0]), 1)
 
     words = vocab // reach
     z = d // 2
-    low_table = after(table.astype(lowp), own_two)
+    low_table = after(table.astype(lowp), steps_two[-2])
     near_table = []
     for m in order[:reach]:
         part = lax.dynamic_slice_in_dim(low_table, (z ^ (m // 2)) * words, words, 0)
         near_table.append(part if m == 0 else swap(part, "dp", m))
     near_table = jnp.concatenate(near_table, axis=1)
-    loss_table = jnp.concatenate([near_table, swap(near_table, "dp", 1)], axis=1)
+    far_table = swap(after(near_table, own_two), "dp", 1)
     slots = -(-words // 256) * 256
-    loss_table = jnp.concatenate([loss_table, jnp.zeros((slots - words, D), lowp)], axis=0)
 
     own_half, far_half = split(table_rows_all, 0, 2)
     looked_far = swap(lookup(far_half, table), "head", 1)
-    looked = (lookup(own_half, table) + looked_far).reshape(2, -1, width)
+    looked = (lookup(after(own_half, steps_one[0]), table) + looked_far).reshape(2, -1, width)
     looked = looked[0] + swap(looked[1], "head", 2)
     looked = lax.all_to_all(looked.reshape(dp_size, half, width), "dp", 0, 0)
-    embedded_low, normed = place_embedding(place, looked, gain_vals[0])
+    embedded_low, normed = place_embedding(place, after(looked, steps_two[0]), gain_vals[0])
     embedded = embedded_low.astype(single)
-    normed = jnp.concatenate([normed, swap(normed, "head", 1)], axis=0)
 
     mem_normed = state_norm(place, gain_vals[0], memory, 1)[0]
-    old_normed = state_norm(place, gain_vals[0], old_states, RATE)
-    comp, old_raw = compress(old_normed, pair_weight, full_conv)
-    mem = mm(mem_normed, pair_weight, NT).astype(lowp)
-    query = mm(normed, query_weight, NT).astype(lowp)
-    seg = mm(normed, pair_weight, NT).astype(lowp)
-    info = jnp.stack(
-        [
-            lax.dynamic_index_in_dim(comp_fill, x, 0, keepdims=False),
-            lax.dynamic_index_in_dim(mem_fill, x, 0, keepdims=False),
-            c * half,
-        ]
-    ).astype(jnp.int32)
-    mixed, lse = attend(info, query, seg, comp, mem)
+    old_normed = state_norm(after(place, steps_one[1]), gain_vals[0], old_states, RATE)
+    comp_counts = jnp.where(x == 1, jnp.flip(comp_fill), comp_fill)
+    mem_counts = jnp.where(x == 1, jnp.flip(mem_fill), mem_fill)
+    info = jnp.stack([comp_counts[0], mem_counts[0], comp_counts[1], mem_counts[1], c * half])
+    info = info.astype(jnp.int32)
 
     def core_sum(part):
         rows = part.shape[0] // 2
-        return part[:rows] + swap(part[rows:].astype(lowp), "head", 1).astype(single)
+        more = swap(part[rows:].astype(lowp), "head", 1)
+        return part[:rows].astype(single) + more.astype(single)
 
     def core_both(part):
         return jnp.concatenate([part, swap(part, "head", 1)], axis=0)
 
-    def group_sum(part):
+    def group_sum(part, beside=()):
         part = core_sum(part)
         rows = part.shape[0] // 2
-        return part[:rows] + swap(part[rows:].astype(lowp), "head", 2).astype(single)
-
-    def group_both(part):
-        return core_both(jnp.concatenate([part, swap(part, "head", 2)], axis=0))
-
-    after_attn = embedded + core_sum(mm(mixed, full_out))
+        more = swap(part[rows:].astype(lowp), "head", 2)
+        more, *beside = together(more, *beside)
+        part = part[:rows] + more.astype(single)
+        return (part, beside) if beside else part
+
+    def group_both(part, beside=()):
+        far, *beside = together(swap(part, "head", 2), *beside)
+        both = core_both(jnp.concatenate([part, far], axis=0))
+        return (both, beside) if beside else both
+
+    normed = group_both(normed)
+    in_weight = own_one[: 3 * wide]
+    comp, old_raw = compress(old_normed, own_one, full_conv)
+    mem = mm(mem_normed, own_one[wide : 3 * wide], NT).astype(lowp)
+    seg = mm(normed, in_weight, NT).astype(lowp).reshape(2, streams, half, 3 * wide)
+    mixed, lse = attend(info, after(seg, steps_two[1]), comp, mem)
+    mixed = mixed.reshape(-1, wide)
+    attn_sum, (full_up, full_down) = group_sum(
+        mm(mixed, own_one[3 * wide : 4 * wide]), split(own_two, 0, 2)
+    )
+    after_attn = embedded + attn_sum
     ffn_in, inv_second = rms(after_attn, gain_vals[1])
-    ffn_in = group_both(ffn_in)
+    ffn_in, (near_table,) = group_both(ffn_in, (near_table,))
     hidden_pre = mm(ffn_in, full_up, NT)
     hidden_act = jax.nn.gelu(hidden_pre).astype(lowp)
-    after_ffn = after_attn + group_sum(mm(hidden_act, full_down))
+    ffn_sum, (far_table,) = group_sum(mm(hidden_act, full_down), (far_table,))
+    after_ffn = after_attn + ffn_sum
+    loss_table = jnp.concatenate([near_table, far_table], axis=1)
+    loss_table = jnp.concatenate([loss_table, jnp.zeros((slots - words, D), lowp)], axis=0)
     final_in, inv_third = rms(after_ffn, gain_vals[2])
 
     word_start = (h * vocab + z * words).astype(single)
     wanted_all = targets_all - word_start
     wanted_all = jnp.where((wanted_all >= 0) & (wanted_all < words), wanted_all, -1.0)
-    groups = [(0, 1)]
+    info_all = jnp.stack([wanted_all, mask_all] + [jnp.zeros_like(mask_all)] * 6)
+    info_all = jnp.transpose(info_all, (1, 0, 2, 3, 4)).reshape(reach, 8, per_group)
     pieces = [final_in]
+    chunks = []
+    raised = []
+    stats = []
+
+    def next_chunk():
+        i = len(chunks)
+        if i < 2:
+            chunks.append(group_both(pieces[i]))
+        else:
+            chunk, (stats[i - 2],) = group_both(pieces[i], (stats[i - 2],))
+            chunks.append(chunk)
+        out, stat = logits_part(words, info_all[i], chunks[i], loss_table)
+        raised.append(out)
+        stats.append(stat)
+
     mask = dp_size // 2
     while mask > 1:
         joined = jnp.concatenate(pieces) if len(pieces) > 1 else pieces[0]
-        pieces.append(swap(reorder(joined, mask), "dp", mask))
-        groups.append((groups[-1][1], 2 * groups[-1][1]))
+        moved = swap(reorder(joined, mask), "dp", mask)
+        if len(pieces) == 1:
+            next_chunk()
+            moved, own_codes, own_count, early = together(
+                moved, *own_list(after(token_codes, final_in)), early
+            )
+        elif len(pieces) == 2:
+            moved, stats[0] = together(moved, stats[0])
+        pieces += split(moved, 0, len(pieces))
         mask //= 2
-    info_all = jnp.stack([wanted_all, mask_all] + [jnp.zeros_like(mask_all)] * 6)
-    chunks = []
-    infos = []
-    raised = []
-    stats = []
-    for (first, last), piece in zip(groups, pieces):
-        chunk = group_both(piece)
-        packed = jnp.transpose(info_all[:, first:last], (0, 2, 3, 1, 4)).reshape(8, -1)
-        out, stat = logits_part(words, packed, chunk, loss_table)
-        chunks.append(chunk)
-        infos.append(packed)
-        raised.append(out)
-        stats.append(stat[:3].reshape(3, 2, 2, last - first, half))
-    own_stats = jnp.concatenate(stats, axis=3)
+    while len(chunks) < reach:
+        next_chunk()
+    stats = [stat[:3].reshape(3, 1, 2, 2, half) for stat in stats]
+    own_stats = jnp.concatenate(stats, axis=1)
 
     def combine(first, second):
         top = jnp.maximum(first[0], second[0])
@@ -962,74 +1022,87 @@
         return jnp.stack([top, total, first[2] + second[2]])
 
     merged = own_stats
-    merged = combine(merged, jnp.flip(swap(merged, "head", 1), 1))
-    merged = combine(merged, jnp.flip(swap(merged, "head", 2), 2))
+    merged = combine(merged, jnp.flip(swap(merged, "head", 1), 2))
+    merged = combine(merged, jnp.flip(swap(merged, "head", 2), 3))
     mask = 2
     while mask < dp_size:
-        other = split(swap(merged, "dp", mask), 3, reach)
+        other = split(swap(merged, "dp", mask), 1, reach)
         other = [other[order.index(j ^ mask)] for j in order[:reach]]
-        merged = combine(merged, jnp.concatenate(other, axis=3))
+        merged = combine(merged, jnp.concatenate(other, axis=1))
         mask *= 2
     log_total = merged[0] + jnp.log(merged[1])
     loss_local = jnp.sum(mask_all[0, 0, 0] * (log_total[0, 0, 0] - merged[2, 0, 0, 0]))
     factor_all = jnp.exp(own_stats[0] - log_total)
 
-    dlogits = [None] * len(groups)
-    parts = []
-    for i in reversed(range(len(groups))):
-        first, last = groups[i]
-        factor = factor_all[:, :, first:last].reshape(1, -1) * infos[i][1:2]
-        factor = jnp.broadcast_to(factor, infos[i].shape)
-        dlogits[i], part = logits_back(infos[i], factor, raised[i], loss_table)
-        parts.append(group_sum(part.astype(single)))
+    factor_all = factor_all.reshape(reach, 1, per_group) * info_all[:, 1:2]
+    factor_all = jnp.broadcast_to(factor_all, info_all.shape)
+    dlogits = [None] * reach
+    parts = [None] * reach
+    for i in reversed(range(reach)):
+        factor = factor_all[i]
+        if i + 2 < reach:
+            factor = after(factor, parts[i + 2])
+        dlogits[i], part = logits_back(info_all[i], factor, raised[i], loss_table)
+        parts[i] = group_sum(part)
+    table_parts = table_grad_part(dlogits, chunks)
     mask = 2
-    total = jnp.zeros(())
-    for i in range(len(groups) - 1):
-        moved = swap(reorder(parts[0].astype(lowp), mask), "dp", mask).astype(single)
-        rest = []
-        start = 0
-        for part in reversed(parts[1:]):
-            rest.append(part + moved[start : start + part.shape[0]])
-            start += part.shape[0]
-        parts = rest[::-1]
+    while len(parts) > 1:
+        count = len(parts) // 2
+        moved = jnp.concatenate([part.astype(lowp) for part in parts[count:]])
+        moved = swap(reorder(moved, mask), "dp", mask)
+        if mask == 2:
+            moved, *table_parts = together(moved, *table_parts)
+        moved = split(moved.astype(single), 0, count)
+        parts = [part + more for part, more in zip(parts, moved)]
         mask *= 2
     final_grad = parts[0]
 
-    keep, send = table_grad_part(dlogits, chunks)
-    keep = keep + swap(send, "dp", 1).astype(single)
-    table_base = jnp.zeros((vocab, width), single)
-    for m, part in zip(order[:reach], split(keep[:words], 1, reach)):
-        part = part if m == 0 else swap(part.astype(lowp), "dp", m).astype(single)
-        table_base = lax.dynamic_update_slice_in_dim(table_base, part, (z ^ (m // 2)) * words, 0)
+    keep, send = table_parts
+    moved_table = swap(send, "dp", 1)
 
     grad_after_ffn = rms_back(after_ffn, inv_third, gain_vals[2], final_grad)
     down_in = group_both(grad_after_ffn.astype(lowp))
     act_grad = mm(down_in, full_down, NT)
     pre_grad = jax.vjp(jax.nn.gelu, hidden_pre)[1](act_grad)[0].astype(lowp)
-    ffn_in_grad = group_sum(mm(pre_grad, full_up))
+    two = hidden_grads(pre_grad, hidden_act, ffn_in, down_in)
+    ffn_in_grad, (*two, moved_table) = group_sum(mm(pre_grad, full_up), (*two, moved_table))
+    two_moved = swap(two[1], "dp", 1)
+    keep = keep + moved_table.astype(single)
+    table_pieces = split(keep[:words], 1, reach)
+    for i in range(1, reach):
+        table_pieces[i] = swap(table_pieces[i].astype(lowp), "dp", order[i])
     grad_after_attn = grad_after_ffn + rms_back(after_attn, inv_second, gain_vals[1], ffn_in_grad)
-    attn_in = core_both(grad_after_attn.astype(lowp))
-
-    mixed_grad = mm(attn_in, full_out, NT).astype(lowp)
-    seg_grad, comp_grad, mem_grad = attend_back(info, query, seg, comp, mem, lse, mixed_grad)
-    seg_in = mm(seg_grad, jnp.concatenate([query_weight, pair_weight]))
+    attn_in = group_both(grad_after_attn.astype(lowp))
+
+    mixed_grad = mm(attn_in, own_one[3 * wide : 4 * wide], NT).astype(lowp)
+    mixed_grad = mixed_grad.reshape(2, streams, half, wide)
+    seg_grad, comp_grad, mem_grad = attend_back(info, seg, comp, mem, lse, mixed_grad)
+    seg_grad = seg_grad.reshape(-1, 3 * wide)
+    seg_in = core_sum(mm(seg_grad, in_weight))
+    seg_in_far = swap(seg_in[half:].astype(lowp), "head", 2)
+    seg_in_far, two_moved, *table_pieces = together(seg_in_far, two_moved, *table_pieces)
+    table_base = jnp.zeros((vocab, width), single)
+    for m, part in zip(order[:reach], table_pieces):
+        part = part.astype(single)
+        table_base = lax.dynamic_update_slice_in_dim(table_base, part, (z ^ (m // 2)) * words, 0)
     rows_grad = embed_back(
         place,
         embedded_low,
         gain_vals[0],
         seg_in[:half],
-        swap(seg_in[half:].astype(lowp), "head", 1),
+        seg_in_far,
         grad_after_attn,
     )
     rows_grad = lax.all_to_all(rows_grad, "dp", 0, 0)
     rows_grad = jnp.stack([rows_grad, swap(rows_grad, "head", 2)])
     rows_grad = jnp.stack([rows_grad, swap(rows_grad, "head", 1)]).reshape(-1, width)
 
-    two = reduce_blocks(*hidden_grads(pre_grad, hidden_act, ffn_in, down_in))
+    two = two[0] + two_moved.astype(single)
+    two = reduce_blocks(*split(two, 1, 2), 2)
     up_grad = two[:hidden_own].T
     down_grad = two[hidden_own:]
     old_grad, conv_sum = expand(comp_grad, old_raw, full_conv)
-    far_sum, own_sum = attn_grads(
+    one = attn_grads(
         seg_grad,
         mixed,
         mem_grad,
@@ -1039,15 +1112,13 @@
         mem_normed,
         old_normed.reshape(-1, D),
     )
-    far_sum = jnp.concatenate([far_sum, conv_block_order(conv_sum[heads_own:])])
-    own_sum = jnp.concatenate([own_sum, conv_block_order(conv_sum[:heads_own]).astype(single)])
-    one = own_sum + swap(far_sum, "head", 2).astype(single)
-    one = reduce_blocks(*split(one, 1, 2))
+    conv_sum = split(conv_block_order(conv_sum), 1, 2)
+    one = [jnp.concatenate([part, more.astype(part.dtype)]) for part, more in zip(one, conv_sum)]
+    one = reduce_blocks(*one)
     qkv_grad = jnp.swapaxes(one[: 3 * wide].reshape(3, wide, width), 1, 2)
     out_grad = one[3 * wide : 4 * wide]
     conv_grad = one[4 * wide :].reshape(wconv.shape)
-    tok_list, row_list, list_count = own_list(after(table_rows_all, final_in), vocab)
-    table_grad = scatter(list_count, tok_list, row_list, table_base, rows_grad)
+    table_grad = scatter(bits, own_count, own_codes, table_base, rows_grad)
 
     gains_low = gains.astype(lowp).astype(single)
     gain_part = jnp.stack(
@@ -1059,13 +1130,6 @@
     )
 
     grads = (table_grad, qkv_grad, out_grad, conv_grad, up_grad, down_grad)
-    weights_now = (table, qkv, wout, wconv, wup, wdown)
-    rows_old = (table_rows, qkv_rows, out_rows, conv_rows, up_rows, down_rows)
-    cols_old = (table_cols, qkv_cols, out_cols, conv_cols, up_cols, down_cols)
-    sizes = {"dp": dp_size, "head": head_size}
-    row_axes = ("head", "dp", "head", "head", "dp", "head")
-    col_axes = ("dp", "head", "dp", "dp", "head", "dp")
-
     def sum_over_dp(joined):
         mask = 1
         while mask < dp_size:
@@ -1075,19 +1139,11 @@
 
     row_part = []
     col_part = []
-    scalar_list = []
-    for index in range(6):
-        square = grads[index] * grads[index]
+    for grad in grads:
+        square = grad * grad
         row_part.append(jnp.sum(square, axis=-1))
         col_part.append(jnp.sum(square, axis=tuple(range(square.ndim - 1))))
-        scalar_list.append(jnp.sum(square))
-        scalar_list.append(jnp.sum(rows_old[index]) / sizes[col_axes[index]])
-    for weight in weights_now:
-        scalar_list.append(jnp.sum(weight * weight))
-    for which in range(3):
-        scalar_list.append(jnp.sum(gains[which] * gains[which]) / head_size)
-    scalar_list.append(loss_local)
-    row_q, row_u, col_e, col_o, col_c, col_d, gain_raw, scalars = lax.psum(
+    row_q, row_u, col_e, col_o, col_c, col_d, gain_raw, early = lax.psum(
         (
             row_part[1],
             row_part[4],
@@ -1096,11 +1152,13 @@
             col_part[3],
             col_part[5],
             gain_part,
-            jnp.stack(scalar_list),
+            early + scalar_row([0.0] * 15 + [loss_local]),
         ),
         "head",
     )
-    members = [col_part[4], row_part[5], row_part[3], row_part[2], col_part[1], scalars, row_part[0]]
+    lanes = [col_e, jnp.sum(row_q, axis=0), col_o]
+    lanes += [jnp.concatenate([col_c, jnp.zeros((width - col_c.shape[0],), single)]), row_u, col_d]
+    members = [col_part[4], row_part[5], row_part[3], row_part[2], col_part[1], *lanes, row_part[0], early]
     joined = jnp.concatenate([m.reshape(-1) for m in members])
     joined = sum_over_dp(jnp.concatenate([joined, jnp.zeros((-joined.shape[0] % 1024,), single)]))
     sums = []
@@ -1108,11 +1166,12 @@
     for member in members:
         sums.append(joined[start : start + member.size].reshape(member.shape))
         start += member.size
-    col_u, row_d, row_c, row_o, col_q, scalars, row_e = sums
+    col_u, row_d, row_c, row_o, col_q, *lanes, row_e, early = sums
+    square_total = [jnp.sum(lane) for lane in lanes]
     row_sums = [row_e, row_q, row_o, row_c, row_u, row_d]
     col_sums = [col_e, col_q, col_o, col_c, col_u, col_d]
-    weight_total = scalars[12:21]
-    loss_all = scalars[21]
+    weight_total = early[6:15]
+    loss_all = early[15]
     inverse = 1.0 / count_all
     decay = 1.0 - STEP ** (-0.8)
     updates = []
@@ -1130,8 +1189,8 @@
         cols_new = decay * cols_old[index] + (1.0 - decay) * (
             col_sums[index] * inverse * inverse / rows_total + TINY_SQUARE
         )
-        mean_row = decay * scalars[2 * index + 1] / rows_total + (1.0 - decay) * (
-            scalars[2 * index] * inverse * inverse / (rows_total * cols_total) + TINY_SQUARE
+        mean_row = decay * early[index] / rows_total + (1.0 - decay) * (
+            square_total[index] * inverse * inverse / (rows_total * cols_total) + TINY_SQUARE
         )
         second = rows_new[..., None] * cols_new / mean_row
         direction = grad_scaled * lax.rsqrt(second)
@@ -1145,8 +1204,10 @@
     gain_dir = gain_scaled * lax.rsqrt(second_new)
     for which in range(3):
         update_sq.append(jnp.sum(gain_dir[which] * gain_dir[which]) / head_size)
-    update_total = jnp.concatenate([jnp.stack(update_sq), jnp.zeros((1024 - 9,), single)])
-    update_total = sum_over_dp(lax.psum(update_total, "head"))[:9]
+    update_total = scalar_row(update_sq, 1024)
+    for mask in (1, 2):
+        update_total = update_total + swap(update_total, "head", mask)
+    update_total = sum_over_dp(update_total)[:9]
     results = [loss_all, count_all]
     for index in range(6):
         factor = jnp.maximum(0.001, jnp.sqrt(weight_total[index] / counts[index]))

time: 958 us -> 958 us (level)
  local copies, waits for them, and re-layouts: 106 us -> 83.4 us
  other arithmetic: 133 us -> 153 us
    concatenate x7 -> x0, local copies, waits for them, and re-layouts: 19.2 us -> none  [the longest x1 4.7 us: local(): jnp.concatenate([loss_table, jnp.zeros((slots - words, D), lowp)], axis=0)]
    add x7 -> x16, other arithmetic: 9.1 us -> 21.6 us  [the longest x8 8.14 us: core_sum(): return part[:rows].astype(single) + more.astype(single)]
    select_n x1 -> x4, other arithmetic: 0.01 us -> 10.7 us  [the longest x2 10.1 us: scalar_row(): row = jnp.where(lane == i, value, row)]
    concatenate x4 -> x8, other arithmetic: 9.72 us -> 20 us  [core_both(): return jnp.concatenate([part, swap(part, 'head', 1)], axis=0)]
    pallas_call x20 -> x22, Pallas kernels: 239 us -> 248 us  [the longest x4 41.8 us: logits_part(): pl.pallas_call(functools.partial(logits_kernel, words), name='logits_part...]
    ppermute x67 -> x75, waiting for transfers between devices: 309 us -> 302 us  [swap(): return lax.ppermute(value, axis, [(i, i ^ mask) for i in range(size)])]
    reduce_sum x13 -> x15, other arithmetic: 17 us -> 21.2 us  [the longest x6 13.5 us: local(): early += [jnp.sum(weight * weight) for weight in weights_now]]
    unnamed x266 -> x300, local copies, waits for them, and re-layouts: 38 us -> 33.8 us
  transfers between devices with their start and end apart: 69 -> 77, of which waited for: 34 -> 42; matrix products, arithmetic and copies ran while one was open for 21% -> 19% of each run, Pallas kernels for 22% -> 22%
where the time goes in v4:
time: 958 us; the launch traced here: 952 us
  waiting for transfers between devices  306 us (32%)
  Pallas kernels  250 us (26%)
  other arithmetic  153 us (16%)
  starting transfers between devices  89.7 us (9%)
  local copies, waits for them, and re-layouts  83.4 us (9%)
  matrix products  35.1 us (4%)
  between operations  25.9 us (3%)
    ppermute x75, waiting for transfers between devices, swap(): return lax.ppermute(value, axis, [(i, i ^ mask) for i in range(size)])  302 us
    ppermute x75, starting transfers between devices, swap(): return lax.ppermute(value, axis, [(i, i ^ mask) for i in range(size)])  81.3 us
    pallas_call x4, Pallas kernels, logits_part(): pl.pallas_call(functools.partial(logits_kernel, words), name='logits_part...  41.8 us
    pallas_call x4, Pallas kernels, logits_back(): pl.pallas_call(logits_back_kernel, name='logits_back', grid=(rows // tile...  40.9 us
    dot_general x11, matrix products, mm(): return lax.dot_general(left, right, dims, preferred_element_type=single)  35.1 us
    unnamed x300, local copies, waits for them, and re-layouts  33.8 us
    pallas_call x1, Pallas kernels, table_grad_part(): pl.pallas_call(functools.partial(table_grad_kernel, count), name='table_g...  24.1 us
    pallas_call x1, Pallas kernels, own_list(): pl.pallas_call(list_kernel, name='own_list', out_shape=(jax.ShapeDtypeStr...  21.4 us
  transfers between devices with their start and end apart: 77, of which 42 were waited for; matrix products, arithmetic and copies ran while one was open for 19% of the time, Pallas kernels for 22%

profile of v4, /device:TPU:0, one launch (start us, length us, event | category | flops | bytes accessed | tf_op | source)
XLA Modules:
  0.0 952.2 jit_solution(2399996025471594046)
XLA Ops:
  37.3 14.4 %collective-permute-done.3 = bf16[1120,128]{1,0:T(8,128)(2,1)S(1)} collective-permute-done((bf16[1120,128]{1,0:T(8,128)(2,1)S(1)}, bf16[1120,128]{1,0:T(8,128)(2,1)S(1)}, u32[]{:S(2)}, u32[]{:S(2)}) %collective-permute-start.3) | collective-permute-done | bytes 286752 | tf_op jit(solution)/shard_map/ppermute | solution.py:38
  117.0 10.0 %state_norm.2.old_ref = bf16[3,1024,1024]{2,1,0:T(8,128)(2,1)} custom-call(s32[2]{0:T(128)} %pad_add_fusion.place_ref, f32[1,1024]{1,0:T(1,128)} %bitcast.313, bf16[2,1536,1024]{2,1,0:T(8,128)(2,1)} %in_ref.2), custom_call_target="tpu_custom_call" | custom-call | bytes 5033164 | tf_op jit(solution)/shard_map/state_norm/pallas_call | solution.py:322
  139.4 12.2 %compress.1 = (bf16[1024,512]{1,0:T(8,128)(2,1)}, bf16[3,1024,512]{2,1,0:T(8,128)(2,1)}) custom-call(bf16[3,1024,1024]{2,1,0:T(8,128)(2,1)} %state_norm.2.old_ref, bf16[1120,1024]{1,0:T(8,128)(2,1)} %copy-done.5, bf16[1120,1024]{1,0:T(8,128)(2,1)} %copy-done.5, bf16[2,384,128]{2,1,0:T(8,128)(2,1)} %bitcast.282), custom_call_target="tpu_custom_call" | custom-call | flops 1288490240 | bytes 5033164 | tf_op jit(solution)/shard_map/compress/pallas_call | solution.py:364
  159.7 11.1 %attend.1 = (bf16[2,2,256,256]{3,2,1,0:T(8,128)(2,1)}, f32[2,2,512,1]{3,2,1,0:T(8,128)}) custom-call(s32[5]{0:T(128)} %stack.88.info_ref, bf16[2,2,256,768]{3,2,1,0:T(8,128)(2,1)} %bitcast.339, bf16[2,2,256,768]{3,2,1,0:T(8,128)(2,1)} %bitcast.340, bf16[2,2,256,768]{3,2,1,0:T(8,128)(2,1)} %bitcast.341, bf16[1024,512]{1,0:T(8,128)(2,1)} %get-tuple-element.113.kc_ref.vc_ref, ...), custom_call_target="tpu_custom_call" | custom-call | flops 2936012800 | bytes 2516582 | tf_op jit(solution)/shard_map/attend/pallas_call | solution.py:516
  200.9 9.4 collective-permute-done.17
  210.3 15.9 %collective-permute-done.16 = bf16[2000,128]{1,0:T(8,128)(2,1)S(1)} collective-permute-done((bf16[2000,128]{1,0:T(8,128)(2,1)S(1)}, bf16[2000,128]{1,0:T(8,128)(2,1)S(1)}, u32[]{:S(2)}, u32[]{:S(2)}) %collective-permute-start.16) | collective-permute-done | bytes 512032 | tf_op jit(solution)/shard_map/ppermute | solution.py:38
  242.8 30.8 %collective-permute-done.22 = bf16[2000,512]{1,0:T(8,128)(2,1)S(1)} collective-permute-done((bf16[2000,512]{1,0:T(8,128)(2,1)S(1)}, bf16[2000,512]{1,0:T(8,128)(2,1)S(1)}, u32[]{:S(2)}, u32[]{:S(2)}) %collective-permute-start.22) | collective-permute-done | bytes 2048032 | tf_op jit(solution)/shard_map/ppermute | solution.py:38
  298.6 21.4 %own_list.1 = (s32[8200]{0:T(1024)}, s32[1]{0:T(128)}) custom-call(s32[8192]{0:T(1024)} %get-tuple-element.122.code_ref), custom_call_target="tpu_custom_call" | custom-call | bytes 25165824 | tf_op jit(solution)/shard_map/own_list/pallas_call | solution.py:178
  320.7 12.6 %collective-permute-done.29 = bf16[256,1024]{1,0:T(8,128)(2,1)S(1)} collective-permute-done((bf16[256,1024]{1,0:T(8,128)(2,1)S(1)}, bf16[256,1024]{1,0:T(8,128)(2,1)S(1)}, u32[]{:S(2)}, u32[]{:S(2)}) %collective-permute-start.29) | collective-permute-done | bytes 524320 | tf_op jit(solution)/shard_map/ppermute | solution.py:38
  349.4 10.4 %logits_part.4 = (bf16[1024,2048]{1,0:T(8,128)(2,1)}, f32[8,1024]{1,0:T(8,128)}) custom-call(f32[8,1024]{1,0:T(8,128)} %squeeze.66.info_ref, bf16[1024,1024]{1,0:T(8,128)(2,1)} %pad_maximum_fusion.2.in_ref.refs_4_, bf16[2048,1024]{1,0:T(8,128)(2,1)} %fusion.9.table_ref), custom_call_target="tpu_custom_call" | custom-call | flops 3435973888 | bytes 4194304 | tf_op jit(solution)/shard_map/logits_part/pallas_call | solution.py:587
  372.2 10.5 %logits_part.5 = (bf16[1024,2048]{1,0:T(8,128)(2,1)}, f32[8,1024]{1,0:T(8,128)}) custom-call(f32[8,1024]{1,0:T(8,128)} %squeeze.72.info_ref, bf16[1024,1024]{1,0:T(8,128)(2,1)} %pad_maximum_fusion.3.in_ref.refs_5_, bf16[2048,1024]{1,0:T(8,128)(2,1)} %fusion.9.table_ref), custom_call_target="tpu_custom_call" | custom-call | flops 3435973888 | bytes 4194304 | tf_op jit(solution)/shard_map/logits_part/pallas_call | solution.py:587
  398.2 10.5 %logits_part.7 = (bf16[1024,2048]{1,0:T(8,128)(2,1)}, f32[8,1024]{1,0:T(8,128)}) custom-call(f32[8,1024]{1,0:T(8,128)} %squeeze.74.info_ref, bf16[1024,1024]{1,0:T(8,128)(2,1)} %pad_maximum_fusion.5.in_ref.refs_7_, bf16[2048,1024]{1,0:T(8,128)(2,1)} %fusion.9.table_ref), custom_call_target="tpu_custom_call" | custom-call | flops 3435973888 | bytes 4194304 | tf_op jit(solution)/shard_map/logits_part/pallas_call | solution.py:587
  412.2 10.4 %logits_part.6 = (bf16[1024,2048]{1,0:T(8,128)(2,1)}, f32[8,1024]{1,0:T(8,128)}) custom-call(f32[8,1024]{1,0:T(8,128)} %squeeze.73.info_ref, bf16[1024,1024]{1,0:T(8,128)(2,1)} %pad_maximum_fusion.4.in_ref.refs_6_, bf16[2048,1024]{1,0:T(8,128)(2,1)} %fusion.9.table_ref), custom_call_target="tpu_custom_call" | custom-call | flops 3435973888 | bytes 4194304 | tf_op jit(solution)/shard_map/logits_part/pallas_call | solution.py:587
  440.0 10.4 %logits_back.6 = (bf16[1024,2048]{1,0:T(8,128)(2,1)}, bf16[1024,1024]{1,0:T(8,128)(2,1)}) custom-call(f32[8,1024]{1,0:T(8,128)} %squeeze.74.info_ref, f32[8,1024]{1,0:T(8,128)} %broadcast_in_dim.194.factor_ref, bf16[1024,2048]{1,0:T(8,128)(2,1)} %get-tuple-element.143.in_ref, bf16[2048,1024]{1,0:T(8,128)(2,1)} %fusion.9.table_ref), custom_call_target="tpu_custom_call" | custom-call | flops 3435973888 | bytes 5033164 | tf_op jit(solution)/shard_map/logits_back/pallas_call | solution.py:624
  452.3 10.2 %logits_back.4 = (bf16[1024,2048]{1,0:T(8,128)(2,1)}, bf16[1024,1024]{1,0:T(8,128)(2,1)}) custom-call(f32[8,1024]{1,0:T(8,128)} %squeeze.73.info_ref, f32[8,1024]{1,0:T(8,128)} %broadcast_in_dim.192.factor_ref, bf16[1024,2048]{1,0:T(8,128)(2,1)} %get-tuple-element.138.in_ref, bf16[2048,1024]{1,0:T(8,128)(2,1)} %fusion.9.table_ref), custom_call_target="tpu_custom_call" | custom-call | flops 3435973888 | bytes 5033164 | tf_op jit(solution)/shard_map/logits_back/pallas_call | solution.py:624
  470.3 10.8 %collective-permute-done.42 = bf16[256,1024]{1,0:T(8,128)(2,1)S(1)} collective-permute-done((bf16[256,1024]{1,0:T(8,128)(2,1)S(1)}, bf16[256,1024]{1,0:T(8,128)(2,1)S(1)}, u32[]{:S(2)}, u32[]{:S(2)}) %collective-permute-start.42) | collective-permute-done | bytes 524320 | tf_op jit(solution)/shard_map/ppermute | solution.py:38
  481.8 10.2 %logits_back.7 = (bf16[1024,2048]{1,0:T(8,128)(2,1)}, bf16[1024,1024]{1,0:T(8,128)(2,1)}) custom-call(f32[8,1024]{1,0:T(8,128)} %squeeze.72.info_ref, f32[8,1024]{1,0:T(8,128)} %broadcast_in_dim.196.factor_ref, bf16[1024,2048]{1,0:T(8,128)(2,1)} %get-tuple-element.147.in_ref, bf16[2048,1024]{1,0:T(8,128)(2,1)} %fusion.9.table_ref), custom_call_target="tpu_custom_call" | custom-call | flops 3435973888 | bytes 5033164 | tf_op jit(solution)/shard_map/logits_back/pallas_call | solution.py:624
  498.0 10.2 %logits_back.5 = (bf16[1024,2048]{1,0:T(8,128)(2,1)}, bf16[1024,1024]{1,0:T(8,128)(2,1)}) custom-call(f32[8,1024]{1,0:T(8,128)} %squeeze.66.info_ref, f32[8,1024]{1,0:T(8,128)} %broadcast_in_dim.190.factor_ref, bf16[1024,2048]{1,0:T(8,128)(2,1)} %get-tuple-element.141.in_ref, bf16[2048,1024]{1,0:T(8,128)(2,1)} %fusion.9.table_ref), custom_call_target="tpu_custom_call" | custom-call | flops 3435973888 | bytes 5033164 | tf_op jit(solution)/shard_map/logits_back/pallas_call | solution.py:624
  514.4 24.1 %table_grad_part.1 = (f32[2048,512]{1,0:T(8,128)}, bf16[2048,512]{1,0:T(8,128)(2,1)}) custom-call(bf16[1024,2048]{1,0:T(8,128)(2,1)} %get-tuple-element.145.refs_0_, bf16[1024,2048]{1,0:T(8,128)(2,1)} %get-tuple-element.148.refs_1_, bf16[1024,2048]{1,0:T(8,128)(2,1)} %get-tuple-element.149.refs_2_, bf16[1024,2048]{1,0:T(8,128)(2,1)} %get-tuple-element.150.refs_3_, ...), custom_call_target="tpu_custom_call" | custom-call | flops 10307921920 | bytes 12582912 | tf_op jit(solution)/shard_map/table_grad_part/pallas_call | solution.py:671
  546.2 9.6 %collective-permute-done.40 = bf16[256,1024]{1,0:T(8,128)(2,1)S(1)} collective-permute-done((bf16[256,1024]{1,0:T(8,128)(2,1)S(1)}, bf16[256,1024]{1,0:T(8,128)(2,1)S(1)}, u32[]{:S(2)}, u32[]{:S(2)}) %collective-permute-start.40) | collective-permute-done | bytes 524320 | tf_op jit(solution)/shard_map/ppermute | solution.py:38
  555.8 15.0 %collective-permute-done.46 = bf16[256,1024]{1,0:T(8,128)(2,1)S(1)} collective-permute-done((bf16[256,1024]{1,0:T(8,128)(2,1)S(1)}, bf16[256,1024]{1,0:T(8,128)(2,1)S(1)}, u32[]{:S(2)}, u32[]{:S(2)}) %collective-permute-start.46) | collective-permute-done | bytes 524320 | tf_op jit(solution)/shard_map/ppermute | solution.py:38
  572.0 13.3 %collective-permute-done.47 = bf16[256,1024]{1,0:T(8,128)(2,1)S(1)} collective-permute-done((bf16[256,1024]{1,0:T(8,128)(2,1)S(1)}, bf16[256,1024]{1,0:T(8,128)(2,1)S(1)}, u32[]{:S(2)}, u32[]{:S(2)}) %collective-permute-start.47) | collective-permute-done | bytes 524320 | tf_op jit(solution)/shard_map/ppermute | solution.py:38
  606.4 11.4 %hidden_grads.1 = (f32[2048,512]{1,0:T(8,128)}, bf16[2048,512]{1,0:T(8,128)(2,1)}) custom-call(bf16[1024,1024]{1,0:T(8,128)(2,1)} %copy-done.131, bf16[1024,1024]{1,0:T(8,128)(2,1)} %copy-done.130, bf16[1024,1024]{1,0:T(8,128)(2,1)} %pad_maximum_fusion.1.in_ref, bf16[1024,1024]{1,0:T(8,128)(2,1)} %pad_maximum_fusion.6.down_ref), custom_call_target="tpu_custom_call" | custom-call | flops 2576980480 | bytes 6710886 | tf_op jit(solution)/shard_map/hidden_grads/pallas_call | solution.py:706
  617.8 16.0 %collective-permute-done.51 = bf16[2048,512]{1,0:T(8,128)(2,1)} collective-permute-done((bf16[2048,512]{1,0:T(8,128)(2,1)}, bf16[2048,512]{1,0:T(8,128)(2,1)}, u32[]{:S(2)}, u32[]{:S(2)}) %collective-permute-start.51) | collective-permute-done | bytes 2097184 | tf_op jit(solution)/shard_map/ppermute | solution.py:38
  658.8 15.6 %attend_back.1 = (bf16[2,2,256,768]{3,2,1,0:T(8,128)(2,1)}, bf16[1024,512]{1,0:T(8,128)(2,1)}, bf16[1024,512]{1,0:T(8,128)(2,1)}) custom-call(s32[5]{0:T(128)} %stack.88.info_ref, bf16[2,2,256,768]{3,2,1,0:T(8,128)(2,1)} %bitcast.342, bf16[2,2,256,768]{3,2,1,0:T(8,128)(2,1)} %bitcast.343, bf16[2,2,256,768]{3,2,1,0:T(8,128)(2,1)} %bitcast.344, ...), custom_call_target="tpu_custom_call" | custom-call | flops 4613734400 | bytes 3774873 | tf_op jit(solution)/shard_map/attend_back/pallas_call | solution.py:539
  692.2 14.0 %attn_grads.1 = (f32[1024,512]{1,0:T(8,128)}, bf16[1024,512]{1,0:T(8,128)(2,1)}) custom-call(bf16[1024,768]{1,0:T(8,128)(2,1)} %bitcast.285, bf16[1024,256]{1,0:T(8,128)(2,1)} %bitcast.280, bf16[1024,512]{1,0:T(8,128)(2,1)} %get-tuple-element.166.mem_ref, bf16[3072,512]{1,0:T(8,128)(2,1)} %bitcast.281, bf16[1024,1024]{1,0:T(8,128)(2,1)} %pad_maximum_fusion.normed_ref, ...), custom_call_target="tpu_custom_call" | custom-call | flops 3774873600 | bytes 10066329 | tf_op jit(solution)/shard_map/attn_grads/pallas_call | solution.py:756
  719.4 15.7 %collective-permute-done.62 = bf16[1120,512]{1,0:T(8,128)(2,1)S(1)} collective-permute-done((bf16[1120,512]{1,0:T(8,128)(2,1)S(1)}, bf16[1120,512]{1,0:T(8,128)(2,1)S(1)}, u32[]{:S(2)}, u32[]{:S(2)}) %collective-permute-start.62) | collective-permute-done | bytes 1146912 | tf_op jit(solution)/shard_map/ppermute | solution.py:38
  737.8 10.1 %collective-permute-done.58 = bf16[2000,128]{1,0:T(8,128)(2,1)S(1)} collective-permute-done((bf16[2000,128]{1,0:T(8,128)(2,1)S(1)}, bf16[2000,128]{1,0:T(8,128)(2,1)S(1)}, u32[]{:S(2)}, u32[]{:S(2)}) %collective-permute-start.58) | collective-permute-done | bytes 512032 | tf_op jit(solution)/shard_map/ppermute | solution.py:38
  755.3 10.9 %collective-permute-start.60 = (bf16[2048,256]{1,0:T(8,128)(2,1)}, bf16[2048,256]{1,0:T(8,128)(2,1)}, u32[]{:S(2)}, u32[]{:S(2)}) collective-permute-start(bf16[2048,256]{1,0:T(8,128)(2,1)} %slice.1315), channel_id=1, source_target_pairs={{0,8},{4,12},{8,0},{12,4},{16,24},{20,28},{24,16},{28,20},{1,9},{5... | collective-permute-start | bytes 3145736 | tf_op jit(solution)/shard_map/ppermute | solution.py:38
  781.1 22.6 %collective-permute-done.64 = bf16[1120,128]{1,0:T(8,128)(2,1)S(1)} collective-permute-done((bf16[1120,128]{1,0:T(8,128)(2,1)S(1)}, bf16[1120,128]{1,0:T(8,128)(2,1)S(1)}, u32[]{:S(2)}, u32[]{:S(2)}) %collective-permute-start.64) | collective-permute-done | bytes 286752 | tf_op jit(solution)/shard_map/ppermute | solution.py:38
  821.0 13.0 %collective-permute-done.61 = bf16[2048,128]{1,0:T(8,128)(2,1)} collective-permute-done((bf16[2048,128]{1,0:T(8,128)(2,1)}, bf16[2048,128]{1,0:T(8,128)(2,1)}, u32[]{:S(2)}, u32[]{:S(2)}) %collective-permute-start.61) | collective-permute-done | bytes 524320 | tf_op jit(solution)/shard_map/ppermute | solution.py:38
  838.7 12.2 %scatter.1 = f32[8000,128]{1,0:T(8,128)} custom-call(s32[1]{0:T(128)} %get-tuple-element.173.count_ref, s32[8200]{0:T(1024)} %get-tuple-element.174.code_ref, f32[8000,128]{1,0:T(8,128)} %copy-done, bf16[8192,128]{1,0:T(8,128)(2,1)} %bitcast.276), custom_call_target="tpu_custom_call" | custom-call | bytes 12582912 | tf_op jit(solution)/shard_map/scatter/pallas_call | solution.py:274
  (731 shorter events, 491.6 us)
Async XLA Ops:
  33.6 27.6 %collective-permute-start.4 = (bf16[4096,128]{1,0:T(8,128)(2,1)}, bf16[4096,128]{1,0:T(8,128)(2,1)}, u32[]{:S(2)}, u32[]{:S(2)}) collective-permute-start(bf16[4096,128]{1,0:T(8,128)(2,1)} %lookup.3), channel_id=1, source_target_pairs={{0,1},{1,0},{2,3},{3,2},{4,5},{5,4},{6,7},{7,6},{8,9},{9,8},{10,11... | collective-permute-start | bytes 3145736 | tf_op jit(solution)/shard_map/ppermute | solution.py:38
  64.7 29.7 %collective-permute-start.9 = (bf16[1120,256]{1,0:T(8,128)(2,1)}, bf16[1120,256]{1,0:T(8,128)(2,1)}, u32[]{:S(2)}, u32[]{:S(2)}) collective-permute-start(bf16[1120,256]{1,0:T(8,128)(2,1)} %get-tuple-element.403), channel_id=1, source_target_pairs={{0,8},{4,12},{8,0},{12,4},{16,24},{20,28},{24,16},{28,20},{1,9},{5... | collective-permute-start | bytes 1720328 | tf_op jit(solution)/shard_map/ppermute | solution.py:38
  92.1 34.9 %collective-permute-start.11 = (bf16[2048,256]{1,0:T(8,128)(2,1)}, bf16[2048,256]{1,0:T(8,128)(2,1)}, u32[]{:S(2)}, u32[]{:S(2)}) collective-permute-start(bf16[2048,256]{1,0:T(8,128)(2,1)} %get-tuple-element.395), channel_id=1, source_target_pairs={{0,8},{4,12},{8,0},{12,4},{16,24},{20,28},{24,16},{28,20},{1,9},{5... | collective-permute-start | bytes 3145736 | tf_op jit(solution)/shard_map/ppermute | solution.py:38
  96.3 36.2 %collective-permute-start.10 = (bf16[1120,512]{1,0:T(8,128)(2,1)}, bf16[1120,512]{1,0:T(8,128)(2,1)}, u32[]{:S(2)}, u32[]{:S(2)}) collective-permute-start(bf16[1120,512]{1,0:T(8,128)(2,1)} %get-tuple-element.386), channel_id=1, source_target_pairs={{0,4},{4,0},{8,12},{12,8},{16,20},{20,16},{24,28},{28,24},{1,5},{5... | collective-permute-start | bytes 3440648 | tf_op jit(solution)/shard_map/ppermute | solution.py:38
  104.7 26.7 %collective-permute-start.7 = (bf16[256,1024]{1,0:T(8,128)(2,1)}, bf16[256,1024]{1,0:T(8,128)(2,1)S(1)}, u32[]{:S(2)}, u32[]{:S(2)}) collective-permute-start(bf16[256,1024]{1,0:T(8,128)(2,1)} %get-tuple-element.110), channel_id=1, source_target_pairs={{0,2},{1,3},{2,0},{3,1},{4,6},{5,7},{6,4},{7,5},{8,10},{9,11},{10,... | collective-permute-start | bytes 1572872 | tf_op jit(solution)/shard_map/ppermute | solution.py:38
  129.8 57.5 %collective-permute-start.14 = (bf16[2048,512]{1,0:T(8,128)(2,1)}, bf16[2048,512]{1,0:T(8,128)(2,1)}, u32[]{:S(2)}, u32[]{:S(2)}) collective-permute-start(bf16[2048,512]{1,0:T(8,128)(2,1)} %get-tuple-element.385), channel_id=1, source_target_pairs={{0,4},{4,0},{8,12},{12,8},{16,20},{20,16},{24,28},{28,24},{1,5},{5... | collective-permute-start | bytes 6291464 | tf_op jit(solution)/shard_map/ppermute | solution.py:38
  183.0 27.3 %collective-permute-start.17 = (bf16[2000,128]{1,0:T(8,128)(2,1)S(1)}, bf16[2000,128]{1,0:T(8,128)(2,1)S(1)}, u32[]{:S(2)}, u32[]{:S(2)}) collective-permute-start(bf16[2000,128]{1,0:T(8,128)(2,1)S(1)} %get-tuple-element.372), channel_id=1, source_target_pairs={{0,8},{4,12},{8,0},{12,4},{16,24},{20,28},{24,16},{28,20},{1,9},{5... | collective-permute-start | bytes 1536008 | tf_op jit(solution)/shard_map/ppermute | solution.py:38
  183.0 43.2 %collective-permute-start.16 = (bf16[2000,128]{1,0:T(8,128)(2,1)S(1)}, bf16[2000,128]{1,0:T(8,128)(2,1)S(1)}, u32[]{:S(2)}, u32[]{:S(2)}) collective-permute-start(bf16[2000,128]{1,0:T(8,128)(2,1)S(1)} %get-tuple-element.373), channel_id=1, source_target_pairs={{0,16},{4,20},{8,24},{12,28},{16,0},{20,4},{24,8},{28,12},{1,17},{... | collective-permute-start | bytes 1536008 | tf_op jit(solution)/shard_map/ppermute | solution.py:38
  199.4 27.1 %collective-permute-start.15 = (bf16[256,1024]{1,0:T(8,128)(2,1)S(1)}, bf16[256,1024]{1,0:T(8,128)(2,1)S(1)}, u32[]{:S(2)}, u32[]{:S(2)}) collective-permute-start(bf16[256,1024]{1,0:T(8,128)(2,1)S(1)} %multiply_convert_fusion.2), channel_id=1, source_target_pairs={{0,2},{1,3},{2,0},{3,1},{4,6},{5,7},{6,4},{7,5},{8,10},{9,11},{10,... | collective-permute-start | bytes 1572872 | tf_op jit(solution)/shard_map/ppermute | solution.py:38
  226.7 47.0 %collective-permute-start.22 = (bf16[2000,512]{1,0:T(8,128)(2,1)S(1)}, bf16[2000,512]{1,0:T(8,128)(2,1)S(1)}, u32[]{:S(2)}, u32[]{:S(2)}) collective-permute-start(bf16[2000,512]{1,0:T(8,128)(2,1)S(1)} %pad_maximum_fusion.9), channel_id=1, source_target_pairs={{0,4},{4,0},{8,12},{12,8},{16,20},{20,16},{24,28},{28,24},{1,5},{5... | collective-permute-start | bytes 6144008 | tf_op jit(solution)/shard_map/ppermute | solution.py:38
  241.2 32.5 %collective-permute-start.21 = (bf16[256,1024]{1,0:T(8,128)(2,1)S(1)}, bf16[256,1024]{1,0:T(8,128)(2,1)S(1)}, u32[]{:S(2)}, u32[]{:S(2)}) collective-permute-start(bf16[256,1024]{1,0:T(8,128)(2,1)S(1)} %slice.1328), channel_id=1, source_target_pairs={{0,2},{1,3},{2,0},{3,1},{4,6},{5,7},{6,4},{7,5},{8,10},{9,11},{10,... | collective-permute-start | bytes 1572872 | tf_op jit(solution)/shard_map/ppermute | solution.py:38
  280.2 39.8 %collective-permute-start.23 = (bf16[256,1024]{1,0:T(8,128)(2,1)}, bf16[256,1024]{1,0:T(8,128)(2,1)S(1)}, u32[]{:S(2)}, u32[]{:S(2)}) collective-permute-start(bf16[256,1024]{1,0:T(8,128)(2,1)} %constant_dynamic-update-slice_fusion.19), channel_id=1, source_target_pairs={{0,16},{4,20},{8,24},{12,28},{16,0},{20,4},{24,8},{28,12},{1,17},{... | collective-permute-start | bytes 1572872 | tf_op jit(solution)/shard_map/ppermute | solution.py:38
  338.4 26.2 %collective-permute-start.24 = (bf16[512,1024]{1,0:T(8,128)(2,1)}, bf16[512,1024]{1,0:T(8,128)(2,1)}, u32[]{:S(2)}, u32[]{:S(2)}) collective-permute-start(bf16[512,1024]{1,0:T(8,128)(2,1)} %get-tuple-element.389), channel_id=1, source_target_pairs={{0,8},{4,12},{8,0},{12,4},{16,24},{20,28},{24,16},{28,20},{1,9},{5... | collective-permute-start | bytes 3145736 | tf_op jit(solution)/shard_map/ppermute | solution.py:38
  341.2 28.2 %collective-permute-start.30 = (bf16[512,1024]{1,0:T(8,128)(2,1)}, bf16[512,1024]{1,0:T(8,128)(2,1)}, u32[]{:S(2)}, u32[]{:S(2)}) collective-permute-start(bf16[512,1024]{1,0:T(8,128)(2,1)} %get-tuple-element.388), channel_id=1, source_target_pairs={{0,1},{1,0},{2,3},{3,2},{4,5},{5,4},{6,7},{7,6},{8,9},{9,8},{10,11... | collective-permute-start | bytes 3145736 | tf_op jit(solution)/shard_map/ppermute | solution.py:38
  468.7 25.8 %collective-permute-start.38 = (bf16[256,1024]{1,0:T(8,128)(2,1)S(1)}, bf16[256,1024]{1,0:T(8,128)(2,1)S(1)}, u32[]{:S(2)}, u32[]{:S(2)}) collective-permute-start(bf16[256,1024]{1,0:T(8,128)(2,1)S(1)} %slice.1327), channel_id=1, source_target_pairs={{0,2},{1,3},{2,0},{3,1},{4,6},{5,7},{6,4},{7,5},{8,10},{9,11},{10,... | collective-permute-start | bytes 1572872 | tf_op jit(solution)/shard_map/ppermute | solution.py:38
  495.8 42.8 %collective-permute-start.43 = (bf16[512,1024]{1,0:T(8,128)(2,1)}, bf16[512,1024]{1,0:T(8,128)(2,1)S(1)}, u32[]{:S(2)}, u32[]{:S(2)}) collective-permute-start(bf16[512,1024]{1,0:T(8,128)(2,1)} %fusion.20), channel_id=1, source_target_pairs={{0,8},{4,12},{8,0},{12,4},{16,24},{20,28},{24,16},{28,20},{1,9},{5... | collective-permute-start | bytes 3145736 | tf_op jit(solution)/shard_map/ppermute | solution.py:38
  510.6 28.3 %collective-permute-start.39 = (bf16[512,1024]{1,0:T(8,128)(2,1)}, bf16[512,1024]{1,0:T(8,128)(2,1)}, u32[]{:S(2)}, u32[]{:S(2)}) collective-permute-start(bf16[512,1024]{1,0:T(8,128)(2,1)} %slice.744), channel_id=1, source_target_pairs={{0,1},{1,0},{2,3},{3,2},{4,5},{5,4},{6,7},{7,6},{8,9},{9,8},{10,11... | collective-permute-start | bytes 3145736 | tf_op jit(solution)/shard_map/ppermute | solution.py:38
  513.8 29.6 %collective-permute-start.45 = (bf16[256,1024]{1,0:T(8,128)(2,1)S(1)}, bf16[256,1024]{1,0:T(8,128)(2,1)}, u32[]{:S(2)}, u32[]{:S(2)}) collective-permute-start(bf16[256,1024]{1,0:T(8,128)(2,1)S(1)} %slice.1324), channel_id=1, source_target_pairs={{0,2},{1,3},{2,0},{3,1},{4,6},{5,7},{6,4},{7,5},{8,10},{9,11},{10,... | collective-permute-start | bytes 1572872 | tf_op jit(solution)/shard_map/ppermute | solution.py:38
  545.0 25.7 %collective-permute-start.46 = (bf16[256,1024]{1,0:T(8,128)(2,1)S(1)}, bf16[256,1024]{1,0:T(8,128)(2,1)S(1)}, u32[]{:S(2)}, u32[]{:S(2)}) collective-permute-start(bf16[256,1024]{1,0:T(8,128)(2,1)S(1)} %constant_dynamic-update-slice_fusion.27), channel_id=1, source_target_pairs={{0,16},{4,20},{8,24},{12,28},{16,0},{20,4},{24,8},{28,12},{1,17},{... | collective-permute-start | bytes 1572872 | tf_op jit(solution)/shard_map/ppermute | solution.py:38
  585.4 48.4 %collective-permute-start.51 = (bf16[2048,512]{1,0:T(8,128)(2,1)}, bf16[2048,512]{1,0:T(8,128)(2,1)}, u32[]{:S(2)}, u32[]{:S(2)}) collective-permute-start(bf16[2048,512]{1,0:T(8,128)(2,1)} %get-tuple-element.157), channel_id=1, source_target_pairs={{0,4},{4,0},{8,12},{12,8},{16,20},{20,16},{24,28},{28,24},{1,5},{5... | collective-permute-start | bytes 6291464 | tf_op jit(solution)/shard_map/ppermute | solution.py:38
  602.9 30.9 %collective-permute-start.50 = (bf16[256,1024]{1,0:T(8,128)(2,1)}, bf16[256,1024]{1,0:T(8,128)(2,1)S(1)}, u32[]{:S(2)}, u32[]{:S(2)}) collective-permute-start(bf16[256,1024]{1,0:T(8,128)(2,1)} %slice.1323), channel_id=1, source_target_pairs={{0,2},{1,3},{2,0},{3,1},{4,6},{5,7},{6,4},{7,5},{8,10},{9,11},{10,... | collective-permute-start | bytes 1572872 | tf_op jit(solution)/shard_map/ppermute | solution.py:38
  654.5 94.2 %collective-permute-start.56 = (bf16[2048,512]{1,0:T(8,128)(2,1)}, bf16[2048,512]{1,0:T(8,128)(2,1)}, u32[]{:S(2)}, u32[]{:S(2)}) collective-permute-start(bf16[2048,512]{1,0:T(8,128)(2,1)} %get-tuple-element.162), channel_id=1, source_target_pairs={{0,4},{4,0},{8,12},{12,8},{16,20},{20,16},{24,28},{28,24},{1,5},{5... | collective-permute-start | bytes 6291464 | tf_op jit(solution)/shard_map/ppermute | solution.py:38
  680.7 34.1 %collective-permute-start.54 = (bf16[512,1024]{1,0:T(8,128)(2,1)}, bf16[512,1024]{1,0:T(8,128)(2,1)}, u32[]{:S(2)}, u32[]{:S(2)}) collective-permute-start(bf16[512,1024]{1,0:T(8,128)(2,1)} %slice.1316), channel_id=1, source_target_pairs={{0,1},{1,0},{2,3},{3,2},{4,5},{5,4},{6,7},{7,6},{8,9},{9,8},{10,11... | collective-permute-start | bytes 3145736 | tf_op jit(solution)/shard_map/ppermute | solution.py:38
  707.5 27.6 %collective-permute-start.62 = (bf16[1120,512]{1,0:T(8,128)(2,1)S(1)}, bf16[1120,512]{1,0:T(8,128)(2,1)S(1)}, u32[]{:S(2)}, u32[]{:S(2)}) collective-permute-start(bf16[1120,512]{1,0:T(8,128)(2,1)S(1)} %pad_maximum_fusion.11), channel_id=1, source_target_pairs={{0,4},{4,0},{8,12},{12,8},{16,20},{20,16},{24,28},{28,24},{1,5},{5... | collective-permute-start | bytes 3440648 | tf_op jit(solution)/shard_map/ppermute | solution.py:38
  712.1 25.7 %collective-permute-start.57 = (bf16[2000,128]{1,0:T(8,128)(2,1)S(1)}, bf16[2000,128]{1,0:T(8,128)(2,1)S(1)}, u32[]{:S(2)}, u32[]{:S(2)}) collective-permute-start(bf16[2000,128]{1,0:T(8,128)(2,1)S(1)} %get-tuple-element.369), channel_id=1, source_target_pairs={{0,16},{4,20},{8,24},{12,28},{16,0},{20,4},{24,8},{28,12},{1,17},{... | collective-permute-start | bytes 1536008 | tf_op jit(solution)/shard_map/ppermute | solution.py:38
  712.2 35.7 %collective-permute-start.58 = (bf16[2000,128]{1,0:T(8,128)(2,1)S(1)}, bf16[2000,128]{1,0:T(8,128)(2,1)S(1)}, u32[]{:S(2)}, u32[]{:S(2)}) collective-permute-start(bf16[2000,128]{1,0:T(8,128)(2,1)S(1)} %get-tuple-element.368), channel_id=1, source_target_pairs={{0,8},{4,12},{8,0},{12,4},{16,24},{20,28},{24,16},{28,20},{1,9},{5... | collective-permute-start | bytes 1536008 | tf_op jit(solution)/shard_map/ppermute | solution.py:38
  714.8 33.9 %collective-permute-start.59 = (bf16[2000,128]{1,0:T(8,128)(2,1)S(1)}, bf16[2000,128]{1,0:T(8,128)(2,1)S(1)}, u32[]{:S(2)}, u32[]{:S(2)}) collective-permute-start(bf16[2000,128]{1,0:T(8,128)(2,1)S(1)} %get-tuple-element.367), channel_id=1, source_target_pairs={{0,24},{4,28},{8,16},{12,20},{16,8},{20,12},{24,0},{28,4},{1,25},{... | collective-permute-start | bytes 1536008 | tf_op jit(solution)/shard_map/ppermute | solution.py:38
  737.8 37.4 %collective-permute-start.63 = (bf16[1120,256]{1,0:T(8,128)(2,1)}, bf16[1120,256]{1,0:T(8,128)(2,1)}, u32[]{:S(2)}, u32[]{:S(2)}) collective-permute-start(bf16[1120,256]{1,0:T(8,128)(2,1)} %slice.1320), channel_id=1, source_target_pairs={{0,8},{4,12},{8,0},{12,4},{16,24},{20,28},{24,16},{28,20},{1,9},{5... | collective-permute-start | bytes 1720328 | tf_op jit(solution)/shard_map/ppermute | solution.py:38
  755.3 50.1 %collective-permute-start.60 = (bf16[2048,256]{1,0:T(8,128)(2,1)}, bf16[2048,256]{1,0:T(8,128)(2,1)}, u32[]{:S(2)}, u32[]{:S(2)}) collective-permute-start(bf16[2048,256]{1,0:T(8,128)(2,1)} %slice.1315), channel_id=1, source_target_pairs={{0,8},{4,12},{8,0},{12,4},{16,24},{20,28},{24,16},{28,20},{1,9},{5... | collective-permute-start | bytes 3145736 | tf_op jit(solution)/shard_map/ppermute | solution.py:38
  769.3 35.6 %all-to-all-start.1 = ((bf16[8,256,128]{2,1,0:T(8,128)(2,1)}), bf16[8,256,128]{2,1,0:T(8,128)(2,1)}, u32[]{:S(2)}, u32[]{:S(2)}) async-start(bf16[8,256,128]{2,1,0:T(8,128)(2,1)} %embed_back.1), calls=%async_computation.1 | async-start | bytes 1048576 | tf_op jit(solution)/shard_map/all_to_all | solution.py:1096
  777.1 26.5 %collective-permute-start.64 = (bf16[1120,128]{1,0:T(8,128)(2,1)S(1)}, bf16[1120,128]{1,0:T(8,128)(2,1)S(1)}, u32[]{:S(2)}, u32[]{:S(2)}) collective-permute-start(bf16[1120,128]{1,0:T(8,128)(2,1)S(1)} %slice.1330), channel_id=1, source_target_pairs={{0,16},{4,20},{8,24},{12,28},{16,0},{20,4},{24,8},{28,12},{1,17},{... | collective-permute-start | bytes 860168 | tf_op jit(solution)/shard_map/ppermute | solution.py:38
  808.4 25.6 %collective-permute-start.61 = (bf16[2048,128]{1,0:T(8,128)(2,1)}, bf16[2048,128]{1,0:T(8,128)(2,1)}, u32[]{:S(2)}, u32[]{:S(2)}) collective-permute-start(bf16[2048,128]{1,0:T(8,128)(2,1)} %slice.1321), channel_id=1, source_target_pairs={{0,16},{4,20},{8,24},{12,28},{16,0},{20,4},{24,8},{28,12},{1,17},{... | collective-permute-start | bytes 1572872 | tf_op jit(solution)/shard_map/ppermute | solution.py:38
  (178 other events, 2493.2 us)

commit v5 on v4

--- a/solution.py
+++ b/solution.py
@@ -55,14 +55,17 @@
     return order
 
 
-def gather_blocks(piece, axis, start=None):
+def gather_blocks(piece, axis, beside=()):
     steps = []
     mask = lax.axis_size("dp") // 2
     while mask:
-        piece = jnp.concatenate([piece, swap(piece, "dp", mask)], axis=axis)
+        moved = swap(piece, "dp", mask)
+        if not steps and beside:
+            moved, *beside = together(moved, *beside)
+        piece = jnp.concatenate([piece, moved], axis=axis)
         steps.append(piece)
         mask //= 2
-    return piece, steps
+    return piece, steps, beside
 
 
 def split(value, axis, parts):
@@ -117,7 +120,7 @@
 
 def cost(flops, size, exps=0):
     return pl.CostEstimate(
-        flops=int(0.4 * flops), bytes_accessed=int(0.4 * size), transcendentals=exps
+        flops=int(0.02 * flops), bytes_accessed=int(0.02 * size), transcendentals=exps
     )
 
 
@@ -565,8 +568,18 @@
     return jnp.transpose(tall)
 
 
-def logits_kernel(words, info_ref, in_ref, table_ref, out_ref, stat_ref):
-    logits = mm(in_ref[...], table_ref[...], NT)
+def logits_kernel(words, tiles, info_ref, pair_ref, near_ref, table_ref, out_ref, stat_ref, held):
+    step = pl.program_id(0)
+
+    @pl.when(step < tiles)
+    def _():
+        held[...] = pair_ref[...]
+
+    @pl.when(step >= tiles)
+    def _():
+        held[...] = near_ref[...]
+
+    logits = mm(held[...], table_ref[...], NT)
     wanted = columns_of(info_ref[...])[:, 0:1].astype(jnp.int32)
     col = lax.broadcasted_iota(jnp.int32, logits.shape, 1)
     hit = jnp.sum(jnp.where(col == wanted, logits, 0.0), axis=-1, keepdims=True)
@@ -580,33 +593,37 @@
     stat_ref[...] = jnp.transpose(packed)[:8]
 
 
-def logits_part(words, info, inputs, table):
-    rows = inputs.shape[0]
+def logits_part(words, info, pair, near, table):
+    rows = pair.shape[0] + near.shape[0]
     slots = table.shape[0]
     tile = 256
-    return pl.pallas_call(
-        functools.partial(logits_kernel, words),
+    tiles = pair.shape[0] // tile
+    return pl.pallas_call(
+        functools.partial(logits_kernel, words, tiles),
         name="logits_part",
-        grid=(rows // tile,),
+        grid=(2 * tiles,),
         out_shape=(
             jax.ShapeDtypeStruct((rows, slots), lowp),
             jax.ShapeDtypeStruct((8, rows), single),
         ),
         in_specs=[
             pl.BlockSpec((8, tile), lambda i: (0, i)),
-            pl.BlockSpec((tile, D), lambda i: (i, 0)),
+            pl.BlockSpec((tile, D), lambda i: (jnp.minimum(i, tiles - 1), 0)),
+            pl.BlockSpec((tile, D), lambda i: (jnp.maximum(i - tiles, 0), 0)),
             pl.BlockSpec(table.shape, lambda i: (0, 0)),
         ],
         out_specs=(
             pl.BlockSpec((tile, slots), lambda i: (i, 0)),
             pl.BlockSpec((8, tile), lambda i: (0, i)),
         ),
+        scratch_shapes=[pltpu.VMEM((tile, D), lowp)],
         compiler_params=params(60),
         cost_estimate=cost(4 * rows * slots * D, 10 * MIB),
-    )(info, inputs, table)
-
-
-def logits_back_kernel(info_ref, factor_ref, in_ref, table_ref, out_ref, grad_ref):
+    )(info, pair, near, table)
+
+
+def logits_back_kernel(tiles, info_ref, factor_ref, in_ref, table_ref, out_ref, keep_ref, send_ref):
+    step = pl.program_id(0)
     info = columns_of(info_ref[...])
     wanted = info[:, 0:1].astype(jnp.int32)
     counted = info[:, 1:2]
@@ -615,29 +632,44 @@
     col = lax.broadcasted_iota(jnp.int32, raised.shape, 1)
     grads = (raised * factor - jnp.where(col == wanted, counted, 0.0)).astype(lowp)
     out_ref[...] = grads
-    grad_ref[...] = mm(grads, table_ref[...]).astype(lowp)
+    total = mm(grads, table_ref[...]).astype(lowp)
+
+    @pl.when(step < tiles)
+    def _():
+        send_ref[...] = total
+
+    @pl.when(step >= tiles)
+    def _():
+        keep_ref[...] = total
 
 
 def logits_back(info, factor, raised, table):
     rows, slots = raised.shape
     tile = 256
-    return pl.pallas_call(
-        logits_back_kernel,
+    tiles = rows // (2 * tile)
+
+    def at(i):
+        return (i + tiles) % (2 * tiles)
+
+    return pl.pallas_call(
+        functools.partial(logits_back_kernel, tiles),
         name="logits_back",
-        grid=(rows // tile,),
+        grid=(2 * tiles,),
         out_shape=(
             jax.ShapeDtypeStruct((rows, slots), lowp),
-            jax.ShapeDtypeStruct((rows, D), lowp),
+            jax.ShapeDtypeStruct((rows // 2, D), lowp),
+            jax.ShapeDtypeStruct((rows // 2, D), lowp),
         ),
         in_specs=[
-            pl.BlockSpec((8, tile), lambda i: (0, i)),
-            pl.BlockSpec((8, tile), lambda i: (0, i)),
-            pl.BlockSpec((tile, slots), lambda i: (i, 0)),
+            pl.BlockSpec((8, tile), lambda i: (0, at(i))),
+            pl.BlockSpec((8, tile), lambda i: (0, at(i))),
+            pl.BlockSpec((tile, slots), lambda i: (at(i), 0)),
             pl.BlockSpec(table.shape, lambda i: (0, 0)),
         ],
         out_specs=(
-            pl.BlockSpec((tile, slots), lambda i: (i, 0)),
-            pl.BlockSpec((tile, D), lambda i: (i, 0)),
+            pl.BlockSpec((tile, slots), lambda i: (at(i), 0)),
+            pl.BlockSpec((tile, D), lambda i: (jnp.maximum(i - tiles, 0), 0)),
+            pl.BlockSpec((tile, D), lambda i: (jnp.minimum(i, tiles - 1), 0)),
         ),
         compiler_params=params(60),
         cost_estimate=cost(4 * rows * slots * D, 12 * MIB),
@@ -651,12 +683,13 @@
 
 
 def table_grad_kernel(count, *refs):
-    grads = refs[:count]
-    inputs = refs[count : 2 * count]
-    total = mm(grads[0][...], inputs[0][...], TN)
-    for i in range(1, count):
-        total = total + mm(grads[i][...], inputs[i][...], TN)
-    halves(total, *refs[2 * count :])
+    total = None
+    for i in range(count):
+        rows = refs[count + 2 * i].shape[0]
+        for j in range(2):
+            term = mm(refs[i][j * rows : (j + 1) * rows, :], refs[count + 2 * i + j][...], TN)
+            total = term if total is None else total + term
+    halves(total, *refs[3 * count :])
 
 
 def table_grad_part(grads, inputs):
@@ -665,9 +698,10 @@
     slots = grads[0].shape[1]
     block = 256
     if rows > 4096:
-        total = sum(mm(g, v, TN) for g, v in zip(grads, inputs))
+        total = sum(mm(g, jnp.concatenate(v), TN) for g, v in zip(grads, inputs))
         keep, send = split(total, 1, 2)
         return keep, send.astype(lowp)
+    inputs = [part for pair in inputs for part in pair]
     return pl.pallas_call(
         functools.partial(table_grad_kernel, count),
         name="table_grad_part",
@@ -849,7 +883,7 @@
     )
     room = -flat.shape[0] % 1024
     flat = jnp.concatenate([flat, jnp.zeros((room,), single)]).reshape(1, -1, 128)
-    small, small_steps = gather_blocks(flat, 0)
+    small, small_steps, _ = gather_blocks(flat, 0)
     small = small.reshape(dp_size, -1)
     place = jnp.stack([x, d])
 
@@ -883,7 +917,15 @@
             wconv.astype(lowp).reshape(conv_rows_own, width),
         ]
     )
-    own_one, steps_one = gather_blocks(after(pack_one, small_steps[0]), 1)
+    own_half, far_half = split(table_rows_all, 0, 2)
+    looked_far = lookup(far_half, table)
+    looked_own = lookup(own_half, table)
+    own_one, steps_one, (looked_far, looked_own) = gather_blocks(
+        after(pack_one, small_steps[0]), 1, (looked_far, looked_own)
+    )
+    mem_normed = state_norm(place, gain_vals[0], memory, 1)[0]
+    old_normed = state_norm(place, gain_vals[0], old_states, RATE)
+    own_one, mem_normed, old_normed = together(own_one, mem_normed, old_normed)
     conv_lanes = jnp.arange(DH, dtype=jnp.int32)
     conv_width = DH // dp_size
     conv_natural = (jnp.asarray(order, jnp.int32)[conv_lanes // conv_width] ^ d) * conv_width
@@ -907,74 +949,68 @@
 
     hidden_own = wup.shape[1]
     pack_two = jnp.concatenate([wup.astype(lowp).T, wdown.astype(lowp)])
-    own_two, steps_two = gather_blocks(after(pack_two, steps_one[0]), 1)
+    own_two, steps_two, _ = gather_blocks(after(pack_two, steps_one[0]), 1)
 
     words = vocab // reach
     z = d // 2
-    low_table = after(table.astype(lowp), steps_two[-2])
-    near_table = []
-    for m in order[:reach]:
-        part = lax.dynamic_slice_in_dim(low_table, (z ^ (m // 2)) * words, words, 0)
-        near_table.append(part if m == 0 else swap(part, "dp", m))
-    near_table = jnp.concatenate(near_table, axis=1)
-    far_table = swap(after(near_table, own_two), "dp", 1)
+    z_groups = [[2 * i + b for i in range(reach)] for b in range(2)]
+    low_table = after(table.astype(lowp), steps_two[0]).reshape(reach, words, width)
+    low_table = lax.all_to_all(low_table, "dp", 0, 0, axis_index_groups=z_groups)
     slots = -(-words // 256) * 256
 
-    own_half, far_half = split(table_rows_all, 0, 2)
-    looked_far = swap(lookup(far_half, table), "head", 1)
-    looked = (lookup(after(own_half, steps_one[0]), table) + looked_far).reshape(2, -1, width)
+    looked = (looked_own + swap(looked_far, "head", 1)).reshape(2, -1, width)
     looked = looked[0] + swap(looked[1], "head", 2)
     looked = lax.all_to_all(looked.reshape(dp_size, half, width), "dp", 0, 0)
-    embedded_low, normed = place_embedding(place, after(looked, steps_two[0]), gain_vals[0])
+    embedded_low, normed = place_embedding(place, looked, gain_vals[0])
     embedded = embedded_low.astype(single)
 
-    mem_normed = state_norm(place, gain_vals[0], memory, 1)[0]
-    old_normed = state_norm(after(place, steps_one[1]), gain_vals[0], old_states, RATE)
     comp_counts = jnp.where(x == 1, jnp.flip(comp_fill), comp_fill)
     mem_counts = jnp.where(x == 1, jnp.flip(mem_fill), mem_fill)
     info = jnp.stack([comp_counts[0], mem_counts[0], comp_counts[1], mem_counts[1], c * half])
     info = info.astype(jnp.int32)
 
-    def core_sum(part):
-        rows = part.shape[0] // 2
-        more = swap(part[rows:].astype(lowp), "head", 1)
-        return part[:rows].astype(single) + more.astype(single)
-
-    def core_both(part):
-        return jnp.concatenate([part, swap(part, "head", 1)], axis=0)
+    def core_sum(keep, send):
+        more = swap(send.astype(lowp), "head", 1)
+        return keep.astype(single) + more.astype(single)
 
     def group_sum(part, beside=()):
-        part = core_sum(part)
-        rows = part.shape[0] // 2
-        more = swap(part[rows:].astype(lowp), "head", 2)
-        more, *beside = together(more, *beside)
-        part = part[:rows] + more.astype(single)
+        keep, send = split(part, 0, 2) if not isinstance(part, (tuple, list)) else part
+        keep, send = split(core_sum(keep, send), 0, 2)
+        more, *beside = together(swap(send.astype(lowp), "head", 2), *beside)
+        part = keep + more.astype(single)
         return (part, beside) if beside else part
 
     def group_both(part, beside=()):
         far, *beside = together(swap(part, "head", 2), *beside)
-        both = core_both(jnp.concatenate([part, far], axis=0))
+        pair = jnp.concatenate([part, far], axis=0)
+        both = (pair, swap(pair, "head", 1))
         return (both, beside) if beside else both
 
-    normed = group_both(normed)
+    normed = jnp.concatenate(group_both(normed))
     in_weight = own_one[: 3 * wide]
     comp, old_raw = compress(old_normed, own_one, full_conv)
     mem = mm(mem_normed, own_one[wide : 3 * wide], NT).astype(lowp)
     seg = mm(normed, in_weight, NT).astype(lowp).reshape(2, streams, half, 3 * wide)
     mixed, lse = attend(info, after(seg, steps_two[1]), comp, mem)
-    mixed = mixed.reshape(-1, wide)
-    attn_sum, (full_up, full_down) = group_sum(
-        mm(mixed, own_one[3 * wide : 4 * wide]), split(own_two, 0, 2)
+    mixed, low_parts = together(mixed.reshape(-1, wide), low_table)
+    near_table = [
+        lax.dynamic_index_in_dim(low_parts, z ^ (m // 2), 0, keepdims=False) for m in order[:reach]
+    ]
+    near_table = jnp.concatenate(near_table, axis=1)
+    full_up, full_down = split(own_two, 0, 2)
+    attn_sum, (full_up, full_down, near_table) = group_sum(
+        mm(mixed, own_one[3 * wide : 4 * wide]), (full_up, full_down, near_table)
     )
+    far_table = swap(near_table, "dp", 1)
+    loss_table = jnp.concatenate([near_table, far_table], axis=1)
+    loss_table = jnp.concatenate([loss_table, jnp.zeros((slots - words, D), lowp)], axis=0)
     after_attn = embedded + attn_sum
     ffn_in, inv_second = rms(after_attn, gain_vals[1])
-    ffn_in, (near_table,) = group_both(ffn_in, (near_table,))
+    ffn_in = jnp.concatenate(group_both(ffn_in))
     hidden_pre = mm(ffn_in, full_up, NT)
     hidden_act = jax.nn.gelu(hidden_pre).astype(lowp)
-    ffn_sum, (far_table,) = group_sum(mm(hidden_act, full_down), (far_table,))
+    ffn_sum, (loss_table,) = group_sum(mm(hidden_act, full_down), (loss_table,))
     after_ffn = after_attn + ffn_sum
-    loss_table = jnp.concatenate([near_table, far_table], axis=1)
-    loss_table = jnp.concatenate([loss_table, jnp.zeros((slots - words, D), lowp)], axis=0)
     final_in, inv_third = rms(after_ffn, gain_vals[2])
 
     word_start = (h * vocab + z * words).astype(single)
@@ -994,7 +1030,7 @@
         else:
             chunk, (stats[i - 2],) = group_both(pieces[i], (stats[i - 2],))
             chunks.append(chunk)
-        out, stat = logits_part(words, info_all[i], chunks[i], loss_table)
+        out, stat = logits_part(words, info_all[i], *chunks[i], loss_table)
         raised.append(out)
         stats.append(stat)
 
@@ -1039,11 +1075,9 @@
     dlogits = [None] * reach
     parts = [None] * reach
     for i in reversed(range(reach)):
-        factor = factor_all[i]
-        if i + 2 < reach:
-            factor = after(factor, parts[i + 2])
-        dlogits[i], part = logits_back(info_all[i], factor, raised[i], loss_table)
+        dlogits[i], *part = logits_back(info_all[i], factor_all[i], raised[i], loss_table)
         parts[i] = group_sum(part)
+    dlogits[0] = after(dlogits[0], parts[min(1, reach - 1)])
     table_parts = table_grad_part(dlogits, chunks)
     mask = 2
     while len(parts) > 1:
@@ -1061,46 +1095,30 @@
     moved_table = swap(send, "dp", 1)
 
     grad_after_ffn = rms_back(after_ffn, inv_third, gain_vals[2], final_grad)
-    down_in = group_both(grad_after_ffn.astype(lowp))
+    down_in, (moved_table,) = group_both(grad_after_ffn.astype(lowp), (moved_table,))
+    down_in = jnp.concatenate(down_in)
     act_grad = mm(down_in, full_down, NT)
     pre_grad = jax.vjp(jax.nn.gelu, hidden_pre)[1](act_grad)[0].astype(lowp)
     two = hidden_grads(pre_grad, hidden_act, ffn_in, down_in)
-    ffn_in_grad, (*two, moved_table) = group_sum(mm(pre_grad, full_up), (*two, moved_table))
+    ffn_in_grad, two = group_sum(mm(pre_grad, full_up), two)
     two_moved = swap(two[1], "dp", 1)
     keep = keep + moved_table.astype(single)
-    table_pieces = split(keep[:words], 1, reach)
-    for i in range(1, reach):
-        table_pieces[i] = swap(table_pieces[i].astype(lowp), "dp", order[i])
+    table_pieces = jnp.stack(split(keep[:words].astype(lowp), 1, reach))
+    position = [order.index(2 * i) for i in range(reach)]
+    position = jnp.asarray(position, jnp.int32)[jnp.arange(reach) ^ z]
+    table_pieces = jnp.concatenate(
+        [lax.dynamic_index_in_dim(table_pieces, position[i], 0) for i in range(reach)]
+    )
+    table_pieces = lax.all_to_all(table_pieces, "dp", 0, 0, axis_index_groups=z_groups)
     grad_after_attn = grad_after_ffn + rms_back(after_attn, inv_second, gain_vals[1], ffn_in_grad)
-    attn_in = group_both(grad_after_attn.astype(lowp))
+    attn_in = jnp.concatenate(group_both(grad_after_attn.astype(lowp)))
 
     mixed_grad = mm(attn_in, own_one[3 * wide : 4 * wide], NT).astype(lowp)
     mixed_grad = mixed_grad.reshape(2, streams, half, wide)
     seg_grad, comp_grad, mem_grad = attend_back(info, seg, comp, mem, lse, mixed_grad)
-    seg_grad = seg_grad.reshape(-1, 3 * wide)
-    seg_in = core_sum(mm(seg_grad, in_weight))
+    seg_grad, table_pieces = together(seg_grad.reshape(-1, 3 * wide), table_pieces)
+    seg_in = core_sum(*split(mm(seg_grad, in_weight), 0, 2))
     seg_in_far = swap(seg_in[half:].astype(lowp), "head", 2)
-    seg_in_far, two_moved, *table_pieces = together(seg_in_far, two_moved, *table_pieces)
-    table_base = jnp.zeros((vocab, width), single)
-    for m, part in zip(order[:reach], table_pieces):
-        part = part.astype(single)
-        table_base = lax.dynamic_update_slice_in_dim(table_base, part, (z ^ (m // 2)) * words, 0)
-    rows_grad = embed_back(
-        place,
-        embedded_low,
-        gain_vals[0],
-        seg_in[:half],
-        seg_in_far,
-        grad_after_attn,
-    )
-    rows_grad = lax.all_to_all(rows_grad, "dp", 0, 0)
-    rows_grad = jnp.stack([rows_grad, swap(rows_grad, "head", 2)])
-    rows_grad = jnp.stack([rows_grad, swap(rows_grad, "head", 1)]).reshape(-1, width)
-
-    two = two[0] + two_moved.astype(single)
-    two = reduce_blocks(*split(two, 1, 2), 2)
-    up_grad = two[:hidden_own].T
-    down_grad = two[hidden_own:]
     old_grad, conv_sum = expand(comp_grad, old_raw, full_conv)
     one = attn_grads(
         seg_grad,
@@ -1112,6 +1130,27 @@
         mem_normed,
         old_normed.reshape(-1, D),
     )
+    seg_in_far, two_moved, *one = together(seg_in_far, two_moved, *one)
+    table_base = table_pieces.astype(single).reshape(vocab, width)
+    rows_grad = embed_back(
+        place,
+        embedded_low,
+        gain_vals[0],
+        seg_in[:half],
+        seg_in_far,
+        grad_after_attn,
+    )
+    rows_grad = lax.all_to_all(rows_grad, "dp", 0, 0)
+    two = two[0] + two_moved.astype(single)
+    two_keep, two_send = split(two, 1, 2)
+    two_send, rows_grad = together(swap(two_send.astype(lowp), "dp", 2), rows_grad)
+    two = two_keep + two_send.astype(single)
+    rows_grad = jnp.stack([rows_grad, swap(rows_grad, "head", 2)])
+    rows_grad = jnp.stack([rows_grad, swap(rows_grad, "head", 1)]).reshape(-1, width)
+
+    two = reduce_blocks(*split(two, 1, 2), 4)
+    up_grad = two[:hidden_own].T
+    down_grad = two[hidden_own:]
     conv_sum = split(conv_block_order(conv_sum), 1, 2)
     one = [jnp.concatenate([part, more.astype(part.dtype)]) for part, more in zip(one, conv_sum)]
     one = reduce_blocks(*one)
@@ -1204,7 +1243,7 @@
     gain_dir = gain_scaled * lax.rsqrt(second_new)
     for which in range(3):
         update_sq.append(jnp.sum(gain_dir[which] * gain_dir[which]) / head_size)
-    update_total = scalar_row(update_sq, 1024)
+    update_total = after(scalar_row(update_sq, 1024), loss_all)
     for mask in (1, 2):
         update_total = update_total + swap(update_total, "head", mask)
     update_total = sum_over_dp(update_total)[:9]

time: 958 us -> 923 us (0.963)
  waiting for transfers between devices: 306 us -> 276 us
    ppermute x75 -> x69, waiting for transfers between devices: 302 us -> 257 us  [swap(): return lax.ppermute(value, axis, [(i, i ^ mask) for i in range(size)])]
    all_to_all x1, waiting for transfers between devices: 0.79 us -> 16.1 us  [local(): rows_grad = lax.all_to_all(rows_grad, 'dp', 0, 0)]
    ppermute x75 -> x69, starting transfers between devices: 81.3 us -> 67.1 us  [swap(): return lax.ppermute(value, axis, [(i, i ^ mask) for i in range(size)])]
    slice x17 -> x3, local copies, waits for them, and re-layouts: 10.5 us -> 0.62 us  [the longest x1 0.6 us: local(): position[i]]
    all_to_all x0 -> x2, starting transfers between devices: none -> 9.84 us  [the longest x1 4.99 us: local(): lax.all_to_all(low_table, 'dp', 0, 0, axis_index_groups=z_groups)]
    concatenate x17 -> x16, other arithmetic: 30.7 us -> 25.1 us  [the longest x7 10.3 us: group_both(): pair = jnp.concatenate([part, far], axis=0)]
    unnamed x300 -> x309, local copies, waits for them, and re-layouts: 33.8 us -> 29.2 us
  transfers between devices with their start and end apart: 77 -> 73, of which waited for: 42 -> 42; matrix products, arithmetic and copies ran while one was open for 19% -> 18% of each run, Pallas kernels for 22% -> 24%
where the time goes in v5:
time: 923 us; the launch traced here: 915 us
  waiting for transfers between devices  276 us (30%)
  Pallas kernels  255 us (28%)
  other arithmetic  145 us (16%)
  starting transfers between devices  84.4 us (9%)
  local copies, waits for them, and re-layouts  77.8 us (8%)
  between operations  33.8 us (4%)
  matrix products  33.7 us (4%)
  blocking collectives  9.85 us (1%)
    ppermute x69, waiting for transfers between devices, swap(): return lax.ppermute(value, axis, [(i, i ^ mask) for i in range(size)])  257 us
    ppermute x69, starting transfers between devices, swap(): return lax.ppermute(value, axis, [(i, i ^ mask) for i in range(size)])  67.1 us
    pallas_call x4, Pallas kernels, logits_back(): pl.pallas_call(functools.partial(logits_back_kernel, tiles), name='logits...  44.4 us
    pallas_call x4, Pallas kernels, logits_part(): pl.pallas_call(functools.partial(logits_kernel, words, tiles), name='logi...  44.2 us
    dot_general x11, matrix products, mm(): return lax.dot_general(left, right, dims, preferred_element_type=single)  33.7 us
    unnamed x309, local copies, waits for them, and re-layouts  29.2 us
    pallas_call x1, Pallas kernels, table_grad_part(): pl.pallas_call(functools.partial(table_grad_kernel, count), name='table_g...  24.1 us
    pallas_call x1, Pallas kernels, own_list(): pl.pallas_call(list_kernel, name='own_list', out_shape=(jax.ShapeDtypeStr...  21.4 us
  transfers between devices with their start and end apart: 73, of which 42 were waited for; matrix products, arithmetic and copies ran while one was open for 18% of the time, Pallas kernels for 24%

profile of v5, /device:TPU:0, one launch (start us, length us, event | category | flops | bytes accessed | tf_op | source)
XLA Modules:
  0.0 915.0 jit_solution(7912705514690689863)
XLA Ops:
  33.2 8.8 lookup.3
  49.5 11.2 %collective-permute-done.5 = bf16[2048,128]{1,0:T(8,128)(2,1)S(1)} collective-permute-done((bf16[2048,128]{1,0:T(8,128)(2,1)S(1)}, bf16[2048,128]{1,0:T(8,128)(2,1)S(1)}, u32[]{:S(2)}, u32[]{:S(2)}) %collective-permute-start.5) | collective-permute-done | bytes 524320 | tf_op jit(solution)/shard_map/ppermute | solution.py:38
  112.7 9.9 %state_norm.3.old_ref = bf16[3,1024,1024]{2,1,0:T(8,128)(2,1)} custom-call(s32[2]{0:T(128)} %pad_add_fusion.place_ref, f32[1,1024]{1,0:T(1,128)} %bitcast.349, bf16[2,1536,1024]{2,1,0:T(8,128)(2,1)} %in_ref.3), custom_call_target="tpu_custom_call" | custom-call | bytes 251658 | tf_op jit(solution)/shard_map/state_norm/pallas_call | solution.py:325
  122.6 17.8 %collective-permute-done.11 = bf16[2048,256]{1,0:T(8,128)(2,1)} collective-permute-done((bf16[2048,256]{1,0:T(8,128)(2,1)}, bf16[2048,256]{1,0:T(8,128)(2,1)}, u32[]{:S(2)}, u32[]{:S(2)}) %collective-permute-start.11) | collective-permute-done | bytes 1048608 | tf_op jit(solution)/shard_map/ppermute | solution.py:38
  152.1 12.2 %compress.1 = (bf16[1024,512]{1,0:T(8,128)(2,1)}, bf16[3,1024,512]{2,1,0:T(8,128)(2,1)}) custom-call(bf16[3,1024,1024]{2,1,0:T(8,128)(2,1)} %state_norm.3.old_ref, bf16[1120,1024]{1,0:T(8,128)(2,1)} %copy-done.4, bf16[1120,1024]{1,0:T(8,128)(2,1)} %copy-done.4, bf16[2,384,128]{2,1,0:T(8,128)(2,1)} %bitcast.317), custom_call_target="tpu_custom_call" | custom-call | flops 64424508 | bytes 251658 | tf_op jit(solution)/shard_map/compress/pallas_call | solution.py:367
  172.5 11.0 %attend.1 = (bf16[2,2,256,256]{3,2,1,0:T(8,128)(2,1)}, f32[2,2,512,1]{3,2,1,0:T(8,128)}) custom-call(s32[5]{0:T(128)} %stack.103.info_ref, bf16[2,2,256,768]{3,2,1,0:T(8,128)(2,1)} %bitcast.302, bf16[2,2,256,768]{3,2,1,0:T(8,128)(2,1)} %bitcast.303, bf16[2,2,256,768]{3,2,1,0:T(8,128)(2,1)} %bitcast.304, bf16[1024,512]{1,0:T(8,128)(2,1)} %get-tuple-element.125.kc_ref.vc_ref, ...), custom_call_target="tpu_custom_call" | custom-call | flops 146800640 | bytes 125829 | tf_op jit(solution)/shard_map/attend/pallas_call | solution.py:519
  200.3 10.5 %collective-permute-done.13 = bf16[256,1024]{1,0:T(8,128)(2,1)S(1)} collective-permute-done((bf16[256,1024]{1,0:T(8,128)(2,1)S(1)}, bf16[256,1024]{1,0:T(8,128)(2,1)S(1)}, u32[]{:S(2)}, u32[]{:S(2)}) %collective-permute-start.13) | collective-permute-done | bytes 524320 | tf_op jit(solution)/shard_map/ppermute | solution.py:38
  211.9 11.4 %collective-permute-done.15 = bf16[256,1024]{1,0:T(8,128)(2,1)S(1)} collective-permute-done((bf16[256,1024]{1,0:T(8,128)(2,1)S(1)}, bf16[256,1024]{1,0:T(8,128)(2,1)S(1)}, u32[]{:S(2)}, u32[]{:S(2)}) %collective-permute-start.15) | collective-permute-done | bytes 524320 | tf_op jit(solution)/shard_map/ppermute | solution.py:38
  239.3 31.1 %collective-permute-done.19 = bf16[2000,512]{1,0:T(8,128)(2,1)S(1)} collective-permute-done((bf16[2000,512]{1,0:T(8,128)(2,1)S(1)}, bf16[2000,512]{1,0:T(8,128)(2,1)S(1)}, u32[]{:S(2)}, u32[]{:S(2)}) %collective-permute-start.19) | collective-permute-done | bytes 2048032 | tf_op jit(solution)/shard_map/ppermute | solution.py:38
  295.0 21.4 %own_list.1 = (s32[8200]{0:T(1024)}, s32[1]{0:T(128)}) custom-call(s32[8192]{0:T(1024)} %get-tuple-element.136.code_ref), custom_call_target="tpu_custom_call" | custom-call | bytes 1258291 | tf_op jit(solution)/shard_map/own_list/pallas_call | solution.py:181
  318.6 11.2 %collective-permute-done.26 = bf16[256,1024]{1,0:T(8,128)(2,1)} collective-permute-done((bf16[256,1024]{1,0:T(8,128)(2,1)S(1)}, bf16[256,1024]{1,0:T(8,128)(2,1)}, u32[]{:S(2)}, u32[]{:S(2)}) %collective-permute-start.26) | collective-permute-done | bytes 524320 | tf_op jit(solution)/shard_map/ppermute | solution.py:38
  337.0 11.3 %logits_part.4 = (bf16[1024,2048]{1,0:T(8,128)(2,1)}, f32[8,1024]{1,0:T(8,128)}) custom-call(f32[8,1024]{1,0:T(8,128)} %squeeze.166.info_ref, bf16[512,1024]{1,0:T(8,128)(2,1)} %get-tuple-element.411.pair_ref.refs_4_, bf16[512,1024]{1,0:T(8,128)(2,1)} %collective-permute-done.23.near_ref.refs_5_, bf16[2048,1024]{1,0:T(8,128)(2,1)} %fusion.9.table_ref), custom_call_target="tpu_custom_call" | custom-call | flops 171798688 | bytes 209715 | tf_op jit(solution)/shard_map/logits_part/pallas_call | solution.py:601
  361.9 10.9 %logits_part.5 = (bf16[1024,2048]{1,0:T(8,128)(2,1)}, f32[8,1024]{1,0:T(8,128)}) custom-call(f32[8,1024]{1,0:T(8,128)} %squeeze.176.info_ref, bf16[512,1024]{1,0:T(8,128)(2,1)} %copy-done.11, bf16[512,1024]{1,0:T(8,128)(2,1)} %collective-permute-done.27.near_ref.refs_7_, bf16[2048,1024]{1,0:T(8,128)(2,1)} %fusion.9.table_ref), custom_call_target="tpu_custom_call" | custom-call | flops 171798688 | bytes 209715 | tf_op jit(solution)/shard_map/logits_part/pallas_call | solution.py:601
  385.8 11.0 %logits_part.7 = (bf16[1024,2048]{1,0:T(8,128)(2,1)}, f32[8,1024]{1,0:T(8,128)}) custom-call(f32[8,1024]{1,0:T(8,128)} %squeeze.178.info_ref, bf16[512,1024]{1,0:T(8,128)(2,1)} %copy-done.10, bf16[512,1024]{1,0:T(8,128)(2,1)} %collective-permute-done.29.near_ref.refs_11_, bf16[2048,1024]{1,0:T(8,128)(2,1)} %fusion.9.table_ref), custom_call_target="tpu_custom_call" | custom-call | flops 171798688 | bytes 209715 | tf_op jit(solution)/shard_map/logits_part/pallas_call | solution.py:601
  397.6 11.0 %logits_part.6 = (bf16[1024,2048]{1,0:T(8,128)(2,1)}, f32[8,1024]{1,0:T(8,128)}) custom-call(f32[8,1024]{1,0:T(8,128)} %squeeze.177.info_ref, bf16[512,1024]{1,0:T(8,128)(2,1)} %pad_maximum_fusion.15.pair_ref.refs_8_, bf16[512,1024]{1,0:T(8,128)(2,1)} %collective-permute-done.28.near_ref.refs_9_, bf16[2048,1024]{1,0:T(8,128)(2,1)} %fusion.9.table_ref), custom_call_target="tpu_custom_call" | custom-call | flops 171798688 | bytes 209715 | tf_op jit(solution)/shard_map/logits_part/pallas_call | solution.py:601
  426.2 11.1 %logits_back.6 = (bf16[1024,2048]{1,0:T(8,128)(2,1)}, bf16[512,1024]{1,0:T(8,128)(2,1)}, bf16[512,1024]{1,0:T(8,128)(2,1)}) custom-call(f32[8,1024]{1,0:T(8,128)} %squeeze.178.info_ref, f32[8,1024]{1,0:T(8,128)} %broadcast_in_dim.192.factor_ref, bf16[1024,2048]{1,0:T(8,128)(2,1)} %get-tuple-element.157.in_ref, bf16[2048,1024]{1,0:T(8,128)(2,1)} %fusion.9.table_ref), custom_call_target="tpu_custom_call" | custom-call | flops 171798688 | bytes 251658 | tf_op jit(solution)/shard_map/logits_back/pallas_call | solution.py:654
  437.9 11.3 %logits_back.5 = (bf16[1024,2048]{1,0:T(8,128)(2,1)}, bf16[512,1024]{1,0:T(8,128)(2,1)}, bf16[512,1024]{1,0:T(8,128)(2,1)}) custom-call(f32[8,1024]{1,0:T(8,128)} %squeeze.177.info_ref, f32[8,1024]{1,0:T(8,128)} %broadcast_in_dim.190.factor_ref, bf16[1024,2048]{1,0:T(8,128)(2,1)} %get-tuple-element.154.in_ref, bf16[2048,1024]{1,0:T(8,128)(2,1)} %fusion.9.table_ref), custom_call_target="tpu_custom_call" | custom-call | flops 171798688 | bytes 251658 | tf_op jit(solution)/shard_map/logits_back/pallas_call | solution.py:654
  456.5 11.0 %logits_back.7 = (bf16[1024,2048]{1,0:T(8,128)(2,1)}, bf16[512,1024]{1,0:T(8,128)(2,1)}, bf16[512,1024]{1,0:T(8,128)(2,1)}) custom-call(f32[8,1024]{1,0:T(8,128)} %squeeze.176.info_ref, f32[8,1024]{1,0:T(8,128)} %broadcast_in_dim.194.factor_ref, bf16[1024,2048]{1,0:T(8,128)(2,1)} %get-tuple-element.161.in_ref, bf16[2048,1024]{1,0:T(8,128)(2,1)} %fusion.9.table_ref), custom_call_target="tpu_custom_call" | custom-call | flops 171798688 | bytes 251658 | tf_op jit(solution)/shard_map/logits_back/pallas_call | solution.py:654
  468.1 11.0 %logits_back.4 = (bf16[1024,2048]{1,0:T(8,128)(2,1)}, bf16[512,1024]{1,0:T(8,128)(2,1)}, bf16[512,1024]{1,0:T(8,128)(2,1)}) custom-call(f32[8,1024]{1,0:T(8,128)} %squeeze.166.info_ref, f32[8,1024]{1,0:T(8,128)} %broadcast_in_dim.188.factor_ref, bf16[1024,2048]{1,0:T(8,128)(2,1)} %get-tuple-element.151.in_ref, bf16[2048,1024]{1,0:T(8,128)(2,1)} %fusion.9.table_ref), custom_call_target="tpu_custom_call" | custom-call | flops 171798688 | bytes 251658 | tf_op jit(solution)/shard_map/logits_back/pallas_call | solution.py:654
  489.1 10.1 %collective-permute-done.42 = bf16[256,1024]{1,0:T(8,128)(2,1)S(1)} collective-permute-done((bf16[256,1024]{1,0:T(8,128)(2,1)S(1)}, bf16[256,1024]{1,0:T(8,128)(2,1)S(1)}, u32[]{:S(2)}, u32[]{:S(2)}) %collective-permute-start.42) | collective-permute-done | bytes 524320 | tf_op jit(solution)/shard_map/ppermute | solution.py:38
  499.3 24.1 %table_grad_part.1 = (f32[2048,512]{1,0:T(8,128)}, bf16[2048,512]{1,0:T(8,128)(2,1)}) custom-call(bf16[1024,2048]{1,0:T(8,128)(2,1)} %get-tuple-element.164.refs_0_, bf16[1024,2048]{1,0:T(8,128)(2,1)} %get-tuple-element.165.refs_1_, bf16[1024,2048]{1,0:T(8,128)(2,1)} %get-tuple-element.166.refs_2_, bf16[1024,2048]{1,0:T(8,128)(2,1)} %get-tuple-element.167.refs_3_, ...), custom_call_target="tpu_custom_call" | custom-call | flops 515396064 | bytes 629145 | tf_op jit(solution)/shard_map/table_grad_part/pallas_call | solution.py:705
  529.4 23.0 %collective-permute-done.43 = bf16[256,1024]{1,0:T(8,128)(2,1)S(1)} collective-permute-done((bf16[256,1024]{1,0:T(8,128)(2,1)S(1)}, bf16[256,1024]{1,0:T(8,128)(2,1)S(1)}, u32[]{:S(2)}, u32[]{:S(2)}) %collective-permute-start.43) | collective-permute-done | bytes 524320 | tf_op jit(solution)/shard_map/ppermute | solution.py:38
  554.4 11.9 %collective-permute-done.44 = bf16[256,1024]{1,0:T(8,128)(2,1)S(1)} collective-permute-done((bf16[256,1024]{1,0:T(8,128)(2,1)S(1)}, bf16[256,1024]{1,0:T(8,128)(2,1)S(1)}, u32[]{:S(2)}, u32[]{:S(2)}) %collective-permute-start.44) | collective-permute-done | bytes 524320 | tf_op jit(solution)/shard_map/ppermute | solution.py:38
  615.5 11.4 %hidden_grads.1 = (f32[2048,512]{1,0:T(8,128)}, bf16[2048,512]{1,0:T(8,128)(2,1)}) custom-call(bf16[1024,1024]{1,0:T(8,128)(2,1)} %copy-done.45, bf16[1024,1024]{1,0:T(8,128)(2,1)} %copy-done.42, bf16[1024,1024]{1,0:T(8,128)(2,1)} %pad_maximum_fusion.2.in_ref, bf16[1024,1024]{1,0:T(8,128)(2,1)} %pad_maximum_fusion.3.down_ref), custom_call_target="tpu_custom_call" | custom-call | flops 128849016 | bytes 335544 | tf_op jit(solution)/shard_map/hidden_grads/pallas_call | solution.py:740
  632.2 13.1 %collective-permute-done.49 = bf16[256,1024]{1,0:T(8,128)(2,1)S(1)} collective-permute-done((bf16[256,1024]{1,0:T(8,128)(2,1)S(1)}, bf16[256,1024]{1,0:T(8,128)(2,1)S(1)}, u32[]{:S(2)}, u32[]{:S(2)}) %collective-permute-start.49) | collective-permute-done | bytes 524320 | tf_op jit(solution)/shard_map/ppermute | solution.py:38
  656.1 15.2 %attend_back.1 = (bf16[2,2,256,768]{3,2,1,0:T(8,128)(2,1)}, bf16[1024,512]{1,0:T(8,128)(2,1)}, bf16[1024,512]{1,0:T(8,128)(2,1)}) custom-call(s32[5]{0:T(128)} %stack.103.info_ref, bf16[2,2,256,768]{3,2,1,0:T(8,128)(2,1)} %bitcast.305, bf16[2,2,256,768]{3,2,1,0:T(8,128)(2,1)} %bitcast.306, bf16[2,2,256,768]{3,2,1,0:T(8,128)(2,1)} %bitcast.307, ...), custom_call_target="tpu_custom_call" | custom-call | flops 230686720 | bytes 188743 | tf_op jit(solution)/shard_map/attend_back/pallas_call | solution.py:542
  697.5 14.2 %attn_grads.1 = (f32[1024,512]{1,0:T(8,128)}, bf16[1024,512]{1,0:T(8,128)(2,1)}) custom-call(bf16[1024,768]{1,0:T(8,128)(2,1)} %bitcast.320, bf16[1024,256]{1,0:T(8,128)(2,1)} %bitcast.314, bf16[1024,512]{1,0:T(8,128)(2,1)} %get-tuple-element.183.mem_ref, bf16[3072,512]{1,0:T(8,128)(2,1)} %bitcast.315, bf16[1024,1024]{1,0:T(8,128)(2,1)} %pad_maximum_fusion.1.normed_ref, ...), custom_call_target="tpu_custom_call" | custom-call | flops 188743680 | bytes 503316 | tf_op jit(solution)/shard_map/attn_grads/pallas_call | solution.py:790
  738.5 16.1 %all-to-all-done.3 = bf16[8,256,128]{2,1,0:T(8,128)(2,1)S(1)} async-done(((bf16[8,256,128]{2,1,0:T(8,128)(2,1)}), bf16[8,256,128]{2,1,0:T(8,128)(2,1)S(1)}, u32[]{:S(2)}, u32[]{:S(2)}) %all-to-all-start.3) | async-done | bytes 524320 | tf_op jit(solution)/shard_map/all_to_all | solution.py:1143
  771.8 9.2 %collective-permute-done.55 = bf16[2048,128]{1,0:T(8,128)(2,1)S(1)} collective-permute-done((bf16[2048,128]{1,0:T(8,128)(2,1)S(1)}, bf16[2048,128]{1,0:T(8,128)(2,1)S(1)}, u32[]{:S(2)}, u32[]{:S(2)}) %collective-permute-start.55) | collective-permute-done | bytes 524320 | tf_op jit(solution)/shard_map/ppermute | solution.py:38
  790.2 11.0 %collective-permute-done.58 = bf16[1120,128]{1,0:T(8,128)(2,1)S(1)} collective-permute-done((bf16[1120,128]{1,0:T(8,128)(2,1)S(1)}, bf16[1120,128]{1,0:T(8,128)(2,1)S(1)}, u32[]{:S(2)}, u32[]{:S(2)}) %collective-permute-start.58) | collective-permute-done | bytes 286752 | tf_op jit(solution)/shard_map/ppermute | solution.py:38
  807.8 11.4 %scatter.1 = f32[8000,128]{1,0:T(8,128)} custom-call(s32[1]{0:T(128)} %get-tuple-element.195.count_ref, s32[8200]{0:T(1024)} %get-tuple-element.196.code_ref, f32[8000,128]{1,0:T(8,128)} %bitcast_convert_fusion.base_ref, bf16[8192,128]{1,0:T(8,128)(2,1)} %bitcast.310), custom_call_target="tpu_custom_call" | custom-call | bytes 629145 | tf_op jit(solution)/shard_map/scatter/pallas_call | solution.py:277
  822.7 9.9 %all-reduce.1 = (f32[128]{0:T(128)S(1)}, f32[3,128]{1,0:T(4,128)S(1)}, f32[128]{0:T(128)S(1)}, f32[16]{0:T(128)S(1)}, f32[128]{0:T(128)S(1)}, /*index=5*/f32[128...) all-reduce(f32[128]{0:T(128)S(1)} %get-tuple-element.318, ...), channel_id=1, replica_groups=mesh['dp'=8,'head'=4] {'head'}, use_global_device_ids=true, to_apply=%region_23.24 | all-reduce | flops 1424 | bytes 11392 | tf_op jit(solution)/shard_map/psum | solution.py:1185
  (728 shorter events, 455.5 us)
Async XLA Ops:
  19.2 22.8 %collective-permute-start.3 = (bf16[1120,128]{1,0:T(8,128)(2,1)S(1)}, bf16[1120,128]{1,0:T(8,128)(2,1)S(1)}, u32[]{:S(2)}, u32[]{:S(2)}) collective-permute-start(bf16[1120,128]{1,0:T(8,128)(2,1)S(1)} %pad_maximum_fusion.21), channel_id=1, source_target_pairs={{0,16},{4,20},{8,24},{12,28},{16,0},{20,4},{24,8},{28,12},{1,17},{... | collective-permute-start | bytes 860168 | tf_op jit(solution)/shard_map/ppermute | solution.py:38
  49.2 32.6 %collective-permute-start.10 = (bf16[2048,128]{1,0:T(8,128)(2,1)S(1)}, bf16[2048,128]{1,0:T(8,128)(2,1)S(1)}, u32[]{:S(2)}, u32[]{:S(2)}) collective-permute-start(bf16[2048,128]{1,0:T(8,128)(2,1)S(1)} %pad_maximum_fusion.20), channel_id=1, source_target_pairs={{0,16},{4,20},{8,24},{12,28},{16,0},{20,4},{24,8},{28,12},{1,17},{... | collective-permute-start | bytes 1572872 | tf_op jit(solution)/shard_map/ppermute | solution.py:38
  61.6 24.8 %all-to-all-start = ((bf16[8,256,128]{2,1,0:T(8,128)(2,1)}), bf16[8,256,128]{2,1,0:T(8,128)(2,1)S(1)}, u32[]{:S(2)}, u32[]{:S(2)}) async-start(bf16[8,256,128]{2,1,0:T(8,128)(2,1)} %bitcast.22), calls=%async_computation | async-start | bytes 1048576 | tf_op jit(solution)/shard_map/all_to_all | solution.py:963
  71.9 23.9 %collective-permute-start.8 = (bf16[1120,256]{1,0:T(8,128)(2,1)}, bf16[1120,256]{1,0:T(8,128)(2,1)S(1)}, u32[]{:S(2)}, u32[]{:S(2)}) collective-permute-start(bf16[1120,256]{1,0:T(8,128)(2,1)} %copy-done.71), channel_id=1, source_target_pairs={{0,8},{4,12},{8,0},{12,4},{16,24},{20,28},{24,16},{28,20},{1,9},{5... | collective-permute-start | bytes 1720328 | tf_op jit(solution)/shard_map/ppermute | solution.py:38
  82.9 57.5 %collective-permute-start.11 = (bf16[2048,256]{1,0:T(8,128)(2,1)}, bf16[2048,256]{1,0:T(8,128)(2,1)}, u32[]{:S(2)}, u32[]{:S(2)}) collective-permute-start(bf16[2048,256]{1,0:T(8,128)(2,1)} %get-tuple-element.416), channel_id=1, source_target_pairs={{0,8},{4,12},{8,0},{12,4},{16,24},{20,28},{24,16},{28,20},{1,9},{5... | collective-permute-start | bytes 3145736 | tf_op jit(solution)/shard_map/ppermute | solution.py:38
  86.4 97.1 %all-to-all-start.1 = ((bf16[4,2000,128]{2,1,0:T(8,128)(2,1)}), bf16[4,2000,128]{2,1,0:T(8,128)(2,1)}, u32[]{:S(2)}, u32[]{:S(2)}) async-start(bf16[4,2000,128]{2,1,0:T(8,128)(2,1)} %bitcast.36), calls=%async_computation.1 | async-start | bytes 4096000 | tf_op jit(solution)/shard_map/all_to_all | solution.py:958
  96.0 49.8 %collective-permute-start.9 = (bf16[1120,512]{1,0:T(8,128)(2,1)S(1)}, bf16[1120,512]{1,0:T(8,128)(2,1)}, u32[]{:S(2)}, u32[]{:S(2)}) collective-permute-start(bf16[1120,512]{1,0:T(8,128)(2,1)S(1)} %pad_maximum_fusion.10), channel_id=1, source_target_pairs={{0,4},{4,0},{8,12},{12,8},{16,20},{20,16},{24,28},{28,24},{1,5},{5... | collective-permute-start | bytes 3440648 | tf_op jit(solution)/shard_map/ppermute | solution.py:38
  100.9 43.7 %collective-permute-start.6 = (bf16[256,1024]{1,0:T(8,128)(2,1)}, bf16[256,1024]{1,0:T(8,128)(2,1)S(1)}, u32[]{:S(2)}, u32[]{:S(2)}) collective-permute-start(bf16[256,1024]{1,0:T(8,128)(2,1)} %get-tuple-element.119), channel_id=1, source_target_pairs={{0,2},{1,3},{2,0},{3,1},{4,6},{5,7},{6,4},{7,5},{8,10},{9,11},{10,... | collective-permute-start | bytes 1572872 | tf_op jit(solution)/shard_map/ppermute | solution.py:38
  143.1 47.8 %collective-permute-start.14 = (bf16[2048,512]{1,0:T(8,128)(2,1)}, bf16[2048,512]{1,0:T(8,128)(2,1)}, u32[]{:S(2)}, u32[]{:S(2)}) collective-permute-start(bf16[2048,512]{1,0:T(8,128)(2,1)} %get-tuple-element.408), channel_id=1, source_target_pairs={{0,4},{4,0},{8,12},{12,8},{16,20},{20,16},{24,28},{28,24},{1,5},{5... | collective-permute-start | bytes 6291464 | tf_op jit(solution)/shard_map/ppermute | solution.py:38
  145.8 22.5 %collective-permute-start.7 = (bf16[512,1024]{1,0:T(8,128)(2,1)}, bf16[512,1024]{1,0:T(8,128)(2,1)}, u32[]{:S(2)}, u32[]{:S(2)}) collective-permute-start(bf16[512,1024]{1,0:T(8,128)(2,1)} %pad_maximum_fusion.12), channel_id=1, source_target_pairs={{0,1},{1,0},{2,3},{3,2},{4,5},{5,4},{6,7},{7,6},{8,9},{9,8},{10,11... | collective-permute-start | bytes 3145736 | tf_op jit(solution)/shard_map/ppermute | solution.py:38
  223.5 47.0 %collective-permute-start.19 = (bf16[2000,512]{1,0:T(8,128)(2,1)S(1)}, bf16[2000,512]{1,0:T(8,128)(2,1)S(1)}, u32[]{:S(2)}, u32[]{:S(2)}) collective-permute-start(bf16[2000,512]{1,0:T(8,128)(2,1)S(1)} %pad_maximum_fusion.6), channel_id=1, source_target_pairs={{0,4},{4,0},{8,12},{12,8},{16,20},{20,16},{24,28},{28,24},{1,5},{5... | collective-permute-start | bytes 6144008 | tf_op jit(solution)/shard_map/ppermute | solution.py:38
  238.0 36.0 %collective-permute-start.18 = (bf16[256,1024]{1,0:T(8,128)(2,1)S(1)}, bf16[256,1024]{1,0:T(8,128)(2,1)S(1)}, u32[]{:S(2)}, u32[]{:S(2)}) collective-permute-start(bf16[256,1024]{1,0:T(8,128)(2,1)S(1)} %slice.1310), channel_id=1, source_target_pairs={{0,2},{1,3},{2,0},{3,1},{4,6},{5,7},{6,4},{7,5},{8,10},{9,11},{10,... | collective-permute-start | bytes 1572872 | tf_op jit(solution)/shard_map/ppermute | solution.py:38
  279.8 36.6 %collective-permute-start.20 = (bf16[256,1024]{1,0:T(8,128)(2,1)}, bf16[256,1024]{1,0:T(8,128)(2,1)S(1)}, u32[]{:S(2)}, u32[]{:S(2)}) collective-permute-start(bf16[256,1024]{1,0:T(8,128)(2,1)} %slice_dynamic-update-slice_fusion.8), channel_id=1, source_target_pairs={{0,16},{4,20},{8,24},{12,28},{16,0},{20,4},{24,8},{28,12},{1,17},{... | collective-permute-start | bytes 1572872 | tf_op jit(solution)/shard_map/ppermute | solution.py:38
  279.9 38.6 %collective-permute-start.22 = (bf16[256,1024]{1,0:T(8,128)(2,1)S(1)}, bf16[256,1024]{1,0:T(8,128)(2,1)}, u32[]{:S(2)}, u32[]{:S(2)}) collective-permute-start(bf16[256,1024]{1,0:T(8,128)(2,1)S(1)} %multiply_convert_fusion.1), channel_id=1, source_target_pairs={{0,2},{1,3},{2,0},{3,1},{4,6},{5,7},{6,4},{7,5},{8,10},{9,11},{10,... | collective-permute-start | bytes 1572872 | tf_op jit(solution)/shard_map/ppermute | solution.py:38
  333.1 23.9 %collective-permute-start.21 = (bf16[512,1024]{1,0:T(8,128)(2,1)}, bf16[512,1024]{1,0:T(8,128)(2,1)}, u32[]{:S(2)}, u32[]{:S(2)}) collective-permute-start(bf16[512,1024]{1,0:T(8,128)(2,1)} %get-tuple-element.410), channel_id=1, source_target_pairs={{0,8},{4,12},{8,0},{12,4},{16,24},{20,28},{24,16},{28,20},{1,9},{5... | collective-permute-start | bytes 3145736 | tf_op jit(solution)/shard_map/ppermute | solution.py:38
  334.7 27.3 %collective-permute-start.27 = (bf16[512,1024]{1,0:T(8,128)(2,1)S(1)}, bf16[512,1024]{1,0:T(8,128)(2,1)}, u32[]{:S(2)}, u32[]{:S(2)}) collective-permute-start(bf16[512,1024]{1,0:T(8,128)(2,1)S(1)} %get-tuple-element.409.pair_ref.refs_6_), channel_id=1, source_target_pairs={{0,1},{1,0},{2,3},{3,2},{4,5},{5,4},{6,7},{7,6},{8,9},{9,8},{10,11... | collective-permute-start | bytes 3145736 | tf_op jit(solution)/shard_map/ppermute | solution.py:38
  451.6 28.1 %collective-permute-start.39 = (bf16[256,1024]{1,0:T(8,128)(2,1)S(1)}, bf16[256,1024]{1,0:T(8,128)(2,1)}, u32[]{:S(2)}, u32[]{:S(2)}) collective-permute-start(bf16[256,1024]{1,0:T(8,128)(2,1)S(1)} %slice.1307), channel_id=1, source_target_pairs={{0,2},{1,3},{2,0},{3,1},{4,6},{5,7},{6,4},{7,5},{8,10},{9,11},{10,... | collective-permute-start | bytes 1572872 | tf_op jit(solution)/shard_map/ppermute | solution.py:38
  455.1 24.6 %collective-permute-start.37 = (bf16[256,1024]{1,0:T(8,128)(2,1)}, bf16[256,1024]{1,0:T(8,128)(2,1)}, u32[]{:S(2)}, u32[]{:S(2)}) collective-permute-start(bf16[256,1024]{1,0:T(8,128)(2,1)} %slice.1308), channel_id=1, source_target_pairs={{0,2},{1,3},{2,0},{3,1},{4,6},{5,7},{6,4},{7,5},{8,10},{9,11},{10,... | collective-permute-start | bytes 1572872 | tf_op jit(solution)/shard_map/ppermute | solution.py:38
  483.7 39.8 %collective-permute-start.40 = (bf16[512,1024]{1,0:T(8,128)(2,1)}, bf16[512,1024]{1,0:T(8,128)(2,1)}, u32[]{:S(2)}, u32[]{:S(2)}) collective-permute-start(bf16[512,1024]{1,0:T(8,128)(2,1)} %fusion.20), channel_id=1, source_target_pairs={{0,8},{4,12},{8,0},{12,4},{16,24},{20,28},{24,16},{28,20},{1,9},{5... | collective-permute-start | bytes 3145736 | tf_op jit(solution)/shard_map/ppermute | solution.py:38
  488.3 41.1 %collective-permute-start.35 = (bf16[256,1024]{1,0:T(8,128)(2,1)}, bf16[256,1024]{1,0:T(8,128)(2,1)S(1)}, u32[]{:S(2)}, u32[]{:S(2)}) collective-permute-start(bf16[256,1024]{1,0:T(8,128)(2,1)} %slice.1309), channel_id=1, source_target_pairs={{0,2},{1,3},{2,0},{3,1},{4,6},{5,7},{6,4},{7,5},{8,10},{9,11},{10,... | collective-permute-start | bytes 1572872 | tf_op jit(solution)/shard_map/ppermute | solution.py:38
  525.5 46.9 %collective-permute-start.45 = (bf16[2048,512]{1,0:T(8,128)(2,1)S(1)}, bf16[2048,512]{1,0:T(8,128)(2,1)S(1)}, u32[]{:S(2)}, u32[]{:S(2)}) collective-permute-start(bf16[2048,512]{1,0:T(8,128)(2,1)S(1)} %copy-done.136), channel_id=1, source_target_pairs={{0,4},{4,0},{8,12},{12,8},{16,20},{20,16},{24,28},{28,24},{1,5},{5... | collective-permute-start | bytes 6291464 | tf_op jit(solution)/shard_map/ppermute | solution.py:38
  527.4 25.0 %collective-permute-start.43 = (bf16[256,1024]{1,0:T(8,128)(2,1)S(1)}, bf16[256,1024]{1,0:T(8,128)(2,1)S(1)}, u32[]{:S(2)}, u32[]{:S(2)}) collective-permute-start(bf16[256,1024]{1,0:T(8,128)(2,1)S(1)} %slice_dynamic-update-slice_fusion), channel_id=1, source_target_pairs={{0,16},{4,20},{8,24},{12,28},{16,0},{20,4},{24,8},{28,12},{1,17},{... | collective-permute-start | bytes 1572872 | tf_op jit(solution)/shard_map/ppermute | solution.py:38
  601.9 24.9 %collective-permute-start.48 = (bf16[256,1024]{1,0:T(8,128)(2,1)}, bf16[256,1024]{1,0:T(8,128)(2,1)}, u32[]{:S(2)}, u32[]{:S(2)}) collective-permute-start(bf16[256,1024]{1,0:T(8,128)(2,1)} %slice.1305), channel_id=1, source_target_pairs={{0,2},{1,3},{2,0},{3,1},{4,6},{5,7},{6,4},{7,5},{8,10},{9,11},{10,... | collective-permute-start | bytes 1572872 | tf_op jit(solution)/shard_map/ppermute | solution.py:38
  604.8 66.6 %all-to-all-start.2 = ((bf16[4,2000,128]{2,1,0:T(8,128)(2,1)}), bf16[4,2000,128]{2,1,0:T(8,128)(2,1)}, u32[]{:S(2)}, u32[]{:S(2)}) async-start(bf16[4,2000,128]{2,1,0:T(8,128)(2,1)} %pad_maximum_fusion.8), calls=%async_computation.2 | async-start | bytes 4096000 | tf_op jit(solution)/shard_map/all_to_all | solution.py:1112
  651.5 61.2 %collective-permute-start.53 = (bf16[2048,512]{1,0:T(8,128)(2,1)}, bf16[2048,512]{1,0:T(8,128)(2,1)}, u32[]{:S(2)}, u32[]{:S(2)}) collective-permute-start(bf16[2048,512]{1,0:T(8,128)(2,1)} %get-tuple-element.182), channel_id=1, source_target_pairs={{0,4},{4,0},{8,12},{12,8},{16,20},{20,16},{24,28},{28,24},{1,5},{5... | collective-permute-start | bytes 6291464 | tf_op jit(solution)/shard_map/ppermute | solution.py:38
  690.2 22.6 %collective-permute-start.52 = (bf16[256,1024]{1,0:T(8,128)(2,1)}, bf16[256,1024]{1,0:T(8,128)(2,1)S(1)}, u32[]{:S(2)}, u32[]{:S(2)}) collective-permute-start(bf16[256,1024]{1,0:T(8,128)(2,1)} %slice.1304), channel_id=1, source_target_pairs={{0,2},{1,3},{2,0},{3,1},{4,6},{5,7},{6,4},{7,5},{8,10},{9,11},{10,... | collective-permute-start | bytes 1572872 | tf_op jit(solution)/shard_map/ppermute | solution.py:38
  719.7 34.9 %collective-permute-start.54 = (bf16[2048,256]{1,0:T(8,128)(2,1)}, bf16[2048,256]{1,0:T(8,128)(2,1)}, u32[]{:S(2)}, u32[]{:S(2)}) collective-permute-start(bf16[2048,256]{1,0:T(8,128)(2,1)} %slice.1297), channel_id=1, source_target_pairs={{0,8},{4,12},{8,0},{12,4},{16,24},{20,28},{24,16},{28,20},{1,9},{5... | collective-permute-start | bytes 3145736 | tf_op jit(solution)/shard_map/ppermute | solution.py:38
  724.7 29.9 %all-to-all-start.3 = ((bf16[8,256,128]{2,1,0:T(8,128)(2,1)}), bf16[8,256,128]{2,1,0:T(8,128)(2,1)S(1)}, u32[]{:S(2)}, u32[]{:S(2)}) async-start(bf16[8,256,128]{2,1,0:T(8,128)(2,1)} %embed_back.1), calls=%async_computation.3 | async-start | bytes 1048576 | tf_op jit(solution)/shard_map/all_to_all | solution.py:1143
  729.4 32.0 %collective-permute-start.56 = (bf16[1120,512]{1,0:T(8,128)(2,1)}, bf16[1120,512]{1,0:T(8,128)(2,1)}, u32[]{:S(2)}, u32[]{:S(2)}) collective-permute-start(bf16[1120,512]{1,0:T(8,128)(2,1)} %pad_maximum_fusion.11), channel_id=1, source_target_pairs={{0,4},{4,0},{8,12},{12,8},{16,20},{20,16},{24,28},{28,24},{1,5},{5... | collective-permute-start | bytes 3440648 | tf_op jit(solution)/shard_map/ppermute | solution.py:38
  756.8 24.2 %collective-permute-start.55 = (bf16[2048,128]{1,0:T(8,128)(2,1)S(1)}, bf16[2048,128]{1,0:T(8,128)(2,1)S(1)}, u32[]{:S(2)}, u32[]{:S(2)}) collective-permute-start(bf16[2048,128]{1,0:T(8,128)(2,1)S(1)} %slice.1303), channel_id=1, source_target_pairs={{0,16},{4,20},{8,24},{12,28},{16,0},{20,4},{24,8},{28,12},{1,17},{... | collective-permute-start | bytes 1572872 | tf_op jit(solution)/shard_map/ppermute | solution.py:38
  763.1 23.6 %collective-permute-start.57 = (bf16[1120,256]{1,0:T(8,128)(2,1)S(1)}, bf16[1120,256]{1,0:T(8,128)(2,1)S(1)}, u32[]{:S(2)}, u32[]{:S(2)}) collective-permute-start(bf16[1120,256]{1,0:T(8,128)(2,1)S(1)} %slice.1302), channel_id=1, source_target_pairs={{0,8},{4,12},{8,0},{12,4},{16,24},{20,28},{24,16},{28,20},{1,9},{5... | collective-permute-start | bytes 1720328 | tf_op jit(solution)/shard_map/ppermute | solution.py:38
  771.8 33.3 %collective-permute-start.60 = (bf16[2,8,256,128]{3,2,1,0:T(8,128)(2,1)}, bf16[2,8,256,128]{3,2,1,0:T(8,128)(2,1)}, u32[]{:S(2)}, u32[]{:S(2)}) collective-permute-start(bf16[2,8,256,128]{3,2,1,0:T(8,128)(2,1)} %get-tuple-element.398), channel_id=1, source_target_pairs={{0,1},{1,0},{2,3},{3,2},{4,5},{5,4},{6,7},{7,6},{8,9},{9,8},{10,11... | collective-permute-start | bytes 3145736 | tf_op jit(solution)/shard_map/ppermute | solution.py:38
  (179 other events, 2515.9 us)

commit v6 on v5

--- a/solution.py
+++ b/solution.py
@@ -60,12 +60,12 @@
     mask = lax.axis_size("dp") // 2
     while mask:
         moved = swap(piece, "dp", mask)
-        if not steps and beside:
-            moved, *beside = together(moved, *beside)
+        if len(steps) < len(beside):
+            moved = beside[len(steps)](moved)
         piece = jnp.concatenate([piece, moved], axis=axis)
         steps.append(piece)
         mask //= 2
-    return piece, steps, beside
+    return piece, steps
 
 
 def split(value, axis, parts):
@@ -73,12 +73,15 @@
     return [lax.slice_in_dim(value, i * width, (i + 1) * width, axis=axis) for i in range(parts)]
 
 
-def reduce_blocks(keep, send, mask=1):
-    total = keep + swap(send.astype(lowp), "dp", mask).astype(single)
+def reduce_blocks(keep, send, beside=(), mask=1):
+    moved = swap(send.astype(lowp), "dp", mask)
+    if beside:
+        moved = beside[0](moved)
+    total = keep + moved.astype(single)
     mask *= 2
     if mask == lax.axis_size("dp"):
         return total
-    return reduce_blocks(*split(total, 1, 2), mask)
+    return reduce_blocks(*split(total, 1, 2), beside[1:], mask)
 
 
 def reorder(value, mask):
@@ -692,16 +695,19 @@
     halves(total, *refs[3 * count :])
 
 
-def table_grad_part(grads, inputs):
+def table_grad_part(grads, inputs, part):
     count = len(grads)
     rows = sum(g.shape[0] for g in grads)
-    slots = grads[0].shape[1]
+    slots = grads[0].shape[1] // 2
     block = 256
+    first = part * (slots // block)
     if rows > 4096:
-        total = sum(mm(g, jnp.concatenate(v), TN) for g, v in zip(grads, inputs))
+        total = sum(
+            mm(split(g, 1, 2)[part], jnp.concatenate(v), TN) for g, v in zip(grads, inputs)
+        )
         keep, send = split(total, 1, 2)
         return keep, send.astype(lowp)
-    inputs = [part for pair in inputs for part in pair]
+    inputs = [half for pair in inputs for half in pair]
     return pl.pallas_call(
         functools.partial(table_grad_kernel, count),
         name="table_grad_part",
@@ -710,7 +716,7 @@
             jax.ShapeDtypeStruct((slots, D // 2), single),
             jax.ShapeDtypeStruct((slots, D // 2), lowp),
         ),
-        in_specs=[pl.BlockSpec((g.shape[0], block), lambda i: (0, i)) for g in grads]
+        in_specs=[pl.BlockSpec((g.shape[0], block), lambda i: (0, first + i)) for g in grads]
         + [pl.BlockSpec(v.shape, lambda i: (0, 0)) for v in inputs],
         out_specs=(
             pl.BlockSpec((block, D // 2), lambda i: (i, 0)),
@@ -883,7 +889,7 @@
     )
     room = -flat.shape[0] % 1024
     flat = jnp.concatenate([flat, jnp.zeros((room,), single)]).reshape(1, -1, 128)
-    small, small_steps, _ = gather_blocks(flat, 0)
+    small, small_steps = gather_blocks(flat, 0)
     small = small.reshape(dp_size, -1)
     place = jnp.stack([x, d])
 
@@ -918,14 +924,25 @@
         ]
     )
     own_half, far_half = split(table_rows_all, 0, 2)
-    looked_far = lookup(far_half, table)
-    looked_own = lookup(own_half, table)
-    own_one, steps_one, (looked_far, looked_own) = gather_blocks(
-        after(pack_one, small_steps[0]), 1, (looked_far, looked_own)
+    kept = {}
+
+    def beside_lookup(moved):
+        moved, kept["far"], kept["own"] = together(
+            moved, lookup(far_half, table), lookup(own_half, table)
+        )
+        return moved
+
+    def beside_memory(moved):
+        looked = (kept["own"] + swap(kept["far"], "head", 1)).reshape(2, -1, width)
+        mem_normed = state_norm(place, gain_vals[0], memory, 1)[0]
+        moved, more, kept["mem"] = together(moved, swap(looked[1], "head", 2), mem_normed)
+        looked = (looked[0] + more).reshape(dp_size, half, width)
+        kept["looked"] = lax.all_to_all(looked, "dp", 0, 0)
+        return moved
+
+    own_one, steps_one = gather_blocks(
+        after(pack_one, small_steps[0]), 1, (beside_lookup, beside_memory)
     )
-    mem_normed = state_norm(place, gain_vals[0], memory, 1)[0]
-    old_normed = state_norm(place, gain_vals[0], old_states, RATE)
-    own_one, mem_normed, old_normed = together(own_one, mem_normed, old_normed)
     conv_lanes = jnp.arange(DH, dtype=jnp.int32)
     conv_width = DH // dp_size
     conv_natural = (jnp.asarray(order, jnp.int32)[conv_lanes // conv_width] ^ d) * conv_width
@@ -949,19 +966,30 @@
 
     hidden_own = wup.shape[1]
     pack_two = jnp.concatenate([wup.astype(lowp).T, wdown.astype(lowp)])
-    own_two, steps_two, _ = gather_blocks(after(pack_two, steps_one[0]), 1)
+
+    def beside_old(moved):
+        old_normed = state_norm(place, gain_vals[0], old_states, RATE)
+        moved, kept["looked"], kept["old"] = together(moved, kept["looked"], old_normed)
+        return moved
+
+    def beside_compress(moved):
+        moved, *kept["comp"] = together(moved, *compress(kept["old"], own_one, full_conv))
+        return moved
+
+    own_two, steps_two = gather_blocks(
+        after(pack_two, steps_one[1]), 1, (beside_old, beside_compress)
+    )
+    mem_normed, old_normed = kept["mem"], kept["old"]
+    comp, old_raw = kept["comp"]
 
     words = vocab // reach
     z = d // 2
     z_groups = [[2 * i + b for i in range(reach)] for b in range(2)]
-    low_table = after(table.astype(lowp), steps_two[0]).reshape(reach, words, width)
+    low_table = after(table.astype(lowp), steps_two[1]).reshape(reach, words, width)
     low_table = lax.all_to_all(low_table, "dp", 0, 0, axis_index_groups=z_groups)
     slots = -(-words // 256) * 256
 
-    looked = (looked_own + swap(looked_far, "head", 1)).reshape(2, -1, width)
-    looked = looked[0] + swap(looked[1], "head", 2)
-    looked = lax.all_to_all(looked.reshape(dp_size, half, width), "dp", 0, 0)
-    embedded_low, normed = place_embedding(place, looked, gain_vals[0])
+    embedded_low, normed = place_embedding(place, kept["looked"], gain_vals[0])
     embedded = embedded_low.astype(single)
 
     comp_counts = jnp.where(x == 1, jnp.flip(comp_fill), comp_fill)
@@ -973,12 +1001,14 @@
         more = swap(send.astype(lowp), "head", 1)
         return keep.astype(single) + more.astype(single)
 
-    def group_sum(part, beside=()):
-        keep, send = split(part, 0, 2) if not isinstance(part, (tuple, list)) else part
-        keep, send = split(core_sum(keep, send), 0, 2)
+    def stream_sum(part, beside=()):
+        keep, send = split(part, 0, 2)
         more, *beside = together(swap(send.astype(lowp), "head", 2), *beside)
         part = keep + more.astype(single)
         return (part, beside) if beside else part
+
+    def group_sum(part, beside=()):
+        return stream_sum(core_sum(*split(part, 0, 2)), beside)
 
     def group_both(part, beside=()):
         far, *beside = together(swap(part, "head", 2), *beside)
@@ -988,29 +1018,28 @@
 
     normed = jnp.concatenate(group_both(normed))
     in_weight = own_one[: 3 * wide]
-    comp, old_raw = compress(old_normed, own_one, full_conv)
     mem = mm(mem_normed, own_one[wide : 3 * wide], NT).astype(lowp)
     seg = mm(normed, in_weight, NT).astype(lowp).reshape(2, streams, half, 3 * wide)
-    mixed, lse = attend(info, after(seg, steps_two[1]), comp, mem)
-    mixed, low_parts = together(mixed.reshape(-1, wide), low_table)
+    mixed, lse = attend(info, seg, comp, mem)
+    mixed = mixed.reshape(-1, wide)
+    attn_sum, (own_codes, own_count, own_two, low_table) = group_sum(
+        mm(mixed, own_one[3 * wide : 4 * wide]),
+        (*own_list(after(token_codes, mixed)), own_two, low_table),
+    )
+    after_attn = embedded + attn_sum
+    ffn_in, inv_second = rms(after_attn, gain_vals[1])
+    ffn_in = jnp.concatenate(group_both(ffn_in))
+    full_up, full_down = split(own_two, 0, 2)
     near_table = [
-        lax.dynamic_index_in_dim(low_parts, z ^ (m // 2), 0, keepdims=False) for m in order[:reach]
+        lax.dynamic_index_in_dim(low_table, z ^ (m // 2), 0, keepdims=False) for m in order[:reach]
     ]
     near_table = jnp.concatenate(near_table, axis=1)
-    full_up, full_down = split(own_two, 0, 2)
-    attn_sum, (full_up, full_down, near_table) = group_sum(
-        mm(mixed, own_one[3 * wide : 4 * wide]), (full_up, full_down, near_table)
-    )
     far_table = swap(near_table, "dp", 1)
     loss_table = jnp.concatenate([near_table, far_table], axis=1)
     loss_table = jnp.concatenate([loss_table, jnp.zeros((slots - words, D), lowp)], axis=0)
-    after_attn = embedded + attn_sum
-    ffn_in, inv_second = rms(after_attn, gain_vals[1])
-    ffn_in = jnp.concatenate(group_both(ffn_in))
     hidden_pre = mm(ffn_in, full_up, NT)
     hidden_act = jax.nn.gelu(hidden_pre).astype(lowp)
-    ffn_sum, (loss_table,) = group_sum(mm(hidden_act, full_down), (loss_table,))
-    after_ffn = after_attn + ffn_sum
+    after_ffn = after_attn + group_sum(mm(hidden_act, full_down))
     final_in, inv_third = rms(after_ffn, gain_vals[2])
 
     word_start = (h * vocab + z * words).astype(single)
@@ -1025,10 +1054,10 @@
 
     def next_chunk():
         i = len(chunks)
-        if i < 2:
+        if i == 0:
             chunks.append(group_both(pieces[i]))
         else:
-            chunk, (stats[i - 2],) = group_both(pieces[i], (stats[i - 2],))
+            chunk, (stats[i - 1],) = group_both(pieces[i], (stats[i - 1],))
             chunks.append(chunk)
         out, stat = logits_part(words, info_all[i], *chunks[i], loss_table)
         raised.append(out)
@@ -1039,10 +1068,8 @@
         joined = jnp.concatenate(pieces) if len(pieces) > 1 else pieces[0]
         moved = swap(reorder(joined, mask), "dp", mask)
         if len(pieces) == 1:
+            moved, loss_table, early = together(moved, loss_table, early)
             next_chunk()
-            moved, own_codes, own_count, early = together(
-                moved, *own_list(after(token_codes, final_in)), early
-            )
         elif len(pieces) == 2:
             moved, stats[0] = together(moved, stats[0])
         pieces += split(moved, 0, len(pieces))
@@ -1075,34 +1102,37 @@
     dlogits = [None] * reach
     parts = [None] * reach
     for i in reversed(range(reach)):
-        dlogits[i], *part = logits_back(info_all[i], factor_all[i], raised[i], loss_table)
-        parts[i] = group_sum(part)
-    dlogits[0] = after(dlogits[0], parts[min(1, reach - 1)])
-    table_parts = table_grad_part(dlogits, chunks)
+        dlogits[i], *core = logits_back(info_all[i], factor_all[i], raised[i], loss_table)
+        if i + 1 < reach:
+            parts[i + 1], (dlogits[i], *core) = stream_sum(parts[i + 1], (dlogits[i], *core))
+        parts[i] = core_sum(*core)
+    parts[0] = stream_sum(parts[0])
+    table_parts = []
     mask = 2
     while len(parts) > 1:
         count = len(parts) // 2
         moved = jnp.concatenate([part.astype(lowp) for part in parts[count:]])
         moved = swap(reorder(moved, mask), "dp", mask)
-        if mask == 2:
-            moved, *table_parts = together(moved, *table_parts)
+        if len(table_parts) < 2:
+            more = table_grad_part(dlogits, chunks, len(table_parts))
+            moved, *more = together(moved, *more, *[part[1] for part in table_parts])
+            table_parts = [(part[0], done) for part, done in zip(table_parts, more[2:])]
+            table_parts.append((more[0], swap(more[1], "dp", 1)))
         moved = split(moved.astype(single), 0, count)
         parts = [part + more for part, more in zip(parts, moved)]
         mask *= 2
     final_grad = parts[0]
 
-    keep, send = table_parts
-    moved_table = swap(send, "dp", 1)
-
     grad_after_ffn = rms_back(after_ffn, inv_third, gain_vals[2], final_grad)
-    down_in, (moved_table,) = group_both(grad_after_ffn.astype(lowp), (moved_table,))
+    moved_table = [part[1] for part in table_parts]
+    down_in, (moved_table[1],) = group_both(grad_after_ffn.astype(lowp), (moved_table[1],))
     down_in = jnp.concatenate(down_in)
     act_grad = mm(down_in, full_down, NT)
     pre_grad = jax.vjp(jax.nn.gelu, hidden_pre)[1](act_grad)[0].astype(lowp)
     two = hidden_grads(pre_grad, hidden_act, ffn_in, down_in)
     ffn_in_grad, two = group_sum(mm(pre_grad, full_up), two)
-    two_moved = swap(two[1], "dp", 1)
-    keep = keep + moved_table.astype(single)
+    keep = [part + more.astype(single) for (part, _), more in zip(table_parts, moved_table)]
+    keep = jnp.concatenate(keep)
     table_pieces = jnp.stack(split(keep[:words].astype(lowp), 1, reach))
     position = [order.index(2 * i) for i in range(reach)]
     position = jnp.asarray(position, jnp.int32)[jnp.arange(reach) ^ z]
@@ -1115,45 +1145,53 @@
 
     mixed_grad = mm(attn_in, own_one[3 * wide : 4 * wide], NT).astype(lowp)
     mixed_grad = mixed_grad.reshape(2, streams, half, wide)
-    seg_grad, comp_grad, mem_grad = attend_back(info, seg, comp, mem, lse, mixed_grad)
-    seg_grad, table_pieces = together(seg_grad.reshape(-1, 3 * wide), table_pieces)
-    seg_in = core_sum(*split(mm(seg_grad, in_weight), 0, 2))
-    seg_in_far = swap(seg_in[half:].astype(lowp), "head", 2)
-    old_grad, conv_sum = expand(comp_grad, old_raw, full_conv)
-    one = attn_grads(
-        seg_grad,
-        mixed,
-        mem_grad,
-        old_grad.reshape(-1, old_grad.shape[-1]),
-        normed,
-        attn_in,
-        mem_normed,
-        old_normed.reshape(-1, D),
-    )
-    seg_in_far, two_moved, *one = together(seg_in_far, two_moved, *one)
-    table_base = table_pieces.astype(single).reshape(vocab, width)
-    rows_grad = embed_back(
-        place,
-        embedded_low,
-        gain_vals[0],
-        seg_in[:half],
-        seg_in_far,
-        grad_after_attn,
-    )
-    rows_grad = lax.all_to_all(rows_grad, "dp", 0, 0)
-    two = two[0] + two_moved.astype(single)
-    two_keep, two_send = split(two, 1, 2)
-    two_send, rows_grad = together(swap(two_send.astype(lowp), "dp", 2), rows_grad)
-    two = two_keep + two_send.astype(single)
-    rows_grad = jnp.stack([rows_grad, swap(rows_grad, "head", 2)])
+    def beside_attend(moved):
+        grads = attend_back(info, seg, comp, mem, lse, mixed_grad)
+        moved, kept["table"], *kept["grads"] = together(moved, table_pieces, *grads)
+        return moved
+
+    def beside_sums(moved):
+        seg_grad, comp_grad, mem_grad = kept["grads"]
+        seg_grad = seg_grad.reshape(-1, 3 * wide)
+        seg_in = core_sum(*split(mm(seg_grad, in_weight), 0, 2))
+        seg_in_far = swap(seg_in[half:].astype(lowp), "head", 2)
+        old_grad, conv_sum = expand(comp_grad, old_raw, full_conv)
+        sums = attn_grads(
+            seg_grad,
+            mixed,
+            mem_grad,
+            old_grad.reshape(-1, old_grad.shape[-1]),
+            normed,
+            attn_in,
+            mem_normed,
+            old_normed.reshape(-1, D),
+        )
+        conv_sum = split(conv_block_order(conv_sum), 1, 2)
+        sums = [jnp.concatenate([part, more.astype(part.dtype)]) for part, more in zip(sums, conv_sum)]
+        moved, seg_in_far, *kept["sums"] = together(moved, seg_in_far, *sums)
+        rows_grad = embed_back(
+            place, embedded_low, gain_vals[0], seg_in[:half], seg_in_far, grad_after_attn
+        )
+        kept["rows"] = lax.all_to_all(rows_grad, "dp", 0, 0)
+        return moved
+
+    def beside_rows(moved):
+        moved, kept["rows"] = together(moved, kept["rows"])
+        return moved
+
+    def beside_streams(moved):
+        moved, far = together(moved, swap(kept["rows"], "head", 2))
+        kept["rows"] = jnp.stack([kept["rows"], far])
+        return moved
+
+    two = reduce_blocks(*two, (beside_attend, beside_sums))
+    one = reduce_blocks(*kept["sums"], (beside_rows, beside_streams))
+    rows_grad = kept["rows"]
     rows_grad = jnp.stack([rows_grad, swap(rows_grad, "head", 1)]).reshape(-1, width)
-
-    two = reduce_blocks(*split(two, 1, 2), 4)
+    table_base = kept["table"].astype(single).reshape(vocab, width)
+
     up_grad = two[:hidden_own].T
     down_grad = two[hidden_own:]
-    conv_sum = split(conv_block_order(conv_sum), 1, 2)
-    one = [jnp.concatenate([part, more.astype(part.dtype)]) for part, more in zip(one, conv_sum)]
-    one = reduce_blocks(*one)
     qkv_grad = jnp.swapaxes(one[: 3 * wide].reshape(3, wide, width), 1, 2)
     out_grad = one[3 * wide : 4 * wide]
     conv_grad = one[4 * wide :].reshape(wconv.shape)

time: 923 us -> 897 us (0.972)
  waiting for transfers between devices: 276 us -> 219 us
  local copies, waits for them, and re-layouts: 77.8 us -> 99.7 us
  Pallas kernels: 255 us -> 265 us
    ppermute x69 -> x70, waiting for transfers between devices: 257 us -> 206 us  [swap(): return lax.ppermute(value, axis, [(i, i ^ mask) for i in range(size)])]
    unnamed x309 -> x308, local copies, waits for them, and re-layouts: 29.2 us -> 44.3 us
    concatenate x0 -> x3, local copies, waits for them, and re-layouts: none -> 9.43 us  [the longest x1 4.56 us: local(): jnp.concatenate([loss_table, jnp.zeros((slots - words, D), lowp)], axis=0)]
    ppermute x69 -> x70, starting transfers between devices: 67.1 us -> 60.8 us  [swap(): return lax.ppermute(value, axis, [(i, i ^ mask) for i in range(size)])]
    pallas_call x1 -> x2, Pallas kernels: 24.1 us -> 29.1 us  [table_grad_part(): pl.pallas_call(functools.partial(table_grad_kernel, count), name='table_g...]
  transfers between devices with their start and end apart: 73 -> 74, of which waited for: 42 -> 44; matrix products, arithmetic and copies ran while one was open for 18% -> 19% of each run, Pallas kernels for 24% -> 25%
where the time goes in v6:
time: 897 us; the launch traced here: 887 us
  Pallas kernels  265 us (30%)
  waiting for transfers between devices  219 us (24%)
  other arithmetic  146 us (16%)
  local copies, waits for them, and re-layouts  99.7 us (11%)
  starting transfers between devices  78.9 us (9%)
  matrix products  37.8 us (4%)
  between operations  33.8 us (4%)
    ppermute x70, waiting for transfers between devices, swap(): return lax.ppermute(value, axis, [(i, i ^ mask) for i in range(size)])  206 us
    ppermute x70, starting transfers between devices, swap(): return lax.ppermute(value, axis, [(i, i ^ mask) for i in range(size)])  60.8 us
    pallas_call x4, Pallas kernels, logits_back(): pl.pallas_call(functools.partial(logits_back_kernel, tiles), name='logits...  44.5 us
    unnamed x308, local copies, waits for them, and re-layouts  44.3 us
    pallas_call x4, Pallas kernels, logits_part(): pl.pallas_call(functools.partial(logits_kernel, words, tiles), name='logi...  43.9 us
    dot_general x11, matrix products, mm(): return lax.dot_general(left, right, dims, preferred_element_type=single)  37.8 us
    pallas_call x2, Pallas kernels, table_grad_part(): pl.pallas_call(functools.partial(table_grad_kernel, count), name='table_g...  29.1 us
    pallas_call x1, Pallas kernels, own_list(): pl.pallas_call(list_kernel, name='own_list', out_shape=(jax.ShapeDtypeStr...  21.4 us
  transfers between devices with their start and end apart: 74, of which 44 were waited for; matrix products, arithmetic and copies ran while one was open for 19% of the time, Pallas kernels for 25%

profile of v6, /device:TPU:0, one launch (start us, length us, event | category | flops | bytes accessed | tf_op | source)
XLA Modules:
  0.0 886.7 jit_solution(13019843999376182134)
XLA Ops:
  28.1 8.6 lookup.2
  36.8 8.6 lookup.3
  87.7 9.9 %state_norm.3.old_ref = bf16[3,1024,1024]{2,1,0:T(8,128)(2,1)} custom-call(s32[2]{0:T(128)} %pad_add_fusion.place_ref, f32[1,1024]{1,0:T(1,128)} %bitcast.348, bf16[2,1536,1024]{2,1,0:T(8,128)(2,1)} %in_ref.3), custom_call_target="tpu_custom_call" | custom-call | bytes 251658 | tf_op jit(solution)/shard_map/state_norm/pallas_call | solution.py:328
  98.4 9.6 %collective-permute-done.7 = bf16[2048,128]{1,0:T(8,128)(2,1)S(1)} collective-permute-done((bf16[2048,128]{1,0:T(8,128)(2,1)S(1)}, bf16[2048,128]{1,0:T(8,128)(2,1)S(1)}, u32[]{:S(2)}, u32[]{:S(2)}) %collective-permute-start.7) | collective-permute-done | bytes 524320 | tf_op jit(solution)/shard_map/ppermute | solution.py:38
  129.3 12.1 %compress.1 = (bf16[1024,512]{1,0:T(8,128)(2,1)}, bf16[3,1024,512]{2,1,0:T(8,128)(2,1)}) custom-call(bf16[3,1024,1024]{2,1,0:T(8,128)(2,1)} %state_norm.3.old_ref, bf16[1120,1024]{1,0:T(8,128)(2,1)} %copy-done.4, bf16[1120,1024]{1,0:T(8,128)(2,1)} %copy-done.4, bf16[2,384,128]{2,1,0:T(8,128)(2,1)} %bitcast.317), custom_call_target="tpu_custom_call" | custom-call | flops 64424508 | bytes 251658 | tf_op jit(solution)/shard_map/compress/pallas_call | solution.py:370
  158.7 10.9 %attend.1 = (bf16[2,2,256,256]{3,2,1,0:T(8,128)(2,1)}, f32[2,2,512,1]{3,2,1,0:T(8,128)}) custom-call(s32[5]{0:T(128)} %stack.103.info_ref, bf16[2,2,256,768]{3,2,1,0:T(8,128)(2,1)} %bitcast.302, bf16[2,2,256,768]{3,2,1,0:T(8,128)(2,1)} %bitcast.303, bf16[2,2,256,768]{3,2,1,0:T(8,128)(2,1)} %bitcast.304, bf16[1024,512]{1,0:T(8,128)(2,1)} %get-tuple-element.154.kc_ref.vc_ref, ...), custom_call_target="tpu_custom_call" | custom-call | flops 146800640 | bytes 125829 | tf_op jit(solution)/shard_map/attend/pallas_call | solution.py:522
  177.6 21.4 %own_list.1 = (s32[8200]{0:T(1024)}, s32[1]{0:T(128)}) custom-call(s32[8192]{0:T(1024)} %get-tuple-element.157.code_ref), custom_call_target="tpu_custom_call" | custom-call | bytes 1258291 | tf_op jit(solution)/shard_map/own_list/pallas_call | solution.py:184
  209.4 12.2 %collective-permute-done.15 = bf16[256,1024]{1,0:T(8,128)(2,1)S(1)} collective-permute-done((bf16[256,1024]{1,0:T(8,128)(2,1)S(1)}, bf16[256,1024]{1,0:T(8,128)(2,1)S(1)}, u32[]{:S(2)}, u32[]{:S(2)}) %collective-permute-start.15) | collective-permute-done | bytes 524320 | tf_op jit(solution)/shard_map/ppermute | solution.py:38
  279.2 12.4 %collective-permute-done.20 = bf16[2000,512]{1,0:T(8,128)(2,1)} collective-permute-done((bf16[2000,512]{1,0:T(8,128)(2,1)}, bf16[2000,512]{1,0:T(8,128)(2,1)}, u32[]{:S(2)}, u32[]{:S(2)}) %collective-permute-start.20) | collective-permute-done | bytes 2048032 | tf_op jit(solution)/shard_map/ppermute | solution.py:38
  308.5 10.9 %logits_part.4 = (bf16[1024,2048]{1,0:T(8,128)(2,1)}, f32[8,1024]{1,0:T(8,128)}) custom-call(f32[8,1024]{1,0:T(8,128)} %squeeze.176.info_ref, bf16[512,1024]{1,0:T(8,128)(2,1)} %copy-done.1, bf16[512,1024]{1,0:T(8,128)(2,1)} %collective-permute-done.24.near_ref.refs_5_, bf16[2048,1024]{1,0:T(8,128)(2,1)} %concatenate.175.table_ref), custom_call_target="tpu_custom_call" | custom-call | flops 171798688 | bytes 209715 | tf_op jit(solution)/shard_map/logits_part/pallas_call | solution.py:604
  319.4 8.6 collective-permute-done.22
  334.3 11.1 %logits_part.5 = (bf16[1024,2048]{1,0:T(8,128)(2,1)}, f32[8,1024]{1,0:T(8,128)}) custom-call(f32[8,1024]{1,0:T(8,128)} %squeeze.177.info_ref, bf16[512,1024]{1,0:T(8,128)(2,1)} %constant_dynamic-update-slice_fusion.24.pair_ref.refs_6_, bf16[512,1024]{1,0:T(8,128)(2,1)} %copy-done.11, bf16[2048,1024]{1,0:T(8,128)(2,1)} %concatenate.175.table_ref), custom_call_target="tpu_custom_call" | custom-call | flops 171798688 | bytes 209715 | tf_op jit(solution)/shard_map/logits_part/pallas_call | solution.py:604
  350.9 11.0 %logits_part.6 = (bf16[1024,2048]{1,0:T(8,128)(2,1)}, f32[8,1024]{1,0:T(8,128)}) custom-call(f32[8,1024]{1,0:T(8,128)} %squeeze.178.info_ref, bf16[512,1024]{1,0:T(8,128)(2,1)} %copy-done.2, bf16[512,1024]{1,0:T(8,128)(2,1)} %collective-permute-done.28.near_ref.refs_9_, bf16[2048,1024]{1,0:T(8,128)(2,1)} %concatenate.175.table_ref), custom_call_target="tpu_custom_call" | custom-call | flops 171798688 | bytes 209715 | tf_op jit(solution)/shard_map/logits_part/pallas_call | solution.py:604
  367.0 10.9 %logits_part.7 = (bf16[1024,2048]{1,0:T(8,128)(2,1)}, f32[8,1024]{1,0:T(8,128)}) custom-call(f32[8,1024]{1,0:T(8,128)} %squeeze.166.info_ref, bf16[512,1024]{1,0:T(8,128)(2,1)} %copy-done.3, bf16[512,1024]{1,0:T(8,128)(2,1)} %collective-permute-done.29.near_ref.refs_11_, bf16[2048,1024]{1,0:T(8,128)(2,1)} %concatenate.175.table_ref), custom_call_target="tpu_custom_call" | custom-call | flops 171798688 | bytes 209715 | tf_op jit(solution)/shard_map/logits_part/pallas_call | solution.py:604
  395.1 11.0 %logits_back.4 = (bf16[1024,2048]{1,0:T(8,128)(2,1)}, bf16[512,1024]{1,0:T(8,128)(2,1)}, bf16[512,1024]{1,0:T(8,128)(2,1)}) custom-call(f32[8,1024]{1,0:T(8,128)} %squeeze.166.info_ref, f32[8,1024]{1,0:T(8,128)} %broadcast_in_dim.188.factor_ref, bf16[1024,2048]{1,0:T(8,128)(2,1)} %get-tuple-element.179.in_ref, bf16[2048,1024]{1,0:T(8,128)(2,1)} %concatenate.175.table_ref), custom_call_target="tpu_custom_call" | custom-call | flops 171798688 | bytes 251658 | tf_op jit(solution)/shard_map/logits_back/pallas_call | solution.py:657
  413.2 11.1 %logits_back.5 = (bf16[1024,2048]{1,0:T(8,128)(2,1)}, bf16[512,1024]{1,0:T(8,128)(2,1)}, bf16[512,1024]{1,0:T(8,128)(2,1)}) custom-call(f32[8,1024]{1,0:T(8,128)} %squeeze.178.info_ref, f32[8,1024]{1,0:T(8,128)} %broadcast_in_dim.190.factor_ref, bf16[1024,2048]{1,0:T(8,128)(2,1)} %get-tuple-element.182.in_ref, bf16[2048,1024]{1,0:T(8,128)(2,1)} %concatenate.175.table_ref), custom_call_target="tpu_custom_call" | custom-call | flops 171798688 | bytes 251658 | tf_op jit(solution)/shard_map/logits_back/pallas_call | solution.py:657
  433.1 11.4 %logits_back.6 = (bf16[1024,2048]{1,0:T(8,128)(2,1)}, bf16[512,1024]{1,0:T(8,128)(2,1)}, bf16[512,1024]{1,0:T(8,128)(2,1)}) custom-call(f32[8,1024]{1,0:T(8,128)} %squeeze.177.info_ref, f32[8,1024]{1,0:T(8,128)} %broadcast_in_dim.192.factor_ref, bf16[1024,2048]{1,0:T(8,128)(2,1)} %get-tuple-element.188.in_ref, bf16[2048,1024]{1,0:T(8,128)(2,1)} %concatenate.175.table_ref), custom_call_target="tpu_custom_call" | custom-call | flops 171798688 | bytes 251658 | tf_op jit(solution)/shard_map/logits_back/pallas_call | solution.py:657
  453.3 11.0 %logits_back.7 = (bf16[1024,2048]{1,0:T(8,128)(2,1)}, bf16[512,1024]{1,0:T(8,128)(2,1)}, bf16[512,1024]{1,0:T(8,128)(2,1)}) custom-call(f32[8,1024]{1,0:T(8,128)} %squeeze.176.info_ref, f32[8,1024]{1,0:T(8,128)} %broadcast_in_dim.194.factor_ref, bf16[1024,2048]{1,0:T(8,128)(2,1)} %get-tuple-element.194.in_ref, bf16[2048,1024]{1,0:T(8,128)(2,1)} %concatenate.175.table_ref), custom_call_target="tpu_custom_call" | custom-call | flops 171798688 | bytes 251658 | tf_op jit(solution)/shard_map/logits_back/pallas_call | solution.py:657
  466.2 14.5 %table_grad_part.2 = (f32[1024,512]{1,0:T(8,128)}, bf16[1024,512]{1,0:T(8,128)(2,1)}) custom-call(bf16[1024,2048]{1,0:T(8,128)(2,1)} %get-tuple-element.202.refs_0_, bf16[1024,2048]{1,0:T(8,128)(2,1)} %get-tuple-element.203.refs_1_, bf16[1024,2048]{1,0:T(8,128)(2,1)} %get-tuple-element.204.refs_2_, bf16[1024,2048]{1,0:T(8,128)(2,1)} %get-tuple-element.205.refs_3_, ...), custom_call_target="tpu_custom_call" | custom-call | flops 257698032 | bytes 629145 | tf_op jit(solution)/shard_map/table_grad_part/pallas_call | solution.py:711
  497.2 14.5 %table_grad_part.3 = (f32[1024,512]{1,0:T(8,128)}, bf16[1024,512]{1,0:T(8,128)(2,1)}) custom-call(bf16[1024,2048]{1,0:T(8,128)(2,1)} %get-tuple-element.202.refs_0_, bf16[1024,2048]{1,0:T(8,128)(2,1)} %get-tuple-element.203.refs_1_, bf16[1024,2048]{1,0:T(8,128)(2,1)} %get-tuple-element.204.refs_2_, bf16[1024,2048]{1,0:T(8,128)(2,1)} %get-tuple-element.205.refs_3_, ...), custom_call_target="tpu_custom_call" | custom-call | flops 257698032 | bytes 629145 | tf_op jit(solution)/shard_map/table_grad_part/pallas_call | solution.py:711
  522.1 13.4 %collective-permute-done.45 = bf16[256,1024]{1,0:T(8,128)(2,1)S(1)} collective-permute-done((bf16[256,1024]{1,0:T(8,128)(2,1)S(1)}, bf16[256,1024]{1,0:T(8,128)(2,1)S(1)}, u32[]{:S(2)}, u32[]{:S(2)}) %collective-permute-start.45) | collective-permute-done | bytes 524320 | tf_op jit(solution)/shard_map/ppermute | solution.py:38
  535.4 8.1 collective-permute-done.46
  582.5 11.4 %hidden_grads.1 = (f32[2048,512]{1,0:T(8,128)}, bf16[2048,512]{1,0:T(8,128)(2,1)}) custom-call(bf16[1024,1024]{1,0:T(8,128)(2,1)} %copy-done.47, bf16[1024,1024]{1,0:T(8,128)(2,1)} %copy-done.46, bf16[1024,1024]{1,0:T(8,128)(2,1)} %pad_maximum_fusion.3.in_ref, bf16[1024,1024]{1,0:T(8,128)(2,1)} %pad_maximum_fusion.4.down_ref), custom_call_target="tpu_custom_call" | custom-call | flops 128849016 | bytes 335544 | tf_op jit(solution)/shard_map/hidden_grads/pallas_call | solution.py:746
  604.4 8.2 collective-permute-done.51
  620.0 15.2 %attend_back.1 = (bf16[2,2,256,768]{3,2,1,0:T(8,128)(2,1)}, bf16[1024,512]{1,0:T(8,128)(2,1)}, bf16[1024,512]{1,0:T(8,128)(2,1)}) custom-call(s32[5]{0:T(128)} %stack.103.info_ref, bf16[2,2,256,768]{3,2,1,0:T(8,128)(2,1)} %bitcast.305, bf16[2,2,256,768]{3,2,1,0:T(8,128)(2,1)} %bitcast.306, bf16[2,2,256,768]{3,2,1,0:T(8,128)(2,1)} %bitcast.307, ...), custom_call_target="tpu_custom_call" | custom-call | flops 230686720 | bytes 188743 | tf_op jit(solution)/shard_map/attend_back/pallas_call | solution.py:545
  638.1 9.5 %collective-permute-done.50 = bf16[2048,512]{1,0:T(8,128)(2,1)} collective-permute-done((bf16[2048,512]{1,0:T(8,128)(2,1)}, bf16[2048,512]{1,0:T(8,128)(2,1)}, u32[]{:S(2)}, u32[]{:S(2)}) %collective-permute-start.50) | collective-permute-done | bytes 2097184 | tf_op jit(solution)/shard_map/ppermute | solution.py:38
  669.3 14.2 %attn_grads.1 = (f32[1024,512]{1,0:T(8,128)}, bf16[1024,512]{1,0:T(8,128)(2,1)}) custom-call(bf16[1024,768]{1,0:T(8,128)(2,1)} %bitcast.320, bf16[1024,256]{1,0:T(8,128)(2,1)} %bitcast.314, bf16[1024,512]{1,0:T(8,128)(2,1)} %get-tuple-element.231.mem_ref, bf16[3072,512]{1,0:T(8,128)(2,1)} %bitcast.315, bf16[1024,1024]{1,0:T(8,128)(2,1)} %pad_maximum_fusion.2.normed_ref, ...), custom_call_target="tpu_custom_call" | custom-call | flops 188743680 | bytes 503316 | tf_op jit(solution)/shard_map/attn_grads/pallas_call | solution.py:796
  688.8 11.2 %collective-permute-done.55.more_ref = bf16[256,1024]{1,0:T(8,128)(2,1)} collective-permute-done((bf16[256,1024]{1,0:T(8,128)(2,1)S(1)}, bf16[256,1024]{1,0:T(8,128)(2,1)}, u32[]{:S(2)}, u32[]{:S(2)}) %collective-permute-start.55) | collective-permute-done | bytes 524320 | tf_op jit(solution)/shard_map/ppermute | solution.py:38
  721.1 13.7 %all-to-all-done.3 = bf16[8,256,128]{2,1,0:T(8,128)(2,1)S(1)} async-done(((bf16[8,256,128]{2,1,0:T(8,128)(2,1)}), bf16[8,256,128]{2,1,0:T(8,128)(2,1)S(1)}, u32[]{:S(2)}, u32[]{:S(2)}) %all-to-all-start.3) | async-done | bytes 524320 | tf_op jit(solution)/shard_map/all_to_all | solution.py:1175
  746.9 10.1 %collective-permute-done.58 = bf16[1120,256]{1,0:T(8,128)(2,1)S(1)} collective-permute-done((bf16[1120,256]{1,0:T(8,128)(2,1)S(1)}, bf16[1120,256]{1,0:T(8,128)(2,1)S(1)}, u32[]{:S(2)}, u32[]{:S(2)}) %collective-permute-start.58) | collective-permute-done | bytes 573472 | tf_op jit(solution)/shard_map/ppermute | solution.py:38
  758.8 13.7 %collective-permute-done.60 = bf16[1120,128]{1,0:T(8,128)(2,1)S(1)} collective-permute-done((bf16[1120,128]{1,0:T(8,128)(2,1)S(1)}, bf16[1120,128]{1,0:T(8,128)(2,1)S(1)}, u32[]{:S(2)}, u32[]{:S(2)}) %collective-permute-start.60) | collective-permute-done | bytes 286752 | tf_op jit(solution)/shard_map/ppermute | solution.py:38
  779.1 17.4 %scatter.1 = f32[8000,128]{1,0:T(8,128)} custom-call(s32[1]{0:T(128)} %get-tuple-element.245.count_ref, s32[8200]{0:T(1024)} %get-tuple-element.246.code_ref, f32[8000,128]{1,0:T(8,128)} %bitcast_convert_fusion.base_ref, bf16[8192,128]{1,0:T(8,128)(2,1)} %bitcast.310), custom_call_target="tpu_custom_call" | custom-call | bytes 629145 | tf_op jit(solution)/shard_map/scatter/pallas_call | solution.py:280
  (733 shorter events, 474.8 us)
Async XLA Ops:
  22.8 22.7 %collective-permute-start.3 = (bf16[1120,128]{1,0:T(8,128)(2,1)S(1)}, bf16[1120,128]{1,0:T(8,128)(2,1)S(1)}, u32[]{:S(2)}, u32[]{:S(2)}) collective-permute-start(bf16[1120,128]{1,0:T(8,128)(2,1)S(1)} %pad_maximum_fusion.23), channel_id=1, source_target_pairs={{0,16},{4,20},{8,24},{12,28},{16,0},{20,4},{24,8},{28,12},{1,17},{... | collective-permute-start | bytes 860168 | tf_op jit(solution)/shard_map/ppermute | solution.py:38
  47.1 15.5 %collective-permute-start.4 = (bf16[1120,256]{1,0:T(8,128)(2,1)S(1)}, bf16[1120,256]{1,0:T(8,128)(2,1)}, u32[]{:S(2)}, u32[]{:S(2)}) collective-permute-start(bf16[1120,256]{1,0:T(8,128)(2,1)S(1)} %pad_maximum_fusion.20), channel_id=1, source_target_pairs={{0,8},{4,12},{8,0},{12,4},{16,24},{20,28},{24,16},{28,20},{1,9},{5... | collective-permute-start | bytes 1720328 | tf_op jit(solution)/shard_map/ppermute | solution.py:38
  67.2 40.9 %all-to-all-start = ((bf16[8,256,128]{2,1,0:T(8,128)(2,1)}), bf16[8,256,128]{2,1,0:T(8,128)(2,1)}, u32[]{:S(2)}, u32[]{:S(2)}) async-start(bf16[8,256,128]{2,1,0:T(8,128)(2,1)} %bitcast.26), calls=%async_computation | async-start | bytes 1048576 | tf_op jit(solution)/shard_map/all_to_all | solution.py:940
  73.4 40.3 %collective-permute-start.10 = (bf16[1120,512]{1,0:T(8,128)(2,1)}, bf16[1120,512]{1,0:T(8,128)(2,1)}, u32[]{:S(2)}, u32[]{:S(2)}) collective-permute-start(bf16[1120,512]{1,0:T(8,128)(2,1)} %get-tuple-element.459), channel_id=1, source_target_pairs={{0,4},{4,0},{8,12},{12,8},{16,20},{20,16},{24,28},{28,24},{1,5},{5... | collective-permute-start | bytes 3440648 | tf_op jit(solution)/shard_map/ppermute | solution.py:38
  79.0 29.1 %collective-permute-start.7 = (bf16[2048,128]{1,0:T(8,128)(2,1)S(1)}, bf16[2048,128]{1,0:T(8,128)(2,1)S(1)}, u32[]{:S(2)}, u32[]{:S(2)}) collective-permute-start(bf16[2048,128]{1,0:T(8,128)(2,1)S(1)} %pad_maximum_fusion.21), channel_id=1, source_target_pairs={{0,16},{4,20},{8,24},{12,28},{16,0},{20,4},{24,8},{28,12},{1,17},{... | collective-permute-start | bytes 1572872 | tf_op jit(solution)/shard_map/ppermute | solution.py:38
  112.8 28.5 %collective-permute-start.11 = (bf16[2048,256]{1,0:T(8,128)(2,1)}, bf16[2048,256]{1,0:T(8,128)(2,1)}, u32[]{:S(2)}, u32[]{:S(2)}) collective-permute-start(bf16[2048,256]{1,0:T(8,128)(2,1)} %pad_maximum_fusion.13), channel_id=1, source_target_pairs={{0,8},{4,12},{8,0},{12,4},{16,24},{20,28},{24,16},{28,20},{1,9},{5... | collective-permute-start | bytes 3145736 | tf_op jit(solution)/shard_map/ppermute | solution.py:38
  123.9 30.6 %collective-permute-start.9 = (bf16[512,1024]{1,0:T(8,128)(2,1)}, bf16[512,1024]{1,0:T(8,128)(2,1)}, u32[]{:S(2)}, u32[]{:S(2)}) collective-permute-start(bf16[512,1024]{1,0:T(8,128)(2,1)} %pad_maximum_fusion.12), channel_id=1, source_target_pairs={{0,1},{1,0},{2,3},{3,2},{4,5},{5,4},{6,7},{7,6},{8,9},{9,8},{10,11... | collective-permute-start | bytes 3145736 | tf_op jit(solution)/shard_map/ppermute | solution.py:38
  143.6 61.5 %all-to-all-start.1 = ((bf16[4,2000,128]{2,1,0:T(8,128)(2,1)}), bf16[4,2000,128]{2,1,0:T(8,128)(2,1)}, u32[]{:S(2)}, u32[]{:S(2)}) async-start(bf16[4,2000,128]{2,1,0:T(8,128)(2,1)} %bitcast.36), calls=%async_computation.1 | async-start | bytes 4096000 | tf_op jit(solution)/shard_map/all_to_all | solution.py:989
  152.4 48.6 %collective-permute-start.14 = (bf16[2048,512]{1,0:T(8,128)(2,1)}, bf16[2048,512]{1,0:T(8,128)(2,1)}, u32[]{:S(2)}, u32[]{:S(2)}) collective-permute-start(bf16[2048,512]{1,0:T(8,128)(2,1)} %constant_dynamic-update-slice_fusion.8), channel_id=1, source_target_pairs={{0,4},{4,0},{8,12},{12,8},{16,20},{20,16},{24,28},{28,24},{1,5},{5... | collective-permute-start | bytes 6291464 | tf_op jit(solution)/shard_map/ppermute | solution.py:38
  176.1 29.1 %collective-permute-start.13 = (bf16[256,1024]{1,0:T(8,128)(2,1)S(1)}, bf16[256,1024]{1,0:T(8,128)(2,1)S(1)}, u32[]{:S(2)}, u32[]{:S(2)}) collective-permute-start(bf16[256,1024]{1,0:T(8,128)(2,1)S(1)} %slice.1317), channel_id=1, source_target_pairs={{0,2},{1,3},{2,0},{3,1},{4,6},{5,7},{6,4},{7,5},{8,10},{9,11},{10,... | collective-permute-start | bytes 1572872 | tf_op jit(solution)/shard_map/ppermute | solution.py:38
  244.9 46.7 %collective-permute-start.20 = (bf16[2000,512]{1,0:T(8,128)(2,1)}, bf16[2000,512]{1,0:T(8,128)(2,1)}, u32[]{:S(2)}, u32[]{:S(2)}) collective-permute-start(bf16[2000,512]{1,0:T(8,128)(2,1)} %pad_maximum_fusion.7), channel_id=1, source_target_pairs={{0,4},{4,0},{8,12},{12,8},{16,20},{20,16},{24,28},{28,24},{1,5},{5... | collective-permute-start | bytes 6144008 | tf_op jit(solution)/shard_map/ppermute | solution.py:38
  260.2 38.9 %collective-permute-start.19 = (bf16[256,1024]{1,0:T(8,128)(2,1)}, bf16[256,1024]{1,0:T(8,128)(2,1)}, u32[]{:S(2)}, u32[]{:S(2)}) collective-permute-start(bf16[256,1024]{1,0:T(8,128)(2,1)} %constant_dynamic-update-slice_fusion.11), channel_id=1, source_target_pairs={{0,16},{4,20},{8,24},{12,28},{16,0},{20,4},{24,8},{28,12},{1,17},{... | collective-permute-start | bytes 1572872 | tf_op jit(solution)/shard_map/ppermute | solution.py:38
  270.7 29.5 %collective-permute-start.23 = (bf16[256,1024]{1,0:T(8,128)(2,1)S(1)}, bf16[256,1024]{1,0:T(8,128)(2,1)S(1)}, u32[]{:S(2)}, u32[]{:S(2)}) collective-permute-start(bf16[256,1024]{1,0:T(8,128)(2,1)S(1)} %multiply_convert_fusion.1), channel_id=1, source_target_pairs={{0,2},{1,3},{2,0},{3,1},{4,6},{5,7},{6,4},{7,5},{8,10},{9,11},{10,... | collective-permute-start | bytes 1572872 | tf_op jit(solution)/shard_map/ppermute | solution.py:38
  303.7 24.4 %collective-permute-start.22 = (bf16[512,1024]{1,0:T(8,128)(2,1)}, bf16[512,1024]{1,0:T(8,128)(2,1)}, u32[]{:S(2)}, u32[]{:S(2)}) collective-permute-start(bf16[512,1024]{1,0:T(8,128)(2,1)} %get-tuple-element.462), channel_id=1, source_target_pairs={{0,8},{4,12},{8,0},{12,4},{16,24},{20,28},{24,16},{28,20},{1,9},{5... | collective-permute-start | bytes 3145736 | tf_op jit(solution)/shard_map/ppermute | solution.py:38
  305.2 22.8 %collective-permute-start.21 = (bf16[256,1024]{1,0:T(8,128)(2,1)}, bf16[256,1024]{1,0:T(8,128)(2,1)}, u32[]{:S(2)}, u32[]{:S(2)}) collective-permute-start(bf16[256,1024]{1,0:T(8,128)(2,1)} %collective-permute-done.19), channel_id=1, source_target_pairs={{0,2},{1,3},{2,0},{3,1},{4,6},{5,7},{6,4},{7,5},{8,10},{9,11},{10,... | collective-permute-start | bytes 1572872 | tf_op jit(solution)/shard_map/ppermute | solution.py:38
  348.2 14.7 %collective-permute-start.27 = (bf16[256,1024]{1,0:T(8,128)(2,1)}, bf16[256,1024]{1,0:T(8,128)(2,1)}, u32[]{:S(2)}, u32[]{:S(2)}) collective-permute-start(bf16[256,1024]{1,0:T(8,128)(2,1)} %get-tuple-element.455), channel_id=1, source_target_pairs={{0,2},{1,3},{2,0},{3,1},{4,6},{5,7},{6,4},{7,5},{8,10},{9,11},{10,... | collective-permute-start | bytes 1572872 | tf_op jit(solution)/shard_map/ppermute | solution.py:38
  448.6 32.1 %collective-permute-start.42 = (bf16[512,1024]{1,0:T(8,128)(2,1)}, bf16[512,1024]{1,0:T(8,128)(2,1)S(1)}, u32[]{:S(2)}, u32[]{:S(2)}) collective-permute-start(bf16[512,1024]{1,0:T(8,128)(2,1)} %fusion.27), channel_id=1, source_target_pairs={{0,8},{4,12},{8,0},{12,4},{16,24},{20,28},{24,16},{28,20},{1,9},{5... | collective-permute-start | bytes 3145736 | tf_op jit(solution)/shard_map/ppermute | solution.py:38
  486.5 31.6 %collective-permute-start.44 = (bf16[1024,512]{1,0:T(8,128)(2,1)}, bf16[1024,512]{1,0:T(8,128)(2,1)S(1)}, u32[]{:S(2)}, u32[]{:S(2)}) collective-permute-start(bf16[1024,512]{1,0:T(8,128)(2,1)} %get-tuple-element.212), channel_id=1, source_target_pairs={{0,4},{4,0},{8,12},{12,8},{16,20},{20,16},{24,28},{28,24},{1,5},{5... | collective-permute-start | bytes 3145736 | tf_op jit(solution)/shard_map/ppermute | solution.py:38
  491.2 26.9 %collective-permute-start.43 = (bf16[256,1024]{1,0:T(8,128)(2,1)}, bf16[256,1024]{1,0:T(8,128)(2,1)S(1)}, u32[]{:S(2)}, u32[]{:S(2)}) collective-permute-start(bf16[256,1024]{1,0:T(8,128)(2,1)} %constant_dynamic-update-slice_fusion.26), channel_id=1, source_target_pairs={{0,16},{4,20},{8,24},{12,28},{16,0},{20,4},{24,8},{28,12},{1,17},{... | collective-permute-start | bytes 1572872 | tf_op jit(solution)/shard_map/ppermute | solution.py:38
  496.7 22.4 %collective-permute-start.41 = (bf16[256,1024]{1,0:T(8,128)(2,1)}, bf16[256,1024]{1,0:T(8,128)(2,1)}, u32[]{:S(2)}, u32[]{:S(2)}) collective-permute-start(bf16[256,1024]{1,0:T(8,128)(2,1)} %slice.1312), channel_id=1, source_target_pairs={{0,2},{1,3},{2,0},{3,1},{4,6},{5,7},{6,4},{7,5},{8,10},{9,11},{10,... | collective-permute-start | bytes 1572872 | tf_op jit(solution)/shard_map/ppermute | solution.py:38
  518.1 25.4 %collective-permute-start.46 = (bf16[1024,512]{1,0:T(8,128)(2,1)}, bf16[1024,512]{1,0:T(8,128)(2,1)S(1)}, u32[]{:S(2)}, u32[]{:S(2)}) collective-permute-start(bf16[1024,512]{1,0:T(8,128)(2,1)} %get-tuple-element.214), channel_id=1, source_target_pairs={{0,4},{4,0},{8,12},{12,8},{16,20},{20,16},{24,28},{28,24},{1,5},{5... | collective-permute-start | bytes 3145736 | tf_op jit(solution)/shard_map/ppermute | solution.py:38
  572.5 21.4 %collective-permute-start.49 = (bf16[256,1024]{1,0:T(8,128)(2,1)}, bf16[256,1024]{1,0:T(8,128)(2,1)}, u32[]{:S(2)}, u32[]{:S(2)}) collective-permute-start(bf16[256,1024]{1,0:T(8,128)(2,1)} %slice.1311), channel_id=1, source_target_pairs={{0,2},{1,3},{2,0},{3,1},{4,6},{5,7},{6,4},{7,5},{8,10},{9,11},{10,... | collective-permute-start | bytes 1572872 | tf_op jit(solution)/shard_map/ppermute | solution.py:38
  574.8 63.3 %all-to-all-start.2 = ((bf16[4,2000,128]{2,1,0:T(8,128)(2,1)}), bf16[4,2000,128]{2,1,0:T(8,128)(2,1)}, u32[]{:S(2)}, u32[]{:S(2)}) async-start(bf16[4,2000,128]{2,1,0:T(8,128)(2,1)} %pad_maximum_fusion.9), calls=%async_computation.2 | async-start | bytes 4096000 | tf_op jit(solution)/shard_map/all_to_all | solution.py:1142
  600.1 47.5 %collective-permute-start.50 = (bf16[2048,512]{1,0:T(8,128)(2,1)}, bf16[2048,512]{1,0:T(8,128)(2,1)}, u32[]{:S(2)}, u32[]{:S(2)}) collective-permute-start(bf16[2048,512]{1,0:T(8,128)(2,1)} %get-tuple-element.219), channel_id=1, source_target_pairs={{0,4},{4,0},{8,12},{12,8},{16,20},{20,16},{24,28},{28,24},{1,5},{5... | collective-permute-start | bytes 6291464 | tf_op jit(solution)/shard_map/ppermute | solution.py:38
  653.3 30.3 %collective-permute-start.54 = (bf16[512,1024]{1,0:T(8,128)(2,1)}, bf16[512,1024]{1,0:T(8,128)(2,1)}, u32[]{:S(2)}, u32[]{:S(2)}) collective-permute-start(bf16[512,1024]{1,0:T(8,128)(2,1)} %slice.1303), channel_id=1, source_target_pairs={{0,1},{1,0},{2,3},{3,2},{4,5},{5,4},{6,7},{7,6},{8,9},{9,8},{10,11... | collective-permute-start | bytes 3145736 | tf_op jit(solution)/shard_map/ppermute | solution.py:38
  658.7 30.1 %collective-permute-start.53 = (bf16[2048,256]{1,0:T(8,128)(2,1)}, bf16[2048,256]{1,0:T(8,128)(2,1)S(1)}, u32[]{:S(2)}, u32[]{:S(2)}) collective-permute-start(bf16[2048,256]{1,0:T(8,128)(2,1)} %slice.1304), channel_id=1, source_target_pairs={{0,8},{4,12},{8,0},{12,4},{16,24},{20,28},{24,16},{28,20},{1,9},{5... | collective-permute-start | bytes 3145736 | tf_op jit(solution)/shard_map/ppermute | solution.py:38
  700.1 34.7 %collective-permute-start.57 = (bf16[1120,512]{1,0:T(8,128)(2,1)}, bf16[1120,512]{1,0:T(8,128)(2,1)}, u32[]{:S(2)}, u32[]{:S(2)}) collective-permute-start(bf16[1120,512]{1,0:T(8,128)(2,1)} %pad_maximum_fusion.11), channel_id=1, source_target_pairs={{0,4},{4,0},{8,12},{12,8},{16,20},{20,16},{24,28},{28,24},{1,5},{5... | collective-permute-start | bytes 3440648 | tf_op jit(solution)/shard_map/ppermute | solution.py:38
  703.9 30.9 %all-to-all-start.3 = ((bf16[8,256,128]{2,1,0:T(8,128)(2,1)}), bf16[8,256,128]{2,1,0:T(8,128)(2,1)S(1)}, u32[]{:S(2)}, u32[]{:S(2)}) async-start(bf16[8,256,128]{2,1,0:T(8,128)(2,1)} %embed_back.1), calls=%async_computation.3 | async-start | bytes 1048576 | tf_op jit(solution)/shard_map/all_to_all | solution.py:1175
  718.2 26.7 %collective-permute-start.56 = (bf16[2048,128]{1,0:T(8,128)(2,1)}, bf16[2048,128]{1,0:T(8,128)(2,1)}, u32[]{:S(2)}, u32[]{:S(2)}) collective-permute-start(bf16[2048,128]{1,0:T(8,128)(2,1)} %slice.1309), channel_id=1, source_target_pairs={{0,16},{4,20},{8,24},{12,28},{16,0},{20,4},{24,8},{28,12},{1,17},{... | collective-permute-start | bytes 1572872 | tf_op jit(solution)/shard_map/ppermute | solution.py:38
  736.6 20.3 %collective-permute-start.58 = (bf16[1120,256]{1,0:T(8,128)(2,1)S(1)}, bf16[1120,256]{1,0:T(8,128)(2,1)S(1)}, u32[]{:S(2)}, u32[]{:S(2)}) collective-permute-start(bf16[1120,256]{1,0:T(8,128)(2,1)S(1)} %slice.1308), channel_id=1, source_target_pairs={{0,8},{4,12},{8,0},{12,4},{16,24},{20,28},{24,16},{28,20},{1,9},{5... | collective-permute-start | bytes 1720328 | tf_op jit(solution)/shard_map/ppermute | solution.py:38
  757.2 15.3 %collective-permute-start.60 = (bf16[1120,128]{1,0:T(8,128)(2,1)S(1)}, bf16[1120,128]{1,0:T(8,128)(2,1)S(1)}, u32[]{:S(2)}, u32[]{:S(2)}) collective-permute-start(bf16[1120,128]{1,0:T(8,128)(2,1)S(1)} %slice.1318), channel_id=1, source_target_pairs={{0,16},{4,20},{8,24},{12,28},{16,0},{20,4},{24,8},{28,12},{1,17},{... | collective-permute-start | bytes 860168 | tf_op jit(solution)/shard_map/ppermute | solution.py:38
  758.8 17.5 %collective-permute-start.61 = (bf16[2,8,256,128]{3,2,1,0:T(8,128)(2,1)}, bf16[2,8,256,128]{3,2,1,0:T(8,128)(2,1)}, u32[]{:S(2)}, u32[]{:S(2)}) collective-permute-start(bf16[2,8,256,128]{3,2,1,0:T(8,128)(2,1)} %get-tuple-element.450), channel_id=1, source_target_pairs={{0,1},{1,0},{2,3},{3,2},{4,5},{5,4},{6,7},{7,6},{8,9},{9,8},{10,11... | collective-permute-start | bytes 3145736 | tf_op jit(solution)/shard_map/ppermute | solution.py:38
  (177 other events, 1988.0 us)

commit v7 on v6

--- a/solution.py
+++ b/solution.py
@@ -55,10 +55,10 @@
     return order
 
 
-def gather_blocks(piece, axis, beside=()):
+def gather_blocks(piece, axis, beside=(), stop=0):
     steps = []
     mask = lax.axis_size("dp") // 2
-    while mask:
+    while mask > stop:
         moved = swap(piece, "dp", mask)
         if len(steps) < len(beside):
             moved = beside[len(steps)](moved)
@@ -84,10 +84,27 @@
     return reduce_blocks(*split(total, 1, 2), beside[1:], mask)
 
 
+def reorder_kernel(sources, in_ref, out_ref):
+    width = in_ref.shape[1] // len(sources)
+    for p, q in enumerate(sources):
+        out_ref[:, p * width : (p + 1) * width] = in_ref[:, q * width : (q + 1) * width]
+
+
 def reorder(value, mask):
     order = block_order(lax.axis_size("dp"))
-    cols = split(value, 1, len(order))
-    return jnp.concatenate([cols[order.index(j ^ mask)] for j in order], axis=1)
+    sources = [order.index(j ^ mask) for j in order]
+    if value.shape[1] // len(order) % 128:
+        cols = split(value, 1, len(order))
+        return jnp.concatenate([cols[q] for q in sources], axis=1)
+    return pl.pallas_call(
+        functools.partial(reorder_kernel, sources),
+        name="reorder",
+        out_shape=jax.ShapeDtypeStruct(value.shape, value.dtype),
+        in_specs=[vmem()],
+        out_specs=vmem(),
+        compiler_params=params(60),
+        cost_estimate=cost(0, 2 * MIB),
+    )(value)
 
 
 def relative(value, x, c):
@@ -695,15 +712,14 @@
     halves(total, *refs[3 * count :])
 
 
-def table_grad_part(grads, inputs, part):
+def table_grad_part(grads, inputs):
     count = len(grads)
     rows = sum(g.shape[0] for g in grads)
-    slots = grads[0].shape[1] // 2
+    slots = grads[0].shape[1]
     block = 256
-    first = part * (slots // block)
     if rows > 4096:
         total = sum(
-            mm(split(g, 1, 2)[part], jnp.concatenate(v), TN) for g, v in zip(grads, inputs)
+            mm(g, jnp.concatenate(v), TN) for g, v in zip(grads, inputs)
         )
         keep, send = split(total, 1, 2)
         return keep, send.astype(lowp)
@@ -716,7 +732,7 @@
             jax.ShapeDtypeStruct((slots, D // 2), single),
             jax.ShapeDtypeStruct((slots, D // 2), lowp),
         ),
-        in_specs=[pl.BlockSpec((g.shape[0], block), lambda i: (0, first + i)) for g in grads]
+        in_specs=[pl.BlockSpec((g.shape[0], block), lambda i: (0, i)) for g in grads]
         + [pl.BlockSpec(v.shape, lambda i: (0, 0)) for v in inputs],
         out_specs=(
             pl.BlockSpec((block, D // 2), lambda i: (i, 0)),
@@ -874,10 +890,32 @@
     sizes = {"dp": dp_size, "head": head_size}
     row_axes = ("head", "dp", "head", "head", "dp", "head")
     col_axes = ("dp", "head", "dp", "dp", "head", "dp")
-    early = [jnp.sum(old) / sizes[axis] for old, axis in zip(rows_old, col_axes)]
-    early += [jnp.sum(weight * weight) for weight in weights_now]
-    gain_sums = jnp.sum(gains * gains, axis=1) / head_size
-    early = scalar_row(early + [gain_sums[0], gain_sums[1], gain_sums[2]])
+
+    def early_sums(dep):
+        _, *tied = together(dep, *rows_old, *weights_now, gains)
+        sums = [jnp.sum(old) / sizes[axis] for old, axis in zip(tied[:6], col_axes)]
+        sums += [jnp.sum(weight * weight) for weight in tied[6:12]]
+        gain_sums = jnp.sum(tied[12] * tied[12], axis=1) / head_size
+        return scalar_row(sums + [gain_sums[0], gain_sums[1], gain_sums[2]])
+
+    def core_sum(keep, send):
+        more = swap(send.astype(lowp), "head", 1)
+        return keep.astype(single) + more.astype(single)
+
+    def stream_sum(part, beside=()):
+        keep, send = split(part, 0, 2)
+        more, *beside = together(swap(send.astype(lowp), "head", 2), *beside)
+        part = keep + more.astype(single)
+        return (part, beside) if beside else part
+
+    def group_sum(part, beside=()):
+        return stream_sum(core_sum(*split(part, 0, 2)), beside)
+
+    def group_both(part, beside=()):
+        far, *beside = together(swap(part, "head", 2), *beside)
+        pair = jnp.concatenate([part, far], axis=0)
+        both = (pair, swap(pair, "head", 1))
+        return (both, beside) if beside else both
 
     flat = jnp.concatenate(
         [
@@ -967,73 +1005,60 @@
     hidden_own = wup.shape[1]
     pack_two = jnp.concatenate([wup.astype(lowp).T, wdown.astype(lowp)])
 
+    old_normed = state_norm(place, gain_vals[0], old_states, RATE)
+
     def beside_old(moved):
-        old_normed = state_norm(place, gain_vals[0], old_states, RATE)
-        moved, kept["looked"], kept["old"] = together(moved, kept["looked"], old_normed)
+        moved, looked, kept["old"] = together(moved, kept["looked"], old_normed)
+        kept["embedded"], kept["normed"] = place_embedding(place, looked, gain_vals[0])
         return moved
 
     def beside_compress(moved):
         moved, *kept["comp"] = together(moved, *compress(kept["old"], own_one, full_conv))
         return moved
 
-    own_two, steps_two = gather_blocks(
-        after(pack_two, steps_one[1]), 1, (beside_old, beside_compress)
+    near_two, steps_two = gather_blocks(
+        after(pack_two, steps_one[1]), 1, (beside_old, beside_compress), 1
     )
+    near_up, near_down = split(near_two, 0, 2)
+    far_up, far_down = swap(near_up, "dp", 1), swap(near_down, "dp", 1)
     mem_normed, old_normed = kept["mem"], kept["old"]
+    embedded_low = kept["embedded"]
+    embedded = embedded_low.astype(single)
+    normed = jnp.concatenate(group_both(kept["normed"]))
     comp, old_raw = kept["comp"]
 
     words = vocab // reach
     z = d // 2
     z_groups = [[2 * i + b for i in range(reach)] for b in range(2)]
-    low_table = after(table.astype(lowp), steps_two[1]).reshape(reach, words, width)
-    low_table = lax.all_to_all(low_table, "dp", 0, 0, axis_index_groups=z_groups)
     slots = -(-words // 256) * 256
 
-    embedded_low, normed = place_embedding(place, kept["looked"], gain_vals[0])
-    embedded = embedded_low.astype(single)
 
     comp_counts = jnp.where(x == 1, jnp.flip(comp_fill), comp_fill)
     mem_counts = jnp.where(x == 1, jnp.flip(mem_fill), mem_fill)
-    info = jnp.stack([comp_counts[0], mem_counts[0], comp_counts[1], mem_counts[1], c * half])
-    info = info.astype(jnp.int32)
-
-    def core_sum(keep, send):
-        more = swap(send.astype(lowp), "head", 1)
-        return keep.astype(single) + more.astype(single)
-
-    def stream_sum(part, beside=()):
-        keep, send = split(part, 0, 2)
-        more, *beside = together(swap(send.astype(lowp), "head", 2), *beside)
-        part = keep + more.astype(single)
-        return (part, beside) if beside else part
-
-    def group_sum(part, beside=()):
-        return stream_sum(core_sum(*split(part, 0, 2)), beside)
-
-    def group_both(part, beside=()):
-        far, *beside = together(swap(part, "head", 2), *beside)
-        pair = jnp.concatenate([part, far], axis=0)
-        both = (pair, swap(pair, "head", 1))
-        return (both, beside) if beside else both
-
-    normed = jnp.concatenate(group_both(normed))
+    info = [comp_counts[0], mem_counts[0], comp_counts[1], mem_counts[1], c * half]
+    lane = jnp.arange(8, dtype=jnp.int32)
+    info = sum(jnp.where(lane == i, value, 0) for i, value in enumerate(info)).astype(jnp.int32)
+
     in_weight = own_one[: 3 * wide]
     mem = mm(mem_normed, own_one[wide : 3 * wide], NT).astype(lowp)
     seg = mm(normed, in_weight, NT).astype(lowp).reshape(2, streams, half, 3 * wide)
+    low_table = after(table.astype(lowp), seg).reshape(reach, words, width)
+    low_table = lax.all_to_all(low_table, "dp", 0, 0, axis_index_groups=z_groups)
     mixed, lse = attend(info, seg, comp, mem)
     mixed = mixed.reshape(-1, wide)
-    attn_sum, (own_codes, own_count, own_two, low_table) = group_sum(
-        mm(mixed, own_one[3 * wide : 4 * wide]),
-        (*own_list(after(token_codes, mixed)), own_two, low_table),
+    attn_sum, (early, far_up) = group_sum(
+        mm(mixed, own_one[3 * wide : 4 * wide]), (early_sums(mixed), far_up)
     )
     after_attn = embedded + attn_sum
     ffn_in, inv_second = rms(after_attn, gain_vals[1])
-    ffn_in = jnp.concatenate(group_both(ffn_in))
-    full_up, full_down = split(own_two, 0, 2)
+    ffn_in, (far_down, low_table) = group_both(ffn_in, (far_down, low_table))
     near_table = [
         lax.dynamic_index_in_dim(low_table, z ^ (m // 2), 0, keepdims=False) for m in order[:reach]
     ]
     near_table = jnp.concatenate(near_table, axis=1)
+    ffn_in = jnp.concatenate(ffn_in)
+    full_up = jnp.concatenate([near_up, far_up], axis=1)
+    full_down = jnp.concatenate([near_down, far_down], axis=1)
     far_table = swap(near_table, "dp", 1)
     loss_table = jnp.concatenate([near_table, far_table], axis=1)
     loss_table = jnp.concatenate([loss_table, jnp.zeros((slots - words, D), lowp)], axis=0)
@@ -1068,7 +1093,9 @@
         joined = jnp.concatenate(pieces) if len(pieces) > 1 else pieces[0]
         moved = swap(reorder(joined, mask), "dp", mask)
         if len(pieces) == 1:
-            moved, loss_table, early = together(moved, loss_table, early)
+            moved, own_codes, own_count = together(
+                moved, *own_list(after(token_codes, final_in))
+            )
             next_chunk()
         elif len(pieces) == 2:
             moved, stats[0] = together(moved, stats[0])
@@ -1113,26 +1140,24 @@
         count = len(parts) // 2
         moved = jnp.concatenate([part.astype(lowp) for part in parts[count:]])
         moved = swap(reorder(moved, mask), "dp", mask)
-        if len(table_parts) < 2:
-            more = table_grad_part(dlogits, chunks, len(table_parts))
-            moved, *more = together(moved, *more, *[part[1] for part in table_parts])
-            table_parts = [(part[0], done) for part, done in zip(table_parts, more[2:])]
-            table_parts.append((more[0], swap(more[1], "dp", 1)))
+        if mask == 2:
+            moved, dlogits[0] = together(moved, dlogits[0])
+        elif mask == 4:
+            moved, *table_parts = together(moved, *table_grad_part(dlogits, chunks))
         moved = split(moved.astype(single), 0, count)
         parts = [part + more for part, more in zip(parts, moved)]
         mask *= 2
     final_grad = parts[0]
 
     grad_after_ffn = rms_back(after_ffn, inv_third, gain_vals[2], final_grad)
-    moved_table = [part[1] for part in table_parts]
-    down_in, (moved_table[1],) = group_both(grad_after_ffn.astype(lowp), (moved_table[1],))
+    moved_table = swap(table_parts[1], "dp", 1)
+    down_in = group_both(grad_after_ffn.astype(lowp))
     down_in = jnp.concatenate(down_in)
     act_grad = mm(down_in, full_down, NT)
     pre_grad = jax.vjp(jax.nn.gelu, hidden_pre)[1](act_grad)[0].astype(lowp)
     two = hidden_grads(pre_grad, hidden_act, ffn_in, down_in)
-    ffn_in_grad, two = group_sum(mm(pre_grad, full_up), two)
-    keep = [part + more.astype(single) for (part, _), more in zip(table_parts, moved_table)]
-    keep = jnp.concatenate(keep)
+    ffn_in_grad, (*two, moved_table) = group_sum(mm(pre_grad, full_up), (*two, moved_table))
+    keep = table_parts[0] + moved_table.astype(single)
     table_pieces = jnp.stack(split(keep[:words].astype(lowp), 1, reach))
     position = [order.index(2 * i) for i in range(reach)]
     position = jnp.asarray(position, jnp.int32)[jnp.arange(reach) ^ z]
@@ -1145,17 +1170,22 @@
 
     mixed_grad = mm(attn_in, own_one[3 * wide : 4 * wide], NT).astype(lowp)
     mixed_grad = mixed_grad.reshape(2, streams, half, wide)
-    def beside_attend(moved):
-        grads = attend_back(info, seg, comp, mem, lse, mixed_grad)
-        moved, kept["table"], *kept["grads"] = together(moved, table_pieces, *grads)
+    seg_grad, comp_grad, mem_grad = attend_back(info, seg, comp, mem, lse, mixed_grad)
+    seg_grad = seg_grad.reshape(-1, 3 * wide)
+
+    def beside_expand(moved):
+        keep, send = split(mm(seg_grad, in_weight), 0, 2)
+        more = swap(send.astype(lowp), "head", 1)
+        moved, more, *kept["old"] = together(
+            moved, more, *expand(comp_grad, old_raw, full_conv)
+        )
+        kept["seg_in"] = split(keep + more.astype(single), 0, 2)
         return moved
 
     def beside_sums(moved):
-        seg_grad, comp_grad, mem_grad = kept["grads"]
-        seg_grad = seg_grad.reshape(-1, 3 * wide)
-        seg_in = core_sum(*split(mm(seg_grad, in_weight), 0, 2))
-        seg_in_far = swap(seg_in[half:].astype(lowp), "head", 2)
-        old_grad, conv_sum = expand(comp_grad, old_raw, full_conv)
+        seg_in, seg_in_far = kept["seg_in"]
+        seg_in_far = swap(seg_in_far.astype(lowp), "head", 2)
+        old_grad, conv_sum = kept["old"]
         sums = attn_grads(
             seg_grad,
             mixed,
@@ -1168,9 +1198,11 @@
         )
         conv_sum = split(conv_block_order(conv_sum), 1, 2)
         sums = [jnp.concatenate([part, more.astype(part.dtype)]) for part, more in zip(sums, conv_sum)]
-        moved, seg_in_far, *kept["sums"] = together(moved, seg_in_far, *sums)
+        moved, kept["table"], seg_in_far, *kept["sums"] = together(
+            moved, table_pieces, seg_in_far, *sums
+        )
         rows_grad = embed_back(
-            place, embedded_low, gain_vals[0], seg_in[:half], seg_in_far, grad_after_attn
+            place, embedded_low, gain_vals[0], seg_in, seg_in_far, grad_after_attn
         )
         kept["rows"] = lax.all_to_all(rows_grad, "dp", 0, 0)
         return moved
@@ -1184,7 +1216,7 @@
         kept["rows"] = jnp.stack([kept["rows"], far])
         return moved
 
-    two = reduce_blocks(*two, (beside_attend, beside_sums))
+    two = reduce_blocks(*two, (beside_expand, beside_sums))
     one = reduce_blocks(*kept["sums"], (beside_rows, beside_streams))
     rows_grad = kept["rows"]
     rows_grad = jnp.stack([rows_grad, swap(rows_grad, "head", 1)]).reshape(-1, width)

time: 897 us -> 891 us (level)
  waiting for transfers between devices: 219 us -> 194 us
  local copies, waits for them, and re-layouts: 99.7 us -> 112 us
  other arithmetic: 146 us -> 156 us
    ppermute x70, waiting for transfers between devices: 206 us -> 168 us  [swap(): return lax.ppermute(value, axis, [(i, i ^ mask) for i in range(size)])]
    unnamed x308 -> x368, local copies, waits for them, and re-layouts: 44.3 us -> 37.9 us
    pallas_call x2 -> x1, Pallas kernels: 29.1 us -> 24.2 us  [table_grad_part(): pl.pallas_call(functools.partial(table_grad_kernel, count), name='table_g...]
  transfers between devices with their start and end apart: 74 -> 74, of which waited for: 44 -> 44; matrix products, arithmetic and copies ran while one was open for 19% -> 22% of each run, Pallas kernels for 25% -> 25%
where the time goes in v7:
time: 891 us; the launch traced here: 883 us
  Pallas kernels  264 us (30%)
  waiting for transfers between devices  194 us (22%)
  other arithmetic  156 us (18%)
  local copies, waits for them, and re-layouts  112 us (13%)
  starting transfers between devices  75.5 us (8%)
  matrix products  39.1 us (4%)
  between operations  33.9 us (4%)
  blocking collectives  8.93 us (1%)
    ppermute x70, waiting for transfers between devices, swap(): return lax.ppermute(value, axis, [(i, i ^ mask) for i in range(size)])  168 us
    ppermute x70, starting transfers between devices, swap(): return lax.ppermute(value, axis, [(i, i ^ mask) for i in range(size)])  59.2 us
    pallas_call x4, Pallas kernels, logits_back(): pl.pallas_call(functools.partial(logits_back_kernel, tiles), name='logits...  44.4 us
    pallas_call x4, Pallas kernels, logits_part(): pl.pallas_call(functools.partial(logits_kernel, words, tiles), name='logi...  44 us
    dot_general x11, matrix products, mm(): return lax.dot_general(left, right, dims, preferred_element_type=single)  39.1 us
    unnamed x368, local copies, waits for them, and re-layouts  37.9 us
    pallas_call x1, Pallas kernels, table_grad_part(): pl.pallas_call(functools.partial(table_grad_kernel, count), name='table_g...  24.2 us
    pallas_call x1, Pallas kernels, own_list(): pl.pallas_call(list_kernel, name='own_list', out_shape=(jax.ShapeDtypeStr...  21.4 us
  transfers between devices with their start and end apart: 74, of which 44 were waited for; matrix products, arithmetic and copies ran while one was open for 22% of the time, Pallas kernels for 25%

profile of v7, /device:TPU:0, one launch (start us, length us, event | category | flops | bytes accessed | tf_op | source)
XLA Modules:
  0.0 883.4 jit_solution(2458467306667223108)
XLA Ops:
  25.9 8.6 lookup.2
  34.6 8.6 lookup.3
  79.2 9.9 %state_norm.3.old_ref = bf16[3,1024,1024]{2,1,0:T(8,128)(2,1)} custom-call(s32[2]{0:T(128)} %pad_add_fusion.place_ref, f32[1,1024]{1,0:T(1,128)} %bitcast.350, bf16[2,1536,1024]{2,1,0:T(8,128)(2,1)} %in_ref.3), custom_call_target="tpu_custom_call" | custom-call | bytes 251658 | tf_op jit(solution)/shard_map/state_norm/pallas_call | solution.py:345
  89.9 15.4 %collective-permute-done.7 = bf16[2048,128]{1,0:T(8,128)(2,1)} collective-permute-done((bf16[2048,128]{1,0:T(8,128)(2,1)S(1)}, bf16[2048,128]{1,0:T(8,128)(2,1)}, u32[]{:S(2)}, u32[]{:S(2)}) %collective-permute-start.7) | collective-permute-done | bytes 524320 | tf_op jit(solution)/shard_map/ppermute | solution.py:38
  126.6 12.2 %compress.1 = (bf16[1024,512]{1,0:T(8,128)(2,1)}, bf16[3,1024,512]{2,1,0:T(8,128)(2,1)}) custom-call(bf16[3,1024,1024]{2,1,0:T(8,128)(2,1)} %state_norm.3.old_ref, bf16[1120,1024]{1,0:T(8,128)(2,1)} %copy-done.4, bf16[1120,1024]{1,0:T(8,128)(2,1)} %copy-done.4, bf16[2,384,128]{2,1,0:T(8,128)(2,1)} %bitcast.319), custom_call_target="tpu_custom_call" | custom-call | flops 64424508 | bytes 251658 | tf_op jit(solution)/shard_map/compress/pallas_call | solution.py:387
  149.2 10.9 %attend.1 = (bf16[2,2,256,256]{3,2,1,0:T(8,128)(2,1)}, f32[2,2,512,1]{3,2,1,0:T(8,128)}) custom-call(s32[8]{0:T(128)} %fusion.106.info_ref, bf16[2,2,256,768]{3,2,1,0:T(8,128)(2,1)} %bitcast.305, bf16[2,2,256,768]{3,2,1,0:T(8,128)(2,1)} %bitcast.306, bf16[2,2,256,768]{3,2,1,0:T(8,128)(2,1)} %bitcast.307, bf16[1024,512]{1,0:T(8,128)(2,1)} %get-tuple-element.163.kc_ref.vc_ref, ...), custom_call_target="tpu_custom_call" | custom-call | flops 146800640 | bytes 125829 | tf_op jit(solution)/shard_map/attend/pallas_call | solution.py:539
  204.1 12.6 %collective-permute-done.16 = bf16[1024,512]{1,0:T(8,128)(2,1)} collective-permute-done((bf16[1024,512]{1,0:T(8,128)(2,1)}, bf16[1024,512]{1,0:T(8,128)(2,1)}, u32[]{:S(2)}, u32[]{:S(2)}) %collective-permute-start.16) | collective-permute-done | bytes 1048608 | tf_op jit(solution)/shard_map/ppermute | solution.py:38
  250.7 9.1 %collective-permute-done.19 = bf16[256,1024]{1,0:T(8,128)(2,1)S(1)} collective-permute-done((bf16[256,1024]{1,0:T(8,128)(2,1)S(1)}, bf16[256,1024]{1,0:T(8,128)(2,1)S(1)}, u32[]{:S(2)}, u32[]{:S(2)}) %collective-permute-start.19) | collective-permute-done | bytes 524320 | tf_op jit(solution)/shard_map/ppermute | solution.py:38
  265.5 21.4 %own_list.1 = (s32[8200]{0:T(1024)}, s32[1]{0:T(128)}) custom-call(s32[8192]{0:T(1024)} %get-tuple-element.185.code_ref), custom_call_target="tpu_custom_call" | custom-call | bytes 1258291 | tf_op jit(solution)/shard_map/own_list/pallas_call | solution.py:201
  306.6 11.2 %logits_part.4 = (bf16[1024,2048]{1,0:T(8,128)(2,1)}, f32[8,1024]{1,0:T(8,128)}) custom-call(f32[8,1024]{1,0:T(8,128)} %squeeze.188.info_ref, bf16[512,1024]{1,0:T(8,128)(2,1)} %copy-done.10, bf16[512,1024]{1,0:T(8,128)(2,1)} %collective-permute-done.24.near_ref.refs_5_, bf16[2048,1024]{1,0:T(8,128)(2,1)} %concatenate.161.table_ref), custom_call_target="tpu_custom_call" | custom-call | flops 171798688 | bytes 209715 | tf_op jit(solution)/shard_map/logits_part/pallas_call | solution.py:621
  325.1 10.9 %logits_part.5 = (bf16[1024,2048]{1,0:T(8,128)(2,1)}, f32[8,1024]{1,0:T(8,128)}) custom-call(f32[8,1024]{1,0:T(8,128)} %squeeze.193.info_ref, bf16[512,1024]{1,0:T(8,128)(2,1)} %copy-done.18, bf16[512,1024]{1,0:T(8,128)(2,1)} %collective-permute-done.27.near_ref.refs_7_, bf16[2048,1024]{1,0:T(8,128)(2,1)} %concatenate.161.table_ref), custom_call_target="tpu_custom_call" | custom-call | flops 171798688 | bytes 209715 | tf_op jit(solution)/shard_map/logits_part/pallas_call | solution.py:621
  341.2 10.9 %logits_part.6 = (bf16[1024,2048]{1,0:T(8,128)(2,1)}, f32[8,1024]{1,0:T(8,128)}) custom-call(f32[8,1024]{1,0:T(8,128)} %squeeze.194.info_ref, bf16[512,1024]{1,0:T(8,128)(2,1)} %copy-done.11, bf16[512,1024]{1,0:T(8,128)(2,1)} %collective-permute-done.29.near_ref.refs_9_, bf16[2048,1024]{1,0:T(8,128)(2,1)} %concatenate.161.table_ref), custom_call_target="tpu_custom_call" | custom-call | flops 171798688 | bytes 209715 | tf_op jit(solution)/shard_map/logits_part/pallas_call | solution.py:621
  364.0 11.0 %logits_part.7 = (bf16[1024,2048]{1,0:T(8,128)(2,1)}, f32[8,1024]{1,0:T(8,128)}) custom-call(f32[8,1024]{1,0:T(8,128)} %squeeze.178.info_ref, bf16[512,1024]{1,0:T(8,128)(2,1)} %copy-done.12, bf16[512,1024]{1,0:T(8,128)(2,1)} %collective-permute-done.30.near_ref.refs_11_, bf16[2048,1024]{1,0:T(8,128)(2,1)} %concatenate.161.table_ref), custom_call_target="tpu_custom_call" | custom-call | flops 171798688 | bytes 209715 | tf_op jit(solution)/shard_map/logits_part/pallas_call | solution.py:621
  394.0 11.0 %logits_back.4 = (bf16[1024,2048]{1,0:T(8,128)(2,1)}, bf16[512,1024]{1,0:T(8,128)(2,1)}, bf16[512,1024]{1,0:T(8,128)(2,1)}) custom-call(f32[8,1024]{1,0:T(8,128)} %squeeze.178.info_ref, f32[8,1024]{1,0:T(8,128)} %broadcast_in_dim.215.factor_ref, bf16[1024,2048]{1,0:T(8,128)(2,1)} %get-tuple-element.202.in_ref, bf16[2048,1024]{1,0:T(8,128)(2,1)} %concatenate.161.table_ref), custom_call_target="tpu_custom_call" | custom-call | flops 171798688 | bytes 251658 | tf_op jit(solution)/shard_map/logits_back/pallas_call | solution.py:674
  412.7 11.0 %logits_back.5 = (bf16[1024,2048]{1,0:T(8,128)(2,1)}, bf16[512,1024]{1,0:T(8,128)(2,1)}, bf16[512,1024]{1,0:T(8,128)(2,1)}) custom-call(f32[8,1024]{1,0:T(8,128)} %squeeze.194.info_ref, f32[8,1024]{1,0:T(8,128)} %broadcast_in_dim.217.factor_ref, bf16[1024,2048]{1,0:T(8,128)(2,1)} %get-tuple-element.205.in_ref, bf16[2048,1024]{1,0:T(8,128)(2,1)} %concatenate.161.table_ref), custom_call_target="tpu_custom_call" | custom-call | flops 171798688 | bytes 251658 | tf_op jit(solution)/shard_map/logits_back/pallas_call | solution.py:674
  433.5 11.4 %logits_back.6 = (bf16[1024,2048]{1,0:T(8,128)(2,1)}, bf16[512,1024]{1,0:T(8,128)(2,1)}, bf16[512,1024]{1,0:T(8,128)(2,1)}) custom-call(f32[8,1024]{1,0:T(8,128)} %squeeze.193.info_ref, f32[8,1024]{1,0:T(8,128)} %broadcast_in_dim.219.factor_ref, bf16[1024,2048]{1,0:T(8,128)(2,1)} %get-tuple-element.211.in_ref, bf16[2048,1024]{1,0:T(8,128)(2,1)} %concatenate.161.table_ref), custom_call_target="tpu_custom_call" | custom-call | flops 171798688 | bytes 251658 | tf_op jit(solution)/shard_map/logits_back/pallas_call | solution.py:674
  456.5 11.0 %logits_back.7 = (bf16[1024,2048]{1,0:T(8,128)(2,1)}, bf16[512,1024]{1,0:T(8,128)(2,1)}, bf16[512,1024]{1,0:T(8,128)(2,1)}) custom-call(f32[8,1024]{1,0:T(8,128)} %squeeze.188.info_ref, f32[8,1024]{1,0:T(8,128)} %broadcast_in_dim.221.factor_ref, bf16[1024,2048]{1,0:T(8,128)(2,1)} %get-tuple-element.217.in_ref, bf16[2048,1024]{1,0:T(8,128)(2,1)} %concatenate.161.table_ref), custom_call_target="tpu_custom_call" | custom-call | flops 171798688 | bytes 251658 | tf_op jit(solution)/shard_map/logits_back/pallas_call | solution.py:674
  467.7 13.3 %collective-permute-done.43 = bf16[512,1024]{1,0:T(8,128)(2,1)S(1)} collective-permute-done((bf16[512,1024]{1,0:T(8,128)(2,1)}, bf16[512,1024]{1,0:T(8,128)(2,1)S(1)}, u32[]{:S(2)}, u32[]{:S(2)}) %collective-permute-start.43) | collective-permute-done | bytes 1048608 | tf_op jit(solution)/shard_map/ppermute | solution.py:38
  492.0 24.2 %table_grad_part.1 = (f32[2048,512]{1,0:T(8,128)}, bf16[2048,512]{1,0:T(8,128)(2,1)}) custom-call(bf16[1024,2048]{1,0:T(8,128)(2,1)} %get-tuple-element.228.refs_0_, bf16[1024,2048]{1,0:T(8,128)(2,1)} %get-tuple-element.229.refs_1_, bf16[1024,2048]{1,0:T(8,128)(2,1)} %get-tuple-element.230.refs_2_, bf16[1024,2048]{1,0:T(8,128)(2,1)} %get-tuple-element.231.refs_3_, ...), custom_call_target="tpu_custom_call" | custom-call | flops 515396064 | bytes 629145 | tf_op jit(solution)/shard_map/table_grad_part/pallas_call | solution.py:727
  519.7 11.5 %collective-permute-done.45 = bf16[256,1024]{1,0:T(8,128)(2,1)S(1)} collective-permute-done((bf16[256,1024]{1,0:T(8,128)(2,1)S(1)}, bf16[256,1024]{1,0:T(8,128)(2,1)S(1)}, u32[]{:S(2)}, u32[]{:S(2)}) %collective-permute-start.45) | collective-permute-done | bytes 524320 | tf_op jit(solution)/shard_map/ppermute | solution.py:38
  574.4 11.5 %hidden_grads.1 = (f32[2048,512]{1,0:T(8,128)}, bf16[2048,512]{1,0:T(8,128)(2,1)}) custom-call(bf16[1024,1024]{1,0:T(8,128)(2,1)} %copy-done.59, bf16[1024,1024]{1,0:T(8,128)(2,1)} %copy-done.58, bf16[1024,1024]{1,0:T(8,128)(2,1)} %pad_maximum_fusion.2.in_ref, bf16[1024,1024]{1,0:T(8,128)(2,1)} %pad_maximum_fusion.5.down_ref), custom_call_target="tpu_custom_call" | custom-call | flops 128849016 | bytes 335544 | tf_op jit(solution)/shard_map/hidden_grads/pallas_call | solution.py:762
  595.0 9.4 %collective-permute-done.51 = bf16[256,1024]{1,0:T(8,128)(2,1)S(1)} collective-permute-done((bf16[256,1024]{1,0:T(8,128)(2,1)S(1)}, bf16[256,1024]{1,0:T(8,128)(2,1)S(1)}, u32[]{:S(2)}, u32[]{:S(2)}) %collective-permute-start.51) | collective-permute-done | bytes 524320 | tf_op jit(solution)/shard_map/ppermute | solution.py:38
  611.3 15.2 %attend_back.1 = (bf16[2,2,256,768]{3,2,1,0:T(8,128)(2,1)}, bf16[1024,512]{1,0:T(8,128)(2,1)}, bf16[1024,512]{1,0:T(8,128)(2,1)}) custom-call(s32[8]{0:T(128)} %fusion.106.info_ref, bf16[2,2,256,768]{3,2,1,0:T(8,128)(2,1)} %bitcast.308, bf16[2,2,256,768]{3,2,1,0:T(8,128)(2,1)} %bitcast.309, bf16[2,2,256,768]{3,2,1,0:T(8,128)(2,1)} %bitcast.310, ...), custom_call_target="tpu_custom_call" | custom-call | flops 230686720 | bytes 188743 | tf_op jit(solution)/shard_map/attend_back/pallas_call | solution.py:562
  668.3 14.1 %attn_grads.1 = (f32[1024,512]{1,0:T(8,128)}, bf16[1024,512]{1,0:T(8,128)(2,1)}) custom-call(bf16[1024,768]{1,0:T(8,128)(2,1)} %bitcast.322, bf16[1024,256]{1,0:T(8,128)(2,1)} %bitcast.317, bf16[1024,512]{1,0:T(8,128)(2,1)} %get-tuple-element.251.mem_ref, bf16[3072,512]{1,0:T(8,128)(2,1)} %bitcast.318, bf16[1024,1024]{1,0:T(8,128)(2,1)} %pad_maximum_fusion.1.normed_ref, ...), custom_call_target="tpu_custom_call" | custom-call | flops 188743680 | bytes 503316 | tf_op jit(solution)/shard_map/attn_grads/pallas_call | solution.py:812
  686.8 10.5 %collective-permute-done.54 = bf16[2048,256]{1,0:T(8,128)(2,1)S(1)} collective-permute-done((bf16[2048,256]{1,0:T(8,128)(2,1)}, bf16[2048,256]{1,0:T(8,128)(2,1)S(1)}, u32[]{:S(2)}, u32[]{:S(2)}) %collective-permute-start.54) | collective-permute-done | bytes 1048608 | tf_op jit(solution)/shard_map/ppermute | solution.py:38
  718.3 20.3 %all-to-all-done.3 = bf16[8,256,128]{2,1,0:T(8,128)(2,1)} async-done(((bf16[8,256,128]{2,1,0:T(8,128)(2,1)}), bf16[8,256,128]{2,1,0:T(8,128)(2,1)}, u32[]{:S(2)}, u32[]{:S(2)}) %all-to-all-start.3) | async-done | bytes 524320 | tf_op jit(solution)/shard_map/all_to_all | solution.py:1207
  744.2 11.0 %collective-permute-done.59 = bf16[8,256,128]{2,1,0:T(8,128)(2,1)S(1)} collective-permute-done((bf16[8,256,128]{2,1,0:T(8,128)(2,1)}, bf16[8,256,128]{2,1,0:T(8,128)(2,1)S(1)}, u32[]{:S(2)}, u32[]{:S(2)}) %collective-permute-start.59) | collective-permute-done | bytes 524320 | tf_op jit(solution)/shard_map/ppermute | solution.py:38
  759.9 11.3 %collective-permute-done.60 = bf16[1120,128]{1,0:T(8,128)(2,1)S(1)} collective-permute-done((bf16[1120,128]{1,0:T(8,128)(2,1)S(1)}, bf16[1120,128]{1,0:T(8,128)(2,1)S(1)}, u32[]{:S(2)}, u32[]{:S(2)}) %collective-permute-start.60) | collective-permute-done | bytes 286752 | tf_op jit(solution)/shard_map/ppermute | solution.py:38
  778.3 12.5 %scatter.1 = f32[8000,128]{1,0:T(8,128)} custom-call(s32[1]{0:T(128)} %get-tuple-element.263.count_ref, s32[8200]{0:T(1024)} %get-tuple-element.264.code_ref, f32[8000,128]{1,0:T(8,128)} %bitcast_convert_fusion.base_ref, bf16[8192,128]{1,0:T(8,128)(2,1)} %bitcast.313), custom_call_target="tpu_custom_call" | custom-call | bytes 629145 | tf_op jit(solution)/shard_map/scatter/pallas_call | solution.py:297
  794.5 8.9 %all-reduce.1 = (f32[128]{0:T(128)S(1)}, f32[3,128]{1,0:T(4,128)S(1)}, f32[128]{0:T(128)S(1)}, f32[16]{0:T(128)S(1)}, f32[128]{0:T(128)S(1)}, /*index=5*/f32[128...) all-reduce(f32[128]{0:T(128)S(1)} %get-tuple-element.386, ...), channel_id=1, replica_groups=mesh['dp'=8,'head'=4] {'head'}, use_global_device_ids=true, to_apply=%region_23.24 | all-reduce | flops 1424 | bytes 11392 | tf_op jit(solution)/shard_map/psum | solution.py:1255
  829.1 7.1 multiply_reduce_fusion
  872.6 7.8 divide_subtract_fusion
  (796 shorter events, 463.6 us)
Async XLA Ops:
  20.6 22.7 %collective-permute-start.3 = (bf16[1120,128]{1,0:T(8,128)(2,1)S(1)}, bf16[1120,128]{1,0:T(8,128)(2,1)S(1)}, u32[]{:S(2)}, u32[]{:S(2)}) collective-permute-start(bf16[1120,128]{1,0:T(8,128)(2,1)S(1)} %pad_maximum_fusion.31), channel_id=1, source_target_pairs={{0,16},{4,20},{8,24},{12,28},{16,0},{20,4},{24,8},{28,12},{1,17},{... | collective-permute-start | bytes 860168 | tf_op jit(solution)/shard_map/ppermute | solution.py:38
  44.9 15.5 %collective-permute-start.4 = (bf16[1120,256]{1,0:T(8,128)(2,1)S(1)}, bf16[1120,256]{1,0:T(8,128)(2,1)}, u32[]{:S(2)}, u32[]{:S(2)}) collective-permute-start(bf16[1120,256]{1,0:T(8,128)(2,1)S(1)} %pad_maximum_fusion.29), channel_id=1, source_target_pairs={{0,8},{4,12},{8,0},{12,4},{16,24},{20,28},{24,16},{28,20},{1,9},{5... | collective-permute-start | bytes 1720328 | tf_op jit(solution)/shard_map/ppermute | solution.py:38
  64.6 40.7 %all-to-all-start = ((bf16[8,256,128]{2,1,0:T(8,128)(2,1)}), bf16[8,256,128]{2,1,0:T(8,128)(2,1)S(1)}, u32[]{:S(2)}, u32[]{:S(2)}) async-start(bf16[8,256,128]{2,1,0:T(8,128)(2,1)} %bitcast.26), calls=%async_computation | async-start | bytes 1048576 | tf_op jit(solution)/shard_map/all_to_all | solution.py:978
  70.5 43.3 %collective-permute-start.10 = (bf16[1120,512]{1,0:T(8,128)(2,1)}, bf16[1120,512]{1,0:T(8,128)(2,1)}, u32[]{:S(2)}, u32[]{:S(2)}) collective-permute-start(bf16[1120,512]{1,0:T(8,128)(2,1)} %get-tuple-element.471), channel_id=1, source_target_pairs={{0,4},{4,0},{8,12},{12,8},{16,20},{20,16},{24,28},{28,24},{1,5},{5... | collective-permute-start | bytes 3440648 | tf_op jit(solution)/shard_map/ppermute | solution.py:38
  73.1 32.2 %collective-permute-start.7 = (bf16[2048,128]{1,0:T(8,128)(2,1)S(1)}, bf16[2048,128]{1,0:T(8,128)(2,1)}, u32[]{:S(2)}, u32[]{:S(2)}) collective-permute-start(bf16[2048,128]{1,0:T(8,128)(2,1)S(1)} %pad_maximum_fusion.30), channel_id=1, source_target_pairs={{0,16},{4,20},{8,24},{12,28},{16,0},{20,4},{24,8},{28,12},{1,17},{... | collective-permute-start | bytes 1572872 | tf_op jit(solution)/shard_map/ppermute | solution.py:38
  111.9 30.8 %collective-permute-start.11 = (bf16[2048,256]{1,0:T(8,128)(2,1)}, bf16[2048,256]{1,0:T(8,128)(2,1)}, u32[]{:S(2)}, u32[]{:S(2)}) collective-permute-start(bf16[2048,256]{1,0:T(8,128)(2,1)} %pad_maximum_fusion.21), channel_id=1, source_target_pairs={{0,8},{4,12},{8,0},{12,4},{16,24},{20,28},{24,16},{28,20},{1,9},{5... | collective-permute-start | bytes 3145736 | tf_op jit(solution)/shard_map/ppermute | solution.py:38
  121.8 23.1 %collective-permute-start.9 = (bf16[512,1024]{1,0:T(8,128)(2,1)}, bf16[512,1024]{1,0:T(8,128)(2,1)}, u32[]{:S(2)}, u32[]{:S(2)}) collective-permute-start(bf16[512,1024]{1,0:T(8,128)(2,1)} %pad_maximum_fusion.20), channel_id=1, source_target_pairs={{0,1},{1,0},{2,3},{3,2},{4,5},{5,4},{6,7},{7,6},{8,9},{9,8},{10,11... | collective-permute-start | bytes 3145736 | tf_op jit(solution)/shard_map/ppermute | solution.py:38
  168.6 33.4 %collective-permute-start.14 = (bf16[1024,512]{1,0:T(8,128)(2,1)}, bf16[1024,512]{1,0:T(8,128)(2,1)}, u32[]{:S(2)}, u32[]{:S(2)}) collective-permute-start(bf16[1024,512]{1,0:T(8,128)(2,1)} %get-tuple-element.462), channel_id=1, source_target_pairs={{0,4},{4,0},{8,12},{12,8},{16,20},{20,16},{24,28},{28,24},{1,5},{5... | collective-permute-start | bytes 3145736 | tf_op jit(solution)/shard_map/ppermute | solution.py:38
  170.6 46.1 %collective-permute-start.16 = (bf16[1024,512]{1,0:T(8,128)(2,1)}, bf16[1024,512]{1,0:T(8,128)(2,1)}, u32[]{:S(2)}, u32[]{:S(2)}) collective-permute-start(bf16[1024,512]{1,0:T(8,128)(2,1)} %get-tuple-element.461), channel_id=1, source_target_pairs={{0,4},{4,0},{8,12},{12,8},{16,20},{20,16},{24,28},{28,24},{1,5},{5... | collective-permute-start | bytes 3145736 | tf_op jit(solution)/shard_map/ppermute | solution.py:38
  170.7 51.2 %all-to-all-start.1 = ((bf16[4,2000,128]{2,1,0:T(8,128)(2,1)}), bf16[4,2000,128]{2,1,0:T(8,128)(2,1)S(1)}, u32[]{:S(2)}, u32[]{:S(2)}) async-start(bf16[4,2000,128]{2,1,0:T(8,128)(2,1)} %bitcast.43), calls=%async_computation.1 | async-start | bytes 4096000 | tf_op jit(solution)/shard_map/all_to_all | solution.py:1046
  181.1 20.8 %collective-permute-start.13 = (bf16[256,1024]{1,0:T(8,128)(2,1)S(1)}, bf16[256,1024]{1,0:T(8,128)(2,1)}, u32[]{:S(2)}, u32[]{:S(2)}) collective-permute-start(bf16[256,1024]{1,0:T(8,128)(2,1)S(1)} %slice.1125), channel_id=1, source_target_pairs={{0,2},{1,3},{2,0},{3,1},{4,6},{5,7},{6,4},{7,5},{8,10},{9,11},{10,... | collective-permute-start | bytes 1572872 | tf_op jit(solution)/shard_map/ppermute | solution.py:38
  249.0 48.2 %collective-permute-start.25 = (bf16[2000,512]{1,0:T(8,128)(2,1)}, bf16[2000,512]{1,0:T(8,128)(2,1)}, u32[]{:S(2)}, u32[]{:S(2)}) collective-permute-start(bf16[2000,512]{1,0:T(8,128)(2,1)} %pad_maximum_fusion.8), channel_id=1, source_target_pairs={{0,4},{4,0},{8,12},{12,8},{16,20},{20,16},{24,28},{28,24},{1,5},{5... | collective-permute-start | bytes 6144008 | tf_op jit(solution)/shard_map/ppermute | solution.py:38
  260.3 28.0 %collective-permute-start.23 = (bf16[256,1024]{1,0:T(8,128)(2,1)S(1)}, bf16[256,1024]{1,0:T(8,128)(2,1)}, u32[]{:S(2)}, u32[]{:S(2)}) collective-permute-start(bf16[256,1024]{1,0:T(8,128)(2,1)S(1)} %multiply_convert_fusion.1.in_ref), channel_id=1, source_target_pairs={{0,2},{1,3},{2,0},{3,1},{4,6},{5,7},{6,4},{7,5},{8,10},{9,11},{10,... | collective-permute-start | bytes 1572872 | tf_op jit(solution)/shard_map/ppermute | solution.py:38
  263.8 24.5 %collective-permute-start.20 = (bf16[256,1024]{1,0:T(8,128)(2,1)}, bf16[256,1024]{1,0:T(8,128)(2,1)}, u32[]{:S(2)}, u32[]{:S(2)}) collective-permute-start(bf16[256,1024]{1,0:T(8,128)(2,1)} %reorder.4), channel_id=1, source_target_pairs={{0,16},{4,20},{8,24},{12,28},{16,0},{20,4},{24,8},{28,12},{1,17},{... | collective-permute-start | bytes 1572872 | tf_op jit(solution)/shard_map/ppermute | solution.py:38
  293.6 25.4 %collective-permute-start.22 = (bf16[512,1024]{1,0:T(8,128)(2,1)}, bf16[512,1024]{1,0:T(8,128)(2,1)}, u32[]{:S(2)}, u32[]{:S(2)}) collective-permute-start(bf16[512,1024]{1,0:T(8,128)(2,1)} %reorder.5), channel_id=1, source_target_pairs={{0,8},{4,12},{8,0},{12,4},{16,24},{20,28},{24,16},{28,20},{1,9},{5... | collective-permute-start | bytes 3145736 | tf_op jit(solution)/shard_map/ppermute | solution.py:38
  294.3 24.6 %collective-permute-start.21 = (bf16[256,1024]{1,0:T(8,128)(2,1)}, bf16[256,1024]{1,0:T(8,128)(2,1)}, u32[]{:S(2)}, u32[]{:S(2)}) collective-permute-start(bf16[256,1024]{1,0:T(8,128)(2,1)} %collective-permute-done.20), channel_id=1, source_target_pairs={{0,2},{1,3},{2,0},{3,1},{4,6},{5,7},{6,4},{7,5},{8,10},{9,11},{10,... | collective-permute-start | bytes 1572872 | tf_op jit(solution)/shard_map/ppermute | solution.py:38
  451.3 16.3 %collective-permute-start.40 = (bf16[256,1024]{1,0:T(8,128)(2,1)S(1)}, bf16[256,1024]{1,0:T(8,128)(2,1)}, u32[]{:S(2)}, u32[]{:S(2)}) collective-permute-start(bf16[256,1024]{1,0:T(8,128)(2,1)S(1)} %slice.1121), channel_id=1, source_target_pairs={{0,2},{1,3},{2,0},{3,1},{4,6},{5,7},{6,4},{7,5},{8,10},{9,11},{10,... | collective-permute-start | bytes 1572872 | tf_op jit(solution)/shard_map/ppermute | solution.py:38
  455.8 25.1 %collective-permute-start.43 = (bf16[512,1024]{1,0:T(8,128)(2,1)}, bf16[512,1024]{1,0:T(8,128)(2,1)S(1)}, u32[]{:S(2)}, u32[]{:S(2)}) collective-permute-start(bf16[512,1024]{1,0:T(8,128)(2,1)} %reorder.6), channel_id=1, source_target_pairs={{0,8},{4,12},{8,0},{12,4},{16,24},{20,28},{24,16},{28,20},{1,9},{5... | collective-permute-start | bytes 3145736 | tf_op jit(solution)/shard_map/ppermute | solution.py:38
  467.6 20.3 %collective-permute-start.41 = (bf16[512,1024]{1,0:T(8,128)(2,1)}, bf16[512,1024]{1,0:T(8,128)(2,1)}, u32[]{:S(2)}, u32[]{:S(2)}) collective-permute-start(bf16[512,1024]{1,0:T(8,128)(2,1)} %get-tuple-element.222), channel_id=1, source_target_pairs={{0,1},{1,0},{2,3},{3,2},{4,5},{5,4},{6,7},{7,6},{8,9},{9,8},{10,11... | collective-permute-start | bytes 3145736 | tf_op jit(solution)/shard_map/ppermute | solution.py:38
  486.7 29.5 %collective-permute-start.44 = (bf16[256,1024]{1,0:T(8,128)(2,1)}, bf16[256,1024]{1,0:T(8,128)(2,1)S(1)}, u32[]{:S(2)}, u32[]{:S(2)}) collective-permute-start(bf16[256,1024]{1,0:T(8,128)(2,1)} %reorder.7), channel_id=1, source_target_pairs={{0,16},{4,20},{8,24},{12,28},{16,0},{20,4},{24,8},{28,12},{1,17},{... | collective-permute-start | bytes 1572872 | tf_op jit(solution)/shard_map/ppermute | solution.py:38
  490.9 25.3 %collective-permute-start.42 = (bf16[256,1024]{1,0:T(8,128)(2,1)S(1)}, bf16[256,1024]{1,0:T(8,128)(2,1)}, u32[]{:S(2)}, u32[]{:S(2)}) collective-permute-start(bf16[256,1024]{1,0:T(8,128)(2,1)S(1)} %slice.1120), channel_id=1, source_target_pairs={{0,2},{1,3},{2,0},{3,1},{4,6},{5,7},{6,4},{7,5},{8,10},{9,11},{10,... | collective-permute-start | bytes 1572872 | tf_op jit(solution)/shard_map/ppermute | solution.py:38
  531.3 54.6 %collective-permute-start.49 = (bf16[2048,512]{1,0:T(8,128)(2,1)}, bf16[2048,512]{1,0:T(8,128)(2,1)}, u32[]{:S(2)}, u32[]{:S(2)}) collective-permute-start(bf16[2048,512]{1,0:T(8,128)(2,1)} %get-tuple-element.237), channel_id=1, source_target_pairs={{0,4},{4,0},{8,12},{12,8},{16,20},{20,16},{24,28},{28,24},{1,5},{5... | collective-permute-start | bytes 6291464 | tf_op jit(solution)/shard_map/ppermute | solution.py:38
  555.6 30.3 %collective-permute-start.48 = (bf16[256,1024]{1,0:T(8,128)(2,1)}, bf16[256,1024]{1,0:T(8,128)(2,1)}, u32[]{:S(2)}, u32[]{:S(2)}) collective-permute-start(bf16[256,1024]{1,0:T(8,128)(2,1)} %slice.1119), channel_id=1, source_target_pairs={{0,2},{1,3},{2,0},{3,1},{4,6},{5,7},{6,4},{7,5},{8,10},{9,11},{10,... | collective-permute-start | bytes 1572872 | tf_op jit(solution)/shard_map/ppermute | solution.py:38
  593.2 56.5 %collective-permute-start.50 = (bf16[2048,512]{1,0:T(8,128)(2,1)}, bf16[2048,512]{1,0:T(8,128)(2,1)}, u32[]{:S(2)}, u32[]{:S(2)}) collective-permute-start(bf16[2048,512]{1,0:T(8,128)(2,1)} %get-tuple-element.239), channel_id=1, source_target_pairs={{0,4},{4,0},{8,12},{12,8},{16,20},{20,16},{24,28},{28,24},{1,5},{5... | collective-permute-start | bytes 6291464 | tf_op jit(solution)/shard_map/ppermute | solution.py:38
  630.9 18.8 %collective-permute-start.53 = (bf16[512,1024]{1,0:T(8,128)(2,1)}, bf16[512,1024]{1,0:T(8,128)(2,1)}, u32[]{:S(2)}, u32[]{:S(2)}) collective-permute-start(bf16[512,1024]{1,0:T(8,128)(2,1)} %slice.1112), channel_id=1, source_target_pairs={{0,1},{1,0},{2,3},{3,2},{4,5},{5,4},{6,7},{7,6},{8,9},{9,8},{10,11... | collective-permute-start | bytes 3145736 | tf_op jit(solution)/shard_map/ppermute | solution.py:38
  634.5 52.3 %all-to-all-start.2 = ((bf16[4,2000,128]{2,1,0:T(8,128)(2,1)}), bf16[4,2000,128]{2,1,0:T(8,128)(2,1)S(1)}, u32[]{:S(2)}, u32[]{:S(2)}) async-start(bf16[4,2000,128]{2,1,0:T(8,128)(2,1)} %pad_maximum_fusion.10), calls=%async_computation.2 | async-start | bytes 4096000 | tf_op jit(solution)/shard_map/all_to_all | solution.py:1167
  659.0 38.3 %collective-permute-start.54 = (bf16[2048,256]{1,0:T(8,128)(2,1)}, bf16[2048,256]{1,0:T(8,128)(2,1)S(1)}, u32[]{:S(2)}, u32[]{:S(2)}) collective-permute-start(bf16[2048,256]{1,0:T(8,128)(2,1)} %slice.1111), channel_id=1, source_target_pairs={{0,8},{4,12},{8,0},{12,4},{16,24},{20,28},{24,16},{28,20},{1,9},{5... | collective-permute-start | bytes 3145736 | tf_op jit(solution)/shard_map/ppermute | solution.py:38
  661.0 25.8 %collective-permute-start.55 = (bf16[256,1024]{1,0:T(8,128)(2,1)}, bf16[256,1024]{1,0:T(8,128)(2,1)}, u32[]{:S(2)}, u32[]{:S(2)}) collective-permute-start(bf16[256,1024]{1,0:T(8,128)(2,1)} %slice.1118), channel_id=1, source_target_pairs={{0,2},{1,3},{2,0},{3,1},{4,6},{5,7},{6,4},{7,5},{8,10},{9,11},{10,... | collective-permute-start | bytes 1572872 | tf_op jit(solution)/shard_map/ppermute | solution.py:38
  701.3 41.1 %collective-permute-start.56 = (bf16[2048,128]{1,0:T(8,128)(2,1)}, bf16[2048,128]{1,0:T(8,128)(2,1)}, u32[]{:S(2)}, u32[]{:S(2)}) collective-permute-start(bf16[2048,128]{1,0:T(8,128)(2,1)} %slice.1117), channel_id=1, source_target_pairs={{0,16},{4,20},{8,24},{12,28},{16,0},{20,4},{24,8},{28,12},{1,17},{... | collective-permute-start | bytes 1572872 | tf_op jit(solution)/shard_map/ppermute | solution.py:38
  703.7 34.9 %collective-permute-start.57 = (bf16[1120,512]{1,0:T(8,128)(2,1)}, bf16[1120,512]{1,0:T(8,128)(2,1)}, u32[]{:S(2)}, u32[]{:S(2)}) collective-permute-start(bf16[1120,512]{1,0:T(8,128)(2,1)} %pad_maximum_fusion.19), channel_id=1, source_target_pairs={{0,4},{4,0},{8,12},{12,8},{16,20},{20,16},{24,28},{28,24},{1,5},{5... | collective-permute-start | bytes 3440648 | tf_op jit(solution)/shard_map/ppermute | solution.py:38
  708.6 30.0 %all-to-all-start.3 = ((bf16[8,256,128]{2,1,0:T(8,128)(2,1)}), bf16[8,256,128]{2,1,0:T(8,128)(2,1)}, u32[]{:S(2)}, u32[]{:S(2)}) async-start(bf16[8,256,128]{2,1,0:T(8,128)(2,1)} %embed_back.1), calls=%async_computation.3 | async-start | bytes 1048576 | tf_op jit(solution)/shard_map/all_to_all | solution.py:1207
  759.9 15.6 %collective-permute-start.61 = (bf16[2,8,256,128]{3,2,1,0:T(8,128)(2,1)}, bf16[2,8,256,128]{3,2,1,0:T(8,128)(2,1)}, u32[]{:S(2)}, u32[]{:S(2)}) collective-permute-start(bf16[2,8,256,128]{3,2,1,0:T(8,128)(2,1)} %get-tuple-element.468), channel_id=1, source_target_pairs={{0,1},{1,0},{2,3},{3,2},{4,5},{5,4},{6,7},{7,6},{8,9},{9,8},{10,11... | collective-permute-start | bytes 3145736 | tf_op jit(solution)/shard_map/ppermute | solution.py:38
  (214 other events, 2309.0 us)

commit v8 on v7

--- a/solution.py
+++ b/solution.py
@@ -84,27 +84,35 @@
     return reduce_blocks(*split(total, 1, 2), beside[1:], mask)
 
 
-def reorder_kernel(sources, in_ref, out_ref):
-    width = in_ref.shape[1] // len(sources)
-    for p, q in enumerate(sources):
-        out_ref[:, p * width : (p + 1) * width] = in_ref[:, q * width : (q + 1) * width]
-
-
-def reorder(value, mask):
+def reorder_kernel(sources, *refs):
+    out_ref = refs[-1]
+    width = out_ref.shape[1] // len(sources)
+    start = 0
+    for in_ref in refs[:-1]:
+        rows = slice(start, start + in_ref.shape[0])
+        start += in_ref.shape[0]
+        for p, q in enumerate(sources):
+            block = in_ref[:, q * width : (q + 1) * width]
+            out_ref[rows, p * width : (p + 1) * width] = block.astype(out_ref.dtype)
+
+
+def reorder(values, mask):
     order = block_order(lax.axis_size("dp"))
     sources = [order.index(j ^ mask) for j in order]
-    if value.shape[1] // len(order) % 128:
-        cols = split(value, 1, len(order))
+    rows = sum(value.shape[0] for value in values)
+    if D // len(order) % 128:
+        joined = jnp.concatenate([value.astype(lowp) for value in values])
+        cols = split(joined, 1, len(order))
         return jnp.concatenate([cols[q] for q in sources], axis=1)
     return pl.pallas_call(
         functools.partial(reorder_kernel, sources),
         name="reorder",
-        out_shape=jax.ShapeDtypeStruct(value.shape, value.dtype),
-        in_specs=[vmem()],
+        out_shape=jax.ShapeDtypeStruct((rows, D), lowp),
+        in_specs=[vmem()] * len(values),
         out_specs=vmem(),
         compiler_params=params(60),
         cost_estimate=cost(0, 2 * MIB),
-    )(value)
+    )(*values)
 
 
 def relative(value, x, c):
@@ -588,49 +596,56 @@
     return jnp.transpose(tall)
 
 
-def logits_kernel(words, tiles, info_ref, pair_ref, near_ref, table_ref, out_ref, stat_ref, held):
+def logits_kernel(words, info_ref, pair_ref, near_ref, left_ref, right_ref, out_ref, stat_ref, held):
     step = pl.program_id(0)
 
-    @pl.when(step < tiles)
+    @pl.when(step == 0)
     def _():
         held[...] = pair_ref[...]
 
-    @pl.when(step >= tiles)
+    @pl.when(step == 1)
     def _():
         held[...] = near_ref[...]
 
-    logits = mm(held[...], table_ref[...], NT)
-    wanted = columns_of(info_ref[...])[:, 0:1].astype(jnp.int32)
+    half = left_ref.shape[1]
+    slots = left_ref.shape[0]
+    logits = mm(held[:, :half], left_ref[...], NT) + mm(held[:, half:], right_ref[...], NT)
+    wanted = columns_of(info_ref[0])[:, 0:1].astype(jnp.int32)
     col = lax.broadcasted_iota(jnp.int32, logits.shape, 1)
     hit = jnp.sum(jnp.where(col == wanted, logits, 0.0), axis=-1, keepdims=True)
-    logits = jnp.where(col < words, logits, -1e30)
-    top = jnp.max(logits, axis=-1, keepdims=True)
-    raised = jnp.exp(logits - top)
-    total = jnp.sum(raised, axis=-1, keepdims=True)
-    out_ref[...] = raised.astype(lowp)
+    edge = slots - 128
+    last = jnp.where(col[:, edge:] < words, logits[:, edge:], -1e30)
+    top = jnp.max(last, axis=-1, keepdims=True)
+    top = jnp.maximum(top, jnp.max(logits[:, :edge], axis=-1, keepdims=True))
+    raised = jnp.exp(logits[:, :edge] - top)
+    last = jnp.exp(last - top)
+    total = jnp.sum(raised, axis=-1, keepdims=True) + jnp.sum(last, axis=-1, keepdims=True)
+    out_ref[:, :edge] = raised.astype(lowp)
+    out_ref[:, edge:] = last.astype(lowp)
     lane = lax.broadcasted_iota(jnp.int32, (logits.shape[0], 128), 1)
     packed = jnp.where(lane == 0, top, jnp.where(lane == 1, total, jnp.where(lane == 2, hit, 0.0)))
     stat_ref[...] = jnp.transpose(packed)[:8]
 
 
-def logits_part(words, info, pair, near, table):
+def logits_part(words, chunk, info, pair, near, left, right):
     rows = pair.shape[0] + near.shape[0]
-    slots = table.shape[0]
-    tile = 256
-    tiles = pair.shape[0] // tile
-    return pl.pallas_call(
-        functools.partial(logits_kernel, words, tiles),
+    slots = left.shape[0]
+    tile = pair.shape[0]
+    whole = lambda i: (0, 0)
+    return pl.pallas_call(
+        functools.partial(logits_kernel, words),
         name="logits_part",
-        grid=(2 * tiles,),
+        grid=(2,),
         out_shape=(
             jax.ShapeDtypeStruct((rows, slots), lowp),
             jax.ShapeDtypeStruct((8, rows), single),
         ),
         in_specs=[
-            pl.BlockSpec((8, tile), lambda i: (0, i)),
-            pl.BlockSpec((tile, D), lambda i: (jnp.minimum(i, tiles - 1), 0)),
-            pl.BlockSpec((tile, D), lambda i: (jnp.maximum(i - tiles, 0), 0)),
-            pl.BlockSpec(table.shape, lambda i: (0, 0)),
+            pl.BlockSpec((1, 8, tile), lambda i: (chunk, 0, i)),
+            pl.BlockSpec((tile, D), whole),
+            pl.BlockSpec((tile, D), whole),
+            pl.BlockSpec(left.shape, whole),
+            pl.BlockSpec(right.shape, whole),
         ],
         out_specs=(
             pl.BlockSpec((tile, slots), lambda i: (i, 0)),
@@ -639,61 +654,62 @@
         scratch_shapes=[pltpu.VMEM((tile, D), lowp)],
         compiler_params=params(60),
         cost_estimate=cost(4 * rows * slots * D, 10 * MIB),
-    )(info, pair, near, table)
-
-
-def logits_back_kernel(tiles, info_ref, factor_ref, in_ref, table_ref, out_ref, keep_ref, send_ref):
+    )(info, pair, near, left, right)
+
+
+def logits_back_kernel(info_ref, factor_ref, in_ref, left_ref, right_ref, out_ref, keep_ref, send_ref):
     step = pl.program_id(0)
-    info = columns_of(info_ref[...])
+    info = columns_of(info_ref[0])
     wanted = info[:, 0:1].astype(jnp.int32)
     counted = info[:, 1:2]
-    factor = columns_of(factor_ref[...])[:, 0:1]
+    factor = columns_of(factor_ref[0])[:, 0:1]
     raised = in_ref[...].astype(single)
     col = lax.broadcasted_iota(jnp.int32, raised.shape, 1)
     grads = (raised * factor - jnp.where(col == wanted, counted, 0.0)).astype(lowp)
     out_ref[...] = grads
-    total = mm(grads, table_ref[...]).astype(lowp)
-
-    @pl.when(step < tiles)
+    half = left_ref.shape[1]
+    left = mm(grads, left_ref[...]).astype(lowp)
+    right = mm(grads, right_ref[...]).astype(lowp)
+
+    @pl.when(step == 0)
     def _():
-        send_ref[...] = total
-
-    @pl.when(step >= tiles)
+        send_ref[:, :half] = left
+        send_ref[:, half:] = right
+
+    @pl.when(step == 1)
     def _():
-        keep_ref[...] = total
-
-
-def logits_back(info, factor, raised, table):
+        keep_ref[:, :half] = left
+        keep_ref[:, half:] = right
+
+
+def logits_back(chunk, info, factor, raised, left, right):
     rows, slots = raised.shape
-    tile = 256
-    tiles = rows // (2 * tile)
-
-    def at(i):
-        return (i + tiles) % (2 * tiles)
-
-    return pl.pallas_call(
-        functools.partial(logits_back_kernel, tiles),
+    tile = rows // 2
+    whole = lambda i: (0, 0)
+    return pl.pallas_call(
+        logits_back_kernel,
         name="logits_back",
-        grid=(2 * tiles,),
+        grid=(2,),
         out_shape=(
             jax.ShapeDtypeStruct((rows, slots), lowp),
-            jax.ShapeDtypeStruct((rows // 2, D), lowp),
-            jax.ShapeDtypeStruct((rows // 2, D), lowp),
+            jax.ShapeDtypeStruct((tile, D), lowp),
+            jax.ShapeDtypeStruct((tile, D), lowp),
         ),
         in_specs=[
-            pl.BlockSpec((8, tile), lambda i: (0, at(i))),
-            pl.BlockSpec((8, tile), lambda i: (0, at(i))),
-            pl.BlockSpec((tile, slots), lambda i: (at(i), 0)),
-            pl.BlockSpec(table.shape, lambda i: (0, 0)),
+            pl.BlockSpec((1, 8, tile), lambda i: (chunk, 0, 1 - i)),
+            pl.BlockSpec((1, 8, tile), lambda i: (chunk, 0, 1 - i)),
+            pl.BlockSpec((tile, slots), lambda i: (1 - i, 0)),
+            pl.BlockSpec(left.shape, whole),
+            pl.BlockSpec(right.shape, whole),
         ],
         out_specs=(
-            pl.BlockSpec((tile, slots), lambda i: (at(i), 0)),
-            pl.BlockSpec((tile, D), lambda i: (jnp.maximum(i - tiles, 0), 0)),
-            pl.BlockSpec((tile, D), lambda i: (jnp.minimum(i, tiles - 1), 0)),
+            pl.BlockSpec((tile, slots), lambda i: (1 - i, 0)),
+            pl.BlockSpec((tile, D), whole),
+            pl.BlockSpec((tile, D), whole),
         ),
         compiler_params=params(60),
         cost_estimate=cost(4 * rows * slots * D, 12 * MIB),
-    )(info, factor, raised, table)
+    )(info, factor, raised, left, right)
 
 
 def halves(total, keep_ref, send_ref):
@@ -898,9 +914,10 @@
         gain_sums = jnp.sum(tied[12] * tied[12], axis=1) / head_size
         return scalar_row(sums + [gain_sums[0], gain_sums[1], gain_sums[2]])
 
-    def core_sum(keep, send):
-        more = swap(send.astype(lowp), "head", 1)
-        return keep.astype(single) + more.astype(single)
+    def core_sum(keep, send, beside=()):
+        more, *beside = together(swap(send.astype(lowp), "head", 1), *beside)
+        part = keep.astype(single) + more.astype(single)
+        return (part, beside) if beside else part
 
     def stream_sum(part, beside=()):
         keep, send = split(part, 0, 2)
@@ -1046,22 +1063,22 @@
     low_table = lax.all_to_all(low_table, "dp", 0, 0, axis_index_groups=z_groups)
     mixed, lse = attend(info, seg, comp, mem)
     mixed = mixed.reshape(-1, wide)
-    attn_sum, (early, far_up) = group_sum(
-        mm(mixed, own_one[3 * wide : 4 * wide]), (early_sums(mixed), far_up)
+    attn_sum, (far_up,) = core_sum(
+        *split(mm(mixed, own_one[3 * wide : 4 * wide]), 0, 2), (far_up,)
     )
+    attn_sum, (early, far_down) = stream_sum(attn_sum, (early_sums(mixed), far_down))
     after_attn = embedded + attn_sum
     ffn_in, inv_second = rms(after_attn, gain_vals[1])
-    ffn_in, (far_down, low_table) = group_both(ffn_in, (far_down, low_table))
+    ffn_in, (low_table,) = group_both(ffn_in, (low_table,))
     near_table = [
         lax.dynamic_index_in_dim(low_table, z ^ (m // 2), 0, keepdims=False) for m in order[:reach]
     ]
     near_table = jnp.concatenate(near_table, axis=1)
+    near_table = jnp.concatenate([near_table, jnp.zeros((slots - words, D // 2), lowp)], axis=0)
     ffn_in = jnp.concatenate(ffn_in)
     full_up = jnp.concatenate([near_up, far_up], axis=1)
     full_down = jnp.concatenate([near_down, far_down], axis=1)
     far_table = swap(near_table, "dp", 1)
-    loss_table = jnp.concatenate([near_table, far_table], axis=1)
-    loss_table = jnp.concatenate([loss_table, jnp.zeros((slots - words, D), lowp)], axis=0)
     hidden_pre = mm(ffn_in, full_up, NT)
     hidden_act = jax.nn.gelu(hidden_pre).astype(lowp)
     after_ffn = after_attn + group_sum(mm(hidden_act, full_down))
@@ -1084,14 +1101,13 @@
         else:
             chunk, (stats[i - 1],) = group_both(pieces[i], (stats[i - 1],))
             chunks.append(chunk)
-        out, stat = logits_part(words, info_all[i], *chunks[i], loss_table)
+        out, stat = logits_part(words, i, info_all, *chunks[i], near_table, far_table)
         raised.append(out)
         stats.append(stat)
 
     mask = dp_size // 2
     while mask > 1:
-        joined = jnp.concatenate(pieces) if len(pieces) > 1 else pieces[0]
-        moved = swap(reorder(joined, mask), "dp", mask)
+        moved = swap(reorder(pieces, mask), "dp", mask)
         if len(pieces) == 1:
             moved, own_codes, own_count = together(
                 moved, *own_list(after(token_codes, final_in))
@@ -1129,7 +1145,9 @@
     dlogits = [None] * reach
     parts = [None] * reach
     for i in reversed(range(reach)):
-        dlogits[i], *core = logits_back(info_all[i], factor_all[i], raised[i], loss_table)
+        dlogits[i], *core = logits_back(
+            i, info_all, factor_all, raised[i], near_table, far_table
+        )
         if i + 1 < reach:
             parts[i + 1], (dlogits[i], *core) = stream_sum(parts[i + 1], (dlogits[i], *core))
         parts[i] = core_sum(*core)
@@ -1138,8 +1156,7 @@
     mask = 2
     while len(parts) > 1:
         count = len(parts) // 2
-        moved = jnp.concatenate([part.astype(lowp) for part in parts[count:]])
-        moved = swap(reorder(moved, mask), "dp", mask)
+        moved = swap(reorder(parts[count:], mask), "dp", mask)
         if mask == 2:
             moved, dlogits[0] = together(moved, dlogits[0])
         elif mask == 4:
@@ -1176,8 +1193,8 @@
     def beside_expand(moved):
         keep, send = split(mm(seg_grad, in_weight), 0, 2)
         more = swap(send.astype(lowp), "head", 1)
-        moved, more, *kept["old"] = together(
-            moved, more, *expand(comp_grad, old_raw, full_conv)
+        moved, more, kept["table"], *kept["old"] = together(
+            moved, more, table_pieces, *expand(comp_grad, old_raw, full_conv)
         )
         kept["seg_in"] = split(keep + more.astype(single), 0, 2)
         return moved
@@ -1198,13 +1215,11 @@
         )
         conv_sum = split(conv_block_order(conv_sum), 1, 2)
         sums = [jnp.concatenate([part, more.astype(part.dtype)]) for part, more in zip(sums, conv_sum)]
-        moved, kept["table"], seg_in_far, *kept["sums"] = together(
-            moved, table_pieces, seg_in_far, *sums
-        )
+        seg_in_far, *kept["sums"] = together(seg_in_far, *sums)
         rows_grad = embed_back(
             place, embedded_low, gain_vals[0], seg_in, seg_in_far, grad_after_attn
         )
-        kept["rows"] = lax.all_to_all(rows_grad, "dp", 0, 0)
+        moved, kept["rows"] = together(moved, lax.all_to_all(rows_grad, "dp", 0, 0))
         return moved
 
     def beside_rows(moved):

time: 891 us -> 875 us (0.982)
  local copies, waits for them, and re-layouts: 112 us -> 89.3 us
    ppermute x70, waiting for transfers between devices: 168 us -> 183 us  [swap(): return lax.ppermute(value, axis, [(i, i ^ mask) for i in range(size)])]
    all_to_all x1, waiting for transfers between devices: 20.3 us -> 7.73 us  [beside_sums(): moved, kept['rows'] = together(moved, lax.all_to_all(rows_grad, 'dp', 0, 0))]
    unnamed x368 -> x351, local copies, waits for them, and re-layouts: 37.9 us -> 33.1 us
  transfers between devices with their start and end apart: 74 -> 74, of which waited for: 44 -> 43; matrix products, arithmetic and copies ran while one was open for 22% -> 20% of each run, Pallas kernels for 25% -> 27%
where the time goes in v8:
time: 875 us; the launch traced here: 867 us
  Pallas kernels  268 us (31%)
  waiting for transfers between devices  193 us (22%)
  other arithmetic  157 us (18%)
  local copies, waits for them, and re-layouts  89.3 us (10%)
  starting transfers between devices  79.3 us (9%)
  matrix products  40.6 us (5%)
  between operations  34 us (4%)
    ppermute x70, waiting for transfers between devices, swap(): return lax.ppermute(value, axis, [(i, i ^ mask) for i in range(size)])  183 us
    ppermute x70, starting transfers between devices, swap(): return lax.ppermute(value, axis, [(i, i ^ mask) for i in range(size)])  63.2 us
    pallas_call x4, Pallas kernels, logits_part(): pl.pallas_call(functools.partial(logits_kernel, words), name='logits_part...  44.4 us
    pallas_call x4, Pallas kernels, logits_back(): pl.pallas_call(logits_back_kernel, name='logits_back', grid=(2,), out_sha...  43.9 us
    dot_general x11, matrix products, mm(): return lax.dot_general(left, right, dims, preferred_element_type=single)  40.6 us
    unnamed x351, local copies, waits for them, and re-layouts  33.1 us
    pallas_call x1, Pallas kernels, table_grad_part(): pl.pallas_call(functools.partial(table_grad_kernel, count), name='table_g...  24.5 us
    pallas_call x1, Pallas kernels, own_list(): pl.pallas_call(list_kernel, name='own_list', out_shape=(jax.ShapeDtypeStr...  21.4 us
  transfers between devices with their start and end apart: 74, of which 43 were waited for; matrix products, arithmetic and copies ran while one was open for 20% of the time, Pallas kernels for 27%

profile of v8, /device:TPU:0, one launch (start us, length us, event | category | flops | bytes accessed | tf_op | source)
XLA Modules:
  0.0 867.0 jit_solution(11197991349179853800)
XLA Ops:
  24.1 8.7 lookup.2
  32.7 8.8 %lookup.3 = bf16[4096,128]{1,0:T(8,128)(2,1)} custom-call(s32[4096]{0:T(1024)} %get-tuple-element.466.row_ref, f32[8000,128]{1,0:T(8,128)} %table_ref.3), custom_call_target="tpu_custom_call" | custom-call | bytes 629145 | tf_op jit(solution)/shard_map/lookup/pallas_call | solution.py:178
  50.7 7.0 state_norm.2
  80.5 9.9 %state_norm.3.old_ref = bf16[3,1024,1024]{2,1,0:T(8,128)(2,1)} custom-call(s32[2]{0:T(128)} %pad_add_fusion.place_ref, f32[1,1024]{1,0:T(1,128)} %bitcast.346, bf16[2,1536,1024]{2,1,0:T(8,128)(2,1)} %in_ref.3), custom_call_target="tpu_custom_call" | custom-call | bytes 251658 | tf_op jit(solution)/shard_map/state_norm/pallas_call | solution.py:353
  91.2 14.9 %collective-permute-done.7 = bf16[2048,128]{1,0:T(8,128)(2,1)} collective-permute-done((bf16[2048,128]{1,0:T(8,128)(2,1)S(1)}, bf16[2048,128]{1,0:T(8,128)(2,1)}, u32[]{:S(2)}, u32[]{:S(2)}) %collective-permute-start.7) | collective-permute-done | bytes 524320 | tf_op jit(solution)/shard_map/ppermute | solution.py:38
  124.0 12.2 %compress.1 = (bf16[1024,512]{1,0:T(8,128)(2,1)}, bf16[3,1024,512]{2,1,0:T(8,128)(2,1)}) custom-call(bf16[3,1024,1024]{2,1,0:T(8,128)(2,1)} %state_norm.3.old_ref, bf16[1120,1024]{1,0:T(8,128)(2,1)} %copy-done.9, bf16[1120,1024]{1,0:T(8,128)(2,1)} %copy-done.9, bf16[2,384,128]{2,1,0:T(8,128)(2,1)} %bitcast.316), custom_call_target="tpu_custom_call" | custom-call | flops 64424508 | bytes 251658 | tf_op jit(solution)/shard_map/compress/pallas_call | solution.py:395
  149.5 10.9 %attend.1 = (bf16[2,2,256,256]{3,2,1,0:T(8,128)(2,1)}, f32[2,2,512,1]{3,2,1,0:T(8,128)}) custom-call(s32[8]{0:T(128)} %fusion.106.info_ref, bf16[2,2,256,768]{3,2,1,0:T(8,128)(2,1)} %bitcast.290, bf16[2,2,256,768]{3,2,1,0:T(8,128)(2,1)} %bitcast.291, bf16[2,2,256,768]{3,2,1,0:T(8,128)(2,1)} %bitcast.292, bf16[1024,512]{1,0:T(8,128)(2,1)} %get-tuple-element.165.kc_ref.vc_ref, ...), custom_call_target="tpu_custom_call" | custom-call | flops 146800640 | bytes 125829 | tf_op jit(solution)/shard_map/attend/pallas_call | solution.py:547
  203.6 13.0 %collective-permute-done.16 = bf16[256,1024]{1,0:T(8,128)(2,1)S(1)} collective-permute-done((bf16[256,1024]{1,0:T(8,128)(2,1)S(1)}, bf16[256,1024]{1,0:T(8,128)(2,1)S(1)}, u32[]{:S(2)}, u32[]{:S(2)}) %collective-permute-start.16) | collective-permute-done | bytes 524320 | tf_op jit(solution)/shard_map/ppermute | solution.py:38
  221.8 6.8 multiply_convert_fusion
  245.9 9.3 %collective-permute-done.19 = bf16[256,1024]{1,0:T(8,128)(2,1)S(1)} collective-permute-done((bf16[256,1024]{1,0:T(8,128)(2,1)S(1)}, bf16[256,1024]{1,0:T(8,128)(2,1)S(1)}, u32[]{:S(2)}, u32[]{:S(2)}) %collective-permute-start.19) | collective-permute-done | bytes 524320 | tf_op jit(solution)/shard_map/ppermute | solution.py:38
  262.2 21.4 %own_list.1 = (s32[8200]{0:T(1024)}, s32[1]{0:T(128)}) custom-call(s32[8192]{0:T(1024)} %get-tuple-element.188.code_ref), custom_call_target="tpu_custom_call" | custom-call | bytes 1258291 | tf_op jit(solution)/shard_map/own_list/pallas_call | solution.py:209
  302.8 11.3 %logits_part.4 = (bf16[1024,2048]{1,0:T(8,128)(2,1)}, f32[8,1024]{1,0:T(8,128)}) custom-call(f32[4,8,1024]{2,1,0:T(8,128)} %bitcast.296, bf16[512,1024]{1,0:T(8,128)(2,1)} %pad_maximum_fusion.20.pair_ref.refs_4_, bf16[512,1024]{1,0:T(8,128)(2,1)} %collective-permute-done.24.near_ref.refs_5_, bf16[2048,512]{1,0:T(8,128)(2,1)} %copy-done.2, ...), custom_call_target="tpu_custom_call" | custom-call | flops 171798688 | bytes 209715 | tf_op jit(solution)/shard_map/logits_part/pallas_call | solution.py:635
  319.1 10.9 %logits_part.5 = (bf16[1024,2048]{1,0:T(8,128)(2,1)}, f32[8,1024]{1,0:T(8,128)}) custom-call(f32[4,8,1024]{2,1,0:T(8,128)} %bitcast.297, bf16[512,1024]{1,0:T(8,128)(2,1)} %copy-done.22, bf16[512,1024]{1,0:T(8,128)(2,1)} %copy-done.35, bf16[2048,512]{1,0:T(8,128)(2,1)} %copy-done.2, bf16[2048,512]{1,0:T(8,128)(2,1)} %collective-permute-done.25.right_ref), custom_call_target="tpu_custom_call" | custom-call | flops 171798688 | bytes 209715 | tf_op jit(solution)/shard_map/logits_part/pallas_call | solution.py:635
  336.0 11.0 %logits_part.6 = (bf16[1024,2048]{1,0:T(8,128)(2,1)}, f32[8,1024]{1,0:T(8,128)}) custom-call(f32[4,8,1024]{2,1,0:T(8,128)} %bitcast.298, bf16[512,1024]{1,0:T(8,128)(2,1)} %copy-done.14, bf16[512,1024]{1,0:T(8,128)(2,1)} %copy-done.36, bf16[2048,512]{1,0:T(8,128)(2,1)} %copy-done.2, bf16[2048,512]{1,0:T(8,128)(2,1)} %collective-permute-done.25.right_ref), custom_call_target="tpu_custom_call" | custom-call | flops 171798688 | bytes 209715 | tf_op jit(solution)/shard_map/logits_part/pallas_call | solution.py:635
  352.8 11.2 %logits_part.7 = (bf16[1024,2048]{1,0:T(8,128)(2,1)}, f32[8,1024]{1,0:T(8,128)}) custom-call(f32[4,8,1024]{2,1,0:T(8,128)} %bitcast.299, bf16[512,1024]{1,0:T(8,128)(2,1)} %copy-done.15, bf16[512,1024]{1,0:T(8,128)(2,1)} %copy-done.37, bf16[2048,512]{1,0:T(8,128)(2,1)} %copy-done.2, bf16[2048,512]{1,0:T(8,128)(2,1)} %collective-permute-done.25.right_ref), custom_call_target="tpu_custom_call" | custom-call | flops 171798688 | bytes 209715 | tf_op jit(solution)/shard_map/logits_part/pallas_call | solution.py:635
  383.5 11.0 %logits_back.4 = (bf16[1024,2048]{1,0:T(8,128)(2,1)}, bf16[512,1024]{1,0:T(8,128)(2,1)}, bf16[512,1024]{1,0:T(8,128)(2,1)}) custom-call(f32[4,8,1024]{2,1,0:T(8,128)} %bitcast.301, f32[4,8,1024]{2,1,0:T(8,128)} %broadcast_in_dim.203.factor_ref, bf16[1024,2048]{1,0:T(8,128)(2,1)} %get-tuple-element.205.in_ref, bf16[2048,512]{1,0:T(8,128)(2,1)} %copy-done.2, ...), custom_call_target="tpu_custom_call" | custom-call | flops 171798688 | bytes 251658 | tf_op jit(solution)/shard_map/logits_back/pallas_call | solution.py:689
  401.8 10.9 %logits_back.5 = (bf16[1024,2048]{1,0:T(8,128)(2,1)}, bf16[512,1024]{1,0:T(8,128)(2,1)}, bf16[512,1024]{1,0:T(8,128)(2,1)}) custom-call(f32[4,8,1024]{2,1,0:T(8,128)} %bitcast.302, f32[4,8,1024]{2,1,0:T(8,128)} %broadcast_in_dim.203.factor_ref, bf16[1024,2048]{1,0:T(8,128)(2,1)} %get-tuple-element.208.in_ref, bf16[2048,512]{1,0:T(8,128)(2,1)} %copy-done.2, ...), custom_call_target="tpu_custom_call" | custom-call | flops 171798688 | bytes 251658 | tf_op jit(solution)/shard_map/logits_back/pallas_call | solution.py:689
  422.6 11.1 %logits_back.6 = (bf16[1024,2048]{1,0:T(8,128)(2,1)}, bf16[512,1024]{1,0:T(8,128)(2,1)}, bf16[512,1024]{1,0:T(8,128)(2,1)}) custom-call(f32[4,8,1024]{2,1,0:T(8,128)} %bitcast.303, f32[4,8,1024]{2,1,0:T(8,128)} %broadcast_in_dim.203.factor_ref, bf16[1024,2048]{1,0:T(8,128)(2,1)} %get-tuple-element.214.in_ref, bf16[2048,512]{1,0:T(8,128)(2,1)} %copy-done.2, ...), custom_call_target="tpu_custom_call" | custom-call | flops 171798688 | bytes 251658 | tf_op jit(solution)/shard_map/logits_back/pallas_call | solution.py:689
  446.0 10.9 %logits_back.7 = (bf16[1024,2048]{1,0:T(8,128)(2,1)}, bf16[512,1024]{1,0:T(8,128)(2,1)}, bf16[512,1024]{1,0:T(8,128)(2,1)}) custom-call(f32[4,8,1024]{2,1,0:T(8,128)} %bitcast.304, f32[4,8,1024]{2,1,0:T(8,128)} %broadcast_in_dim.203.factor_ref, bf16[1024,2048]{1,0:T(8,128)(2,1)} %get-tuple-element.220.in_ref, bf16[2048,512]{1,0:T(8,128)(2,1)} %copy-done.2, ...), custom_call_target="tpu_custom_call" | custom-call | flops 171798688 | bytes 251658 | tf_op jit(solution)/shard_map/logits_back/pallas_call | solution.py:689
  457.1 14.1 %collective-permute-done.43 = bf16[512,1024]{1,0:T(8,128)(2,1)} collective-permute-done((bf16[512,1024]{1,0:T(8,128)(2,1)}, bf16[512,1024]{1,0:T(8,128)(2,1)}, u32[]{:S(2)}, u32[]{:S(2)}) %collective-permute-start.43) | collective-permute-done | bytes 1048608 | tf_op jit(solution)/shard_map/ppermute | solution.py:38
  483.1 24.5 %table_grad_part.1 = (f32[2048,512]{1,0:T(8,128)}, bf16[2048,512]{1,0:T(8,128)(2,1)}) custom-call(bf16[1024,2048]{1,0:T(8,128)(2,1)} %get-tuple-element.231.refs_0_, bf16[1024,2048]{1,0:T(8,128)(2,1)} %get-tuple-element.232.refs_1_, bf16[1024,2048]{1,0:T(8,128)(2,1)} %get-tuple-element.233.refs_2_, bf16[1024,2048]{1,0:T(8,128)(2,1)} %get-tuple-element.234.refs_3_, ...), custom_call_target="tpu_custom_call" | custom-call | flops 515396064 | bytes 629145 | tf_op jit(solution)/shard_map/table_grad_part/pallas_call | solution.py:743
  510.7 11.5 %collective-permute-done.45 = bf16[256,1024]{1,0:T(8,128)(2,1)S(1)} collective-permute-done((bf16[256,1024]{1,0:T(8,128)(2,1)S(1)}, bf16[256,1024]{1,0:T(8,128)(2,1)S(1)}, u32[]{:S(2)}, u32[]{:S(2)}) %collective-permute-start.45) | collective-permute-done | bytes 524320 | tf_op jit(solution)/shard_map/ppermute | solution.py:38
  556.3 11.4 %hidden_grads.1 = (f32[2048,512]{1,0:T(8,128)}, bf16[2048,512]{1,0:T(8,128)(2,1)}) custom-call(bf16[1024,1024]{1,0:T(8,128)(2,1)} %copy-done.53, bf16[1024,1024]{1,0:T(8,128)(2,1)} %copy-done.52, bf16[1024,1024]{1,0:T(8,128)(2,1)} %pad_maximum_fusion.2.in_ref, bf16[1024,1024]{1,0:T(8,128)(2,1)} %pad_maximum_fusion.5.down_ref), custom_call_target="tpu_custom_call" | custom-call | flops 128849016 | bytes 335544 | tf_op jit(solution)/shard_map/hidden_grads/pallas_call | solution.py:778
  601.4 15.2 %attend_back.1 = (bf16[2,2,256,768]{3,2,1,0:T(8,128)(2,1)}, bf16[1024,512]{1,0:T(8,128)(2,1)}, bf16[1024,512]{1,0:T(8,128)(2,1)}) custom-call(s32[8]{0:T(128)} %fusion.106.info_ref, bf16[2,2,256,768]{3,2,1,0:T(8,128)(2,1)} %bitcast.293, bf16[2,2,256,768]{3,2,1,0:T(8,128)(2,1)} %bitcast.294, bf16[2,2,256,768]{3,2,1,0:T(8,128)(2,1)} %bitcast.295, ...), custom_call_target="tpu_custom_call" | custom-call | flops 230686720 | bytes 188743 | tf_op jit(solution)/shard_map/attend_back/pallas_call | solution.py:570
  635.3 8.9 %collective-permute-done.50 = bf16[2048,512]{1,0:T(8,128)(2,1)} collective-permute-done((bf16[2048,512]{1,0:T(8,128)(2,1)}, bf16[2048,512]{1,0:T(8,128)(2,1)}, u32[]{:S(2)}, u32[]{:S(2)}) %collective-permute-start.50) | collective-permute-done | bytes 2097184 | tf_op jit(solution)/shard_map/ppermute | solution.py:38
  660.6 14.3 %attn_grads.1 = (f32[1024,512]{1,0:T(8,128)}, bf16[1024,512]{1,0:T(8,128)(2,1)}) custom-call(bf16[1024,768]{1,0:T(8,128)(2,1)} %bitcast.319, bf16[1024,256]{1,0:T(8,128)(2,1)} %bitcast.312, bf16[1024,512]{1,0:T(8,128)(2,1)} %get-tuple-element.254.mem_ref, bf16[3072,512]{1,0:T(8,128)(2,1)} %bitcast.313, bf16[1024,1024]{1,0:T(8,128)(2,1)} %pad_maximum_fusion.1.normed_ref, ...), custom_call_target="tpu_custom_call" | custom-call | flops 188743680 | bytes 503316 | tf_op jit(solution)/shard_map/attn_grads/pallas_call | solution.py:828
  693.0 7.7 all-to-all-done.3
  703.7 15.1 %collective-permute-done.57 = bf16[1120,512]{1,0:T(8,128)(2,1)} collective-permute-done((bf16[1120,512]{1,0:T(8,128)(2,1)}, bf16[1120,512]{1,0:T(8,128)(2,1)}, u32[]{:S(2)}, u32[]{:S(2)}) %collective-permute-start.57) | collective-permute-done | bytes 1146912 | tf_op jit(solution)/shard_map/ppermute | solution.py:38
  741.4 13.3 %collective-permute-done.60 = bf16[1120,128]{1,0:T(8,128)(2,1)S(1)} collective-permute-done((bf16[1120,128]{1,0:T(8,128)(2,1)S(1)}, bf16[1120,128]{1,0:T(8,128)(2,1)S(1)}, u32[]{:S(2)}, u32[]{:S(2)}) %collective-permute-start.60) | collective-permute-done | bytes 286752 | tf_op jit(solution)/shard_map/ppermute | solution.py:38
  761.8 15.3 %scatter.1 = f32[8000,128]{1,0:T(8,128)} custom-call(s32[1]{0:T(128)} %get-tuple-element.267.count_ref, s32[8200]{0:T(1024)} %get-tuple-element.268.code_ref, f32[8000,128]{1,0:T(8,128)} %bitcast_convert_fusion.base_ref, bf16[8192,128]{1,0:T(8,128)(2,1)} %bitcast.307), custom_call_target="tpu_custom_call" | custom-call | bytes 629145 | tf_op jit(solution)/shard_map/scatter/pallas_call | solution.py:305
  812.2 7.1 multiply_reduce_fusion
  856.2 7.8 divide_subtract_fusion
  (779 shorter events, 455.4 us)
Async XLA Ops:
  18.7 22.8 %collective-permute-start.3 = (bf16[1120,128]{1,0:T(8,128)(2,1)S(1)}, bf16[1120,128]{1,0:T(8,128)(2,1)S(1)}, u32[]{:S(2)}, u32[]{:S(2)}) collective-permute-start(bf16[1120,128]{1,0:T(8,128)(2,1)S(1)} %pad_maximum_fusion.28), channel_id=1, source_target_pairs={{0,16},{4,20},{8,24},{12,28},{16,0},{20,4},{24,8},{28,12},{1,17},{... | collective-permute-start | bytes 860168 | tf_op jit(solution)/shard_map/ppermute | solution.py:38
  65.0 41.1 %all-to-all-start = ((bf16[8,256,128]{2,1,0:T(8,128)(2,1)}), bf16[8,256,128]{2,1,0:T(8,128)(2,1)}, u32[]{:S(2)}, u32[]{:S(2)}) async-start(bf16[8,256,128]{2,1,0:T(8,128)(2,1)} %bitcast.314), calls=%async_computation | async-start | bytes 1048576 | tf_op jit(solution)/shard_map/all_to_all | solution.py:995
  71.3 42.5 %collective-permute-start.10 = (bf16[1120,512]{1,0:T(8,128)(2,1)}, bf16[1120,512]{1,0:T(8,128)(2,1)}, u32[]{:S(2)}, u32[]{:S(2)}) collective-permute-start(bf16[1120,512]{1,0:T(8,128)(2,1)} %get-tuple-element.413), channel_id=1, source_target_pairs={{0,4},{4,0},{8,12},{12,8},{16,20},{20,16},{24,28},{28,24},{1,5},{5... | collective-permute-start | bytes 3440648 | tf_op jit(solution)/shard_map/ppermute | solution.py:38
  73.9 32.3 %collective-permute-start.7 = (bf16[2048,128]{1,0:T(8,128)(2,1)S(1)}, bf16[2048,128]{1,0:T(8,128)(2,1)}, u32[]{:S(2)}, u32[]{:S(2)}) collective-permute-start(bf16[2048,128]{1,0:T(8,128)(2,1)S(1)} %pad_maximum_fusion.27), channel_id=1, source_target_pairs={{0,16},{4,20},{8,24},{12,28},{16,0},{20,4},{24,8},{28,12},{1,17},{... | collective-permute-start | bytes 1572872 | tf_op jit(solution)/shard_map/ppermute | solution.py:38
  111.9 28.4 %collective-permute-start.11 = (bf16[2048,256]{1,0:T(8,128)(2,1)}, bf16[2048,256]{1,0:T(8,128)(2,1)}, u32[]{:S(2)}, u32[]{:S(2)}) collective-permute-start(bf16[2048,256]{1,0:T(8,128)(2,1)} %pad_maximum_fusion.18), channel_id=1, source_target_pairs={{0,8},{4,12},{8,0},{12,4},{16,24},{20,28},{24,16},{28,20},{1,9},{5... | collective-permute-start | bytes 3145736 | tf_op jit(solution)/shard_map/ppermute | solution.py:38
  123.0 22.1 %collective-permute-start.9 = (bf16[512,1024]{1,0:T(8,128)(2,1)}, bf16[512,1024]{1,0:T(8,128)(2,1)}, u32[]{:S(2)}, u32[]{:S(2)}) collective-permute-start(bf16[512,1024]{1,0:T(8,128)(2,1)} %pad_maximum_fusion.17), channel_id=1, source_target_pairs={{0,1},{1,0},{2,3},{3,2},{4,5},{5,4},{6,7},{7,6},{8,9},{9,8},{10,11... | collective-permute-start | bytes 3145736 | tf_op jit(solution)/shard_map/ppermute | solution.py:38
  143.1 32.2 %collective-permute-start.13 = (bf16[1024,512]{1,0:T(8,128)(2,1)}, bf16[1024,512]{1,0:T(8,128)(2,1)}, u32[]{:S(2)}, u32[]{:S(2)}) collective-permute-start(bf16[1024,512]{1,0:T(8,128)(2,1)} %get-tuple-element.400), channel_id=1, source_target_pairs={{0,4},{4,0},{8,12},{12,8},{16,20},{20,16},{24,28},{28,24},{1,5},{5... | collective-permute-start | bytes 3145736 | tf_op jit(solution)/shard_map/ppermute | solution.py:38
  167.1 33.4 %collective-permute-start.15 = (bf16[1024,512]{1,0:T(8,128)(2,1)}, bf16[1024,512]{1,0:T(8,128)(2,1)}, u32[]{:S(2)}, u32[]{:S(2)}) collective-permute-start(bf16[1024,512]{1,0:T(8,128)(2,1)} %get-tuple-element.399), channel_id=1, source_target_pairs={{0,4},{4,0},{8,12},{12,8},{16,20},{20,16},{24,28},{28,24},{1,5},{5... | collective-permute-start | bytes 3145736 | tf_op jit(solution)/shard_map/ppermute | solution.py:38
  167.4 51.5 %all-to-all-start.1 = ((bf16[4,2000,128]{2,1,0:T(8,128)(2,1)}), bf16[4,2000,128]{2,1,0:T(8,128)(2,1)S(1)}, u32[]{:S(2)}, u32[]{:S(2)}) async-start(bf16[4,2000,128]{2,1,0:T(8,128)(2,1)} %bitcast.308), calls=%async_computation.1 | async-start | bytes 4096000 | tf_op jit(solution)/shard_map/all_to_all | solution.py:1063
  179.8 20.7 %collective-permute-start.14 = (bf16[256,1024]{1,0:T(8,128)(2,1)}, bf16[256,1024]{1,0:T(8,128)(2,1)}, u32[]{:S(2)}, u32[]{:S(2)}) collective-permute-start(bf16[256,1024]{1,0:T(8,128)(2,1)} %slice.1056), channel_id=1, source_target_pairs={{0,2},{1,3},{2,0},{3,1},{4,6},{5,7},{6,4},{7,5},{8,10},{9,11},{10,... | collective-permute-start | bytes 1572872 | tf_op jit(solution)/shard_map/ppermute | solution.py:38
  244.1 58.7 %collective-permute-start.25 = (bf16[2048,512]{1,0:T(8,128)(2,1)S(1)}, bf16[2048,512]{1,0:T(8,128)(2,1)}, u32[]{:S(2)}, u32[]{:S(2)}) collective-permute-start(bf16[2048,512]{1,0:T(8,128)(2,1)S(1)} %fusion.13.left_ref), channel_id=1, source_target_pairs={{0,4},{4,0},{8,12},{12,8},{16,20},{20,16},{24,28},{28,24},{1,5},{5... | collective-permute-start | bytes 6291464 | tf_op jit(solution)/shard_map/ppermute | solution.py:38
  259.5 24.5 %collective-permute-start.20 = (bf16[256,1024]{1,0:T(8,128)(2,1)}, bf16[256,1024]{1,0:T(8,128)(2,1)}, u32[]{:S(2)}, u32[]{:S(2)}) collective-permute-start(bf16[256,1024]{1,0:T(8,128)(2,1)} %reorder.4), channel_id=1, source_target_pairs={{0,16},{4,20},{8,24},{12,28},{16,0},{20,4},{24,8},{28,12},{1,17},{... | collective-permute-start | bytes 1572872 | tf_op jit(solution)/shard_map/ppermute | solution.py:38
  259.8 28.2 %collective-permute-start.23 = (bf16[256,1024]{1,0:T(8,128)(2,1)}, bf16[256,1024]{1,0:T(8,128)(2,1)}, u32[]{:S(2)}, u32[]{:S(2)}) collective-permute-start(bf16[256,1024]{1,0:T(8,128)(2,1)} %multiply_convert_fusion.1.refs_0_), channel_id=1, source_target_pairs={{0,2},{1,3},{2,0},{3,1},{4,6},{5,7},{6,4},{7,5},{8,10},{9,11},{10,... | collective-permute-start | bytes 1572872 | tf_op jit(solution)/shard_map/ppermute | solution.py:38
  286.3 27.9 %collective-permute-start.22 = (bf16[512,1024]{1,0:T(8,128)(2,1)}, bf16[512,1024]{1,0:T(8,128)(2,1)}, u32[]{:S(2)}, u32[]{:S(2)}) collective-permute-start(bf16[512,1024]{1,0:T(8,128)(2,1)} %reorder.5), channel_id=1, source_target_pairs={{0,8},{4,12},{8,0},{12,4},{16,24},{20,28},{24,16},{28,20},{1,9},{5... | collective-permute-start | bytes 3145736 | tf_op jit(solution)/shard_map/ppermute | solution.py:38
  439.3 17.7 %collective-permute-start.40 = (bf16[256,1024]{1,0:T(8,128)(2,1)}, bf16[256,1024]{1,0:T(8,128)(2,1)S(1)}, u32[]{:S(2)}, u32[]{:S(2)}) collective-permute-start(bf16[256,1024]{1,0:T(8,128)(2,1)} %slice.1052), channel_id=1, source_target_pairs={{0,2},{1,3},{2,0},{3,1},{4,6},{5,7},{6,4},{7,5},{8,10},{9,11},{10,... | collective-permute-start | bytes 1572872 | tf_op jit(solution)/shard_map/ppermute | solution.py:38
  446.0 25.2 %collective-permute-start.43 = (bf16[512,1024]{1,0:T(8,128)(2,1)}, bf16[512,1024]{1,0:T(8,128)(2,1)}, u32[]{:S(2)}, u32[]{:S(2)}) collective-permute-start(bf16[512,1024]{1,0:T(8,128)(2,1)} %reorder.6), channel_id=1, source_target_pairs={{0,8},{4,12},{8,0},{12,4},{16,24},{20,28},{24,16},{28,20},{1,9},{5... | collective-permute-start | bytes 3145736 | tf_op jit(solution)/shard_map/ppermute | solution.py:38
  457.0 21.7 %collective-permute-start.41 = (bf16[512,1024]{1,0:T(8,128)(2,1)}, bf16[512,1024]{1,0:T(8,128)(2,1)}, u32[]{:S(2)}, u32[]{:S(2)}) collective-permute-start(bf16[512,1024]{1,0:T(8,128)(2,1)} %get-tuple-element.225), channel_id=1, source_target_pairs={{0,1},{1,0},{2,3},{3,2},{4,5},{5,4},{6,7},{7,6},{8,9},{9,8},{10,11... | collective-permute-start | bytes 3145736 | tf_op jit(solution)/shard_map/ppermute | solution.py:38
  477.5 30.2 %collective-permute-start.44 = (bf16[256,1024]{1,0:T(8,128)(2,1)}, bf16[256,1024]{1,0:T(8,128)(2,1)S(1)}, u32[]{:S(2)}, u32[]{:S(2)}) collective-permute-start(bf16[256,1024]{1,0:T(8,128)(2,1)} %reorder.7), channel_id=1, source_target_pairs={{0,16},{4,20},{8,24},{12,28},{16,0},{20,4},{24,8},{28,12},{1,17},{... | collective-permute-start | bytes 1572872 | tf_op jit(solution)/shard_map/ppermute | solution.py:38
  481.7 25.9 %collective-permute-start.42 = (bf16[256,1024]{1,0:T(8,128)(2,1)S(1)}, bf16[256,1024]{1,0:T(8,128)(2,1)S(1)}, u32[]{:S(2)}, u32[]{:S(2)}) collective-permute-start(bf16[256,1024]{1,0:T(8,128)(2,1)S(1)} %slice.1051), channel_id=1, source_target_pairs={{0,2},{1,3},{2,0},{3,1},{4,6},{5,7},{6,4},{7,5},{8,10},{9,11},{10,... | collective-permute-start | bytes 1572872 | tf_op jit(solution)/shard_map/ppermute | solution.py:38
  522.3 48.4 %collective-permute-start.49 = (bf16[2048,512]{1,0:T(8,128)(2,1)}, bf16[2048,512]{1,0:T(8,128)(2,1)}, u32[]{:S(2)}, u32[]{:S(2)}) collective-permute-start(bf16[2048,512]{1,0:T(8,128)(2,1)} %get-tuple-element.240), channel_id=1, source_target_pairs={{0,4},{4,0},{8,12},{12,8},{16,20},{20,16},{24,28},{28,24},{1,5},{5... | collective-permute-start | bytes 6291464 | tf_op jit(solution)/shard_map/ppermute | solution.py:38
  541.6 29.1 %collective-permute-start.48 = (bf16[256,1024]{1,0:T(8,128)(2,1)}, bf16[256,1024]{1,0:T(8,128)(2,1)}, u32[]{:S(2)}, u32[]{:S(2)}) collective-permute-start(bf16[256,1024]{1,0:T(8,128)(2,1)} %slice.1050), channel_id=1, source_target_pairs={{0,2},{1,3},{2,0},{3,1},{4,6},{5,7},{6,4},{7,5},{8,10},{9,11},{10,... | collective-permute-start | bytes 1572872 | tf_op jit(solution)/shard_map/ppermute | solution.py:38
  581.1 63.1 %all-to-all-start.2 = ((bf16[4,2000,128]{2,1,0:T(8,128)(2,1)}), bf16[4,2000,128]{2,1,0:T(8,128)(2,1)S(1)}, u32[]{:S(2)}, u32[]{:S(2)}) async-start(bf16[4,2000,128]{2,1,0:T(8,128)(2,1)} %pad_maximum_fusion.9), calls=%async_computation.2 | async-start | bytes 4096000 | tf_op jit(solution)/shard_map/all_to_all | solution.py:1184
  595.8 48.4 %collective-permute-start.50 = (bf16[2048,512]{1,0:T(8,128)(2,1)}, bf16[2048,512]{1,0:T(8,128)(2,1)}, u32[]{:S(2)}, u32[]{:S(2)}) collective-permute-start(bf16[2048,512]{1,0:T(8,128)(2,1)} %get-tuple-element.242), channel_id=1, source_target_pairs={{0,4},{4,0},{8,12},{12,8},{16,20},{20,16},{24,28},{28,24},{1,5},{5... | collective-permute-start | bytes 6291464 | tf_op jit(solution)/shard_map/ppermute | solution.py:38
  623.4 20.8 %collective-permute-start.53 = (bf16[512,1024]{1,0:T(8,128)(2,1)}, bf16[512,1024]{1,0:T(8,128)(2,1)}, u32[]{:S(2)}, u32[]{:S(2)}) collective-permute-start(bf16[512,1024]{1,0:T(8,128)(2,1)} %slice.1043), channel_id=1, source_target_pairs={{0,1},{1,0},{2,3},{3,2},{4,5},{5,4},{6,7},{7,6},{8,9},{9,8},{10,11... | collective-permute-start | bytes 3145736 | tf_op jit(solution)/shard_map/ppermute | solution.py:38
  654.0 39.0 %collective-permute-start.54 = (bf16[2048,256]{1,0:T(8,128)(2,1)}, bf16[2048,256]{1,0:T(8,128)(2,1)}, u32[]{:S(2)}, u32[]{:S(2)}) collective-permute-start(bf16[2048,256]{1,0:T(8,128)(2,1)} %slice.1042), channel_id=1, source_target_pairs={{0,8},{4,12},{8,0},{12,4},{16,24},{20,28},{24,16},{28,20},{1,9},{5... | collective-permute-start | bytes 3145736 | tf_op jit(solution)/shard_map/ppermute | solution.py:38
  654.7 24.3 %collective-permute-start.55 = (bf16[256,1024]{1,0:T(8,128)(2,1)}, bf16[256,1024]{1,0:T(8,128)(2,1)S(1)}, u32[]{:S(2)}, u32[]{:S(2)}) collective-permute-start(bf16[256,1024]{1,0:T(8,128)(2,1)} %slice.1049), channel_id=1, source_target_pairs={{0,2},{1,3},{2,0},{3,1},{4,6},{5,7},{6,4},{7,5},{8,10},{9,11},{10,... | collective-permute-start | bytes 1572872 | tf_op jit(solution)/shard_map/ppermute | solution.py:38
  683.0 17.7 %all-to-all-start.3 = ((bf16[8,256,128]{2,1,0:T(8,128)(2,1)}), bf16[8,256,128]{2,1,0:T(8,128)(2,1)S(1)}, u32[]{:S(2)}, u32[]{:S(2)}) async-start(bf16[8,256,128]{2,1,0:T(8,128)(2,1)} %embed_back.1), calls=%async_computation.3 | async-start | bytes 1048576 | tf_op jit(solution)/shard_map/all_to_all | solution.py:1222
  686.8 32.0 %collective-permute-start.57 = (bf16[1120,512]{1,0:T(8,128)(2,1)}, bf16[1120,512]{1,0:T(8,128)(2,1)}, u32[]{:S(2)}, u32[]{:S(2)}) collective-permute-start(bf16[1120,512]{1,0:T(8,128)(2,1)} %pad_maximum_fusion.16), channel_id=1, source_target_pairs={{0,4},{4,0},{8,12},{12,8},{16,20},{20,16},{24,28},{28,24},{1,5},{5... | collective-permute-start | bytes 3440648 | tf_op jit(solution)/shard_map/ppermute | solution.py:38
  702.8 23.6 %collective-permute-start.56 = (bf16[2048,128]{1,0:T(8,128)(2,1)S(1)}, bf16[2048,128]{1,0:T(8,128)(2,1)S(1)}, u32[]{:S(2)}, u32[]{:S(2)}) collective-permute-start(bf16[2048,128]{1,0:T(8,128)(2,1)S(1)} %slice.1048), channel_id=1, source_target_pairs={{0,16},{4,20},{8,24},{12,28},{16,0},{20,4},{24,8},{28,12},{1,17},{... | collective-permute-start | bytes 1572872 | tf_op jit(solution)/shard_map/ppermute | solution.py:38
  720.5 18.1 %collective-permute-start.58 = (bf16[1120,256]{1,0:T(8,128)(2,1)S(1)}, bf16[1120,256]{1,0:T(8,128)(2,1)S(1)}, u32[]{:S(2)}, u32[]{:S(2)}) collective-permute-start(bf16[1120,256]{1,0:T(8,128)(2,1)S(1)} %slice.1047), channel_id=1, source_target_pairs={{0,8},{4,12},{8,0},{12,4},{16,24},{20,28},{24,16},{28,20},{1,9},{5... | collective-permute-start | bytes 1720328 | tf_op jit(solution)/shard_map/ppermute | solution.py:38
  738.8 15.8 %collective-permute-start.60 = (bf16[1120,128]{1,0:T(8,128)(2,1)S(1)}, bf16[1120,128]{1,0:T(8,128)(2,1)S(1)}, u32[]{:S(2)}, u32[]{:S(2)}) collective-permute-start(bf16[1120,128]{1,0:T(8,128)(2,1)S(1)} %slice.1057), channel_id=1, source_target_pairs={{0,16},{4,20},{8,24},{12,28},{16,0},{20,4},{24,8},{28,12},{1,17},{... | collective-permute-start | bytes 860168 | tf_op jit(solution)/shard_map/ppermute | solution.py:38
  741.4 17.7 %collective-permute-start.61 = (bf16[2,8,256,128]{3,2,1,0:T(8,128)(2,1)}, bf16[2,8,256,128]{3,2,1,0:T(8,128)(2,1)}, u32[]{:S(2)}, u32[]{:S(2)}) collective-permute-start(bf16[2,8,256,128]{3,2,1,0:T(8,128)(2,1)} %get-tuple-element.410), channel_id=1, source_target_pairs={{0,1},{1,0},{2,3},{3,2},{4,5},{5,4},{6,7},{7,6},{8,9},{9,8},{10,11... | collective-permute-start | bytes 3145736 | tf_op jit(solution)/shard_map/ppermute | solution.py:38
  (207 other events, 2113.9 us)

commit v9 on v8

--- a/solution.py
+++ b/solution.py
@@ -1024,8 +1024,18 @@
 
     old_normed = state_norm(place, gain_vals[0], old_states, RATE)
 
+    words = vocab // reach
+    z = d // 2
+    word_start = (h * vocab + z * words).astype(single)
+    wanted_all = targets_all - word_start
+    wanted_all = jnp.where((wanted_all >= 0) & (wanted_all < words), wanted_all, -1.0)
+    info_all = jnp.stack([wanted_all, mask_all] + [jnp.zeros_like(mask_all)] * 6)
+    info_all = jnp.transpose(info_all, (1, 0, 2, 3, 4)).reshape(reach, 8, per_group)
+
     def beside_old(moved):
-        moved, looked, kept["old"] = together(moved, kept["looked"], old_normed)
+        moved, looked, kept["old"], kept["info"] = together(
+            moved, kept["looked"], old_normed, info_all
+        )
         kept["embedded"], kept["normed"] = place_embedding(place, looked, gain_vals[0])
         return moved
 
@@ -1046,6 +1056,7 @@
 
     words = vocab // reach
     z = d // 2
+    unsigned_z = z.astype(jnp.uint32)
     z_groups = [[2 * i + b for i in range(reach)] for b in range(2)]
     slots = -(-words // 256) * 256
 
@@ -1066,12 +1077,12 @@
     attn_sum, (far_up,) = core_sum(
         *split(mm(mixed, own_one[3 * wide : 4 * wide]), 0, 2), (far_up,)
     )
-    attn_sum, (early, far_down) = stream_sum(attn_sum, (early_sums(mixed), far_down))
+    attn_sum, (far_down,) = stream_sum(attn_sum, (far_down,))
     after_attn = embedded + attn_sum
     ffn_in, inv_second = rms(after_attn, gain_vals[1])
     ffn_in, (low_table,) = group_both(ffn_in, (low_table,))
     near_table = [
-        lax.dynamic_index_in_dim(low_table, z ^ (m // 2), 0, keepdims=False) for m in order[:reach]
+        lax.dynamic_index_in_dim(low_table, unsigned_z ^ jnp.uint32(m // 2), 0, keepdims=False) for m in order[:reach]
     ]
     near_table = jnp.concatenate(near_table, axis=1)
     near_table = jnp.concatenate([near_table, jnp.zeros((slots - words, D // 2), lowp)], axis=0)
@@ -1084,11 +1095,7 @@
     after_ffn = after_attn + group_sum(mm(hidden_act, full_down))
     final_in, inv_third = rms(after_ffn, gain_vals[2])
 
-    word_start = (h * vocab + z * words).astype(single)
-    wanted_all = targets_all - word_start
-    wanted_all = jnp.where((wanted_all >= 0) & (wanted_all < words), wanted_all, -1.0)
-    info_all = jnp.stack([wanted_all, mask_all] + [jnp.zeros_like(mask_all)] * 6)
-    info_all = jnp.transpose(info_all, (1, 0, 2, 3, 4)).reshape(reach, 8, per_group)
+    info_all = kept["info"]
     pieces = [final_in]
     chunks = []
     raised = []
@@ -1158,7 +1165,7 @@
         count = len(parts) // 2
         moved = swap(reorder(parts[count:], mask), "dp", mask)
         if mask == 2:
-            moved, dlogits[0] = together(moved, dlogits[0])
+            moved, dlogits[0], early = together(moved, dlogits[0], early_sums(log_total))
         elif mask == 4:
             moved, *table_parts = together(moved, *table_grad_part(dlogits, chunks))
         moved = split(moved.astype(single), 0, count)
@@ -1176,10 +1183,15 @@
     ffn_in_grad, (*two, moved_table) = group_sum(mm(pre_grad, full_up), (*two, moved_table))
     keep = table_parts[0] + moved_table.astype(single)
     table_pieces = jnp.stack(split(keep[:words].astype(lowp), 1, reach))
-    position = [order.index(2 * i) for i in range(reach)]
-    position = jnp.asarray(position, jnp.int32)[jnp.arange(reach) ^ z]
+    turned = sum(
+        ((unsigned_z >> bit) & 1) * jnp.uint32(order.index(2 << bit))
+        for bit in range(reach.bit_length() - 1)
+    )
     table_pieces = jnp.concatenate(
-        [lax.dynamic_index_in_dim(table_pieces, position[i], 0) for i in range(reach)]
+        [
+            lax.dynamic_index_in_dim(table_pieces, turned ^ jnp.uint32(order.index(2 * i)), 0)
+            for i in range(reach)
+        ]
     )
     table_pieces = lax.all_to_all(table_pieces, "dp", 0, 0, axis_index_groups=z_groups)
     grad_after_attn = grad_after_ffn + rms_back(after_attn, inv_second, gain_vals[1], ffn_in_grad)
@@ -1190,17 +1202,11 @@
     seg_grad, comp_grad, mem_grad = attend_back(info, seg, comp, mem, lse, mixed_grad)
     seg_grad = seg_grad.reshape(-1, 3 * wide)
 
-    def beside_expand(moved):
+    def beside_sums(moved):
         keep, send = split(mm(seg_grad, in_weight), 0, 2)
         more = swap(send.astype(lowp), "head", 1)
-        moved, more, kept["table"], *kept["old"] = together(
-            moved, more, table_pieces, *expand(comp_grad, old_raw, full_conv)
-        )
-        kept["seg_in"] = split(keep + more.astype(single), 0, 2)
-        return moved
-
-    def beside_sums(moved):
-        seg_in, seg_in_far = kept["seg_in"]
+        more, *kept["old"] = together(more, *expand(comp_grad, old_raw, full_conv))
+        seg_in, seg_in_far = split(keep + more.astype(single), 0, 2)
         seg_in_far = swap(seg_in_far.astype(lowp), "head", 2)
         old_grad, conv_sum = kept["old"]
         sums = attn_grads(
@@ -1215,11 +1221,17 @@
         )
         conv_sum = split(conv_block_order(conv_sum), 1, 2)
         sums = [jnp.concatenate([part, more.astype(part.dtype)]) for part, more in zip(sums, conv_sum)]
-        seg_in_far, *kept["sums"] = together(seg_in_far, *sums)
+        moved, kept["table"], seg_in_far, *kept["sums"] = together(
+            moved, table_pieces, seg_in_far, *sums
+        )
         rows_grad = embed_back(
             place, embedded_low, gain_vals[0], seg_in, seg_in_far, grad_after_attn
         )
-        moved, kept["rows"] = together(moved, lax.all_to_all(rows_grad, "dp", 0, 0))
+        kept["rows"] = lax.all_to_all(rows_grad, "dp", 0, 0)
+        return moved
+
+    def beside_exchange(moved):
+        moved, kept["rows"] = together(moved, kept["rows"])
         return moved
 
     def beside_rows(moved):
@@ -1231,7 +1243,7 @@
         kept["rows"] = jnp.stack([kept["rows"], far])
         return moved
 
-    two = reduce_blocks(*two, (beside_expand, beside_sums))
+    two = reduce_blocks(*two, (beside_sums, beside_exchange))
     one = reduce_blocks(*kept["sums"], (beside_rows, beside_streams))
     rows_grad = kept["rows"]
     rows_grad = jnp.stack([rows_grad, swap(rows_grad, "head", 1)]).reshape(-1, width)

time: 875 us -> 910 us (1.040)
  waiting for transfers between devices: 193 us -> 254 us
  local copies, waits for them, and re-layouts: 89.3 us -> 75.6 us
  starting transfers between devices: 79.3 us -> 89.2 us
    ppermute x70, waiting for transfers between devices: 183 us -> 226 us  [swap(): return lax.ppermute(value, axis, [(i, i ^ mask) for i in range(size)])]
    all_to_all x1, waiting for transfers between devices: 7.73 us -> 20.1 us  [beside_sums(): kept['rows'] = lax.all_to_all(rows_grad, 'dp', 0, 0)]
    ppermute x70, starting transfers between devices: 63.2 us -> 73.6 us  [swap(): return lax.ppermute(value, axis, [(i, i ^ mask) for i in range(size)])]
    unnamed x351 -> x319, local copies, waits for them, and re-layouts: 33.1 us -> 31.1 us
  transfers between devices with their start and end apart: 74 -> 74, of which waited for: 43 -> 43; matrix products, arithmetic and copies ran while one was open for 20% -> 18% of each run, Pallas kernels for 27% -> 26%
where the time goes in v9:
time: 910 us; the launch traced here: 905 us
  Pallas kernels  264 us (29%)
  waiting for transfers between devices  254 us (28%)
  other arithmetic  148 us (16%)
  starting transfers between devices  89.2 us (10%)
  local copies, waits for them, and re-layouts  75.6 us (8%)
  matrix products  36.3 us (4%)
  between operations  26 us (3%)
  blocking collectives  11 us (1%)
    ppermute x70, waiting for transfers between devices, swap(): return lax.ppermute(value, axis, [(i, i ^ mask) for i in range(size)])  226 us
    ppermute x70, starting transfers between devices, swap(): return lax.ppermute(value, axis, [(i, i ^ mask) for i in range(size)])  73.6 us
    pallas_call x4, Pallas kernels, logits_part(): pl.pallas_call(functools.partial(logits_kernel, words), name='logits_part...  44.3 us
    pallas_call x4, Pallas kernels, logits_back(): pl.pallas_call(logits_back_kernel, name='logits_back', grid=(2,), out_sha...  44.1 us
    dot_general x11, matrix products, mm(): return lax.dot_general(left, right, dims, preferred_element_type=single)  36.3 us
    unnamed x319, local copies, waits for them, and re-layouts  31.1 us
    pallas_call x1, Pallas kernels, table_grad_part(): pl.pallas_call(functools.partial(table_grad_kernel, count), name='table_g...  24.6 us
    pallas_call x1, Pallas kernels, own_list(): pl.pallas_call(list_kernel, name='own_list', out_shape=(jax.ShapeDtypeStr...  21.4 us
  transfers between devices with their start and end apart: 74, of which 43 were waited for; matrix products, arithmetic and copies ran while one was open for 18% of the time, Pallas kernels for 26%

profile of v9, /device:TPU:0, one launch (start us, length us, event | category | flops | bytes accessed | tf_op | source)
XLA Modules:
  0.0 904.6 jit_solution(15929710748531570098)
XLA Ops:
  36.7 8.6 lookup.3
  84.0 9.9 %state_norm.3.old_ref = bf16[3,1024,1024]{2,1,0:T(8,128)(2,1)} custom-call(s32[2]{0:T(128)} %pad_add_fusion.place_ref, f32[1,1024]{1,0:T(1,128)} %bitcast.359, bf16[2,1536,1024]{2,1,0:T(8,128)(2,1)} %in_ref.3), custom_call_target="tpu_custom_call" | custom-call | bytes 251658 | tf_op jit(solution)/shard_map/state_norm/pallas_call | solution.py:353
  94.7 18.7 %collective-permute-done.7 = bf16[2048,128]{1,0:T(8,128)(2,1)} collective-permute-done((bf16[2048,128]{1,0:T(8,128)(2,1)S(1)}, bf16[2048,128]{1,0:T(8,128)(2,1)}, u32[]{:S(2)}, u32[]{:S(2)}) %collective-permute-start.7) | collective-permute-done | bytes 524320 | tf_op jit(solution)/shard_map/ppermute | solution.py:38
  130.9 12.2 %compress.1 = (bf16[1024,512]{1,0:T(8,128)(2,1)}, bf16[3,1024,512]{2,1,0:T(8,128)(2,1)}) custom-call(bf16[3,1024,1024]{2,1,0:T(8,128)(2,1)} %state_norm.3.old_ref, bf16[1120,1024]{1,0:T(8,128)(2,1)} %copy-done.9, bf16[1120,1024]{1,0:T(8,128)(2,1)} %copy-done.9, bf16[2,384,128]{2,1,0:T(8,128)(2,1)} %bitcast.329), custom_call_target="tpu_custom_call" | custom-call | flops 64424508 | bytes 251658 | tf_op jit(solution)/shard_map/compress/pallas_call | solution.py:395
  156.1 10.9 %attend.1 = (bf16[2,2,256,256]{3,2,1,0:T(8,128)(2,1)}, f32[2,2,512,1]{3,2,1,0:T(8,128)}) custom-call(s32[8]{0:T(128)} %fusion.115.info_ref, bf16[2,2,256,768]{3,2,1,0:T(8,128)(2,1)} %bitcast.304, bf16[2,2,256,768]{3,2,1,0:T(8,128)(2,1)} %bitcast.305, bf16[2,2,256,768]{3,2,1,0:T(8,128)(2,1)} %bitcast.306, bf16[1024,512]{1,0:T(8,128)(2,1)} %get-tuple-element.167.kc_ref.vc_ref, ...), custom_call_target="tpu_custom_call" | custom-call | flops 146800640 | bytes 125829 | tf_op jit(solution)/shard_map/attend/pallas_call | solution.py:547
  181.5 21.7 %collective-permute-done.15 = bf16[1024,512]{1,0:T(8,128)(2,1)S(1)} collective-permute-done((bf16[1024,512]{1,0:T(8,128)(2,1)}, bf16[1024,512]{1,0:T(8,128)(2,1)S(1)}, u32[]{:S(2)}, u32[]{:S(2)}) %collective-permute-start.15) | collective-permute-done | bytes 1048608 | tf_op jit(solution)/shard_map/ppermute | solution.py:38
  205.7 11.8 %collective-permute-done.16 = bf16[256,1024]{1,0:T(8,128)(2,1)} collective-permute-done((bf16[256,1024]{1,0:T(8,128)(2,1)S(1)}, bf16[256,1024]{1,0:T(8,128)(2,1)}, u32[]{:S(2)}, u32[]{:S(2)}) %collective-permute-start.16) | collective-permute-done | bytes 524320 | tf_op jit(solution)/shard_map/ppermute | solution.py:38
  250.2 10.9 %collective-permute-done.19 = bf16[256,1024]{1,0:T(8,128)(2,1)S(1)} collective-permute-done((bf16[256,1024]{1,0:T(8,128)(2,1)S(1)}, bf16[256,1024]{1,0:T(8,128)(2,1)S(1)}, u32[]{:S(2)}, u32[]{:S(2)}) %collective-permute-start.19) | collective-permute-done | bytes 524320 | tf_op jit(solution)/shard_map/ppermute | solution.py:38
  266.2 9.8 %collective-permute-done.23 = bf16[256,1024]{1,0:T(8,128)(2,1)} collective-permute-done((bf16[256,1024]{1,0:T(8,128)(2,1)S(1)}, bf16[256,1024]{1,0:T(8,128)(2,1)}, u32[]{:S(2)}, u32[]{:S(2)}) %collective-permute-start.23) | collective-permute-done | bytes 524320 | tf_op jit(solution)/shard_map/ppermute | solution.py:38
  277.4 21.4 %own_list.1 = (s32[8200]{0:T(1024)}, s32[1]{0:T(128)}) custom-call(s32[8192]{0:T(1024)} %get-tuple-element.177.code_ref), custom_call_target="tpu_custom_call" | custom-call | bytes 1258291 | tf_op jit(solution)/shard_map/own_list/pallas_call | solution.py:209
  304.7 11.0 %logits_part.4 = (bf16[1024,2048]{1,0:T(8,128)(2,1)}, f32[8,1024]{1,0:T(8,128)}) custom-call(f32[4,8,1024]{2,1,0:T(8,128)} %bitcast.310, bf16[512,1024]{1,0:T(8,128)(2,1)} %copy-done.14, bf16[512,1024]{1,0:T(8,128)(2,1)} %collective-permute-done.24.near_ref.refs_5_, bf16[2048,512]{1,0:T(8,128)(2,1)} %copy-done, ...), custom_call_target="tpu_custom_call" | custom-call | flops 171798688 | bytes 209715 | tf_op jit(solution)/shard_map/logits_part/pallas_call | solution.py:635
  315.7 11.3 %collective-permute-done.22 = bf16[512,1024]{1,0:T(8,128)(2,1)} collective-permute-done((bf16[512,1024]{1,0:T(8,128)(2,1)}, bf16[512,1024]{1,0:T(8,128)(2,1)}, u32[]{:S(2)}, u32[]{:S(2)}) %collective-permute-start.22) | collective-permute-done | bytes 1048608 | tf_op jit(solution)/shard_map/ppermute | solution.py:38
  331.4 11.4 %logits_part.5 = (bf16[1024,2048]{1,0:T(8,128)(2,1)}, f32[8,1024]{1,0:T(8,128)}) custom-call(f32[4,8,1024]{2,1,0:T(8,128)} %bitcast.311, bf16[512,1024]{1,0:T(8,128)(2,1)} %copy-done.23, bf16[512,1024]{1,0:T(8,128)(2,1)} %copy-done.38, bf16[2048,512]{1,0:T(8,128)(2,1)} %copy-done, bf16[2048,512]{1,0:T(8,128)(2,1)} %collective-permute-done.25.right_ref), custom_call_target="tpu_custom_call" | custom-call | flops 171798688 | bytes 209715 | tf_op jit(solution)/shard_map/logits_part/pallas_call | solution.py:635
  346.6 11.0 %logits_part.6 = (bf16[1024,2048]{1,0:T(8,128)(2,1)}, f32[8,1024]{1,0:T(8,128)}) custom-call(f32[4,8,1024]{2,1,0:T(8,128)} %bitcast.312, bf16[512,1024]{1,0:T(8,128)(2,1)} %copy-done.15, bf16[512,1024]{1,0:T(8,128)(2,1)} %copy-done.39, bf16[2048,512]{1,0:T(8,128)(2,1)} %copy-done, bf16[2048,512]{1,0:T(8,128)(2,1)} %collective-permute-done.25.right_ref), custom_call_target="tpu_custom_call" | custom-call | flops 171798688 | bytes 209715 | tf_op jit(solution)/shard_map/logits_part/pallas_call | solution.py:635
  361.4 10.9 %logits_part.7 = (bf16[1024,2048]{1,0:T(8,128)(2,1)}, f32[8,1024]{1,0:T(8,128)}) custom-call(f32[4,8,1024]{2,1,0:T(8,128)} %bitcast.313, bf16[512,1024]{1,0:T(8,128)(2,1)} %copy-done.16, bf16[512,1024]{1,0:T(8,128)(2,1)} %copy-done.40, bf16[2048,512]{1,0:T(8,128)(2,1)} %copy-done, bf16[2048,512]{1,0:T(8,128)(2,1)} %collective-permute-done.25.right_ref), custom_call_target="tpu_custom_call" | custom-call | flops 171798688 | bytes 209715 | tf_op jit(solution)/shard_map/logits_part/pallas_call | solution.py:635
  391.3 11.1 %logits_back.4 = (bf16[1024,2048]{1,0:T(8,128)(2,1)}, bf16[512,1024]{1,0:T(8,128)(2,1)}, bf16[512,1024]{1,0:T(8,128)(2,1)}) custom-call(f32[4,8,1024]{2,1,0:T(8,128)} %bitcast.315, f32[4,8,1024]{2,1,0:T(8,128)} %broadcast_in_dim.187.factor_ref, bf16[1024,2048]{1,0:T(8,128)(2,1)} %get-tuple-element.194.in_ref, bf16[2048,512]{1,0:T(8,128)(2,1)} %copy-done, ...), custom_call_target="tpu_custom_call" | custom-call | flops 171798688 | bytes 251658 | tf_op jit(solution)/shard_map/logits_back/pallas_call | solution.py:689
  408.6 11.0 %logits_back.5 = (bf16[1024,2048]{1,0:T(8,128)(2,1)}, bf16[512,1024]{1,0:T(8,128)(2,1)}, bf16[512,1024]{1,0:T(8,128)(2,1)}) custom-call(f32[4,8,1024]{2,1,0:T(8,128)} %bitcast.316, f32[4,8,1024]{2,1,0:T(8,128)} %broadcast_in_dim.187.factor_ref, bf16[1024,2048]{1,0:T(8,128)(2,1)} %get-tuple-element.197.in_ref, bf16[2048,512]{1,0:T(8,128)(2,1)} %copy-done, ...), custom_call_target="tpu_custom_call" | custom-call | flops 171798688 | bytes 251658 | tf_op jit(solution)/shard_map/logits_back/pallas_call | solution.py:689
  428.6 11.0 %logits_back.6 = (bf16[1024,2048]{1,0:T(8,128)(2,1)}, bf16[512,1024]{1,0:T(8,128)(2,1)}, bf16[512,1024]{1,0:T(8,128)(2,1)}) custom-call(f32[4,8,1024]{2,1,0:T(8,128)} %bitcast.317, f32[4,8,1024]{2,1,0:T(8,128)} %broadcast_in_dim.187.factor_ref, bf16[1024,2048]{1,0:T(8,128)(2,1)} %get-tuple-element.203.in_ref, bf16[2048,512]{1,0:T(8,128)(2,1)} %copy-done, ...), custom_call_target="tpu_custom_call" | custom-call | flops 171798688 | bytes 251658 | tf_op jit(solution)/shard_map/logits_back/pallas_call | solution.py:689
  450.1 11.0 %logits_back.7 = (bf16[1024,2048]{1,0:T(8,128)(2,1)}, bf16[512,1024]{1,0:T(8,128)(2,1)}, bf16[512,1024]{1,0:T(8,128)(2,1)}) custom-call(f32[4,8,1024]{2,1,0:T(8,128)} %bitcast.318, f32[4,8,1024]{2,1,0:T(8,128)} %broadcast_in_dim.187.factor_ref, bf16[1024,2048]{1,0:T(8,128)(2,1)} %get-tuple-element.209.in_ref, bf16[2048,512]{1,0:T(8,128)(2,1)} %copy-done, ...), custom_call_target="tpu_custom_call" | custom-call | flops 171798688 | bytes 251658 | tf_op jit(solution)/shard_map/logits_back/pallas_call | solution.py:689
  507.4 24.6 %table_grad_part.1 = (f32[2048,512]{1,0:T(8,128)}, bf16[2048,512]{1,0:T(8,128)(2,1)}) custom-call(bf16[1024,2048]{1,0:T(8,128)(2,1)} %get-tuple-element.233.refs_0_, bf16[1024,2048]{1,0:T(8,128)(2,1)} %get-tuple-element.234.refs_1_, bf16[1024,2048]{1,0:T(8,128)(2,1)} %get-tuple-element.235.refs_2_, bf16[1024,2048]{1,0:T(8,128)(2,1)} %get-tuple-element.236.refs_3_, ...), custom_call_target="tpu_custom_call" | custom-call | flops 515396064 | bytes 629145 | tf_op jit(solution)/shard_map/table_grad_part/pallas_call | solution.py:743
  535.6 11.9 %collective-permute-done.45 = bf16[256,1024]{1,0:T(8,128)(2,1)S(1)} collective-permute-done((bf16[256,1024]{1,0:T(8,128)(2,1)S(1)}, bf16[256,1024]{1,0:T(8,128)(2,1)S(1)}, u32[]{:S(2)}, u32[]{:S(2)}) %collective-permute-start.45) | collective-permute-done | bytes 524320 | tf_op jit(solution)/shard_map/ppermute | solution.py:38
  571.1 11.4 %hidden_grads.1 = (f32[2048,512]{1,0:T(8,128)}, bf16[2048,512]{1,0:T(8,128)(2,1)}) custom-call(bf16[1024,1024]{1,0:T(8,128)(2,1)} %copy-done.54, bf16[1024,1024]{1,0:T(8,128)(2,1)} %copy-done.53, bf16[1024,1024]{1,0:T(8,128)(2,1)} %pad_maximum_fusion.2.in_ref, bf16[1024,1024]{1,0:T(8,128)(2,1)} %pad_maximum_fusion.5.down_ref), custom_call_target="tpu_custom_call" | custom-call | flops 128849016 | bytes 335544 | tf_op jit(solution)/shard_map/hidden_grads/pallas_call | solution.py:778
  582.6 13.5 %collective-permute-done.49 = bf16[2048,512]{1,0:T(8,128)(2,1)} collective-permute-done((bf16[2048,512]{1,0:T(8,128)(2,1)}, bf16[2048,512]{1,0:T(8,128)(2,1)}, u32[]{:S(2)}, u32[]{:S(2)}) %collective-permute-start.49) | collective-permute-done | bytes 2097184 | tf_op jit(solution)/shard_map/ppermute | solution.py:38
  604.4 9.5 %collective-permute-done.51 = bf16[256,1024]{1,0:T(8,128)(2,1)S(1)} collective-permute-done((bf16[256,1024]{1,0:T(8,128)(2,1)S(1)}, bf16[256,1024]{1,0:T(8,128)(2,1)S(1)}, u32[]{:S(2)}, u32[]{:S(2)}) %collective-permute-start.51) | collective-permute-done | bytes 524320 | tf_op jit(solution)/shard_map/ppermute | solution.py:38
  624.4 15.2 %attend_back.1 = (bf16[2,2,256,768]{3,2,1,0:T(8,128)(2,1)}, bf16[1024,512]{1,0:T(8,128)(2,1)}, bf16[1024,512]{1,0:T(8,128)(2,1)}) custom-call(s32[8]{0:T(128)} %fusion.115.info_ref, bf16[2,2,256,768]{3,2,1,0:T(8,128)(2,1)} %bitcast.307, bf16[2,2,256,768]{3,2,1,0:T(8,128)(2,1)} %bitcast.308, bf16[2,2,256,768]{3,2,1,0:T(8,128)(2,1)} %bitcast.309, ...), custom_call_target="tpu_custom_call" | custom-call | flops 230686720 | bytes 188743 | tf_op jit(solution)/shard_map/attend_back/pallas_call | solution.py:570
  670.8 14.3 %attn_grads.1 = (f32[1024,512]{1,0:T(8,128)}, bf16[1024,512]{1,0:T(8,128)(2,1)}) custom-call(bf16[1024,768]{1,0:T(8,128)(2,1)} %bitcast.332, bf16[1024,256]{1,0:T(8,128)(2,1)} %bitcast.326, bf16[1024,512]{1,0:T(8,128)(2,1)} %get-tuple-element.255.mem_ref, bf16[3072,512]{1,0:T(8,128)(2,1)} %bitcast.327, bf16[1024,1024]{1,0:T(8,128)(2,1)} %pad_maximum_fusion.1.normed_ref, ...), custom_call_target="tpu_custom_call" | custom-call | flops 188743680 | bytes 503316 | tf_op jit(solution)/shard_map/attn_grads/pallas_call | solution.py:828
  689.1 10.5 %collective-permute-done.50 = bf16[2048,512]{1,0:T(8,128)(2,1)} collective-permute-done((bf16[2048,512]{1,0:T(8,128)(2,1)}, bf16[2048,512]{1,0:T(8,128)(2,1)}, u32[]{:S(2)}, u32[]{:S(2)}) %collective-permute-start.50) | collective-permute-done | bytes 2097184 | tf_op jit(solution)/shard_map/ppermute | solution.py:38
  721.5 20.1 %all-to-all-done.3 = bf16[8,256,128]{2,1,0:T(8,128)(2,1)S(1)} async-done(((bf16[8,256,128]{2,1,0:T(8,128)(2,1)}), bf16[8,256,128]{2,1,0:T(8,128)(2,1)S(1)}, u32[]{:S(2)}, u32[]{:S(2)}) %all-to-all-start.3) | async-done | bytes 524320 | tf_op jit(solution)/shard_map/all_to_all | solution.py:1230
  752.5 15.1 %collective-permute-done.56 = bf16[2048,128]{1,0:T(8,128)(2,1)S(1)} collective-permute-done((bf16[2048,128]{1,0:T(8,128)(2,1)S(1)}, bf16[2048,128]{1,0:T(8,128)(2,1)S(1)}, u32[]{:S(2)}, u32[]{:S(2)}) %collective-permute-start.56) | collective-permute-done | bytes 524320 | tf_op jit(solution)/shard_map/ppermute | solution.py:38
  777.5 9.8 %collective-permute-done.60 = bf16[1120,128]{1,0:T(8,128)(2,1)S(1)} collective-permute-done((bf16[1120,128]{1,0:T(8,128)(2,1)S(1)}, bf16[1120,128]{1,0:T(8,128)(2,1)S(1)}, u32[]{:S(2)}, u32[]{:S(2)}) %collective-permute-start.60) | collective-permute-done | bytes 286752 | tf_op jit(solution)/shard_map/ppermute | solution.py:38
  793.9 11.4 %scatter.1 = f32[8000,128]{1,0:T(8,128)} custom-call(s32[1]{0:T(128)} %get-tuple-element.269.count_ref, s32[8200]{0:T(1024)} %get-tuple-element.270.code_ref, f32[8000,128]{1,0:T(8,128)} %bitcast_convert_fusion.base_ref, bf16[8192,128]{1,0:T(8,128)(2,1)} %bitcast.321), custom_call_target="tpu_custom_call" | custom-call | bytes 629145 | tf_op jit(solution)/shard_map/scatter/pallas_call | solution.py:305
  808.9 11.0 %all-reduce.1 = (f32[128]{0:T(128)S(1)}, f32[3,128]{1,0:T(4,128)S(1)}, f32[128]{0:T(128)S(1)}, f32[16]{0:T(128)S(1)}, f32[128]{0:T(128)S(1)}, /*index=5*/f32[128...) all-reduce(f32[128]{0:T(128)S(1)} %get-tuple-element.334, ...), channel_id=1, replica_groups=mesh['dp'=8,'head'=4] {'head'}, use_global_device_ids=true, to_apply=%region_23.24 | all-reduce | flops 1424 | bytes 11392 | tf_op jit(solution)/shard_map/psum | solution.py:1282
  (742 shorter events, 464.5 us)
Async XLA Ops:
  25.0 20.3 %collective-permute-start.3 = (bf16[1120,128]{1,0:T(8,128)(2,1)S(1)}, bf16[1120,128]{1,0:T(8,128)(2,1)S(1)}, u32[]{:S(2)}, u32[]{:S(2)}) collective-permute-start(bf16[1120,128]{1,0:T(8,128)(2,1)S(1)} %pad_maximum_fusion.28), channel_id=1, source_target_pairs={{0,16},{4,20},{8,24},{12,28},{16,0},{20,4},{24,8},{28,12},{1,17},{... | collective-permute-start | bytes 860168 | tf_op jit(solution)/shard_map/ppermute | solution.py:38
  72.7 40.7 %all-to-all-start = ((bf16[8,256,128]{2,1,0:T(8,128)(2,1)}), bf16[8,256,128]{2,1,0:T(8,128)(2,1)S(1)}, u32[]{:S(2)}, u32[]{:S(2)}) async-start(bf16[8,256,128]{2,1,0:T(8,128)(2,1)} %bitcast.20), calls=%async_computation | async-start | bytes 1048576 | tf_op jit(solution)/shard_map/all_to_all | solution.py:995
  78.8 43.2 %collective-permute-start.10 = (bf16[1120,512]{1,0:T(8,128)(2,1)}, bf16[1120,512]{1,0:T(8,128)(2,1)}, u32[]{:S(2)}, u32[]{:S(2)}) collective-permute-start(bf16[1120,512]{1,0:T(8,128)(2,1)} %get-tuple-element.413), channel_id=1, source_target_pairs={{0,4},{4,0},{8,12},{12,8},{16,20},{20,16},{24,28},{28,24},{1,5},{5... | collective-permute-start | bytes 3440648 | tf_op jit(solution)/shard_map/ppermute | solution.py:38
  80.8 32.6 %collective-permute-start.7 = (bf16[2048,128]{1,0:T(8,128)(2,1)S(1)}, bf16[2048,128]{1,0:T(8,128)(2,1)}, u32[]{:S(2)}, u32[]{:S(2)}) collective-permute-start(bf16[2048,128]{1,0:T(8,128)(2,1)S(1)} %pad_maximum_fusion.27), channel_id=1, source_target_pairs={{0,16},{4,20},{8,24},{12,28},{16,0},{20,4},{24,8},{28,12},{1,17},{... | collective-permute-start | bytes 1572872 | tf_op jit(solution)/shard_map/ppermute | solution.py:38
  120.1 27.0 %collective-permute-start.11 = (bf16[2048,256]{1,0:T(8,128)(2,1)}, bf16[2048,256]{1,0:T(8,128)(2,1)}, u32[]{:S(2)}, u32[]{:S(2)}) collective-permute-start(bf16[2048,256]{1,0:T(8,128)(2,1)} %pad_maximum_fusion.18), channel_id=1, source_target_pairs={{0,8},{4,12},{8,0},{12,4},{16,24},{20,28},{24,16},{28,20},{1,9},{5... | collective-permute-start | bytes 3145736 | tf_op jit(solution)/shard_map/ppermute | solution.py:38
  129.9 22.0 %collective-permute-start.9 = (bf16[512,1024]{1,0:T(8,128)(2,1)}, bf16[512,1024]{1,0:T(8,128)(2,1)}, u32[]{:S(2)}, u32[]{:S(2)}) collective-permute-start(bf16[512,1024]{1,0:T(8,128)(2,1)} %pad_maximum_fusion.17), channel_id=1, source_target_pairs={{0,1},{1,0},{2,3},{3,2},{4,5},{5,4},{6,7},{7,6},{8,9},{9,8},{10,11... | collective-permute-start | bytes 3145736 | tf_op jit(solution)/shard_map/ppermute | solution.py:38
  149.9 28.0 %collective-permute-start.13 = (bf16[1024,512]{1,0:T(8,128)(2,1)}, bf16[1024,512]{1,0:T(8,128)(2,1)}, u32[]{:S(2)}, u32[]{:S(2)}) collective-permute-start(bf16[1024,512]{1,0:T(8,128)(2,1)} %get-tuple-element.400), channel_id=1, source_target_pairs={{0,4},{4,0},{8,12},{12,8},{16,20},{20,16},{24,28},{28,24},{1,5},{5... | collective-permute-start | bytes 3145736 | tf_op jit(solution)/shard_map/ppermute | solution.py:38
  173.7 51.7 %all-to-all-start.1 = ((bf16[4,2000,128]{2,1,0:T(8,128)(2,1)}), bf16[4,2000,128]{2,1,0:T(8,128)(2,1)S(1)}, u32[]{:S(2)}, u32[]{:S(2)}) async-start(bf16[4,2000,128]{2,1,0:T(8,128)(2,1)} %bitcast.322), calls=%async_computation.1 | async-start | bytes 4096000 | tf_op jit(solution)/shard_map/all_to_all | solution.py:1074
  177.6 25.6 %collective-permute-start.15 = (bf16[1024,512]{1,0:T(8,128)(2,1)}, bf16[1024,512]{1,0:T(8,128)(2,1)S(1)}, u32[]{:S(2)}, u32[]{:S(2)}) collective-permute-start(bf16[1024,512]{1,0:T(8,128)(2,1)} %get-tuple-element.399), channel_id=1, source_target_pairs={{0,4},{4,0},{8,12},{12,8},{16,20},{20,16},{24,28},{28,24},{1,5},{5... | collective-permute-start | bytes 3145736 | tf_op jit(solution)/shard_map/ppermute | solution.py:38
  179.9 23.3 %collective-permute-start.14 = (bf16[256,1024]{1,0:T(8,128)(2,1)S(1)}, bf16[256,1024]{1,0:T(8,128)(2,1)S(1)}, u32[]{:S(2)}, u32[]{:S(2)}) collective-permute-start(bf16[256,1024]{1,0:T(8,128)(2,1)S(1)} %slice.985), channel_id=1, source_target_pairs={{0,2},{1,3},{2,0},{3,1},{4,6},{5,7},{6,4},{7,5},{8,10},{9,11},{10,... | collective-permute-start | bytes 1572872 | tf_op jit(solution)/shard_map/ppermute | solution.py:38
  250.1 54.6 %collective-permute-start.25 = (bf16[2048,512]{1,0:T(8,128)(2,1)S(1)}, bf16[2048,512]{1,0:T(8,128)(2,1)}, u32[]{:S(2)}, u32[]{:S(2)}) collective-permute-start(bf16[2048,512]{1,0:T(8,128)(2,1)S(1)} %fusion.13.left_ref), channel_id=1, source_target_pairs={{0,4},{4,0},{8,12},{12,8},{16,20},{20,16},{24,28},{28,24},{1,5},{5... | collective-permute-start | bytes 6291464 | tf_op jit(solution)/shard_map/ppermute | solution.py:38
  266.2 32.6 %collective-permute-start.20 = (bf16[256,1024]{1,0:T(8,128)(2,1)}, bf16[256,1024]{1,0:T(8,128)(2,1)}, u32[]{:S(2)}, u32[]{:S(2)}) collective-permute-start(bf16[256,1024]{1,0:T(8,128)(2,1)} %reorder.4), channel_id=1, source_target_pairs={{0,16},{4,20},{8,24},{12,28},{16,0},{20,4},{24,8},{28,12},{1,17},{... | collective-permute-start | bytes 1572872 | tf_op jit(solution)/shard_map/ppermute | solution.py:38
  277.4 27.3 %collective-permute-start.24 = (bf16[512,1024]{1,0:T(8,128)(2,1)S(1)}, bf16[512,1024]{1,0:T(8,128)(2,1)}, u32[]{:S(2)}, u32[]{:S(2)}) collective-permute-start(bf16[512,1024]{1,0:T(8,128)(2,1)S(1)} %pad_maximum_fusion.20.pair_ref.refs_4_), channel_id=1, source_target_pairs={{0,1},{1,0},{2,3},{3,2},{4,5},{5,4},{6,7},{7,6},{8,9},{9,8},{10,11... | collective-permute-start | bytes 3145736 | tf_op jit(solution)/shard_map/ppermute | solution.py:38
  301.2 25.9 %collective-permute-start.22 = (bf16[512,1024]{1,0:T(8,128)(2,1)}, bf16[512,1024]{1,0:T(8,128)(2,1)}, u32[]{:S(2)}, u32[]{:S(2)}) collective-permute-start(bf16[512,1024]{1,0:T(8,128)(2,1)} %reorder.5), channel_id=1, source_target_pairs={{0,8},{4,12},{8,0},{12,4},{16,24},{20,28},{24,16},{28,20},{1,9},{5... | collective-permute-start | bytes 3145736 | tf_op jit(solution)/shard_map/ppermute | solution.py:38
  301.2 25.9 %collective-permute-start.21 = (bf16[256,1024]{1,0:T(8,128)(2,1)}, bf16[256,1024]{1,0:T(8,128)(2,1)S(1)}, u32[]{:S(2)}, u32[]{:S(2)}) collective-permute-start(bf16[256,1024]{1,0:T(8,128)(2,1)} %collective-permute-done.20.refs_1_), channel_id=1, source_target_pairs={{0,2},{1,3},{2,0},{3,1},{4,6},{5,7},{6,4},{7,5},{8,10},{9,11},{10,... | collective-permute-start | bytes 1572872 | tf_op jit(solution)/shard_map/ppermute | solution.py:38
  441.8 23.4 %collective-permute-start.39 = (bf16[512,1024]{1,0:T(8,128)(2,1)}, bf16[512,1024]{1,0:T(8,128)(2,1)S(1)}, u32[]{:S(2)}, u32[]{:S(2)}) collective-permute-start(bf16[512,1024]{1,0:T(8,128)(2,1)} %get-tuple-element.208), channel_id=1, source_target_pairs={{0,1},{1,0},{2,3},{3,2},{4,5},{5,4},{6,7},{7,6},{8,9},{9,8},{10,11... | collective-permute-start | bytes 3145736 | tf_op jit(solution)/shard_map/ppermute | solution.py:38
  472.1 25.5 %collective-permute-start.43 = (bf16[512,1024]{1,0:T(8,128)(2,1)}, bf16[512,1024]{1,0:T(8,128)(2,1)S(1)}, u32[]{:S(2)}, u32[]{:S(2)}) collective-permute-start(bf16[512,1024]{1,0:T(8,128)(2,1)} %reorder.6), channel_id=1, source_target_pairs={{0,8},{4,12},{8,0},{12,4},{16,24},{20,28},{24,16},{28,20},{1,9},{5... | collective-permute-start | bytes 3145736 | tf_op jit(solution)/shard_map/ppermute | solution.py:38
  481.2 22.9 %collective-permute-start.41 = (bf16[512,1024]{1,0:T(8,128)(2,1)}, bf16[512,1024]{1,0:T(8,128)(2,1)}, u32[]{:S(2)}, u32[]{:S(2)}) collective-permute-start(bf16[512,1024]{1,0:T(8,128)(2,1)} %get-tuple-element.214), channel_id=1, source_target_pairs={{0,1},{1,0},{2,3},{3,2},{4,5},{5,4},{6,7},{7,6},{8,9},{9,8},{10,11... | collective-permute-start | bytes 3145736 | tf_op jit(solution)/shard_map/ppermute | solution.py:38
  503.8 28.2 %collective-permute-start.44 = (bf16[256,1024]{1,0:T(8,128)(2,1)}, bf16[256,1024]{1,0:T(8,128)(2,1)S(1)}, u32[]{:S(2)}, u32[]{:S(2)}) collective-permute-start(bf16[256,1024]{1,0:T(8,128)(2,1)} %reorder.7), channel_id=1, source_target_pairs={{0,16},{4,20},{8,24},{12,28},{16,0},{20,4},{24,8},{28,12},{1,17},{... | collective-permute-start | bytes 1572872 | tf_op jit(solution)/shard_map/ppermute | solution.py:38
  505.7 26.2 %collective-permute-start.42 = (bf16[256,1024]{1,0:T(8,128)(2,1)S(1)}, bf16[256,1024]{1,0:T(8,128)(2,1)S(1)}, u32[]{:S(2)}, u32[]{:S(2)}) collective-permute-start(bf16[256,1024]{1,0:T(8,128)(2,1)S(1)} %slice.980), channel_id=1, source_target_pairs={{0,2},{1,3},{2,0},{3,1},{4,6},{5,7},{6,4},{7,5},{8,10},{9,11},{10,... | collective-permute-start | bytes 1572872 | tf_op jit(solution)/shard_map/ppermute | solution.py:38
  547.7 48.4 %collective-permute-start.49 = (bf16[2048,512]{1,0:T(8,128)(2,1)}, bf16[2048,512]{1,0:T(8,128)(2,1)}, u32[]{:S(2)}, u32[]{:S(2)}) collective-permute-start(bf16[2048,512]{1,0:T(8,128)(2,1)} %get-tuple-element.242), channel_id=1, source_target_pairs={{0,4},{4,0},{8,12},{12,8},{16,20},{20,16},{24,28},{28,24},{1,5},{5... | collective-permute-start | bytes 6291464 | tf_op jit(solution)/shard_map/ppermute | solution.py:38
  565.1 31.0 %collective-permute-start.48 = (bf16[256,1024]{1,0:T(8,128)(2,1)}, bf16[256,1024]{1,0:T(8,128)(2,1)}, u32[]{:S(2)}, u32[]{:S(2)}) collective-permute-start(bf16[256,1024]{1,0:T(8,128)(2,1)} %slice.979), channel_id=1, source_target_pairs={{0,2},{1,3},{2,0},{3,1},{4,6},{5,7},{6,4},{7,5},{8,10},{9,11},{10,... | collective-permute-start | bytes 1572872 | tf_op jit(solution)/shard_map/ppermute | solution.py:38
  617.4 82.3 %all-to-all-start.2 = ((bf16[4,2000,128]{2,1,0:T(8,128)(2,1)}), bf16[4,2000,128]{2,1,0:T(8,128)(2,1)S(1)}, u32[]{:S(2)}, u32[]{:S(2)}) async-start(bf16[4,2000,128]{2,1,0:T(8,128)(2,1)} %pad_maximum_fusion.9), calls=%async_computation.2 | async-start | bytes 4096000 | tf_op jit(solution)/shard_map/all_to_all | solution.py:1196
  646.4 16.0 %collective-permute-start.53 = (bf16[512,1024]{1,0:T(8,128)(2,1)}, bf16[512,1024]{1,0:T(8,128)(2,1)}, u32[]{:S(2)}, u32[]{:S(2)}) collective-permute-start(bf16[512,1024]{1,0:T(8,128)(2,1)} %slice.972), channel_id=1, source_target_pairs={{0,1},{1,0},{2,3},{3,2},{4,5},{5,4},{6,7},{7,6},{8,9},{9,8},{10,11... | collective-permute-start | bytes 3145736 | tf_op jit(solution)/shard_map/ppermute | solution.py:38
  651.6 48.0 %collective-permute-start.50 = (bf16[2048,512]{1,0:T(8,128)(2,1)}, bf16[2048,512]{1,0:T(8,128)(2,1)}, u32[]{:S(2)}, u32[]{:S(2)}) collective-permute-start(bf16[2048,512]{1,0:T(8,128)(2,1)} %get-tuple-element.244), channel_id=1, source_target_pairs={{0,4},{4,0},{8,12},{12,8},{16,20},{20,16},{24,28},{28,24},{1,5},{5... | collective-permute-start | bytes 6291464 | tf_op jit(solution)/shard_map/ppermute | solution.py:38
  665.1 34.5 %collective-permute-start.54 = (bf16[256,1024]{1,0:T(8,128)(2,1)S(1)}, bf16[256,1024]{1,0:T(8,128)(2,1)S(1)}, u32[]{:S(2)}, u32[]{:S(2)}) collective-permute-start(bf16[256,1024]{1,0:T(8,128)(2,1)S(1)} %slice.978), channel_id=1, source_target_pairs={{0,2},{1,3},{2,0},{3,1},{4,6},{5,7},{6,4},{7,5},{8,10},{9,11},{10,... | collective-permute-start | bytes 1572872 | tf_op jit(solution)/shard_map/ppermute | solution.py:38
  706.6 35.0 %collective-permute-start.55 = (bf16[2048,256]{1,0:T(8,128)(2,1)}, bf16[2048,256]{1,0:T(8,128)(2,1)}, u32[]{:S(2)}, u32[]{:S(2)}) collective-permute-start(bf16[2048,256]{1,0:T(8,128)(2,1)} %slice.971), channel_id=1, source_target_pairs={{0,8},{4,12},{8,0},{12,4},{16,24},{20,28},{24,16},{28,20},{1,9},{5... | collective-permute-start | bytes 3145736 | tf_op jit(solution)/shard_map/ppermute | solution.py:38
  711.8 29.8 %all-to-all-start.3 = ((bf16[8,256,128]{2,1,0:T(8,128)(2,1)}), bf16[8,256,128]{2,1,0:T(8,128)(2,1)S(1)}, u32[]{:S(2)}, u32[]{:S(2)}) async-start(bf16[8,256,128]{2,1,0:T(8,128)(2,1)} %embed_back.1), calls=%async_computation.3 | async-start | bytes 1048576 | tf_op jit(solution)/shard_map/all_to_all | solution.py:1230
  715.4 32.3 %collective-permute-start.57 = (bf16[1120,512]{1,0:T(8,128)(2,1)}, bf16[1120,512]{1,0:T(8,128)(2,1)}, u32[]{:S(2)}, u32[]{:S(2)}) collective-permute-start(bf16[1120,512]{1,0:T(8,128)(2,1)} %pad_maximum_fusion.16), channel_id=1, source_target_pairs={{0,4},{4,0},{8,12},{12,8},{16,20},{20,16},{24,28},{28,24},{1,5},{5... | collective-permute-start | bytes 3440648 | tf_op jit(solution)/shard_map/ppermute | solution.py:38
  743.7 23.8 %collective-permute-start.56 = (bf16[2048,128]{1,0:T(8,128)(2,1)S(1)}, bf16[2048,128]{1,0:T(8,128)(2,1)S(1)}, u32[]{:S(2)}, u32[]{:S(2)}) collective-permute-start(bf16[2048,128]{1,0:T(8,128)(2,1)S(1)} %slice.977), channel_id=1, source_target_pairs={{0,16},{4,20},{8,24},{12,28},{16,0},{20,4},{24,8},{28,12},{1,17},{... | collective-permute-start | bytes 1572872 | tf_op jit(solution)/shard_map/ppermute | solution.py:38
  749.4 22.8 %collective-permute-start.58 = (bf16[1120,256]{1,0:T(8,128)(2,1)S(1)}, bf16[1120,256]{1,0:T(8,128)(2,1)S(1)}, u32[]{:S(2)}, u32[]{:S(2)}) collective-permute-start(bf16[1120,256]{1,0:T(8,128)(2,1)S(1)} %slice.976), channel_id=1, source_target_pairs={{0,8},{4,12},{8,0},{12,4},{16,24},{20,28},{24,16},{28,20},{1,9},{5... | collective-permute-start | bytes 1720328 | tf_op jit(solution)/shard_map/ppermute | solution.py:38
  750.9 17.4 %collective-permute-start.59 = (bf16[8,256,128]{2,1,0:T(8,128)(2,1)S(1)}, bf16[8,256,128]{2,1,0:T(8,128)(2,1)S(1)}, u32[]{:S(2)}, u32[]{:S(2)}) collective-permute-start(bf16[8,256,128]{2,1,0:T(8,128)(2,1)S(1)} %all-to-all-done.3), channel_id=1, source_target_pairs={{0,2},{1,3},{2,0},{3,1},{4,6},{5,7},{6,4},{7,5},{8,10},{9,11},{10,... | collective-permute-start | bytes 1572872 | tf_op jit(solution)/shard_map/ppermute | solution.py:38
  (191 other events, 2306.3 us)

commit v10 on v9

--- a/solution.py
+++ b/solution.py
@@ -596,120 +596,131 @@
     return jnp.transpose(tall)
 
 
-def logits_kernel(words, info_ref, pair_ref, near_ref, left_ref, right_ref, out_ref, stat_ref, held):
+def logits_kernel(
+    words, pair_info_ref, near_info_ref, pair_ref, near_ref, left_ref, right_ref,
+    pair_out_ref, near_out_ref, stat_ref,
+):
     step = pl.program_id(0)
-
-    @pl.when(step == 0)
-    def _():
-        held[...] = pair_ref[...]
-
-    @pl.when(step == 1)
-    def _():
-        held[...] = near_ref[...]
-
+    tile = pair_ref.shape[0]
     half = left_ref.shape[1]
-    slots = left_ref.shape[0]
-    logits = mm(held[:, :half], left_ref[...], NT) + mm(held[:, half:], right_ref[...], NT)
-    wanted = columns_of(info_ref[0])[:, 0:1].astype(jnp.int32)
-    col = lax.broadcasted_iota(jnp.int32, logits.shape, 1)
-    hit = jnp.sum(jnp.where(col == wanted, logits, 0.0), axis=-1, keepdims=True)
-    edge = slots - 128
-    last = jnp.where(col[:, edge:] < words, logits[:, edge:], -1e30)
-    top = jnp.max(last, axis=-1, keepdims=True)
-    top = jnp.maximum(top, jnp.max(logits[:, :edge], axis=-1, keepdims=True))
-    raised = jnp.exp(logits[:, :edge] - top)
-    last = jnp.exp(last - top)
-    total = jnp.sum(raised, axis=-1, keepdims=True) + jnp.sum(last, axis=-1, keepdims=True)
-    out_ref[:, :edge] = raised.astype(lowp)
-    out_ref[:, edge:] = last.astype(lowp)
-    lane = lax.broadcasted_iota(jnp.int32, (logits.shape[0], 128), 1)
-    packed = jnp.where(lane == 0, top, jnp.where(lane == 1, total, jnp.where(lane == 2, hit, 0.0)))
-    stat_ref[...] = jnp.transpose(packed)[:8]
+    edge = left_ref.shape[0] - 128
+    streams = (
+        (pair_info_ref, pair_ref, pair_out_ref),
+        (near_info_ref, near_ref, near_out_ref),
+    )
+    products = [
+        mm(ref[:, :half], left_ref[...], NT) + mm(ref[:, half:], right_ref[...], NT)
+        for _, ref, _ in streams
+    ]
+    for n, ((info_ref, _, out_ref), logits) in enumerate(zip(streams, products)):
+        wanted = columns_of(info_ref[0])[:, 0:1].astype(jnp.int32)
+        col = lax.broadcasted_iota(jnp.int32, logits.shape, 1)
+        hit = jnp.sum(jnp.where(col == wanted, logits, 0.0), axis=-1, keepdims=True)
+        last = jnp.where(col[:, edge:] < words, logits[:, edge:], -1e30)
+        top = jnp.max(last, axis=-1, keepdims=True)
+        top = jnp.maximum(top, jnp.max(logits[:, :edge], axis=-1, keepdims=True))
+        raised = jnp.exp(logits[:, :edge] - top)
+        last = jnp.exp(last - top)
+        total = jnp.sum(raised, axis=-1, keepdims=True) + jnp.sum(last, axis=-1, keepdims=True)
+        out_ref[:, :edge] = raised.astype(lowp)
+        out_ref[:, edge:] = last.astype(lowp)
+        lane = lax.broadcasted_iota(jnp.int32, (tile, 128), 1)
+        packed = jnp.where(lane == 2, hit, 0.0)
+        packed = jnp.where(lane == 0, top, jnp.where(lane == 1, total, packed))
+        start = n * (stat_ref.shape[1] // 2) + step * tile
+        stat_ref[:, pl.ds(pl.multiple_of(start, tile), tile)] = jnp.transpose(packed)[:8]
 
 
 def logits_part(words, chunk, info, pair, near, left, right):
-    rows = pair.shape[0] + near.shape[0]
+    rows, _ = pair.shape
     slots = left.shape[0]
-    tile = pair.shape[0]
+    tile = 256
+    tiles = rows // tile
     whole = lambda i: (0, 0)
     return pl.pallas_call(
         functools.partial(logits_kernel, words),
         name="logits_part",
-        grid=(2,),
+        grid=(tiles,),
         out_shape=(
             jax.ShapeDtypeStruct((rows, slots), lowp),
-            jax.ShapeDtypeStruct((8, rows), single),
+            jax.ShapeDtypeStruct((rows, slots), lowp),
+            jax.ShapeDtypeStruct((8, 2 * rows), single),
         ),
         in_specs=[
             pl.BlockSpec((1, 8, tile), lambda i: (chunk, 0, i)),
-            pl.BlockSpec((tile, D), whole),
-            pl.BlockSpec((tile, D), whole),
+            pl.BlockSpec((1, 8, tile), lambda i: (chunk, 0, tiles + i)),
+            pl.BlockSpec((tile, D), lambda i: (i, 0)),
+            pl.BlockSpec((tile, D), lambda i: (i, 0)),
             pl.BlockSpec(left.shape, whole),
             pl.BlockSpec(right.shape, whole),
         ],
         out_specs=(
             pl.BlockSpec((tile, slots), lambda i: (i, 0)),
-            pl.BlockSpec((8, tile), lambda i: (0, i)),
-        ),
-        scratch_shapes=[pltpu.VMEM((tile, D), lowp)],
+            pl.BlockSpec((tile, slots), lambda i: (i, 0)),
+            pl.BlockSpec((8, 2 * rows), whole),
+        ),
         compiler_params=params(60),
-        cost_estimate=cost(4 * rows * slots * D, 10 * MIB),
-    )(info, pair, near, left, right)
-
-
-def logits_back_kernel(info_ref, factor_ref, in_ref, left_ref, right_ref, out_ref, keep_ref, send_ref):
-    step = pl.program_id(0)
-    info = columns_of(info_ref[0])
-    wanted = info[:, 0:1].astype(jnp.int32)
-    counted = info[:, 1:2]
-    factor = columns_of(factor_ref[0])[:, 0:1]
-    raised = in_ref[...].astype(single)
-    col = lax.broadcasted_iota(jnp.int32, raised.shape, 1)
-    grads = (raised * factor - jnp.where(col == wanted, counted, 0.0)).astype(lowp)
-    out_ref[...] = grads
+        cost_estimate=cost(8 * rows * slots * D, 10 * MIB),
+    )(info, info, pair, near, left, right)
+
+
+def logits_back_kernel(
+    pair_info_ref, near_info_ref, pair_factor_ref, near_factor_ref, pair_ref, near_ref,
+    left_ref, right_ref, pair_out_ref, near_out_ref, pair_grad_ref, near_grad_ref,
+):
     half = left_ref.shape[1]
-    left = mm(grads, left_ref[...]).astype(lowp)
-    right = mm(grads, right_ref[...]).astype(lowp)
-
-    @pl.when(step == 0)
-    def _():
-        send_ref[:, :half] = left
-        send_ref[:, half:] = right
-
-    @pl.when(step == 1)
-    def _():
-        keep_ref[:, :half] = left
-        keep_ref[:, half:] = right
+    streams = (
+        (near_info_ref, near_factor_ref, near_ref, near_out_ref, near_grad_ref),
+        (pair_info_ref, pair_factor_ref, pair_ref, pair_out_ref, pair_grad_ref),
+    )
+    for info_ref, factor_ref, in_ref, out_ref, grad_ref in streams:
+        info = columns_of(info_ref[0])
+        wanted = info[:, 0:1].astype(jnp.int32)
+        counted = info[:, 1:2]
+        factor = columns_of(factor_ref[0])[:, 0:1]
+        raised = in_ref[...].astype(single)
+        col = lax.broadcasted_iota(jnp.int32, raised.shape, 1)
+        grads = (raised * factor - jnp.where(col == wanted, counted, 0.0)).astype(lowp)
+        out_ref[...] = grads
+        grad_ref[:, :half] = mm(grads, left_ref[...]).astype(lowp)
+        grad_ref[:, half:] = mm(grads, right_ref[...]).astype(lowp)
 
 
 def logits_back(chunk, info, factor, raised, left, right):
-    rows, slots = raised.shape
-    tile = rows // 2
+    rows, slots = raised[0].shape
+    tile = 256
+    tiles = rows // tile
     whole = lambda i: (0, 0)
+
+    def info_specs():
+        return [
+            pl.BlockSpec((1, 8, tile), lambda i: (chunk, 0, i)),
+            pl.BlockSpec((1, 8, tile), lambda i: (chunk, 0, tiles + i)),
+        ]
+
     return pl.pallas_call(
         logits_back_kernel,
         name="logits_back",
-        grid=(2,),
+        grid=(tiles,),
         out_shape=(
             jax.ShapeDtypeStruct((rows, slots), lowp),
-            jax.ShapeDtypeStruct((tile, D), lowp),
-            jax.ShapeDtypeStruct((tile, D), lowp),
-        ),
-        in_specs=[
-            pl.BlockSpec((1, 8, tile), lambda i: (chunk, 0, 1 - i)),
-            pl.BlockSpec((1, 8, tile), lambda i: (chunk, 0, 1 - i)),
-            pl.BlockSpec((tile, slots), lambda i: (1 - i, 0)),
-            pl.BlockSpec(left.shape, whole),
-            pl.BlockSpec(right.shape, whole),
-        ],
+            jax.ShapeDtypeStruct((rows, slots), lowp),
+            jax.ShapeDtypeStruct((rows, D), lowp),
+            jax.ShapeDtypeStruct((rows, D), lowp),
+        ),
+        in_specs=info_specs()
+        + info_specs()
+        + [pl.BlockSpec((tile, slots), lambda i: (i, 0))] * 2
+        + [pl.BlockSpec(left.shape, whole), pl.BlockSpec(right.shape, whole)],
         out_specs=(
-            pl.BlockSpec((tile, slots), lambda i: (1 - i, 0)),
-            pl.BlockSpec((tile, D), whole),
-            pl.BlockSpec((tile, D), whole),
+            pl.BlockSpec((tile, slots), lambda i: (i, 0)),
+            pl.BlockSpec((tile, slots), lambda i: (i, 0)),
+            pl.BlockSpec((tile, D), lambda i: (i, 0)),
+            pl.BlockSpec((tile, D), lambda i: (i, 0)),
         ),
         compiler_params=params(60),
-        cost_estimate=cost(4 * rows * slots * D, 12 * MIB),
-    )(info, factor, raised, left, right)
+        cost_estimate=cost(8 * rows * slots * D, 12 * MIB),
+    )(info, info, factor, factor, *raised, left, right)
 
 
 def halves(total, keep_ref, send_ref):
@@ -719,29 +730,23 @@
 
 
 def table_grad_kernel(count, *refs):
-    total = None
-    for i in range(count):
-        rows = refs[count + 2 * i].shape[0]
-        for j in range(2):
-            term = mm(refs[i][j * rows : (j + 1) * rows, :], refs[count + 2 * i + j][...], TN)
-            total = term if total is None else total + term
-    halves(total, *refs[3 * count :])
+    total = mm(refs[0][...], refs[count][...], TN)
+    for i in range(1, count):
+        total = total + mm(refs[i][...], refs[count + i][...], TN)
+    halves(total, *refs[2 * count :])
 
 
 def table_grad_part(grads, inputs):
-    count = len(grads)
+    grads = [half for pair in grads for half in pair]
+    inputs = [half for pair in inputs for half in pair]
     rows = sum(g.shape[0] for g in grads)
     slots = grads[0].shape[1]
     block = 256
     if rows > 4096:
-        total = sum(
-            mm(g, jnp.concatenate(v), TN) for g, v in zip(grads, inputs)
-        )
-        keep, send = split(total, 1, 2)
+        keep, send = split(sum(mm(g, v, TN) for g, v in zip(grads, inputs)), 1, 2)
         return keep, send.astype(lowp)
-    inputs = [half for pair in inputs for half in pair]
-    return pl.pallas_call(
-        functools.partial(table_grad_kernel, count),
+    return pl.pallas_call(
+        functools.partial(table_grad_kernel, len(grads)),
         name="table_grad_part",
         grid=(slots // block,),
         out_shape=(
@@ -1077,7 +1082,7 @@
     attn_sum, (far_up,) = core_sum(
         *split(mm(mixed, own_one[3 * wide : 4 * wide]), 0, 2), (far_up,)
     )
-    attn_sum, (far_down,) = stream_sum(attn_sum, (far_down,))
+    attn_sum, (early, far_down) = stream_sum(attn_sum, (early_sums(mixed), far_down))
     after_attn = embedded + attn_sum
     ffn_in, inv_second = rms(after_attn, gain_vals[1])
     ffn_in, (low_table,) = group_both(ffn_in, (low_table,))
@@ -1104,11 +1109,12 @@
     def next_chunk():
         i = len(chunks)
         if i == 0:
-            chunks.append(group_both(pieces[i]))
+            chunk, kept["list"] = group_both(pieces[i], own_list(after(token_codes, final_in)))
+            chunks.append(chunk)
         else:
             chunk, (stats[i - 1],) = group_both(pieces[i], (stats[i - 1],))
             chunks.append(chunk)
-        out, stat = logits_part(words, i, info_all, *chunks[i], near_table, far_table)
+        *out, stat = logits_part(words, i, info_all, *chunks[i], near_table, far_table)
         raised.append(out)
         stats.append(stat)
 
@@ -1116,9 +1122,6 @@
     while mask > 1:
         moved = swap(reorder(pieces, mask), "dp", mask)
         if len(pieces) == 1:
-            moved, own_codes, own_count = together(
-                moved, *own_list(after(token_codes, final_in))
-            )
             next_chunk()
         elif len(pieces) == 2:
             moved, stats[0] = together(moved, stats[0])
@@ -1126,6 +1129,7 @@
         mask //= 2
     while len(chunks) < reach:
         next_chunk()
+    own_codes, own_count = kept["list"]
     stats = [stat[:3].reshape(3, 1, 2, 2, half) for stat in stats]
     own_stats = jnp.concatenate(stats, axis=1)
 
@@ -1149,15 +1153,17 @@
 
     factor_all = factor_all.reshape(reach, 1, per_group) * info_all[:, 1:2]
     factor_all = jnp.broadcast_to(factor_all, info_all.shape)
-    dlogits = [None] * reach
+    dlogits = [[] for _ in range(reach)]
     parts = [None] * reach
     for i in reversed(range(reach)):
-        dlogits[i], *core = logits_back(
+        *dlogits[i], keep, send = logits_back(
             i, info_all, factor_all, raised[i], near_table, far_table
         )
         if i + 1 < reach:
-            parts[i + 1], (dlogits[i], *core) = stream_sum(parts[i + 1], (dlogits[i], *core))
-        parts[i] = core_sum(*core)
+            parts[i + 1], (*dlogits[i], keep, send) = stream_sum(
+                parts[i + 1], (*dlogits[i], keep, send)
+            )
+        parts[i] = core_sum(keep, send)
     parts[0] = stream_sum(parts[0])
     table_parts = []
     mask = 2
@@ -1165,7 +1171,7 @@
         count = len(parts) // 2
         moved = swap(reorder(parts[count:], mask), "dp", mask)
         if mask == 2:
-            moved, dlogits[0], early = together(moved, dlogits[0], early_sums(log_total))
+            moved, *dlogits[0] = together(moved, *dlogits[0])
         elif mask == 4:
             moved, *table_parts = together(moved, *table_grad_part(dlogits, chunks))
         moved = split(moved.astype(single), 0, count)
@@ -1202,11 +1208,17 @@
     seg_grad, comp_grad, mem_grad = attend_back(info, seg, comp, mem, lse, mixed_grad)
     seg_grad = seg_grad.reshape(-1, 3 * wide)
 
-    def beside_sums(moved):
+    def beside_expand(moved):
         keep, send = split(mm(seg_grad, in_weight), 0, 2)
         more = swap(send.astype(lowp), "head", 1)
-        more, *kept["old"] = together(more, *expand(comp_grad, old_raw, full_conv))
-        seg_in, seg_in_far = split(keep + more.astype(single), 0, 2)
+        moved, more, kept["table"], *kept["old"] = together(
+            moved, more, table_pieces, *expand(comp_grad, old_raw, full_conv)
+        )
+        kept["seg_in"] = split(keep + more.astype(single), 0, 2)
+        return moved
+
+    def beside_sums(moved):
+        seg_in, seg_in_far = kept["seg_in"]
         seg_in_far = swap(seg_in_far.astype(lowp), "head", 2)
         old_grad, conv_sum = kept["old"]
         sums = attn_grads(
@@ -1221,17 +1233,11 @@
         )
         conv_sum = split(conv_block_order(conv_sum), 1, 2)
         sums = [jnp.concatenate([part, more.astype(part.dtype)]) for part, more in zip(sums, conv_sum)]
-        moved, kept["table"], seg_in_far, *kept["sums"] = together(
-            moved, table_pieces, seg_in_far, *sums
-        )
+        seg_in_far, *kept["sums"] = together(seg_in_far, *sums)
         rows_grad = embed_back(
             place, embedded_low, gain_vals[0], seg_in, seg_in_far, grad_after_attn
         )
-        kept["rows"] = lax.all_to_all(rows_grad, "dp", 0, 0)
-        return moved
-
-    def beside_exchange(moved):
-        moved, kept["rows"] = together(moved, kept["rows"])
+        moved, kept["rows"] = together(moved, lax.all_to_all(rows_grad, "dp", 0, 0))
         return moved
 
     def beside_rows(moved):
@@ -1243,7 +1249,7 @@
         kept["rows"] = jnp.stack([kept["rows"], far])
         return moved
 
-    two = reduce_blocks(*two, (beside_sums, beside_exchange))
+    two = reduce_blocks(*two, (beside_expand, beside_sums))
     one = reduce_blocks(*kept["sums"], (beside_rows, beside_streams))
     rows_grad = kept["rows"]
     rows_grad = jnp.stack([rows_grad, swap(rows_grad, "head", 1)]).reshape(-1, width)

time: 910 us -> 874 us (0.960)
  waiting for transfers between devices: 254 us -> 219 us
  starting transfers between devices: 89.2 us -> 78.5 us
  Pallas kernels: 264 us -> 254 us
    ppermute x70, waiting for transfers between devices: 226 us -> 209 us  [swap(): return lax.ppermute(value, axis, [(i, i ^ mask) for i in range(size)])]
    all_to_all x1, waiting for transfers between devices: 20.1 us -> 7.74 us  [beside_sums(): moved, kept['rows'] = together(moved, lax.all_to_all(rows_grad, 'dp', 0, 0))]
    ppermute x70, starting transfers between devices: 73.6 us -> 62.3 us  [swap(): return lax.ppermute(value, axis, [(i, i ^ mask) for i in range(size)])]
    unnamed x319 -> x331, local copies, waits for them, and re-layouts: 31.1 us -> 32.1 us
  transfers between devices with their start and end apart: 74 -> 74, of which waited for: 43 -> 45; matrix products, arithmetic and copies ran while one was open for 18% -> 20% of each run, Pallas kernels for 26% -> 26%
where the time goes in v10:
time: 874 us; the launch traced here: 867 us
  Pallas kernels  254 us (29%)
  waiting for transfers between devices  219 us (25%)
  other arithmetic  157 us (18%)
  local copies, waits for them, and re-layouts  81.6 us (9%)
  starting transfers between devices  78.5 us (9%)
  matrix products  40.6 us (5%)
  between operations  26.1 us (3%)
  blocking collectives  9.2 us (1%)
    ppermute x70, waiting for transfers between devices, swap(): return lax.ppermute(value, axis, [(i, i ^ mask) for i in range(size)])  209 us
    ppermute x70, starting transfers between devices, swap(): return lax.ppermute(value, axis, [(i, i ^ mask) for i in range(size)])  62.3 us
    dot_general x11, matrix products, mm(): return lax.dot_general(left, right, dims, preferred_element_type=single)  40.6 us
    pallas_call x4, Pallas kernels, logits_part(): pl.pallas_call(functools.partial(logits_kernel, words), name='logits_part...  39 us
    pallas_call x4, Pallas kernels, logits_back(): pl.pallas_call(logits_back_kernel, name='logits_back', grid=(tiles,), out...  38.5 us
    unnamed x331, local copies, waits for them, and re-layouts  32.1 us
    pallas_call x1, Pallas kernels, table_grad_part(): pl.pallas_call(functools.partial(table_grad_kernel, len(grads)), name='ta...  24.3 us
    pallas_call x1, Pallas kernels, own_list(): pl.pallas_call(list_kernel, name='own_list', out_shape=(jax.ShapeDtypeStr...  21.4 us
  transfers between devices with their start and end apart: 74, of which 45 were waited for; matrix products, arithmetic and copies ran while one was open for 20% of the time, Pallas kernels for 26%

profile of v10, /device:TPU:0, one launch (start us, length us, event | category | flops | bytes accessed | tf_op | source)
XLA Modules:
  0.0 866.6 jit_solution(12447270929617581326)
XLA Ops:
  28.1 8.7 lookup.2
  36.8 8.8 %lookup.3 = bf16[4096,128]{1,0:T(8,128)(2,1)} custom-call(s32[4096]{0:T(1024)} %get-tuple-element.492.row_ref, f32[8000,128]{1,0:T(8,128)} %table_ref.3), custom_call_target="tpu_custom_call" | custom-call | bytes 629145 | tf_op jit(solution)/shard_map/lookup/pallas_call | solution.py:178
  82.6 9.9 %state_norm.3.old_ref = bf16[3,1024,1024]{2,1,0:T(8,128)(2,1)} custom-call(s32[2]{0:T(128)} %pad_add_fusion.place_ref, f32[1,1024]{1,0:T(1,128)} %bitcast.348, bf16[2,1536,1024]{2,1,0:T(8,128)(2,1)} %in_ref.3), custom_call_target="tpu_custom_call" | custom-call | bytes 251658 | tf_op jit(solution)/shard_map/state_norm/pallas_call | solution.py:353
  93.4 18.8 %collective-permute-done.7 = bf16[2048,128]{1,0:T(8,128)(2,1)} collective-permute-done((bf16[2048,128]{1,0:T(8,128)(2,1)S(1)}, bf16[2048,128]{1,0:T(8,128)(2,1)}, u32[]{:S(2)}, u32[]{:S(2)}) %collective-permute-start.7) | collective-permute-done | bytes 524320 | tf_op jit(solution)/shard_map/ppermute | solution.py:38
  130.1 12.2 %compress.1 = (bf16[1024,512]{1,0:T(8,128)(2,1)}, bf16[3,1024,512]{2,1,0:T(8,128)(2,1)}) custom-call(bf16[3,1024,1024]{2,1,0:T(8,128)(2,1)} %state_norm.3.old_ref, bf16[1120,1024]{1,0:T(8,128)(2,1)} %copy-done.7, bf16[1120,1024]{1,0:T(8,128)(2,1)} %copy-done.7, bf16[2,384,128]{2,1,0:T(8,128)(2,1)} %bitcast.318), custom_call_target="tpu_custom_call" | custom-call | flops 64424508 | bytes 251658 | tf_op jit(solution)/shard_map/compress/pallas_call | solution.py:395
  155.5 10.9 %attend.1 = (bf16[2,2,256,256]{3,2,1,0:T(8,128)(2,1)}, f32[2,2,512,1]{3,2,1,0:T(8,128)}) custom-call(s32[8]{0:T(128)} %fusion.106.info_ref, bf16[2,2,256,768]{3,2,1,0:T(8,128)(2,1)} %bitcast.284, bf16[2,2,256,768]{3,2,1,0:T(8,128)(2,1)} %bitcast.285, bf16[2,2,256,768]{3,2,1,0:T(8,128)(2,1)} %bitcast.286, bf16[1024,512]{1,0:T(8,128)(2,1)} %get-tuple-element.179.kc_ref.vc_ref, ...), custom_call_target="tpu_custom_call" | custom-call | flops 146800640 | bytes 125829 | tf_op jit(solution)/shard_map/attend/pallas_call | solution.py:547
  209.7 12.3 %collective-permute-done.16 = bf16[256,1024]{1,0:T(8,128)(2,1)S(1)} collective-permute-done((bf16[256,1024]{1,0:T(8,128)(2,1)S(1)}, bf16[256,1024]{1,0:T(8,128)(2,1)S(1)}, u32[]{:S(2)}, u32[]{:S(2)}) %collective-permute-start.16) | collective-permute-done | bytes 524320 | tf_op jit(solution)/shard_map/ppermute | solution.py:38
  251.3 10.0 %collective-permute-done.19 = bf16[256,1024]{1,0:T(8,128)(2,1)S(1)} collective-permute-done((bf16[256,1024]{1,0:T(8,128)(2,1)S(1)}, bf16[256,1024]{1,0:T(8,128)(2,1)S(1)}, u32[]{:S(2)}, u32[]{:S(2)}) %collective-permute-start.19) | collective-permute-done | bytes 524320 | tf_op jit(solution)/shard_map/ppermute | solution.py:38
  265.4 21.4 %own_list.1 = (s32[8200]{0:T(1024)}, s32[1]{0:T(128)}) custom-call(s32[8192]{0:T(1024)} %get-tuple-element.202.code_ref), custom_call_target="tpu_custom_call" | custom-call | bytes 1258291 | tf_op jit(solution)/shard_map/own_list/pallas_call | solution.py:209
  297.1 9.8 %logits_part.4 = (bf16[512,2048]{1,0:T(8,128)(2,1)}, bf16[512,2048]{1,0:T(8,128)(2,1)}, f32[8,1024]{1,0:T(8,128)}) custom-call(f32[4,8,1024]{2,1,0:T(8,128)} %bitcast.290, f32[4,8,1024]{2,1,0:T(8,128)} %bitcast.291, bf16[512,1024]{1,0:T(8,128)(2,1)} %pad_maximum_fusion.20.pair_ref.refs_8_, bf16[512,1024]{1,0:T(8,128)(2,1)} %collective-permute-done.24.near_ref.refs_9_, ...), custom_call_target="tpu_custom_call" | custom-call | flops 171798688 | bytes 209715 | tf_op jit(solution)/shard_map/logits_part/pallas_call | solution.py:640
  306.8 10.6 %collective-permute-done.22 = bf16[512,1024]{1,0:T(8,128)(2,1)} collective-permute-done((bf16[512,1024]{1,0:T(8,128)(2,1)}, bf16[512,1024]{1,0:T(8,128)(2,1)}, u32[]{:S(2)}, u32[]{:S(2)}) %collective-permute-start.22) | collective-permute-done | bytes 1048608 | tf_op jit(solution)/shard_map/ppermute | solution.py:38
  322.2 10.0 %logits_part.5 = (bf16[512,2048]{1,0:T(8,128)(2,1)}, bf16[512,2048]{1,0:T(8,128)(2,1)}, f32[8,1024]{1,0:T(8,128)}) custom-call(f32[4,8,1024]{2,1,0:T(8,128)} %bitcast.292, f32[4,8,1024]{2,1,0:T(8,128)} %bitcast.293, bf16[512,1024]{1,0:T(8,128)(2,1)} %copy-done.19, bf16[512,1024]{1,0:T(8,128)(2,1)} %copy-done.30, bf16[2048,512]{1,0:T(8,128)(2,1)} %copy-done, ...), custom_call_target="tpu_custom_call" | custom-call | flops 171798688 | bytes 209715 | tf_op jit(solution)/shard_map/logits_part/pallas_call | solution.py:640
  339.3 9.6 %logits_part.6 = (bf16[512,2048]{1,0:T(8,128)(2,1)}, bf16[512,2048]{1,0:T(8,128)(2,1)}, f32[8,1024]{1,0:T(8,128)}) custom-call(f32[4,8,1024]{2,1,0:T(8,128)} %bitcast.294, f32[4,8,1024]{2,1,0:T(8,128)} %bitcast.295, bf16[512,1024]{1,0:T(8,128)(2,1)} %copy-done.12, bf16[512,1024]{1,0:T(8,128)(2,1)} %copy-done.31, bf16[2048,512]{1,0:T(8,128)(2,1)} %copy-done, ...), custom_call_target="tpu_custom_call" | custom-call | flops 171798688 | bytes 209715 | tf_op jit(solution)/shard_map/logits_part/pallas_call | solution.py:640
  355.9 9.6 %logits_part.7 = (bf16[512,2048]{1,0:T(8,128)(2,1)}, bf16[512,2048]{1,0:T(8,128)(2,1)}, f32[8,1024]{1,0:T(8,128)}) custom-call(f32[4,8,1024]{2,1,0:T(8,128)} %bitcast.296, f32[4,8,1024]{2,1,0:T(8,128)} %bitcast.297, bf16[512,1024]{1,0:T(8,128)(2,1)} %copy-done.13, bf16[512,1024]{1,0:T(8,128)(2,1)} %copy-done.32, bf16[2048,512]{1,0:T(8,128)(2,1)} %copy-done, ...), custom_call_target="tpu_custom_call" | custom-call | flops 171798688 | bytes 209715 | tf_op jit(solution)/shard_map/logits_part/pallas_call | solution.py:640
  385.0 9.7 %logits_back.4 = (bf16[512,2048]{1,0:T(8,128)(2,1)}, bf16[512,2048]{1,0:T(8,128)(2,1)}, bf16[512,1024]{1,0:T(8,128)(2,1)}, bf16[512,1024]{1,0:T(8,128)(2,1)}) custom-call(f32[4,8,1024]{2,1,0:T(8,128)} %bitcast.299, f32[4,8,1024]{2,1,0:T(8,128)} %bitcast.300, f32[4,8,1024]{2,1,0:T(8,128)} %broadcast_in_dim.202.pair_factor_ref.near_factor_ref, ...), custom_call_target="tpu_custom_call" | custom-call | flops 171798688 | bytes 251658 | tf_op jit(solution)/shard_map/logits_back/pallas_call | solution.py:701
  401.4 9.5 %logits_back.5 = (bf16[512,2048]{1,0:T(8,128)(2,1)}, bf16[512,2048]{1,0:T(8,128)(2,1)}, bf16[512,1024]{1,0:T(8,128)(2,1)}, bf16[512,1024]{1,0:T(8,128)(2,1)}) custom-call(f32[4,8,1024]{2,1,0:T(8,128)} %bitcast.301, f32[4,8,1024]{2,1,0:T(8,128)} %bitcast.302, f32[4,8,1024]{2,1,0:T(8,128)} %broadcast_in_dim.202.pair_factor_ref.near_factor_ref, ...), custom_call_target="tpu_custom_call" | custom-call | flops 171798688 | bytes 251658 | tf_op jit(solution)/shard_map/logits_back/pallas_call | solution.py:701
  422.3 9.5 %logits_back.6 = (bf16[512,2048]{1,0:T(8,128)(2,1)}, bf16[512,2048]{1,0:T(8,128)(2,1)}, bf16[512,1024]{1,0:T(8,128)(2,1)}, bf16[512,1024]{1,0:T(8,128)(2,1)}) custom-call(f32[4,8,1024]{2,1,0:T(8,128)} %bitcast.303, f32[4,8,1024]{2,1,0:T(8,128)} %bitcast.304, f32[4,8,1024]{2,1,0:T(8,128)} %broadcast_in_dim.202.pair_factor_ref.near_factor_ref, ...), custom_call_target="tpu_custom_call" | custom-call | flops 171798688 | bytes 251658 | tf_op jit(solution)/shard_map/logits_back/pallas_call | solution.py:701
  447.3 9.9 %logits_back.7 = (bf16[512,2048]{1,0:T(8,128)(2,1)}, bf16[512,2048]{1,0:T(8,128)(2,1)}, bf16[512,1024]{1,0:T(8,128)(2,1)}, bf16[512,1024]{1,0:T(8,128)(2,1)}) custom-call(f32[4,8,1024]{2,1,0:T(8,128)} %bitcast.305, f32[4,8,1024]{2,1,0:T(8,128)} %bitcast.306, f32[4,8,1024]{2,1,0:T(8,128)} %broadcast_in_dim.202.pair_factor_ref.near_factor_ref, ...), custom_call_target="tpu_custom_call" | custom-call | flops 171798688 | bytes 251658 | tf_op jit(solution)/shard_map/logits_back/pallas_call | solution.py:701
  457.2 13.5 %collective-permute-done.43 = bf16[512,1024]{1,0:T(8,128)(2,1)} collective-permute-done((bf16[512,1024]{1,0:T(8,128)(2,1)}, bf16[512,1024]{1,0:T(8,128)(2,1)}, u32[]{:S(2)}, u32[]{:S(2)}) %collective-permute-start.43) | collective-permute-done | bytes 1048608 | tf_op jit(solution)/shard_map/ppermute | solution.py:38
  483.7 24.3 %table_grad_part.1 = (f32[2048,512]{1,0:T(8,128)}, bf16[2048,512]{1,0:T(8,128)(2,1)}) custom-call(bf16[512,2048]{1,0:T(8,128)(2,1)} %get-tuple-element.253.refs_0_, bf16[512,2048]{1,0:T(8,128)(2,1)} %get-tuple-element.254.refs_1_, bf16[512,2048]{1,0:T(8,128)(2,1)} %get-tuple-element.255.refs_2_, bf16[512,2048]{1,0:T(8,128)(2,1)} %get-tuple-element.256.refs_3_, ...), custom_call_target="tpu_custom_call" | custom-call | flops 515396064 | bytes 629145 | tf_op jit(solution)/shard_map/table_grad_part/pallas_call | solution.py:748
  511.5 11.1 %collective-permute-done.45 = bf16[256,1024]{1,0:T(8,128)(2,1)S(1)} collective-permute-done((bf16[256,1024]{1,0:T(8,128)(2,1)S(1)}, bf16[256,1024]{1,0:T(8,128)(2,1)S(1)}, u32[]{:S(2)}, u32[]{:S(2)}) %collective-permute-start.45) | collective-permute-done | bytes 524320 | tf_op jit(solution)/shard_map/ppermute | solution.py:38
  547.7 11.6 %hidden_grads.1 = (f32[2048,512]{1,0:T(8,128)}, bf16[2048,512]{1,0:T(8,128)(2,1)}) custom-call(bf16[1024,1024]{1,0:T(8,128)(2,1)} %copy-done.47, bf16[1024,1024]{1,0:T(8,128)(2,1)} %copy-done.46, bf16[1024,1024]{1,0:T(8,128)(2,1)} %pad_maximum_fusion.2.in_ref, bf16[1024,1024]{1,0:T(8,128)(2,1)} %pad_maximum_fusion.5.down_ref), custom_call_target="tpu_custom_call" | custom-call | flops 128849016 | bytes 335544 | tf_op jit(solution)/shard_map/hidden_grads/pallas_call | solution.py:783
  559.3 11.7 %collective-permute-done.49 = bf16[2048,512]{1,0:T(8,128)(2,1)} collective-permute-done((bf16[2048,512]{1,0:T(8,128)(2,1)}, bf16[2048,512]{1,0:T(8,128)(2,1)}, u32[]{:S(2)}, u32[]{:S(2)}) %collective-permute-start.49) | collective-permute-done | bytes 2097184 | tf_op jit(solution)/shard_map/ppermute | solution.py:38
  601.8 15.2 %attend_back.1 = (bf16[2,2,256,768]{3,2,1,0:T(8,128)(2,1)}, bf16[1024,512]{1,0:T(8,128)(2,1)}, bf16[1024,512]{1,0:T(8,128)(2,1)}) custom-call(s32[8]{0:T(128)} %fusion.106.info_ref, bf16[2,2,256,768]{3,2,1,0:T(8,128)(2,1)} %bitcast.287, bf16[2,2,256,768]{3,2,1,0:T(8,128)(2,1)} %bitcast.288, bf16[2,2,256,768]{3,2,1,0:T(8,128)(2,1)} %bitcast.289, ...), custom_call_target="tpu_custom_call" | custom-call | flops 230686720 | bytes 188743 | tf_op jit(solution)/shard_map/attend_back/pallas_call | solution.py:570
  635.7 8.9 %collective-permute-done.50 = bf16[2048,512]{1,0:T(8,128)(2,1)} collective-permute-done((bf16[2048,512]{1,0:T(8,128)(2,1)}, bf16[2048,512]{1,0:T(8,128)(2,1)}, u32[]{:S(2)}, u32[]{:S(2)}) %collective-permute-start.50) | collective-permute-done | bytes 2097184 | tf_op jit(solution)/shard_map/ppermute | solution.py:38
  660.1 14.3 %attn_grads.1 = (f32[1024,512]{1,0:T(8,128)}, bf16[1024,512]{1,0:T(8,128)(2,1)}) custom-call(bf16[1024,768]{1,0:T(8,128)(2,1)} %bitcast.321, bf16[1024,256]{1,0:T(8,128)(2,1)} %bitcast.314, bf16[1024,512]{1,0:T(8,128)(2,1)} %get-tuple-element.280.mem_ref, bf16[3072,512]{1,0:T(8,128)(2,1)} %bitcast.315, bf16[1024,1024]{1,0:T(8,128)(2,1)} %pad_maximum_fusion.1.normed_ref, ...), custom_call_target="tpu_custom_call" | custom-call | flops 188743680 | bytes 503316 | tf_op jit(solution)/shard_map/attn_grads/pallas_call | solution.py:833
  692.7 7.7 all-to-all-done.3
  703.4 15.1 %collective-permute-done.57 = bf16[1120,512]{1,0:T(8,128)(2,1)} collective-permute-done((bf16[1120,512]{1,0:T(8,128)(2,1)}, bf16[1120,512]{1,0:T(8,128)(2,1)}, u32[]{:S(2)}, u32[]{:S(2)}) %collective-permute-start.57) | collective-permute-done | bytes 1146912 | tf_op jit(solution)/shard_map/ppermute | solution.py:38
  741.1 13.3 %collective-permute-done.60 = bf16[1120,128]{1,0:T(8,128)(2,1)S(1)} collective-permute-done((bf16[1120,128]{1,0:T(8,128)(2,1)S(1)}, bf16[1120,128]{1,0:T(8,128)(2,1)S(1)}, u32[]{:S(2)}, u32[]{:S(2)}) %collective-permute-start.60) | collective-permute-done | bytes 286752 | tf_op jit(solution)/shard_map/ppermute | solution.py:38
  761.5 12.4 %scatter.1 = f32[8000,128]{1,0:T(8,128)} custom-call(s32[1]{0:T(128)} %get-tuple-element.293.count_ref, s32[8200]{0:T(1024)} %get-tuple-element.294.code_ref, f32[8000,128]{1,0:T(8,128)} %bitcast_convert_fusion.base_ref, bf16[8192,128]{1,0:T(8,128)(2,1)} %bitcast.309), custom_call_target="tpu_custom_call" | custom-call | bytes 629145 | tf_op jit(solution)/shard_map/scatter/pallas_call | solution.py:305
  777.5 9.2 %all-reduce.1 = (f32[128]{0:T(128)S(1)}, f32[3,128]{1,0:T(4,128)S(1)}, f32[128]{0:T(128)S(1)}, f32[16]{0:T(128)S(1)}, f32[128]{0:T(128)S(1)}, /*index=5*/f32[128...) all-reduce(f32[128]{0:T(128)S(1)} %get-tuple-element.358, ...), channel_id=1, replica_groups=mesh['dp'=8,'head'=4] {'head'}, use_global_device_ids=true, to_apply=%region_23.24 | all-reduce | flops 1424 | bytes 11392 | tf_op jit(solution)/shard_map/psum | solution.py:1288
  855.8 7.8 divide_subtract_fusion
  (755 shorter events, 463.2 us)
Async XLA Ops:
  25.1 20.5 %collective-permute-start.3 = (bf16[1120,128]{1,0:T(8,128)(2,1)S(1)}, bf16[1120,128]{1,0:T(8,128)(2,1)S(1)}, u32[]{:S(2)}, u32[]{:S(2)}) collective-permute-start(bf16[1120,128]{1,0:T(8,128)(2,1)S(1)} %pad_maximum_fusion.28), channel_id=1, source_target_pairs={{0,16},{4,20},{8,24},{12,28},{16,0},{20,4},{24,8},{28,12},{1,17},{... | collective-permute-start | bytes 860168 | tf_op jit(solution)/shard_map/ppermute | solution.py:38
  71.1 41.1 %all-to-all-start = ((bf16[8,256,128]{2,1,0:T(8,128)(2,1)}), bf16[8,256,128]{2,1,0:T(8,128)(2,1)}, u32[]{:S(2)}, u32[]{:S(2)}) async-start(bf16[8,256,128]{2,1,0:T(8,128)(2,1)} %bitcast.316), calls=%async_computation | async-start | bytes 1048576 | tf_op jit(solution)/shard_map/all_to_all | solution.py:1000
  77.4 41.9 %collective-permute-start.10 = (bf16[1120,512]{1,0:T(8,128)(2,1)}, bf16[1120,512]{1,0:T(8,128)(2,1)}, u32[]{:S(2)}, u32[]{:S(2)}) collective-permute-start(bf16[1120,512]{1,0:T(8,128)(2,1)} %get-tuple-element.439), channel_id=1, source_target_pairs={{0,4},{4,0},{8,12},{12,8},{16,20},{20,16},{24,28},{28,24},{1,5},{5... | collective-permute-start | bytes 3440648 | tf_op jit(solution)/shard_map/ppermute | solution.py:38
  79.4 32.9 %collective-permute-start.7 = (bf16[2048,128]{1,0:T(8,128)(2,1)S(1)}, bf16[2048,128]{1,0:T(8,128)(2,1)}, u32[]{:S(2)}, u32[]{:S(2)}) collective-permute-start(bf16[2048,128]{1,0:T(8,128)(2,1)S(1)} %pad_maximum_fusion.27), channel_id=1, source_target_pairs={{0,16},{4,20},{8,24},{12,28},{16,0},{20,4},{24,8},{28,12},{1,17},{... | collective-permute-start | bytes 1572872 | tf_op jit(solution)/shard_map/ppermute | solution.py:38
  117.4 29.0 %collective-permute-start.11 = (bf16[2048,256]{1,0:T(8,128)(2,1)}, bf16[2048,256]{1,0:T(8,128)(2,1)}, u32[]{:S(2)}, u32[]{:S(2)}) collective-permute-start(bf16[2048,256]{1,0:T(8,128)(2,1)} %pad_maximum_fusion.18), channel_id=1, source_target_pairs={{0,8},{4,12},{8,0},{12,4},{16,24},{20,28},{24,16},{28,20},{1,9},{5... | collective-permute-start | bytes 3145736 | tf_op jit(solution)/shard_map/ppermute | solution.py:38
  129.1 22.1 %collective-permute-start.9 = (bf16[512,1024]{1,0:T(8,128)(2,1)}, bf16[512,1024]{1,0:T(8,128)(2,1)}, u32[]{:S(2)}, u32[]{:S(2)}) collective-permute-start(bf16[512,1024]{1,0:T(8,128)(2,1)} %pad_maximum_fusion.17), channel_id=1, source_target_pairs={{0,1},{1,0},{2,3},{3,2},{4,5},{5,4},{6,7},{7,6},{8,9},{9,8},{10,11... | collective-permute-start | bytes 3145736 | tf_op jit(solution)/shard_map/ppermute | solution.py:38
  149.2 32.2 %collective-permute-start.13 = (bf16[1024,512]{1,0:T(8,128)(2,1)}, bf16[1024,512]{1,0:T(8,128)(2,1)}, u32[]{:S(2)}, u32[]{:S(2)}) collective-permute-start(bf16[1024,512]{1,0:T(8,128)(2,1)} %get-tuple-element.426), channel_id=1, source_target_pairs={{0,4},{4,0},{8,12},{12,8},{16,20},{20,16},{24,28},{28,24},{1,5},{5... | collective-permute-start | bytes 3145736 | tf_op jit(solution)/shard_map/ppermute | solution.py:38
  173.2 32.7 %collective-permute-start.15 = (bf16[1024,512]{1,0:T(8,128)(2,1)}, bf16[1024,512]{1,0:T(8,128)(2,1)}, u32[]{:S(2)}, u32[]{:S(2)}) collective-permute-start(bf16[1024,512]{1,0:T(8,128)(2,1)} %get-tuple-element.425), channel_id=1, source_target_pairs={{0,4},{4,0},{8,12},{12,8},{16,20},{20,16},{24,28},{28,24},{1,5},{5... | collective-permute-start | bytes 3145736 | tf_op jit(solution)/shard_map/ppermute | solution.py:38
  173.5 51.5 %all-to-all-start.1 = ((bf16[4,2000,128]{2,1,0:T(8,128)(2,1)}), bf16[4,2000,128]{2,1,0:T(8,128)(2,1)S(1)}, u32[]{:S(2)}, u32[]{:S(2)}) async-start(bf16[4,2000,128]{2,1,0:T(8,128)(2,1)} %bitcast.310), calls=%async_computation.1 | async-start | bytes 4096000 | tf_op jit(solution)/shard_map/all_to_all | solution.py:1079
  185.9 20.0 %collective-permute-start.14 = (bf16[256,1024]{1,0:T(8,128)(2,1)}, bf16[256,1024]{1,0:T(8,128)(2,1)}, u32[]{:S(2)}, u32[]{:S(2)}) collective-permute-start(bf16[256,1024]{1,0:T(8,128)(2,1)} %slice.1037), channel_id=1, source_target_pairs={{0,2},{1,3},{2,0},{3,1},{4,6},{5,7},{6,4},{7,5},{8,10},{9,11},{10,... | collective-permute-start | bytes 1572872 | tf_op jit(solution)/shard_map/ppermute | solution.py:38
  249.5 47.6 %collective-permute-start.25 = (bf16[2048,512]{1,0:T(8,128)(2,1)S(1)}, bf16[2048,512]{1,0:T(8,128)(2,1)}, u32[]{:S(2)}, u32[]{:S(2)}) collective-permute-start(bf16[2048,512]{1,0:T(8,128)(2,1)S(1)} %fusion.13.left_ref), channel_id=1, source_target_pairs={{0,4},{4,0},{8,12},{12,8},{16,20},{20,16},{24,28},{28,24},{1,5},{5... | collective-permute-start | bytes 6291464 | tf_op jit(solution)/shard_map/ppermute | solution.py:38
  262.6 24.2 %collective-permute-start.23 = (bf16[256,1024]{1,0:T(8,128)(2,1)}, bf16[256,1024]{1,0:T(8,128)(2,1)}, u32[]{:S(2)}, u32[]{:S(2)}) collective-permute-start(bf16[256,1024]{1,0:T(8,128)(2,1)} %multiply_convert_fusion.1.refs_0_), channel_id=1, source_target_pairs={{0,2},{1,3},{2,0},{3,1},{4,6},{5,7},{6,4},{7,5},{8,10},{9,11},{10,... | collective-permute-start | bytes 1572872 | tf_op jit(solution)/shard_map/ppermute | solution.py:38
  265.4 24.2 %collective-permute-start.20 = (bf16[256,1024]{1,0:T(8,128)(2,1)}, bf16[256,1024]{1,0:T(8,128)(2,1)}, u32[]{:S(2)}, u32[]{:S(2)}) collective-permute-start(bf16[256,1024]{1,0:T(8,128)(2,1)} %reorder.4), channel_id=1, source_target_pairs={{0,16},{4,20},{8,24},{12,28},{16,0},{20,4},{24,8},{28,12},{1,17},{... | collective-permute-start | bytes 1572872 | tf_op jit(solution)/shard_map/ppermute | solution.py:38
  291.9 25.6 %collective-permute-start.22 = (bf16[512,1024]{1,0:T(8,128)(2,1)}, bf16[512,1024]{1,0:T(8,128)(2,1)}, u32[]{:S(2)}, u32[]{:S(2)}) collective-permute-start(bf16[512,1024]{1,0:T(8,128)(2,1)} %reorder.5), channel_id=1, source_target_pairs={{0,8},{4,12},{8,0},{12,4},{16,24},{20,28},{24,16},{28,20},{1,9},{5... | collective-permute-start | bytes 3145736 | tf_op jit(solution)/shard_map/ppermute | solution.py:38
  293.4 24.1 %collective-permute-start.21 = (bf16[256,1024]{1,0:T(8,128)(2,1)}, bf16[256,1024]{1,0:T(8,128)(2,1)S(1)}, u32[]{:S(2)}, u32[]{:S(2)}) collective-permute-start(bf16[256,1024]{1,0:T(8,128)(2,1)} %collective-permute-done.20.refs_1_), channel_id=1, source_target_pairs={{0,2},{1,3},{2,0},{3,1},{4,6},{5,7},{6,4},{7,5},{8,10},{9,11},{10,... | collective-permute-start | bytes 1572872 | tf_op jit(solution)/shard_map/ppermute | solution.py:38
  439.5 17.7 %collective-permute-start.40 = (bf16[256,1024]{1,0:T(8,128)(2,1)}, bf16[256,1024]{1,0:T(8,128)(2,1)S(1)}, u32[]{:S(2)}, u32[]{:S(2)}) collective-permute-start(bf16[256,1024]{1,0:T(8,128)(2,1)} %slice.1033), channel_id=1, source_target_pairs={{0,2},{1,3},{2,0},{3,1},{4,6},{5,7},{6,4},{7,5},{8,10},{9,11},{10,... | collective-permute-start | bytes 1572872 | tf_op jit(solution)/shard_map/ppermute | solution.py:38
  445.5 25.2 %collective-permute-start.43 = (bf16[512,1024]{1,0:T(8,128)(2,1)}, bf16[512,1024]{1,0:T(8,128)(2,1)}, u32[]{:S(2)}, u32[]{:S(2)}) collective-permute-start(bf16[512,1024]{1,0:T(8,128)(2,1)} %reorder.6), channel_id=1, source_target_pairs={{0,8},{4,12},{8,0},{12,4},{16,24},{20,28},{24,16},{28,20},{1,9},{5... | collective-permute-start | bytes 3145736 | tf_op jit(solution)/shard_map/ppermute | solution.py:38
  457.1 22.6 %collective-permute-start.41 = (bf16[512,1024]{1,0:T(8,128)(2,1)}, bf16[512,1024]{1,0:T(8,128)(2,1)}, u32[]{:S(2)}, u32[]{:S(2)}) collective-permute-start(bf16[512,1024]{1,0:T(8,128)(2,1)} %get-tuple-element.246), channel_id=1, source_target_pairs={{0,1},{1,0},{2,3},{3,2},{4,5},{5,4},{6,7},{7,6},{8,9},{9,8},{10,11... | collective-permute-start | bytes 3145736 | tf_op jit(solution)/shard_map/ppermute | solution.py:38
  477.1 30.9 %collective-permute-start.44 = (bf16[256,1024]{1,0:T(8,128)(2,1)}, bf16[256,1024]{1,0:T(8,128)(2,1)S(1)}, u32[]{:S(2)}, u32[]{:S(2)}) collective-permute-start(bf16[256,1024]{1,0:T(8,128)(2,1)} %reorder.7), channel_id=1, source_target_pairs={{0,16},{4,20},{8,24},{12,28},{16,0},{20,4},{24,8},{28,12},{1,17},{... | collective-permute-start | bytes 1572872 | tf_op jit(solution)/shard_map/ppermute | solution.py:38
  482.8 25.2 %collective-permute-start.42 = (bf16[256,1024]{1,0:T(8,128)(2,1)S(1)}, bf16[256,1024]{1,0:T(8,128)(2,1)S(1)}, u32[]{:S(2)}, u32[]{:S(2)}) collective-permute-start(bf16[256,1024]{1,0:T(8,128)(2,1)S(1)} %slice.1032), channel_id=1, source_target_pairs={{0,2},{1,3},{2,0},{3,1},{4,6},{5,7},{6,4},{7,5},{8,10},{9,11},{10,... | collective-permute-start | bytes 1572872 | tf_op jit(solution)/shard_map/ppermute | solution.py:38
  522.7 48.4 %collective-permute-start.49 = (bf16[2048,512]{1,0:T(8,128)(2,1)}, bf16[2048,512]{1,0:T(8,128)(2,1)}, u32[]{:S(2)}, u32[]{:S(2)}) collective-permute-start(bf16[2048,512]{1,0:T(8,128)(2,1)} %get-tuple-element.266), channel_id=1, source_target_pairs={{0,4},{4,0},{8,12},{12,8},{16,20},{20,16},{24,28},{28,24},{1,5},{5... | collective-permute-start | bytes 6291464 | tf_op jit(solution)/shard_map/ppermute | solution.py:38
  542.0 29.1 %collective-permute-start.48 = (bf16[256,1024]{1,0:T(8,128)(2,1)}, bf16[256,1024]{1,0:T(8,128)(2,1)}, u32[]{:S(2)}, u32[]{:S(2)}) collective-permute-start(bf16[256,1024]{1,0:T(8,128)(2,1)} %slice.1031), channel_id=1, source_target_pairs={{0,2},{1,3},{2,0},{3,1},{4,6},{5,7},{6,4},{7,5},{8,10},{9,11},{10,... | collective-permute-start | bytes 1572872 | tf_op jit(solution)/shard_map/ppermute | solution.py:38
  581.7 62.9 %all-to-all-start.2 = ((bf16[4,2000,128]{2,1,0:T(8,128)(2,1)}), bf16[4,2000,128]{2,1,0:T(8,128)(2,1)S(1)}, u32[]{:S(2)}, u32[]{:S(2)}) async-start(bf16[4,2000,128]{2,1,0:T(8,128)(2,1)} %pad_maximum_fusion.9), calls=%async_computation.2 | async-start | bytes 4096000 | tf_op jit(solution)/shard_map/all_to_all | solution.py:1202
  596.2 48.4 %collective-permute-start.50 = (bf16[2048,512]{1,0:T(8,128)(2,1)}, bf16[2048,512]{1,0:T(8,128)(2,1)}, u32[]{:S(2)}, u32[]{:S(2)}) collective-permute-start(bf16[2048,512]{1,0:T(8,128)(2,1)} %get-tuple-element.268), channel_id=1, source_target_pairs={{0,4},{4,0},{8,12},{12,8},{16,20},{20,16},{24,28},{28,24},{1,5},{5... | collective-permute-start | bytes 6291464 | tf_op jit(solution)/shard_map/ppermute | solution.py:38
  623.8 20.8 %collective-permute-start.53 = (bf16[512,1024]{1,0:T(8,128)(2,1)}, bf16[512,1024]{1,0:T(8,128)(2,1)}, u32[]{:S(2)}, u32[]{:S(2)}) collective-permute-start(bf16[512,1024]{1,0:T(8,128)(2,1)} %slice.1024), channel_id=1, source_target_pairs={{0,1},{1,0},{2,3},{3,2},{4,5},{5,4},{6,7},{7,6},{8,9},{9,8},{10,11... | collective-permute-start | bytes 3145736 | tf_op jit(solution)/shard_map/ppermute | solution.py:38
  654.4 38.3 %collective-permute-start.54 = (bf16[2048,256]{1,0:T(8,128)(2,1)}, bf16[2048,256]{1,0:T(8,128)(2,1)}, u32[]{:S(2)}, u32[]{:S(2)}) collective-permute-start(bf16[2048,256]{1,0:T(8,128)(2,1)} %slice.1023), channel_id=1, source_target_pairs={{0,8},{4,12},{8,0},{12,4},{16,24},{20,28},{24,16},{28,20},{1,9},{5... | collective-permute-start | bytes 3145736 | tf_op jit(solution)/shard_map/ppermute | solution.py:38
  654.7 23.7 %collective-permute-start.55 = (bf16[256,1024]{1,0:T(8,128)(2,1)}, bf16[256,1024]{1,0:T(8,128)(2,1)S(1)}, u32[]{:S(2)}, u32[]{:S(2)}) collective-permute-start(bf16[256,1024]{1,0:T(8,128)(2,1)} %slice.1030), channel_id=1, source_target_pairs={{0,2},{1,3},{2,0},{3,1},{4,6},{5,7},{6,4},{7,5},{8,10},{9,11},{10,... | collective-permute-start | bytes 1572872 | tf_op jit(solution)/shard_map/ppermute | solution.py:38
  682.4 18.0 %all-to-all-start.3 = ((bf16[8,256,128]{2,1,0:T(8,128)(2,1)}), bf16[8,256,128]{2,1,0:T(8,128)(2,1)S(1)}, u32[]{:S(2)}, u32[]{:S(2)}) async-start(bf16[8,256,128]{2,1,0:T(8,128)(2,1)} %embed_back.1), calls=%async_computation.3 | async-start | bytes 1048576 | tf_op jit(solution)/shard_map/all_to_all | solution.py:1240
  686.6 32.0 %collective-permute-start.57 = (bf16[1120,512]{1,0:T(8,128)(2,1)}, bf16[1120,512]{1,0:T(8,128)(2,1)}, u32[]{:S(2)}, u32[]{:S(2)}) collective-permute-start(bf16[1120,512]{1,0:T(8,128)(2,1)} %pad_maximum_fusion.16), channel_id=1, source_target_pairs={{0,4},{4,0},{8,12},{12,8},{16,20},{20,16},{24,28},{28,24},{1,5},{5... | collective-permute-start | bytes 3440648 | tf_op jit(solution)/shard_map/ppermute | solution.py:38
  702.5 23.6 %collective-permute-start.56 = (bf16[2048,128]{1,0:T(8,128)(2,1)S(1)}, bf16[2048,128]{1,0:T(8,128)(2,1)S(1)}, u32[]{:S(2)}, u32[]{:S(2)}) collective-permute-start(bf16[2048,128]{1,0:T(8,128)(2,1)S(1)} %slice.1029), channel_id=1, source_target_pairs={{0,16},{4,20},{8,24},{12,28},{16,0},{20,4},{24,8},{28,12},{1,17},{... | collective-permute-start | bytes 1572872 | tf_op jit(solution)/shard_map/ppermute | solution.py:38
  720.2 18.1 %collective-permute-start.58 = (bf16[1120,256]{1,0:T(8,128)(2,1)S(1)}, bf16[1120,256]{1,0:T(8,128)(2,1)S(1)}, u32[]{:S(2)}, u32[]{:S(2)}) collective-permute-start(bf16[1120,256]{1,0:T(8,128)(2,1)S(1)} %slice.1028), channel_id=1, source_target_pairs={{0,8},{4,12},{8,0},{12,4},{16,24},{20,28},{24,16},{28,20},{1,9},{5... | collective-permute-start | bytes 1720328 | tf_op jit(solution)/shard_map/ppermute | solution.py:38
  741.1 17.7 %collective-permute-start.61 = (bf16[2,8,256,128]{3,2,1,0:T(8,128)(2,1)}, bf16[2,8,256,128]{3,2,1,0:T(8,128)(2,1)}, u32[]{:S(2)}, u32[]{:S(2)}) collective-permute-start(bf16[2,8,256,128]{3,2,1,0:T(8,128)(2,1)} %get-tuple-element.436), channel_id=1, source_target_pairs={{0,1},{1,0},{2,3},{3,2},{4,5},{5,4},{6,7},{7,6},{8,9},{9,8},{10,11... | collective-permute-start | bytes 3145736 | tf_op jit(solution)/shard_map/ppermute | solution.py:38
  (197 other events, 2477.4 us)

commit v11 on v10

--- a/solution.py
+++ b/solution.py
@@ -1066,6 +1066,7 @@
     slots = -(-words // 256) * 256
 
 
+    comp_fill, mem_fill, _ = together(comp_fill, mem_fill, kept["mem"])
     comp_counts = jnp.where(x == 1, jnp.flip(comp_fill), comp_fill)
     mem_counts = jnp.where(x == 1, jnp.flip(mem_fill), mem_fill)
     info = [comp_counts[0], mem_counts[0], comp_counts[1], mem_counts[1], c * half]
@@ -1186,7 +1187,10 @@
     act_grad = mm(down_in, full_down, NT)
     pre_grad = jax.vjp(jax.nn.gelu, hidden_pre)[1](act_grad)[0].astype(lowp)
     two = hidden_grads(pre_grad, hidden_act, ffn_in, down_in)
-    ffn_in_grad, (*two, moved_table) = group_sum(mm(pre_grad, full_up), (*two, moved_table))
+    ffn_in_grad, two = group_sum(mm(pre_grad, full_up), two)
+    grad_after_attn = grad_after_ffn + rms_back(after_attn, inv_second, gain_vals[1], ffn_in_grad)
+    attn_in, (moved_table,) = group_both(grad_after_attn.astype(lowp), (moved_table,))
+    attn_in = jnp.concatenate(attn_in)
     keep = table_parts[0] + moved_table.astype(single)
     table_pieces = jnp.stack(split(keep[:words].astype(lowp), 1, reach))
     turned = sum(
@@ -1200,8 +1204,6 @@
         ]
     )
     table_pieces = lax.all_to_all(table_pieces, "dp", 0, 0, axis_index_groups=z_groups)
-    grad_after_attn = grad_after_ffn + rms_back(after_attn, inv_second, gain_vals[1], ffn_in_grad)
-    attn_in = jnp.concatenate(group_both(grad_after_attn.astype(lowp)))
 
     mixed_grad = mm(attn_in, own_one[3 * wide : 4 * wide], NT).astype(lowp)
     mixed_grad = mixed_grad.reshape(2, streams, half, wide)
@@ -1240,27 +1242,27 @@
         moved, kept["rows"] = together(moved, lax.all_to_all(rows_grad, "dp", 0, 0))
         return moved
 
-    def beside_rows(moved):
-        moved, kept["rows"] = together(moved, kept["rows"])
-        return moved
-
     def beside_streams(moved):
         moved, far = together(moved, swap(kept["rows"], "head", 2))
-        kept["rows"] = jnp.stack([kept["rows"], far])
+        rows_grad = jnp.stack([kept["rows"], far])
+        kept["rows"] = jnp.stack([rows_grad, swap(rows_grad, "head", 1)]).reshape(-1, width)
         return moved
 
+    def beside_scatter(moved):
+        table_base = kept["table"].astype(single).reshape(vocab, width)
+        table_grad = scatter(bits, own_count, own_codes, table_base, kept["rows"])
+        moved, kept["table"], kept["table_grad"] = together(moved, table_base, table_grad)
+        return moved
+
     two = reduce_blocks(*two, (beside_expand, beside_sums))
-    one = reduce_blocks(*kept["sums"], (beside_rows, beside_streams))
-    rows_grad = kept["rows"]
-    rows_grad = jnp.stack([rows_grad, swap(rows_grad, "head", 1)]).reshape(-1, width)
-    table_base = kept["table"].astype(single).reshape(vocab, width)
+    one = reduce_blocks(*kept["sums"], (beside_streams, beside_scatter))
+    table_base, table_grad = kept["table"], kept["table_grad"]
 
     up_grad = two[:hidden_own].T
     down_grad = two[hidden_own:]
     qkv_grad = jnp.swapaxes(one[: 3 * wide].reshape(3, wide, width), 1, 2)
     out_grad = one[3 * wide : 4 * wide]
     conv_grad = one[4 * wide :].reshape(wconv.shape)
-    table_grad = scatter(bits, own_count, own_codes, table_base, rows_grad)
 
     gains_low = gains.astype(lowp).astype(single)
     gain_part = jnp.stack(

time: 874 us -> 864 us (0.989)
    unnamed x331 -> x303, local copies, waits for them, and re-layouts: 32.1 us -> 34.7 us
  transfers between devices with their start and end apart: 74 -> 74, of which waited for: 45 -> 42; matrix products, arithmetic and copies ran while one was open for 20% -> 18% of each run, Pallas kernels for 26% -> 28%
where the time goes in v11:
time: 864 us; the launch traced here: 856 us
  Pallas kernels  256 us (30%)
  waiting for transfers between devices  222 us (26%)
  other arithmetic  151 us (17%)
  starting transfers between devices  78.8 us (9%)
  local copies, waits for them, and re-layouts  75.9 us (9%)
  matrix products  39.6 us (5%)
  between operations  26.1 us (3%)
    ppermute x70, waiting for transfers between devices, swap(): return lax.ppermute(value, axis, [(i, i ^ mask) for i in range(size)])  210 us
    ppermute x70, starting transfers between devices, swap(): return lax.ppermute(value, axis, [(i, i ^ mask) for i in range(size)])  61.2 us
    dot_general x11, matrix products, mm(): return lax.dot_general(left, right, dims, preferred_element_type=single)  39.6 us
    pallas_call x4, Pallas kernels, logits_part(): pl.pallas_call(functools.partial(logits_kernel, words), name='logits_part...  38.9 us
    pallas_call x4, Pallas kernels, logits_back(): pl.pallas_call(logits_back_kernel, name='logits_back', grid=(tiles,), out...  38.5 us
    unnamed x303, local copies, waits for them, and re-layouts  34.7 us
    pallas_call x1, Pallas kernels, table_grad_part(): pl.pallas_call(functools.partial(table_grad_kernel, len(grads)), name='ta...  24.3 us
    pallas_call x1, Pallas kernels, own_list(): pl.pallas_call(list_kernel, name='own_list', out_shape=(jax.ShapeDtypeStr...  21.4 us
  transfers between devices with their start and end apart: 74, of which 42 were waited for; matrix products, arithmetic and copies ran while one was open for 18% of the time, Pallas kernels for 28%

profile of v11, /device:TPU:0, one launch (start us, length us, event | category | flops | bytes accessed | tf_op | source)
XLA Modules:
  0.0 855.7 jit_solution(13965555239453096749)
XLA Ops:
  31.3 8.7 %lookup.2 = bf16[4096,128]{1,0:T(8,128)(2,1)} custom-call(s32[4096]{0:T(1024)} %get-tuple-element.501.row_ref, f32[8000,128]{1,0:T(8,128)} %table_ref.3), custom_call_target="tpu_custom_call" | custom-call | bytes 629145 | tf_op jit(solution)/shard_map/lookup/pallas_call | solution.py:178
  40.0 8.8 %lookup.3 = bf16[4096,128]{1,0:T(8,128)(2,1)} custom-call(s32[4096]{0:T(1024)} %get-tuple-element.500.row_ref, f32[8000,128]{1,0:T(8,128)} %table_ref.3), custom_call_target="tpu_custom_call" | custom-call | bytes 629145 | tf_op jit(solution)/shard_map/lookup/pallas_call | solution.py:178
  64.1 9.9 %state_norm.3.old_ref = bf16[3,1024,1024]{2,1,0:T(8,128)(2,1)} custom-call(s32[2]{0:T(128)} %pad_add_fusion.place_ref, f32[1,1024]{1,0:T(1,128)} %bitcast.347, bf16[2,1536,1024]{2,1,0:T(8,128)(2,1)} %in_ref.3), custom_call_target="tpu_custom_call" | custom-call | bytes 251658 | tf_op jit(solution)/shard_map/state_norm/pallas_call | solution.py:353
  93.8 25.6 %collective-permute-done.7 = bf16[2048,128]{1,0:T(8,128)(2,1)} collective-permute-done((bf16[2048,128]{1,0:T(8,128)(2,1)S(1)}, bf16[2048,128]{1,0:T(8,128)(2,1)}, u32[]{:S(2)}, u32[]{:S(2)}) %collective-permute-start.7) | collective-permute-done | bytes 524320 | tf_op jit(solution)/shard_map/ppermute | solution.py:38
  137.8 12.2 %compress.1 = (bf16[1024,512]{1,0:T(8,128)(2,1)}, bf16[3,1024,512]{2,1,0:T(8,128)(2,1)}) custom-call(bf16[3,1024,1024]{2,1,0:T(8,128)(2,1)} %state_norm.3.old_ref, bf16[1120,1024]{1,0:T(8,128)(2,1)} %copy-done.8, bf16[1120,1024]{1,0:T(8,128)(2,1)} %copy-done.8, bf16[2,384,128]{2,1,0:T(8,128)(2,1)} %bitcast.316), custom_call_target="tpu_custom_call" | custom-call | flops 64424508 | bytes 251658 | tf_op jit(solution)/shard_map/compress/pallas_call | solution.py:395
  162.7 10.9 %attend.1 = (bf16[2,2,256,256]{3,2,1,0:T(8,128)(2,1)}, f32[2,2,512,1]{3,2,1,0:T(8,128)}) custom-call(s32[8]{0:T(128)} %fusion.106.info_ref, bf16[2,2,256,768]{3,2,1,0:T(8,128)(2,1)} %bitcast.282, bf16[2,2,256,768]{3,2,1,0:T(8,128)(2,1)} %bitcast.283, bf16[2,2,256,768]{3,2,1,0:T(8,128)(2,1)} %bitcast.284, bf16[1024,512]{1,0:T(8,128)(2,1)} %get-tuple-element.186.kc_ref.vc_ref, ...), custom_call_target="tpu_custom_call" | custom-call | flops 146800640 | bytes 125829 | tf_op jit(solution)/shard_map/attend/pallas_call | solution.py:547
  216.1 12.1 %collective-permute-done.16 = bf16[256,1024]{1,0:T(8,128)(2,1)S(1)} collective-permute-done((bf16[256,1024]{1,0:T(8,128)(2,1)S(1)}, bf16[256,1024]{1,0:T(8,128)(2,1)S(1)}, u32[]{:S(2)}, u32[]{:S(2)}) %collective-permute-start.16) | collective-permute-done | bytes 524320 | tf_op jit(solution)/shard_map/ppermute | solution.py:38
  258.2 10.4 %collective-permute-done.19 = bf16[256,1024]{1,0:T(8,128)(2,1)S(1)} collective-permute-done((bf16[256,1024]{1,0:T(8,128)(2,1)S(1)}, bf16[256,1024]{1,0:T(8,128)(2,1)S(1)}, u32[]{:S(2)}, u32[]{:S(2)}) %collective-permute-start.19) | collective-permute-done | bytes 524320 | tf_op jit(solution)/shard_map/ppermute | solution.py:38
  272.4 21.4 %own_list.1 = (s32[8200]{0:T(1024)}, s32[1]{0:T(128)}) custom-call(s32[8192]{0:T(1024)} %get-tuple-element.208.code_ref), custom_call_target="tpu_custom_call" | custom-call | bytes 1258291 | tf_op jit(solution)/shard_map/own_list/pallas_call | solution.py:209
  304.1 9.7 %logits_part.4 = (bf16[512,2048]{1,0:T(8,128)(2,1)}, bf16[512,2048]{1,0:T(8,128)(2,1)}, f32[8,1024]{1,0:T(8,128)}) custom-call(f32[4,8,1024]{2,1,0:T(8,128)} %bitcast.288, f32[4,8,1024]{2,1,0:T(8,128)} %bitcast.289, bf16[512,1024]{1,0:T(8,128)(2,1)} %pad_maximum_fusion.20.pair_ref.refs_8_, bf16[512,1024]{1,0:T(8,128)(2,1)} %collective-permute-done.24.near_ref.refs_9_, ...), custom_call_target="tpu_custom_call" | custom-call | flops 171798688 | bytes 209715 | tf_op jit(solution)/shard_map/logits_part/pallas_call | solution.py:640
  313.8 10.9 %collective-permute-done.22 = bf16[512,1024]{1,0:T(8,128)(2,1)} collective-permute-done((bf16[512,1024]{1,0:T(8,128)(2,1)}, bf16[512,1024]{1,0:T(8,128)(2,1)}, u32[]{:S(2)}, u32[]{:S(2)}) %collective-permute-start.22) | collective-permute-done | bytes 1048608 | tf_op jit(solution)/shard_map/ppermute | solution.py:38
  329.4 10.0 %logits_part.5 = (bf16[512,2048]{1,0:T(8,128)(2,1)}, bf16[512,2048]{1,0:T(8,128)(2,1)}, f32[8,1024]{1,0:T(8,128)}) custom-call(f32[4,8,1024]{2,1,0:T(8,128)} %bitcast.290, f32[4,8,1024]{2,1,0:T(8,128)} %bitcast.291, bf16[512,1024]{1,0:T(8,128)(2,1)} %copy-done.24, bf16[512,1024]{1,0:T(8,128)(2,1)} %copy-done.36, bf16[2048,512]{1,0:T(8,128)(2,1)} %copy-done, ...), custom_call_target="tpu_custom_call" | custom-call | flops 171798688 | bytes 209715 | tf_op jit(solution)/shard_map/logits_part/pallas_call | solution.py:640
  346.5 9.6 %logits_part.6 = (bf16[512,2048]{1,0:T(8,128)(2,1)}, bf16[512,2048]{1,0:T(8,128)(2,1)}, f32[8,1024]{1,0:T(8,128)}) custom-call(f32[4,8,1024]{2,1,0:T(8,128)} %bitcast.292, f32[4,8,1024]{2,1,0:T(8,128)} %bitcast.293, bf16[512,1024]{1,0:T(8,128)(2,1)} %copy-done.14, bf16[512,1024]{1,0:T(8,128)(2,1)} %copy-done.37, bf16[2048,512]{1,0:T(8,128)(2,1)} %copy-done, ...), custom_call_target="tpu_custom_call" | custom-call | flops 171798688 | bytes 209715 | tf_op jit(solution)/shard_map/logits_part/pallas_call | solution.py:640
  362.2 9.6 %logits_part.7 = (bf16[512,2048]{1,0:T(8,128)(2,1)}, bf16[512,2048]{1,0:T(8,128)(2,1)}, f32[8,1024]{1,0:T(8,128)}) custom-call(f32[4,8,1024]{2,1,0:T(8,128)} %bitcast.294, f32[4,8,1024]{2,1,0:T(8,128)} %bitcast.295, bf16[512,1024]{1,0:T(8,128)(2,1)} %copy-done.15, bf16[512,1024]{1,0:T(8,128)(2,1)} %copy-done.38, bf16[2048,512]{1,0:T(8,128)(2,1)} %copy-done, ...), custom_call_target="tpu_custom_call" | custom-call | flops 171798688 | bytes 209715 | tf_op jit(solution)/shard_map/logits_part/pallas_call | solution.py:640
  390.5 9.7 %logits_back.4 = (bf16[512,2048]{1,0:T(8,128)(2,1)}, bf16[512,2048]{1,0:T(8,128)(2,1)}, bf16[512,1024]{1,0:T(8,128)(2,1)}, bf16[512,1024]{1,0:T(8,128)(2,1)}) custom-call(f32[4,8,1024]{2,1,0:T(8,128)} %bitcast.297, f32[4,8,1024]{2,1,0:T(8,128)} %bitcast.298, f32[4,8,1024]{2,1,0:T(8,128)} %broadcast_in_dim.202.pair_factor_ref.near_factor_ref, ...), custom_call_target="tpu_custom_call" | custom-call | flops 171798688 | bytes 251658 | tf_op jit(solution)/shard_map/logits_back/pallas_call | solution.py:701
  406.8 9.5 %logits_back.5 = (bf16[512,2048]{1,0:T(8,128)(2,1)}, bf16[512,2048]{1,0:T(8,128)(2,1)}, bf16[512,1024]{1,0:T(8,128)(2,1)}, bf16[512,1024]{1,0:T(8,128)(2,1)}) custom-call(f32[4,8,1024]{2,1,0:T(8,128)} %bitcast.299, f32[4,8,1024]{2,1,0:T(8,128)} %bitcast.300, f32[4,8,1024]{2,1,0:T(8,128)} %broadcast_in_dim.202.pair_factor_ref.near_factor_ref, ...), custom_call_target="tpu_custom_call" | custom-call | flops 171798688 | bytes 251658 | tf_op jit(solution)/shard_map/logits_back/pallas_call | solution.py:701
  427.7 9.5 %logits_back.6 = (bf16[512,2048]{1,0:T(8,128)(2,1)}, bf16[512,2048]{1,0:T(8,128)(2,1)}, bf16[512,1024]{1,0:T(8,128)(2,1)}, bf16[512,1024]{1,0:T(8,128)(2,1)}) custom-call(f32[4,8,1024]{2,1,0:T(8,128)} %bitcast.301, f32[4,8,1024]{2,1,0:T(8,128)} %bitcast.302, f32[4,8,1024]{2,1,0:T(8,128)} %broadcast_in_dim.202.pair_factor_ref.near_factor_ref, ...), custom_call_target="tpu_custom_call" | custom-call | flops 171798688 | bytes 251658 | tf_op jit(solution)/shard_map/logits_back/pallas_call | solution.py:701
  452.7 9.9 %logits_back.7 = (bf16[512,2048]{1,0:T(8,128)(2,1)}, bf16[512,2048]{1,0:T(8,128)(2,1)}, bf16[512,1024]{1,0:T(8,128)(2,1)}, bf16[512,1024]{1,0:T(8,128)(2,1)}) custom-call(f32[4,8,1024]{2,1,0:T(8,128)} %bitcast.303, f32[4,8,1024]{2,1,0:T(8,128)} %bitcast.304, f32[4,8,1024]{2,1,0:T(8,128)} %broadcast_in_dim.202.pair_factor_ref.near_factor_ref, ...), custom_call_target="tpu_custom_call" | custom-call | flops 171798688 | bytes 251658 | tf_op jit(solution)/shard_map/logits_back/pallas_call | solution.py:701
  462.7 13.5 %collective-permute-done.43 = bf16[512,1024]{1,0:T(8,128)(2,1)} collective-permute-done((bf16[512,1024]{1,0:T(8,128)(2,1)}, bf16[512,1024]{1,0:T(8,128)(2,1)}, u32[]{:S(2)}, u32[]{:S(2)}) %collective-permute-start.43) | collective-permute-done | bytes 1048608 | tf_op jit(solution)/shard_map/ppermute | solution.py:38
  488.8 24.3 %table_grad_part.1 = (f32[2048,512]{1,0:T(8,128)}, bf16[2048,512]{1,0:T(8,128)(2,1)}) custom-call(bf16[512,2048]{1,0:T(8,128)(2,1)} %get-tuple-element.259.refs_0_, bf16[512,2048]{1,0:T(8,128)(2,1)} %get-tuple-element.260.refs_1_, bf16[512,2048]{1,0:T(8,128)(2,1)} %get-tuple-element.261.refs_2_, bf16[512,2048]{1,0:T(8,128)(2,1)} %get-tuple-element.262.refs_3_, ...), custom_call_target="tpu_custom_call" | custom-call | flops 515396064 | bytes 629145 | tf_op jit(solution)/shard_map/table_grad_part/pallas_call | solution.py:748
  516.8 10.8 %collective-permute-done.45 = bf16[256,1024]{1,0:T(8,128)(2,1)S(1)} collective-permute-done((bf16[256,1024]{1,0:T(8,128)(2,1)S(1)}, bf16[256,1024]{1,0:T(8,128)(2,1)S(1)}, u32[]{:S(2)}, u32[]{:S(2)}) %collective-permute-start.45) | collective-permute-done | bytes 524320 | tf_op jit(solution)/shard_map/ppermute | solution.py:38
  551.0 11.5 %hidden_grads.1 = (f32[2048,512]{1,0:T(8,128)}, bf16[2048,512]{1,0:T(8,128)(2,1)}) custom-call(bf16[1024,1024]{1,0:T(8,128)(2,1)} %copy-done.51, bf16[1024,1024]{1,0:T(8,128)(2,1)} %copy-done.50, bf16[1024,1024]{1,0:T(8,128)(2,1)} %pad_maximum_fusion.2.in_ref, bf16[1024,1024]{1,0:T(8,128)(2,1)} %pad_maximum_fusion.5.down_ref), custom_call_target="tpu_custom_call" | custom-call | flops 128849016 | bytes 335544 | tf_op jit(solution)/shard_map/hidden_grads/pallas_call | solution.py:783
  566.7 23.0 %collective-permute-done.51 = bf16[2048,512]{1,0:T(8,128)(2,1)} collective-permute-done((bf16[2048,512]{1,0:T(8,128)(2,1)}, bf16[2048,512]{1,0:T(8,128)(2,1)}, u32[]{:S(2)}, u32[]{:S(2)}) %collective-permute-start.51) | collective-permute-done | bytes 2097184 | tf_op jit(solution)/shard_map/ppermute | solution.py:38
  611.3 15.2 %attend_back.1 = (bf16[2,2,256,768]{3,2,1,0:T(8,128)(2,1)}, bf16[1024,512]{1,0:T(8,128)(2,1)}, bf16[1024,512]{1,0:T(8,128)(2,1)}) custom-call(s32[8]{0:T(128)} %fusion.106.info_ref, bf16[2,2,256,768]{3,2,1,0:T(8,128)(2,1)} %bitcast.285, bf16[2,2,256,768]{3,2,1,0:T(8,128)(2,1)} %bitcast.286, bf16[2,2,256,768]{3,2,1,0:T(8,128)(2,1)} %bitcast.287, ...), custom_call_target="tpu_custom_call" | custom-call | flops 230686720 | bytes 188743 | tf_op jit(solution)/shard_map/attend_back/pallas_call | solution.py:570
  643.9 11.2 %collective-permute-done.49 = bf16[2048,512]{1,0:T(8,128)(2,1)} collective-permute-done((bf16[2048,512]{1,0:T(8,128)(2,1)}, bf16[2048,512]{1,0:T(8,128)(2,1)}, u32[]{:S(2)}, u32[]{:S(2)}) %collective-permute-start.49) | collective-permute-done | bytes 2097184 | tf_op jit(solution)/shard_map/ppermute | solution.py:38
  669.4 14.3 %attn_grads.1 = (f32[1024,512]{1,0:T(8,128)}, bf16[1024,512]{1,0:T(8,128)(2,1)}) custom-call(bf16[1024,768]{1,0:T(8,128)(2,1)} %bitcast.319, bf16[1024,256]{1,0:T(8,128)(2,1)} %bitcast.312, bf16[1024,512]{1,0:T(8,128)(2,1)} %get-tuple-element.287.mem_ref, bf16[3072,512]{1,0:T(8,128)(2,1)} %bitcast.313, bf16[1024,1024]{1,0:T(8,128)(2,1)} %pad_maximum_fusion.1.normed_ref, ...), custom_call_target="tpu_custom_call" | custom-call | flops 188743680 | bytes 503316 | tf_op jit(solution)/shard_map/attn_grads/pallas_call | solution.py:833
  700.7 8.0 all-to-all-done.3
  712.3 14.6 %collective-permute-done.57 = bf16[1120,512]{1,0:T(8,128)(2,1)} collective-permute-done((bf16[1120,512]{1,0:T(8,128)(2,1)}, bf16[1120,512]{1,0:T(8,128)(2,1)}, u32[]{:S(2)}, u32[]{:S(2)}) %collective-permute-start.57) | collective-permute-done | bytes 1146912 | tf_op jit(solution)/shard_map/ppermute | solution.py:38
  738.2 13.9 %scatter.1 = f32[8000,128]{1,0:T(8,128)} custom-call(s32[1]{0:T(128)} %get-tuple-element.299.count_ref, s32[8200]{0:T(1024)} %get-tuple-element.300.code_ref, f32[8000,128]{1,0:T(8,128)} %bitcast_convert_fusion.base_ref, bf16[8192,128]{1,0:T(8,128)(2,1)} %bitcast.307), custom_call_target="tpu_custom_call" | custom-call | bytes 629145 | tf_op jit(solution)/shard_map/scatter/pallas_call | solution.py:305
  758.9 10.0 %collective-permute-done.61 = bf16[1120,128]{1,0:T(8,128)(2,1)S(1)} collective-permute-done((bf16[1120,128]{1,0:T(8,128)(2,1)S(1)}, bf16[1120,128]{1,0:T(8,128)(2,1)S(1)}, u32[]{:S(2)}, u32[]{:S(2)}) %collective-permute-start.61) | collective-permute-done | bytes 286752 | tf_op jit(solution)/shard_map/ppermute | solution.py:38
  801.4 7.2 multiply_reduce_fusion
  844.8 7.8 divide_subtract_fusion
  (727 shorter events, 435.8 us)
Async XLA Ops:
  18.3 30.5 %collective-permute-start.3 = (bf16[1120,128]{1,0:T(8,128)(2,1)}, bf16[1120,128]{1,0:T(8,128)(2,1)}, u32[]{:S(2)}, u32[]{:S(2)}) collective-permute-start(bf16[1120,128]{1,0:T(8,128)(2,1)} %pad_maximum_fusion.28), channel_id=1, source_target_pairs={{0,16},{4,20},{8,24},{12,28},{16,0},{20,4},{24,8},{28,12},{1,17},{... | collective-permute-start | bytes 860168 | tf_op jit(solution)/shard_map/ppermute | solution.py:38
  50.9 24.8 %collective-permute-start.4 = (bf16[1120,256]{1,0:T(8,128)(2,1)S(1)}, bf16[1120,256]{1,0:T(8,128)(2,1)}, u32[]{:S(2)}, u32[]{:S(2)}) collective-permute-start(bf16[1120,256]{1,0:T(8,128)(2,1)S(1)} %pad_maximum_fusion.26), channel_id=1, source_target_pairs={{0,8},{4,12},{8,0},{12,4},{16,24},{20,28},{24,16},{28,20},{1,9},{5... | collective-permute-start | bytes 1720328 | tf_op jit(solution)/shard_map/ppermute | solution.py:38
  55.1 20.6 %collective-permute-start.6 = (bf16[2048,128]{1,0:T(8,128)(2,1)}, bf16[2048,128]{1,0:T(8,128)(2,1)}, u32[]{:S(2)}, u32[]{:S(2)}) collective-permute-start(bf16[2048,128]{1,0:T(8,128)(2,1)} %slice.661), channel_id=1, source_target_pairs={{0,2},{1,3},{2,0},{3,1},{4,6},{5,7},{6,4},{7,5},{8,10},{9,11},{10,... | collective-permute-start | bytes 1572872 | tf_op jit(solution)/shard_map/ppermute | solution.py:38
  77.8 41.6 %all-to-all-start = ((bf16[8,256,128]{2,1,0:T(8,128)(2,1)}), bf16[8,256,128]{2,1,0:T(8,128)(2,1)}, u32[]{:S(2)}, u32[]{:S(2)}) async-start(bf16[8,256,128]{2,1,0:T(8,128)(2,1)} %bitcast.314), calls=%async_computation | async-start | bytes 1048576 | tf_op jit(solution)/shard_map/all_to_all | solution.py:1000
  84.3 41.9 %collective-permute-start.10 = (bf16[1120,512]{1,0:T(8,128)(2,1)}, bf16[1120,512]{1,0:T(8,128)(2,1)}, u32[]{:S(2)}, u32[]{:S(2)}) collective-permute-start(bf16[1120,512]{1,0:T(8,128)(2,1)} %get-tuple-element.447), channel_id=1, source_target_pairs={{0,4},{4,0},{8,12},{12,8},{16,20},{20,16},{24,28},{28,24},{1,5},{5... | collective-permute-start | bytes 3440648 | tf_op jit(solution)/shard_map/ppermute | solution.py:38
  86.3 33.1 %collective-permute-start.7 = (bf16[2048,128]{1,0:T(8,128)(2,1)S(1)}, bf16[2048,128]{1,0:T(8,128)(2,1)}, u32[]{:S(2)}, u32[]{:S(2)}) collective-permute-start(bf16[2048,128]{1,0:T(8,128)(2,1)S(1)} %pad_maximum_fusion.27), channel_id=1, source_target_pairs={{0,16},{4,20},{8,24},{12,28},{16,0},{20,4},{24,8},{28,12},{1,17},{... | collective-permute-start | bytes 1572872 | tf_op jit(solution)/shard_map/ppermute | solution.py:38
  124.3 29.8 %collective-permute-start.11 = (bf16[2048,256]{1,0:T(8,128)(2,1)}, bf16[2048,256]{1,0:T(8,128)(2,1)}, u32[]{:S(2)}, u32[]{:S(2)}) collective-permute-start(bf16[2048,256]{1,0:T(8,128)(2,1)} %pad_maximum_fusion.18), channel_id=1, source_target_pairs={{0,8},{4,12},{8,0},{12,4},{16,24},{20,28},{24,16},{28,20},{1,9},{5... | collective-permute-start | bytes 3145736 | tf_op jit(solution)/shard_map/ppermute | solution.py:38
  136.8 21.6 %collective-permute-start.9 = (bf16[512,1024]{1,0:T(8,128)(2,1)}, bf16[512,1024]{1,0:T(8,128)(2,1)}, u32[]{:S(2)}, u32[]{:S(2)}) collective-permute-start(bf16[512,1024]{1,0:T(8,128)(2,1)} %pad_maximum_fusion.17), channel_id=1, source_target_pairs={{0,1},{1,0},{2,3},{3,2},{4,5},{5,4},{6,7},{7,6},{8,9},{9,8},{10,11... | collective-permute-start | bytes 3145736 | tf_op jit(solution)/shard_map/ppermute | solution.py:38
  156.8 31.7 %collective-permute-start.13 = (bf16[1024,512]{1,0:T(8,128)(2,1)}, bf16[1024,512]{1,0:T(8,128)(2,1)}, u32[]{:S(2)}, u32[]{:S(2)}) collective-permute-start(bf16[1024,512]{1,0:T(8,128)(2,1)} %get-tuple-element.434), channel_id=1, source_target_pairs={{0,4},{4,0},{8,12},{12,8},{16,20},{20,16},{24,28},{28,24},{1,5},{5... | collective-permute-start | bytes 3145736 | tf_op jit(solution)/shard_map/ppermute | solution.py:38
  180.4 31.7 %collective-permute-start.15 = (bf16[1024,512]{1,0:T(8,128)(2,1)}, bf16[1024,512]{1,0:T(8,128)(2,1)}, u32[]{:S(2)}, u32[]{:S(2)}) collective-permute-start(bf16[1024,512]{1,0:T(8,128)(2,1)} %get-tuple-element.433), channel_id=1, source_target_pairs={{0,4},{4,0},{8,12},{12,8},{16,20},{20,16},{24,28},{28,24},{1,5},{5... | collective-permute-start | bytes 3145736 | tf_op jit(solution)/shard_map/ppermute | solution.py:38
  180.9 51.5 %all-to-all-start.1 = ((bf16[4,2000,128]{2,1,0:T(8,128)(2,1)}), bf16[4,2000,128]{2,1,0:T(8,128)(2,1)S(1)}, u32[]{:S(2)}, u32[]{:S(2)}) async-start(bf16[4,2000,128]{2,1,0:T(8,128)(2,1)} %bitcast.308), calls=%async_computation.1 | async-start | bytes 4096000 | tf_op jit(solution)/shard_map/all_to_all | solution.py:1080
  192.2 19.8 %collective-permute-start.14 = (bf16[256,1024]{1,0:T(8,128)(2,1)S(1)}, bf16[256,1024]{1,0:T(8,128)(2,1)}, u32[]{:S(2)}, u32[]{:S(2)}) collective-permute-start(bf16[256,1024]{1,0:T(8,128)(2,1)S(1)} %slice.1037), channel_id=1, source_target_pairs={{0,2},{1,3},{2,0},{3,1},{4,6},{5,7},{6,4},{7,5},{8,10},{9,11},{10,... | collective-permute-start | bytes 1572872 | tf_op jit(solution)/shard_map/ppermute | solution.py:38
  256.6 47.6 %collective-permute-start.25 = (bf16[2048,512]{1,0:T(8,128)(2,1)S(1)}, bf16[2048,512]{1,0:T(8,128)(2,1)}, u32[]{:S(2)}, u32[]{:S(2)}) collective-permute-start(bf16[2048,512]{1,0:T(8,128)(2,1)S(1)} %fusion.13.left_ref), channel_id=1, source_target_pairs={{0,4},{4,0},{8,12},{12,8},{16,20},{20,16},{24,28},{28,24},{1,5},{5... | collective-permute-start | bytes 6291464 | tf_op jit(solution)/shard_map/ppermute | solution.py:38
  269.9 23.9 %collective-permute-start.23 = (bf16[256,1024]{1,0:T(8,128)(2,1)}, bf16[256,1024]{1,0:T(8,128)(2,1)}, u32[]{:S(2)}, u32[]{:S(2)}) collective-permute-start(bf16[256,1024]{1,0:T(8,128)(2,1)} %multiply_convert_fusion.1.refs_0_), channel_id=1, source_target_pairs={{0,2},{1,3},{2,0},{3,1},{4,6},{5,7},{6,4},{7,5},{8,10},{9,11},{10,... | collective-permute-start | bytes 1572872 | tf_op jit(solution)/shard_map/ppermute | solution.py:38
  272.4 24.5 %collective-permute-start.20 = (bf16[256,1024]{1,0:T(8,128)(2,1)}, bf16[256,1024]{1,0:T(8,128)(2,1)}, u32[]{:S(2)}, u32[]{:S(2)}) collective-permute-start(bf16[256,1024]{1,0:T(8,128)(2,1)} %reorder.4), channel_id=1, source_target_pairs={{0,16},{4,20},{8,24},{12,28},{16,0},{20,4},{24,8},{28,12},{1,17},{... | collective-permute-start | bytes 1572872 | tf_op jit(solution)/shard_map/ppermute | solution.py:38
  299.1 25.6 %collective-permute-start.22 = (bf16[512,1024]{1,0:T(8,128)(2,1)}, bf16[512,1024]{1,0:T(8,128)(2,1)}, u32[]{:S(2)}, u32[]{:S(2)}) collective-permute-start(bf16[512,1024]{1,0:T(8,128)(2,1)} %reorder.5), channel_id=1, source_target_pairs={{0,8},{4,12},{8,0},{12,4},{16,24},{20,28},{24,16},{28,20},{1,9},{5... | collective-permute-start | bytes 3145736 | tf_op jit(solution)/shard_map/ppermute | solution.py:38
  300.6 24.1 %collective-permute-start.21 = (bf16[256,1024]{1,0:T(8,128)(2,1)}, bf16[256,1024]{1,0:T(8,128)(2,1)S(1)}, u32[]{:S(2)}, u32[]{:S(2)}) collective-permute-start(bf16[256,1024]{1,0:T(8,128)(2,1)} %collective-permute-done.20.refs_1_), channel_id=1, source_target_pairs={{0,2},{1,3},{2,0},{3,1},{4,6},{5,7},{6,4},{7,5},{8,10},{9,11},{10,... | collective-permute-start | bytes 1572872 | tf_op jit(solution)/shard_map/ppermute | solution.py:38
  450.9 25.2 %collective-permute-start.43 = (bf16[512,1024]{1,0:T(8,128)(2,1)}, bf16[512,1024]{1,0:T(8,128)(2,1)}, u32[]{:S(2)}, u32[]{:S(2)}) collective-permute-start(bf16[512,1024]{1,0:T(8,128)(2,1)} %reorder.6), channel_id=1, source_target_pairs={{0,8},{4,12},{8,0},{12,4},{16,24},{20,28},{24,16},{28,20},{1,9},{5... | collective-permute-start | bytes 3145736 | tf_op jit(solution)/shard_map/ppermute | solution.py:38
  462.6 22.5 %collective-permute-start.41 = (bf16[512,1024]{1,0:T(8,128)(2,1)}, bf16[512,1024]{1,0:T(8,128)(2,1)}, u32[]{:S(2)}, u32[]{:S(2)}) collective-permute-start(bf16[512,1024]{1,0:T(8,128)(2,1)} %get-tuple-element.252), channel_id=1, source_target_pairs={{0,1},{1,0},{2,3},{3,2},{4,5},{5,4},{6,7},{7,6},{8,9},{9,8},{10,11... | collective-permute-start | bytes 3145736 | tf_op jit(solution)/shard_map/ppermute | solution.py:38
  482.5 30.6 %collective-permute-start.44 = (bf16[256,1024]{1,0:T(8,128)(2,1)}, bf16[256,1024]{1,0:T(8,128)(2,1)S(1)}, u32[]{:S(2)}, u32[]{:S(2)}) collective-permute-start(bf16[256,1024]{1,0:T(8,128)(2,1)} %reorder.7), channel_id=1, source_target_pairs={{0,16},{4,20},{8,24},{12,28},{16,0},{20,4},{24,8},{28,12},{1,17},{... | collective-permute-start | bytes 1572872 | tf_op jit(solution)/shard_map/ppermute | solution.py:38
  488.2 25.0 %collective-permute-start.42 = (bf16[256,1024]{1,0:T(8,128)(2,1)S(1)}, bf16[256,1024]{1,0:T(8,128)(2,1)S(1)}, u32[]{:S(2)}, u32[]{:S(2)}) collective-permute-start(bf16[256,1024]{1,0:T(8,128)(2,1)S(1)} %slice.1032), channel_id=1, source_target_pairs={{0,2},{1,3},{2,0},{3,1},{4,6},{5,7},{6,4},{7,5},{8,10},{9,11},{10,... | collective-permute-start | bytes 1572872 | tf_op jit(solution)/shard_map/ppermute | solution.py:38
  541.4 48.2 %collective-permute-start.51 = (bf16[2048,512]{1,0:T(8,128)(2,1)}, bf16[2048,512]{1,0:T(8,128)(2,1)}, u32[]{:S(2)}, u32[]{:S(2)}) collective-permute-start(bf16[2048,512]{1,0:T(8,128)(2,1)} %get-tuple-element.276), channel_id=1, source_target_pairs={{0,4},{4,0},{8,12},{12,8},{16,20},{20,16},{24,28},{28,24},{1,5},{5... | collective-permute-start | bytes 6291464 | tf_op jit(solution)/shard_map/ppermute | solution.py:38
  566.1 23.5 %collective-permute-start.50 = (bf16[256,1024]{1,0:T(8,128)(2,1)}, bf16[256,1024]{1,0:T(8,128)(2,1)S(1)}, u32[]{:S(2)}, u32[]{:S(2)}) collective-permute-start(bf16[256,1024]{1,0:T(8,128)(2,1)} %get-tuple-element.413), channel_id=1, source_target_pairs={{0,2},{1,3},{2,0},{3,1},{4,6},{5,7},{6,4},{7,5},{8,10},{9,11},{10,... | collective-permute-start | bytes 1572872 | tf_op jit(solution)/shard_map/ppermute | solution.py:38
  595.6 59.5 %all-to-all-start.2 = ((bf16[4,2000,128]{2,1,0:T(8,128)(2,1)}), bf16[4,2000,128]{2,1,0:T(8,128)(2,1)}, u32[]{:S(2)}, u32[]{:S(2)}) async-start(bf16[4,2000,128]{2,1,0:T(8,128)(2,1)} %pad_maximum_fusion.9), calls=%async_computation.2 | async-start | bytes 4096000 | tf_op jit(solution)/shard_map/all_to_all | solution.py:1206
  606.7 48.4 %collective-permute-start.49 = (bf16[2048,512]{1,0:T(8,128)(2,1)}, bf16[2048,512]{1,0:T(8,128)(2,1)}, u32[]{:S(2)}, u32[]{:S(2)}) collective-permute-start(bf16[2048,512]{1,0:T(8,128)(2,1)} %get-tuple-element.273), channel_id=1, source_target_pairs={{0,4},{4,0},{8,12},{12,8},{16,20},{20,16},{24,28},{28,24},{1,5},{5... | collective-permute-start | bytes 6291464 | tf_op jit(solution)/shard_map/ppermute | solution.py:38
  631.8 23.3 %collective-permute-start.53 = (bf16[512,1024]{1,0:T(8,128)(2,1)S(1)}, bf16[512,1024]{1,0:T(8,128)(2,1)S(1)}, u32[]{:S(2)}, u32[]{:S(2)}) collective-permute-start(bf16[512,1024]{1,0:T(8,128)(2,1)S(1)} %slice.1024), channel_id=1, source_target_pairs={{0,1},{1,0},{2,3},{3,2},{4,5},{5,4},{6,7},{7,6},{8,9},{9,8},{10,11... | collective-permute-start | bytes 3145736 | tf_op jit(solution)/shard_map/ppermute | solution.py:38
  663.8 37.0 %collective-permute-start.54 = (bf16[2048,256]{1,0:T(8,128)(2,1)}, bf16[2048,256]{1,0:T(8,128)(2,1)}, u32[]{:S(2)}, u32[]{:S(2)}) collective-permute-start(bf16[2048,256]{1,0:T(8,128)(2,1)} %slice.1023), channel_id=1, source_target_pairs={{0,8},{4,12},{8,0},{12,4},{16,24},{20,28},{24,16},{28,20},{1,9},{5... | collective-permute-start | bytes 3145736 | tf_op jit(solution)/shard_map/ppermute | solution.py:38
  665.7 20.6 %collective-permute-start.55 = (bf16[256,1024]{1,0:T(8,128)(2,1)S(1)}, bf16[256,1024]{1,0:T(8,128)(2,1)S(1)}, u32[]{:S(2)}, u32[]{:S(2)}) collective-permute-start(bf16[256,1024]{1,0:T(8,128)(2,1)S(1)} %slice.1030), channel_id=1, source_target_pairs={{0,2},{1,3},{2,0},{3,1},{4,6},{5,7},{6,4},{7,5},{8,10},{9,11},{10,... | collective-permute-start | bytes 1572872 | tf_op jit(solution)/shard_map/ppermute | solution.py:38
  690.2 18.5 %all-to-all-start.3 = ((bf16[8,256,128]{2,1,0:T(8,128)(2,1)}), bf16[8,256,128]{2,1,0:T(8,128)(2,1)S(1)}, u32[]{:S(2)}, u32[]{:S(2)}) async-start(bf16[8,256,128]{2,1,0:T(8,128)(2,1)} %embed_back.1), calls=%async_computation.3 | async-start | bytes 1048576 | tf_op jit(solution)/shard_map/all_to_all | solution.py:1242
  694.9 32.0 %collective-permute-start.57 = (bf16[1120,512]{1,0:T(8,128)(2,1)}, bf16[1120,512]{1,0:T(8,128)(2,1)}, u32[]{:S(2)}, u32[]{:S(2)}) collective-permute-start(bf16[1120,512]{1,0:T(8,128)(2,1)} %pad_maximum_fusion.16), channel_id=1, source_target_pairs={{0,4},{4,0},{8,12},{12,8},{16,20},{20,16},{24,28},{28,24},{1,5},{5... | collective-permute-start | bytes 3440648 | tf_op jit(solution)/shard_map/ppermute | solution.py:38
  711.5 23.3 %collective-permute-start.56 = (bf16[2048,128]{1,0:T(8,128)(2,1)S(1)}, bf16[2048,128]{1,0:T(8,128)(2,1)S(1)}, u32[]{:S(2)}, u32[]{:S(2)}) collective-permute-start(bf16[2048,128]{1,0:T(8,128)(2,1)S(1)} %slice.1029), channel_id=1, source_target_pairs={{0,16},{4,20},{8,24},{12,28},{16,0},{20,4},{24,8},{28,12},{1,17},{... | collective-permute-start | bytes 1572872 | tf_op jit(solution)/shard_map/ppermute | solution.py:38
  729.7 22.4 %collective-permute-start.59 = (bf16[1120,256]{1,0:T(8,128)(2,1)}, bf16[1120,256]{1,0:T(8,128)(2,1)}, u32[]{:S(2)}, u32[]{:S(2)}) collective-permute-start(bf16[1120,256]{1,0:T(8,128)(2,1)} %slice.1028), channel_id=1, source_target_pairs={{0,8},{4,12},{8,0},{12,4},{16,24},{20,28},{24,16},{28,20},{1,9},{5... | collective-permute-start | bytes 1720328 | tf_op jit(solution)/shard_map/ppermute | solution.py:38
  (183 other events, 1819.6 us)

commit v12 on v11

--- a/solution.py
+++ b/solution.py
@@ -55,9 +55,9 @@
     return order
 
 
-def gather_blocks(piece, axis, beside=(), stop=0):
+def gather_blocks(piece, axis, beside=(), stop=0, mask=None):
     steps = []
-    mask = lax.axis_size("dp") // 2
+    mask = mask or lax.axis_size("dp") // 2
     while mask > stop:
         moved = swap(piece, "dp", mask)
         if len(steps) < len(beside):
@@ -985,17 +985,23 @@
     )
     own_half, far_half = split(table_rows_all, 0, 2)
     kept = {}
+    hidden_own = wup.shape[1]
+    pack_two = jnp.concatenate([wup.astype(lowp).T, wdown.astype(lowp)])
 
     def beside_lookup(moved):
         moved, kept["far"], kept["own"] = together(
             moved, lookup(far_half, table), lookup(own_half, table)
         )
+        kept["two"] = after(pack_two, moved)
         return moved
 
     def beside_memory(moved):
         looked = (kept["own"] + swap(kept["far"], "head", 1)).reshape(2, -1, width)
         mem_normed = state_norm(place, gain_vals[0], memory, 1)[0]
-        moved, more, kept["mem"] = together(moved, swap(looked[1], "head", 2), mem_normed)
+        moved, more, kept["mem"], second = together(
+            moved, swap(looked[1], "head", 2), mem_normed, swap(kept["two"], "dp", dp_size // 2)
+        )
+        kept["two"] = jnp.concatenate([kept["two"], second], axis=1)
         looked = (looked[0] + more).reshape(dp_size, half, width)
         kept["looked"] = lax.all_to_all(looked, "dp", 0, 0)
         return moved
@@ -1024,8 +1030,6 @@
 
     full_conv = conv_natural_order(own_one[4 * wide :])
 
-    hidden_own = wup.shape[1]
-    pack_two = jnp.concatenate([wup.astype(lowp).T, wdown.astype(lowp)])
 
     old_normed = state_norm(place, gain_vals[0], old_states, RATE)
 
@@ -1037,26 +1041,21 @@
     info_all = jnp.stack([wanted_all, mask_all] + [jnp.zeros_like(mask_all)] * 6)
     info_all = jnp.transpose(info_all, (1, 0, 2, 3, 4)).reshape(reach, 8, per_group)
 
-    def beside_old(moved):
-        moved, looked, kept["old"], kept["info"] = together(
-            moved, kept["looked"], old_normed, info_all
-        )
-        kept["embedded"], kept["normed"] = place_embedding(place, looked, gain_vals[0])
+    looked, old_normed, info_all = together(kept["looked"], old_normed, info_all)
+    embedded_low, normed = place_embedding(place, looked, gain_vals[0])
+    embedded = embedded_low.astype(single)
+
+    def beside_compress(moved):
+        moved, *kept["comp"] = together(moved, *compress(old_normed, own_one, full_conv))
         return moved
 
-    def beside_compress(moved):
-        moved, *kept["comp"] = together(moved, *compress(kept["old"], own_one, full_conv))
-        return moved
-
     near_two, steps_two = gather_blocks(
-        after(pack_two, steps_one[1]), 1, (beside_old, beside_compress), 1
+        kept["two"], 1, (beside_compress,), 1, dp_size // 4
     )
     near_up, near_down = split(near_two, 0, 2)
     far_up, far_down = swap(near_up, "dp", 1), swap(near_down, "dp", 1)
-    mem_normed, old_normed = kept["mem"], kept["old"]
-    embedded_low = kept["embedded"]
-    embedded = embedded_low.astype(single)
-    normed = jnp.concatenate(group_both(kept["normed"]))
+    mem_normed = kept["mem"]
+    normed = jnp.concatenate(group_both(normed))
     comp, old_raw = kept["comp"]
 
     words = vocab // reach
@@ -1101,7 +1100,6 @@
     after_ffn = after_attn + group_sum(mm(hidden_act, full_down))
     final_in, inv_third = rms(after_ffn, gain_vals[2])
 
-    info_all = kept["info"]
     pieces = [final_in]
     chunks = []
     raised = []
@@ -1187,10 +1185,7 @@
     act_grad = mm(down_in, full_down, NT)
     pre_grad = jax.vjp(jax.nn.gelu, hidden_pre)[1](act_grad)[0].astype(lowp)
     two = hidden_grads(pre_grad, hidden_act, ffn_in, down_in)
-    ffn_in_grad, two = group_sum(mm(pre_grad, full_up), two)
-    grad_after_attn = grad_after_ffn + rms_back(after_attn, inv_second, gain_vals[1], ffn_in_grad)
-    attn_in, (moved_table,) = group_both(grad_after_attn.astype(lowp), (moved_table,))
-    attn_in = jnp.concatenate(attn_in)
+    ffn_in_grad, (*two, moved_table) = group_sum(mm(pre_grad, full_up), (*two, moved_table))
     keep = table_parts[0] + moved_table.astype(single)
     table_pieces = jnp.stack(split(keep[:words].astype(lowp), 1, reach))
     turned = sum(
@@ -1204,6 +1199,8 @@
         ]
     )
     table_pieces = lax.all_to_all(table_pieces, "dp", 0, 0, axis_index_groups=z_groups)
+    grad_after_attn = grad_after_ffn + rms_back(after_attn, inv_second, gain_vals[1], ffn_in_grad)
+    attn_in = jnp.concatenate(group_both(grad_after_attn.astype(lowp)))
 
     mixed_grad = mm(attn_in, own_one[3 * wide : 4 * wide], NT).astype(lowp)
     mixed_grad = mixed_grad.reshape(2, streams, half, wide)

time: 864 us -> 853 us (0.987)
  waiting for transfers between devices: 222 us -> 209 us
    ppermute x70, waiting for transfers between devices: 210 us -> 182 us  [swap(): return lax.ppermute(value, axis, [(i, i ^ mask) for i in range(size)])]
    all_to_all x1, waiting for transfers between devices: 0.01 us -> 15.9 us  [beside_memory(): kept['looked'] = lax.all_to_all(looked, 'dp', 0, 0)]
    unnamed x303 -> x316, local copies, waits for them, and re-layouts: 34.7 us -> 34 us
  transfers between devices with their start and end apart: 74 -> 74, of which waited for: 42 -> 43; matrix products, arithmetic and copies ran while one was open for 18% -> 20% of each run, Pallas kernels for 28% -> 28%
where the time goes in v12:
time: 853 us; the launch traced here: 846 us
  Pallas kernels  256 us (30%)
  waiting for transfers between devices  209 us (25%)
  other arithmetic  156 us (18%)
  starting transfers between devices  78.1 us (9%)
  local copies, waits for them, and re-layouts  76.1 us (9%)
  matrix products  38.2 us (4%)
  between operations  26.1 us (3%)
    ppermute x70, waiting for transfers between devices, swap(): return lax.ppermute(value, axis, [(i, i ^ mask) for i in range(size)])  182 us
    ppermute x70, starting transfers between devices, swap(): return lax.ppermute(value, axis, [(i, i ^ mask) for i in range(size)])  59.5 us
    pallas_call x4, Pallas kernels, logits_part(): pl.pallas_call(functools.partial(logits_kernel, words), name='logits_part...  39 us
    pallas_call x4, Pallas kernels, logits_back(): pl.pallas_call(logits_back_kernel, name='logits_back', grid=(tiles,), out...  38.5 us
    dot_general x11, matrix products, mm(): return lax.dot_general(left, right, dims, preferred_element_type=single)  38.2 us
    unnamed x316, local copies, waits for them, and re-layouts  34 us
    pallas_call x1, Pallas kernels, table_grad_part(): pl.pallas_call(functools.partial(table_grad_kernel, len(grads)), name='ta...  24.3 us
    pallas_call x1, Pallas kernels, own_list(): pl.pallas_call(list_kernel, name='own_list', out_shape=(jax.ShapeDtypeStr...  21.4 us
  transfers between devices with their start and end apart: 74, of which 43 were waited for; matrix products, arithmetic and copies ran while one was open for 20% of the time, Pallas kernels for 28%

profile of v12, /device:TPU:0, one launch (start us, length us, event | category | flops | bytes accessed | tf_op | source)
XLA Modules:
  0.0 846.0 jit_solution(10809370021550466213)
XLA Ops:
  31.3 8.6 %lookup.2 = bf16[4096,128]{1,0:T(8,128)(2,1)} custom-call(s32[4096]{0:T(1024)} %get-tuple-element.493.row_ref, f32[8000,128]{1,0:T(8,128)} %table_ref.3), custom_call_target="tpu_custom_call" | custom-call | bytes 629145 | tf_op jit(solution)/shard_map/lookup/pallas_call | solution.py:178
  40.0 8.8 %lookup.3 = bf16[4096,128]{1,0:T(8,128)(2,1)} custom-call(s32[4096]{0:T(1024)} %get-tuple-element.492.row_ref, f32[8000,128]{1,0:T(8,128)} %table_ref.3), custom_call_target="tpu_custom_call" | custom-call | bytes 629145 | tf_op jit(solution)/shard_map/lookup/pallas_call | solution.py:178
  65.8 10.0 %state_norm.3.old_ref = bf16[3,1024,1024]{2,1,0:T(8,128)(2,1)} custom-call(s32[2]{0:T(128)} %pad_add_fusion.place_ref, f32[1,1024]{1,0:T(1,128)} %bitcast.347, bf16[2,1536,1024]{2,1,0:T(8,128)(2,1)} %in_ref.3), custom_call_target="tpu_custom_call" | custom-call | bytes 251658 | tf_op jit(solution)/shard_map/state_norm/pallas_call | solution.py:353
  98.4 15.9 %all-to-all-done.in_ref = bf16[8,256,128]{2,1,0:T(8,128)(2,1)} async-done(((bf16[8,256,128]{2,1,0:T(8,128)(2,1)}), bf16[8,256,128]{2,1,0:T(8,128)(2,1)}, u32[]{:S(2)}, u32[]{:S(2)}) %all-to-all-start) | async-done | bytes 524320 | tf_op jit(solution)/shard_map/all_to_all | solution.py:1006
  131.6 12.1 %compress.1 = (bf16[1024,512]{1,0:T(8,128)(2,1)}, bf16[3,1024,512]{2,1,0:T(8,128)(2,1)}) custom-call(bf16[3,1024,1024]{2,1,0:T(8,128)(2,1)} %state_norm.3.old_ref, bf16[1120,1024]{1,0:T(8,128)(2,1)} %copy-done.8, bf16[1120,1024]{1,0:T(8,128)(2,1)} %copy-done.8, bf16[2,384,128]{2,1,0:T(8,128)(2,1)} %bitcast.316), custom_call_target="tpu_custom_call" | custom-call | flops 64424508 | bytes 251658 | tf_op jit(solution)/shard_map/compress/pallas_call | solution.py:395
  157.4 10.9 %attend.1 = (bf16[2,2,256,256]{3,2,1,0:T(8,128)(2,1)}, f32[2,2,512,1]{3,2,1,0:T(8,128)}) custom-call(s32[8]{0:T(128)} %fusion.106.info_ref, bf16[2,2,256,768]{3,2,1,0:T(8,128)(2,1)} %bitcast.282, bf16[2,2,256,768]{3,2,1,0:T(8,128)(2,1)} %bitcast.283, bf16[2,2,256,768]{3,2,1,0:T(8,128)(2,1)} %bitcast.284, bf16[1024,512]{1,0:T(8,128)(2,1)} %get-tuple-element.185.kc_ref.vc_ref, ...), custom_call_target="tpu_custom_call" | custom-call | flops 146800640 | bytes 125829 | tf_op jit(solution)/shard_map/attend/pallas_call | solution.py:547
  212.8 12.7 %collective-permute-done.16 = bf16[256,1024]{1,0:T(8,128)(2,1)S(1)} collective-permute-done((bf16[256,1024]{1,0:T(8,128)(2,1)S(1)}, bf16[256,1024]{1,0:T(8,128)(2,1)S(1)}, u32[]{:S(2)}, u32[]{:S(2)}) %collective-permute-start.16) | collective-permute-done | bytes 524320 | tf_op jit(solution)/shard_map/ppermute | solution.py:38
  255.5 9.5 %collective-permute-done.19 = bf16[256,1024]{1,0:T(8,128)(2,1)S(1)} collective-permute-done((bf16[256,1024]{1,0:T(8,128)(2,1)S(1)}, bf16[256,1024]{1,0:T(8,128)(2,1)S(1)}, u32[]{:S(2)}, u32[]{:S(2)}) %collective-permute-start.19) | collective-permute-done | bytes 524320 | tf_op jit(solution)/shard_map/ppermute | solution.py:38
  269.7 21.4 %own_list.1 = (s32[8200]{0:T(1024)}, s32[1]{0:T(128)}) custom-call(s32[8192]{0:T(1024)} %get-tuple-element.207.code_ref), custom_call_target="tpu_custom_call" | custom-call | bytes 1258291 | tf_op jit(solution)/shard_map/own_list/pallas_call | solution.py:209
  301.5 9.7 %logits_part.4 = (bf16[512,2048]{1,0:T(8,128)(2,1)}, bf16[512,2048]{1,0:T(8,128)(2,1)}, f32[8,1024]{1,0:T(8,128)}) custom-call(f32[4,8,1024]{2,1,0:T(8,128)} %bitcast.288, f32[4,8,1024]{2,1,0:T(8,128)} %bitcast.289, bf16[512,1024]{1,0:T(8,128)(2,1)} %pad_maximum_fusion.21.pair_ref.refs_8_, bf16[512,1024]{1,0:T(8,128)(2,1)} %collective-permute-done.24.near_ref.refs_9_, ...), custom_call_target="tpu_custom_call" | custom-call | flops 171798688 | bytes 209715 | tf_op jit(solution)/shard_map/logits_part/pallas_call | solution.py:640
  311.2 10.7 %collective-permute-done.22 = bf16[512,1024]{1,0:T(8,128)(2,1)} collective-permute-done((bf16[512,1024]{1,0:T(8,128)(2,1)}, bf16[512,1024]{1,0:T(8,128)(2,1)}, u32[]{:S(2)}, u32[]{:S(2)}) %collective-permute-start.22) | collective-permute-done | bytes 1048608 | tf_op jit(solution)/shard_map/ppermute | solution.py:38
  325.9 10.0 %logits_part.5 = (bf16[512,2048]{1,0:T(8,128)(2,1)}, bf16[512,2048]{1,0:T(8,128)(2,1)}, f32[8,1024]{1,0:T(8,128)}) custom-call(f32[4,8,1024]{2,1,0:T(8,128)} %bitcast.290, f32[4,8,1024]{2,1,0:T(8,128)} %bitcast.291, bf16[512,1024]{1,0:T(8,128)(2,1)} %copy-done.25, bf16[512,1024]{1,0:T(8,128)(2,1)} %copy-done.37, bf16[2048,512]{1,0:T(8,128)(2,1)} %copy-done, ...), custom_call_target="tpu_custom_call" | custom-call | flops 171798688 | bytes 209715 | tf_op jit(solution)/shard_map/logits_part/pallas_call | solution.py:640
  343.7 9.6 %logits_part.6 = (bf16[512,2048]{1,0:T(8,128)(2,1)}, bf16[512,2048]{1,0:T(8,128)(2,1)}, f32[8,1024]{1,0:T(8,128)}) custom-call(f32[4,8,1024]{2,1,0:T(8,128)} %bitcast.292, f32[4,8,1024]{2,1,0:T(8,128)} %bitcast.293, bf16[512,1024]{1,0:T(8,128)(2,1)} %copy-done.14, bf16[512,1024]{1,0:T(8,128)(2,1)} %copy-done.38, bf16[2048,512]{1,0:T(8,128)(2,1)} %copy-done, ...), custom_call_target="tpu_custom_call" | custom-call | flops 171798688 | bytes 209715 | tf_op jit(solution)/shard_map/logits_part/pallas_call | solution.py:640
  359.4 9.6 %logits_part.7 = (bf16[512,2048]{1,0:T(8,128)(2,1)}, bf16[512,2048]{1,0:T(8,128)(2,1)}, f32[8,1024]{1,0:T(8,128)}) custom-call(f32[4,8,1024]{2,1,0:T(8,128)} %bitcast.294, f32[4,8,1024]{2,1,0:T(8,128)} %bitcast.295, bf16[512,1024]{1,0:T(8,128)(2,1)} %copy-done.15, bf16[512,1024]{1,0:T(8,128)(2,1)} %copy-done.39, bf16[2048,512]{1,0:T(8,128)(2,1)} %copy-done, ...), custom_call_target="tpu_custom_call" | custom-call | flops 171798688 | bytes 209715 | tf_op jit(solution)/shard_map/logits_part/pallas_call | solution.py:640
  387.6 9.7 %logits_back.4 = (bf16[512,2048]{1,0:T(8,128)(2,1)}, bf16[512,2048]{1,0:T(8,128)(2,1)}, bf16[512,1024]{1,0:T(8,128)(2,1)}, bf16[512,1024]{1,0:T(8,128)(2,1)}) custom-call(f32[4,8,1024]{2,1,0:T(8,128)} %bitcast.297, f32[4,8,1024]{2,1,0:T(8,128)} %bitcast.298, f32[4,8,1024]{2,1,0:T(8,128)} %broadcast_in_dim.202.pair_factor_ref.near_factor_ref, ...), custom_call_target="tpu_custom_call" | custom-call | flops 171798688 | bytes 251658 | tf_op jit(solution)/shard_map/logits_back/pallas_call | solution.py:701
  403.3 9.5 %logits_back.5 = (bf16[512,2048]{1,0:T(8,128)(2,1)}, bf16[512,2048]{1,0:T(8,128)(2,1)}, bf16[512,1024]{1,0:T(8,128)(2,1)}, bf16[512,1024]{1,0:T(8,128)(2,1)}) custom-call(f32[4,8,1024]{2,1,0:T(8,128)} %bitcast.299, f32[4,8,1024]{2,1,0:T(8,128)} %bitcast.300, f32[4,8,1024]{2,1,0:T(8,128)} %broadcast_in_dim.202.pair_factor_ref.near_factor_ref, ...), custom_call_target="tpu_custom_call" | custom-call | flops 171798688 | bytes 251658 | tf_op jit(solution)/shard_map/logits_back/pallas_call | solution.py:701
  424.2 9.5 %logits_back.6 = (bf16[512,2048]{1,0:T(8,128)(2,1)}, bf16[512,2048]{1,0:T(8,128)(2,1)}, bf16[512,1024]{1,0:T(8,128)(2,1)}, bf16[512,1024]{1,0:T(8,128)(2,1)}) custom-call(f32[4,8,1024]{2,1,0:T(8,128)} %bitcast.301, f32[4,8,1024]{2,1,0:T(8,128)} %bitcast.302, f32[4,8,1024]{2,1,0:T(8,128)} %broadcast_in_dim.202.pair_factor_ref.near_factor_ref, ...), custom_call_target="tpu_custom_call" | custom-call | flops 171798688 | bytes 251658 | tf_op jit(solution)/shard_map/logits_back/pallas_call | solution.py:701
  449.2 9.9 %logits_back.7 = (bf16[512,2048]{1,0:T(8,128)(2,1)}, bf16[512,2048]{1,0:T(8,128)(2,1)}, bf16[512,1024]{1,0:T(8,128)(2,1)}, bf16[512,1024]{1,0:T(8,128)(2,1)}) custom-call(f32[4,8,1024]{2,1,0:T(8,128)} %bitcast.303, f32[4,8,1024]{2,1,0:T(8,128)} %bitcast.304, f32[4,8,1024]{2,1,0:T(8,128)} %broadcast_in_dim.202.pair_factor_ref.near_factor_ref, ...), custom_call_target="tpu_custom_call" | custom-call | flops 171798688 | bytes 251658 | tf_op jit(solution)/shard_map/logits_back/pallas_call | solution.py:701
  459.1 13.5 %collective-permute-done.43 = bf16[512,1024]{1,0:T(8,128)(2,1)} collective-permute-done((bf16[512,1024]{1,0:T(8,128)(2,1)}, bf16[512,1024]{1,0:T(8,128)(2,1)}, u32[]{:S(2)}, u32[]{:S(2)}) %collective-permute-start.43) | collective-permute-done | bytes 1048608 | tf_op jit(solution)/shard_map/ppermute | solution.py:38
  486.2 24.3 %table_grad_part.1 = (f32[2048,512]{1,0:T(8,128)}, bf16[2048,512]{1,0:T(8,128)(2,1)}) custom-call(bf16[512,2048]{1,0:T(8,128)(2,1)} %get-tuple-element.258.refs_0_, bf16[512,2048]{1,0:T(8,128)(2,1)} %get-tuple-element.259.refs_1_, bf16[512,2048]{1,0:T(8,128)(2,1)} %get-tuple-element.260.refs_2_, bf16[512,2048]{1,0:T(8,128)(2,1)} %get-tuple-element.261.refs_3_, ...), custom_call_target="tpu_custom_call" | custom-call | flops 515396064 | bytes 629145 | tf_op jit(solution)/shard_map/table_grad_part/pallas_call | solution.py:748
  513.3 11.7 %collective-permute-done.45 = bf16[256,1024]{1,0:T(8,128)(2,1)S(1)} collective-permute-done((bf16[256,1024]{1,0:T(8,128)(2,1)S(1)}, bf16[256,1024]{1,0:T(8,128)(2,1)S(1)}, u32[]{:S(2)}, u32[]{:S(2)}) %collective-permute-start.45) | collective-permute-done | bytes 524320 | tf_op jit(solution)/shard_map/ppermute | solution.py:38
  549.5 11.5 %hidden_grads.1 = (f32[2048,512]{1,0:T(8,128)}, bf16[2048,512]{1,0:T(8,128)(2,1)}) custom-call(bf16[1024,1024]{1,0:T(8,128)(2,1)} %copy-done.55, bf16[1024,1024]{1,0:T(8,128)(2,1)} %copy-done.54, bf16[1024,1024]{1,0:T(8,128)(2,1)} %pad_maximum_fusion.2.in_ref, bf16[1024,1024]{1,0:T(8,128)(2,1)} %pad_maximum_fusion.5.down_ref), custom_call_target="tpu_custom_call" | custom-call | flops 128849016 | bytes 335544 | tf_op jit(solution)/shard_map/hidden_grads/pallas_call | solution.py:783
  561.1 12.5 %collective-permute-done.49 = bf16[2048,512]{1,0:T(8,128)(2,1)} collective-permute-done((bf16[2048,512]{1,0:T(8,128)(2,1)}, bf16[2048,512]{1,0:T(8,128)(2,1)}, u32[]{:S(2)}, u32[]{:S(2)}) %collective-permute-start.49) | collective-permute-done | bytes 2097184 | tf_op jit(solution)/shard_map/ppermute | solution.py:38
  602.8 15.2 %attend_back.1 = (bf16[2,2,256,768]{3,2,1,0:T(8,128)(2,1)}, bf16[1024,512]{1,0:T(8,128)(2,1)}, bf16[1024,512]{1,0:T(8,128)(2,1)}) custom-call(s32[8]{0:T(128)} %fusion.106.info_ref, bf16[2,2,256,768]{3,2,1,0:T(8,128)(2,1)} %bitcast.285, bf16[2,2,256,768]{3,2,1,0:T(8,128)(2,1)} %bitcast.286, bf16[2,2,256,768]{3,2,1,0:T(8,128)(2,1)} %bitcast.287, ...), custom_call_target="tpu_custom_call" | custom-call | flops 230686720 | bytes 188743 | tf_op jit(solution)/shard_map/attend_back/pallas_call | solution.py:570
  635.4 11.2 %collective-permute-done.50 = bf16[2048,512]{1,0:T(8,128)(2,1)} collective-permute-done((bf16[2048,512]{1,0:T(8,128)(2,1)}, bf16[2048,512]{1,0:T(8,128)(2,1)}, u32[]{:S(2)}, u32[]{:S(2)}) %collective-permute-start.50) | collective-permute-done | bytes 2097184 | tf_op jit(solution)/shard_map/ppermute | solution.py:38
  658.3 14.3 %attn_grads.1 = (f32[1024,512]{1,0:T(8,128)}, bf16[1024,512]{1,0:T(8,128)(2,1)}) custom-call(bf16[1024,768]{1,0:T(8,128)(2,1)} %bitcast.319, bf16[1024,256]{1,0:T(8,128)(2,1)} %bitcast.312, bf16[1024,512]{1,0:T(8,128)(2,1)} %get-tuple-element.285.mem_ref, bf16[3072,512]{1,0:T(8,128)(2,1)} %bitcast.313, bf16[1024,1024]{1,0:T(8,128)(2,1)} %pad_maximum_fusion.1.normed_ref, ...), custom_call_target="tpu_custom_call" | custom-call | flops 188743680 | bytes 503316 | tf_op jit(solution)/shard_map/attn_grads/pallas_call | solution.py:833
  689.0 8.0 all-to-all-done.3
  701.5 13.6 %collective-permute-done.57 = bf16[1120,512]{1,0:T(8,128)(2,1)} collective-permute-done((bf16[1120,512]{1,0:T(8,128)(2,1)}, bf16[1120,512]{1,0:T(8,128)(2,1)}, u32[]{:S(2)}, u32[]{:S(2)}) %collective-permute-start.57) | collective-permute-done | bytes 1146912 | tf_op jit(solution)/shard_map/ppermute | solution.py:38
  727.4 14.6 %scatter.1 = f32[8000,128]{1,0:T(8,128)} custom-call(s32[1]{0:T(128)} %get-tuple-element.297.count_ref, s32[8200]{0:T(1024)} %get-tuple-element.298.code_ref, f32[8000,128]{1,0:T(8,128)} %bitcast_convert_fusion.base_ref, bf16[8192,128]{1,0:T(8,128)(2,1)} %bitcast.307), custom_call_target="tpu_custom_call" | custom-call | bytes 629145 | tf_op jit(solution)/shard_map/scatter/pallas_call | solution.py:305
  748.9 11.3 %collective-permute-done.61 = bf16[1120,128]{1,0:T(8,128)(2,1)S(1)} collective-permute-done((bf16[1120,128]{1,0:T(8,128)(2,1)S(1)}, bf16[1120,128]{1,0:T(8,128)(2,1)S(1)}, u32[]{:S(2)}, u32[]{:S(2)}) %collective-permute-start.61) | collective-permute-done | bytes 286752 | tf_op jit(solution)/shard_map/ppermute | solution.py:38
  791.2 7.2 multiply_reduce_fusion
  835.1 7.8 divide_subtract_fusion
  (740 shorter events, 444.8 us)
Async XLA Ops:
  18.3 30.5 %collective-permute-start.3 = (bf16[1120,128]{1,0:T(8,128)(2,1)}, bf16[1120,128]{1,0:T(8,128)(2,1)}, u32[]{:S(2)}, u32[]{:S(2)}) collective-permute-start(bf16[1120,128]{1,0:T(8,128)(2,1)} %pad_maximum_fusion.29), channel_id=1, source_target_pairs={{0,16},{4,20},{8,24},{12,28},{16,0},{20,4},{24,8},{28,12},{1,17},{... | collective-permute-start | bytes 860168 | tf_op jit(solution)/shard_map/ppermute | solution.py:38
  51.7 29.0 %collective-permute-start.5 = (bf16[1120,256]{1,0:T(8,128)(2,1)}, bf16[1120,256]{1,0:T(8,128)(2,1)}, u32[]{:S(2)}, u32[]{:S(2)}) collective-permute-start(bf16[1120,256]{1,0:T(8,128)(2,1)} %pad_maximum_fusion.27), channel_id=1, source_target_pairs={{0,8},{4,12},{8,0},{12,4},{16,24},{20,28},{24,16},{28,20},{1,9},{5... | collective-permute-start | bytes 1720328 | tf_op jit(solution)/shard_map/ppermute | solution.py:38
  53.7 26.2 %collective-permute-start.7 = (bf16[2048,128]{1,0:T(8,128)(2,1)S(1)}, bf16[2048,128]{1,0:T(8,128)(2,1)S(1)}, u32[]{:S(2)}, u32[]{:S(2)}) collective-permute-start(bf16[2048,128]{1,0:T(8,128)(2,1)S(1)} %pad_maximum_fusion.28), channel_id=1, source_target_pairs={{0,16},{4,20},{8,24},{12,28},{16,0},{20,4},{24,8},{28,12},{1,17},{... | collective-permute-start | bytes 1572872 | tf_op jit(solution)/shard_map/ppermute | solution.py:38
  56.8 23.9 %collective-permute-start.6 = (bf16[2048,128]{1,0:T(8,128)(2,1)}, bf16[2048,128]{1,0:T(8,128)(2,1)}, u32[]{:S(2)}, u32[]{:S(2)}) collective-permute-start(bf16[2048,128]{1,0:T(8,128)(2,1)} %slice.662), channel_id=1, source_target_pairs={{0,2},{1,3},{2,0},{3,1},{4,6},{5,7},{6,4},{7,5},{8,10},{9,11},{10,... | collective-permute-start | bytes 1572872 | tf_op jit(solution)/shard_map/ppermute | solution.py:38
  83.3 37.7 %collective-permute-start.10 = (bf16[1120,512]{1,0:T(8,128)(2,1)}, bf16[1120,512]{1,0:T(8,128)(2,1)}, u32[]{:S(2)}, u32[]{:S(2)}) collective-permute-start(bf16[1120,512]{1,0:T(8,128)(2,1)} %pad_maximum_fusion.16), channel_id=1, source_target_pairs={{0,4},{4,0},{8,12},{12,8},{16,20},{20,16},{24,28},{28,24},{1,5},{5... | collective-permute-start | bytes 3440648 | tf_op jit(solution)/shard_map/ppermute | solution.py:38
  86.8 27.5 %all-to-all-start = ((bf16[8,256,128]{2,1,0:T(8,128)(2,1)}), bf16[8,256,128]{2,1,0:T(8,128)(2,1)}, u32[]{:S(2)}, u32[]{:S(2)}) async-start(bf16[8,256,128]{2,1,0:T(8,128)(2,1)} %bitcast.314), calls=%async_computation | async-start | bytes 1048576 | tf_op jit(solution)/shard_map/all_to_all | solution.py:1006
  93.3 50.4 %collective-permute-start.11 = (bf16[2048,256]{1,0:T(8,128)(2,1)}, bf16[2048,256]{1,0:T(8,128)(2,1)}, u32[]{:S(2)}, u32[]{:S(2)}) collective-permute-start(bf16[2048,256]{1,0:T(8,128)(2,1)} %pad_maximum_fusion.19), channel_id=1, source_target_pairs={{0,8},{4,12},{8,0},{12,4},{16,24},{20,28},{24,16},{28,20},{1,9},{5... | collective-permute-start | bytes 3145736 | tf_op jit(solution)/shard_map/ppermute | solution.py:38
  130.7 22.5 %collective-permute-start.9 = (bf16[512,1024]{1,0:T(8,128)(2,1)}, bf16[512,1024]{1,0:T(8,128)(2,1)}, u32[]{:S(2)}, u32[]{:S(2)}) collective-permute-start(bf16[512,1024]{1,0:T(8,128)(2,1)} %pad_maximum_fusion.18), channel_id=1, source_target_pairs={{0,1},{1,0},{2,3},{3,2},{4,5},{5,4},{6,7},{7,6},{8,9},{9,8},{10,11... | collective-permute-start | bytes 3145736 | tf_op jit(solution)/shard_map/ppermute | solution.py:38
  149.4 35.9 %collective-permute-start.13 = (bf16[1024,512]{1,0:T(8,128)(2,1)}, bf16[1024,512]{1,0:T(8,128)(2,1)}, u32[]{:S(2)}, u32[]{:S(2)}) collective-permute-start(bf16[1024,512]{1,0:T(8,128)(2,1)} %get-tuple-element.432), channel_id=1, source_target_pairs={{0,4},{4,0},{8,12},{12,8},{16,20},{20,16},{24,28},{28,24},{1,5},{5... | collective-permute-start | bytes 3145736 | tf_op jit(solution)/shard_map/ppermute | solution.py:38
  175.1 34.5 %collective-permute-start.15 = (bf16[1024,512]{1,0:T(8,128)(2,1)}, bf16[1024,512]{1,0:T(8,128)(2,1)}, u32[]{:S(2)}, u32[]{:S(2)}) collective-permute-start(bf16[1024,512]{1,0:T(8,128)(2,1)} %get-tuple-element.431), channel_id=1, source_target_pairs={{0,4},{4,0},{8,12},{12,8},{16,20},{20,16},{24,28},{28,24},{1,5},{5... | collective-permute-start | bytes 3145736 | tf_op jit(solution)/shard_map/ppermute | solution.py:38
  175.7 53.1 %all-to-all-start.1 = ((bf16[4,2000,128]{2,1,0:T(8,128)(2,1)}), bf16[4,2000,128]{2,1,0:T(8,128)(2,1)S(1)}, u32[]{:S(2)}, u32[]{:S(2)}) async-start(bf16[4,2000,128]{2,1,0:T(8,128)(2,1)} %bitcast.308), calls=%async_computation.1 | async-start | bytes 4096000 | tf_op jit(solution)/shard_map/all_to_all | solution.py:1079
  188.9 20.8 %collective-permute-start.14 = (bf16[256,1024]{1,0:T(8,128)(2,1)S(1)}, bf16[256,1024]{1,0:T(8,128)(2,1)}, u32[]{:S(2)}, u32[]{:S(2)}) collective-permute-start(bf16[256,1024]{1,0:T(8,128)(2,1)S(1)} %slice.1037), channel_id=1, source_target_pairs={{0,2},{1,3},{2,0},{3,1},{4,6},{5,7},{6,4},{7,5},{8,10},{9,11},{10,... | collective-permute-start | bytes 1572872 | tf_op jit(solution)/shard_map/ppermute | solution.py:38
  253.9 47.6 %collective-permute-start.25 = (bf16[2048,512]{1,0:T(8,128)(2,1)S(1)}, bf16[2048,512]{1,0:T(8,128)(2,1)}, u32[]{:S(2)}, u32[]{:S(2)}) collective-permute-start(bf16[2048,512]{1,0:T(8,128)(2,1)S(1)} %fusion.13.left_ref), channel_id=1, source_target_pairs={{0,4},{4,0},{8,12},{12,8},{16,20},{20,16},{24,28},{28,24},{1,5},{5... | collective-permute-start | bytes 6291464 | tf_op jit(solution)/shard_map/ppermute | solution.py:38
  266.3 24.9 %collective-permute-start.23 = (bf16[256,1024]{1,0:T(8,128)(2,1)}, bf16[256,1024]{1,0:T(8,128)(2,1)}, u32[]{:S(2)}, u32[]{:S(2)}) collective-permute-start(bf16[256,1024]{1,0:T(8,128)(2,1)} %multiply_convert_fusion.1.refs_0_), channel_id=1, source_target_pairs={{0,2},{1,3},{2,0},{3,1},{4,6},{5,7},{6,4},{7,5},{8,10},{9,11},{10,... | collective-permute-start | bytes 1572872 | tf_op jit(solution)/shard_map/ppermute | solution.py:38
  269.7 24.2 %collective-permute-start.20 = (bf16[256,1024]{1,0:T(8,128)(2,1)}, bf16[256,1024]{1,0:T(8,128)(2,1)}, u32[]{:S(2)}, u32[]{:S(2)}) collective-permute-start(bf16[256,1024]{1,0:T(8,128)(2,1)} %reorder.4), channel_id=1, source_target_pairs={{0,16},{4,20},{8,24},{12,28},{16,0},{20,4},{24,8},{28,12},{1,17},{... | collective-permute-start | bytes 1572872 | tf_op jit(solution)/shard_map/ppermute | solution.py:38
  296.2 25.6 %collective-permute-start.22 = (bf16[512,1024]{1,0:T(8,128)(2,1)}, bf16[512,1024]{1,0:T(8,128)(2,1)}, u32[]{:S(2)}, u32[]{:S(2)}) collective-permute-start(bf16[512,1024]{1,0:T(8,128)(2,1)} %reorder.5), channel_id=1, source_target_pairs={{0,8},{4,12},{8,0},{12,4},{16,24},{20,28},{24,16},{28,20},{1,9},{5... | collective-permute-start | bytes 3145736 | tf_op jit(solution)/shard_map/ppermute | solution.py:38
  297.7 24.1 %collective-permute-start.21 = (bf16[256,1024]{1,0:T(8,128)(2,1)}, bf16[256,1024]{1,0:T(8,128)(2,1)S(1)}, u32[]{:S(2)}, u32[]{:S(2)}) collective-permute-start(bf16[256,1024]{1,0:T(8,128)(2,1)} %collective-permute-done.20.refs_1_), channel_id=1, source_target_pairs={{0,2},{1,3},{2,0},{3,1},{4,6},{5,7},{6,4},{7,5},{8,10},{9,11},{10,... | collective-permute-start | bytes 1572872 | tf_op jit(solution)/shard_map/ppermute | solution.py:38
  447.4 25.2 %collective-permute-start.43 = (bf16[512,1024]{1,0:T(8,128)(2,1)}, bf16[512,1024]{1,0:T(8,128)(2,1)}, u32[]{:S(2)}, u32[]{:S(2)}) collective-permute-start(bf16[512,1024]{1,0:T(8,128)(2,1)} %reorder.6), channel_id=1, source_target_pairs={{0,8},{4,12},{8,0},{12,4},{16,24},{20,28},{24,16},{28,20},{1,9},{5... | collective-permute-start | bytes 3145736 | tf_op jit(solution)/shard_map/ppermute | solution.py:38
  459.1 22.6 %collective-permute-start.41 = (bf16[512,1024]{1,0:T(8,128)(2,1)}, bf16[512,1024]{1,0:T(8,128)(2,1)}, u32[]{:S(2)}, u32[]{:S(2)}) collective-permute-start(bf16[512,1024]{1,0:T(8,128)(2,1)} %get-tuple-element.251), channel_id=1, source_target_pairs={{0,1},{1,0},{2,3},{3,2},{4,5},{5,4},{6,7},{7,6},{8,9},{9,8},{10,11... | collective-permute-start | bytes 3145736 | tf_op jit(solution)/shard_map/ppermute | solution.py:38
  479.0 31.6 %collective-permute-start.44 = (bf16[256,1024]{1,0:T(8,128)(2,1)}, bf16[256,1024]{1,0:T(8,128)(2,1)S(1)}, u32[]{:S(2)}, u32[]{:S(2)}) collective-permute-start(bf16[256,1024]{1,0:T(8,128)(2,1)} %reorder.7), channel_id=1, source_target_pairs={{0,16},{4,20},{8,24},{12,28},{16,0},{20,4},{24,8},{28,12},{1,17},{... | collective-permute-start | bytes 1572872 | tf_op jit(solution)/shard_map/ppermute | solution.py:38
  484.7 25.9 %collective-permute-start.42 = (bf16[256,1024]{1,0:T(8,128)(2,1)S(1)}, bf16[256,1024]{1,0:T(8,128)(2,1)S(1)}, u32[]{:S(2)}, u32[]{:S(2)}) collective-permute-start(bf16[256,1024]{1,0:T(8,128)(2,1)S(1)} %slice.1032), channel_id=1, source_target_pairs={{0,2},{1,3},{2,0},{3,1},{4,6},{5,7},{6,4},{7,5},{8,10},{9,11},{10,... | collective-permute-start | bytes 1572872 | tf_op jit(solution)/shard_map/ppermute | solution.py:38
  525.2 48.4 %collective-permute-start.49 = (bf16[2048,512]{1,0:T(8,128)(2,1)}, bf16[2048,512]{1,0:T(8,128)(2,1)}, u32[]{:S(2)}, u32[]{:S(2)}) collective-permute-start(bf16[2048,512]{1,0:T(8,128)(2,1)} %get-tuple-element.271), channel_id=1, source_target_pairs={{0,4},{4,0},{8,12},{12,8},{16,20},{20,16},{24,28},{28,24},{1,5},{5... | collective-permute-start | bytes 6291464 | tf_op jit(solution)/shard_map/ppermute | solution.py:38
  544.5 29.1 %collective-permute-start.48 = (bf16[256,1024]{1,0:T(8,128)(2,1)}, bf16[256,1024]{1,0:T(8,128)(2,1)}, u32[]{:S(2)}, u32[]{:S(2)}) collective-permute-start(bf16[256,1024]{1,0:T(8,128)(2,1)} %slice.1031), channel_id=1, source_target_pairs={{0,2},{1,3},{2,0},{3,1},{4,6},{5,7},{6,4},{7,5},{8,10},{9,11},{10,... | collective-permute-start | bytes 1572872 | tf_op jit(solution)/shard_map/ppermute | solution.py:38
  583.4 63.2 %all-to-all-start.2 = ((bf16[4,2000,128]{2,1,0:T(8,128)(2,1)}), bf16[4,2000,128]{2,1,0:T(8,128)(2,1)}, u32[]{:S(2)}, u32[]{:S(2)}) async-start(bf16[4,2000,128]{2,1,0:T(8,128)(2,1)} %pad_maximum_fusion.9), calls=%async_computation.2 | async-start | bytes 4096000 | tf_op jit(solution)/shard_map/all_to_all | solution.py:1201
  598.3 48.4 %collective-permute-start.50 = (bf16[2048,512]{1,0:T(8,128)(2,1)}, bf16[2048,512]{1,0:T(8,128)(2,1)}, u32[]{:S(2)}, u32[]{:S(2)}) collective-permute-start(bf16[2048,512]{1,0:T(8,128)(2,1)} %get-tuple-element.273), channel_id=1, source_target_pairs={{0,4},{4,0},{8,12},{12,8},{16,20},{20,16},{24,28},{28,24},{1,5},{5... | collective-permute-start | bytes 6291464 | tf_op jit(solution)/shard_map/ppermute | solution.py:38
  623.4 23.3 %collective-permute-start.53 = (bf16[512,1024]{1,0:T(8,128)(2,1)S(1)}, bf16[512,1024]{1,0:T(8,128)(2,1)S(1)}, u32[]{:S(2)}, u32[]{:S(2)}) collective-permute-start(bf16[512,1024]{1,0:T(8,128)(2,1)S(1)} %slice.1024), channel_id=1, source_target_pairs={{0,1},{1,0},{2,3},{3,2},{4,5},{5,4},{6,7},{7,6},{8,9},{9,8},{10,11... | collective-permute-start | bytes 3145736 | tf_op jit(solution)/shard_map/ppermute | solution.py:38
  655.3 33.7 %collective-permute-start.54 = (bf16[2048,256]{1,0:T(8,128)(2,1)}, bf16[2048,256]{1,0:T(8,128)(2,1)}, u32[]{:S(2)}, u32[]{:S(2)}) collective-permute-start(bf16[2048,256]{1,0:T(8,128)(2,1)} %slice.1023), channel_id=1, source_target_pairs={{0,8},{4,12},{8,0},{12,4},{16,24},{20,28},{24,16},{28,20},{1,9},{5... | collective-permute-start | bytes 3145736 | tf_op jit(solution)/shard_map/ppermute | solution.py:38
  655.6 19.7 %collective-permute-start.55 = (bf16[256,1024]{1,0:T(8,128)(2,1)S(1)}, bf16[256,1024]{1,0:T(8,128)(2,1)S(1)}, u32[]{:S(2)}, u32[]{:S(2)}) collective-permute-start(bf16[256,1024]{1,0:T(8,128)(2,1)S(1)} %slice.1030), channel_id=1, source_target_pairs={{0,2},{1,3},{2,0},{3,1},{4,6},{5,7},{6,4},{7,5},{8,10},{9,11},{10,... | collective-permute-start | bytes 1572872 | tf_op jit(solution)/shard_map/ppermute | solution.py:38
  683.2 32.0 %collective-permute-start.57 = (bf16[1120,512]{1,0:T(8,128)(2,1)}, bf16[1120,512]{1,0:T(8,128)(2,1)}, u32[]{:S(2)}, u32[]{:S(2)}) collective-permute-start(bf16[1120,512]{1,0:T(8,128)(2,1)} %pad_maximum_fusion.17), channel_id=1, source_target_pairs={{0,4},{4,0},{8,12},{12,8},{16,20},{20,16},{24,28},{28,24},{1,5},{5... | collective-permute-start | bytes 3440648 | tf_op jit(solution)/shard_map/ppermute | solution.py:38
  697.1 18.1 %collective-permute-start.58 = (bf16[8,256,128]{2,1,0:T(8,128)(2,1)S(1)}, bf16[8,256,128]{2,1,0:T(8,128)(2,1)S(1)}, u32[]{:S(2)}, u32[]{:S(2)}) collective-permute-start(bf16[8,256,128]{2,1,0:T(8,128)(2,1)S(1)} %all-to-all-done.3), channel_id=1, source_target_pairs={{0,2},{1,3},{2,0},{3,1},{4,6},{5,7},{6,4},{7,5},{8,10},{9,11},{10,... | collective-permute-start | bytes 1572872 | tf_op jit(solution)/shard_map/ppermute | solution.py:38
  700.7 23.3 %collective-permute-start.56 = (bf16[2048,128]{1,0:T(8,128)(2,1)S(1)}, bf16[2048,128]{1,0:T(8,128)(2,1)S(1)}, u32[]{:S(2)}, u32[]{:S(2)}) collective-permute-start(bf16[2048,128]{1,0:T(8,128)(2,1)S(1)} %slice.1029), channel_id=1, source_target_pairs={{0,16},{4,20},{8,24},{12,28},{16,0},{20,4},{24,8},{28,12},{1,17},{... | collective-permute-start | bytes 1572872 | tf_op jit(solution)/shard_map/ppermute | solution.py:38
  718.0 24.1 %collective-permute-start.59 = (bf16[1120,256]{1,0:T(8,128)(2,1)}, bf16[1120,256]{1,0:T(8,128)(2,1)}, u32[]{:S(2)}, u32[]{:S(2)}) collective-permute-start(bf16[1120,256]{1,0:T(8,128)(2,1)} %slice.1028), channel_id=1, source_target_pairs={{0,8},{4,12},{8,0},{12,4},{16,24},{20,28},{24,16},{28,20},{1,9},{5... | collective-permute-start | bytes 1720328 | tf_op jit(solution)/shard_map/ppermute | solution.py:38
  (189 other events, 1895.5 us)

commit v13 on v12

--- a/solution.py
+++ b/solution.py
@@ -1082,7 +1082,7 @@
     attn_sum, (far_up,) = core_sum(
         *split(mm(mixed, own_one[3 * wide : 4 * wide]), 0, 2), (far_up,)
     )
-    attn_sum, (early, far_down) = stream_sum(attn_sum, (early_sums(mixed), far_down))
+    attn_sum, (far_down,) = stream_sum(attn_sum, (far_down,))
     after_attn = embedded + attn_sum
     ffn_in, inv_second = rms(after_attn, gain_vals[1])
     ffn_in, (low_table,) = group_both(ffn_in, (low_table,))
@@ -1180,7 +1180,7 @@
 
     grad_after_ffn = rms_back(after_ffn, inv_third, gain_vals[2], final_grad)
     moved_table = swap(table_parts[1], "dp", 1)
-    down_in = group_both(grad_after_ffn.astype(lowp))
+    down_in, (early,) = group_both(grad_after_ffn.astype(lowp), (early_sums(final_grad),))
     down_in = jnp.concatenate(down_in)
     act_grad = mm(down_in, full_down, NT)
     pre_grad = jax.vjp(jax.nn.gelu, hidden_pre)[1](act_grad)[0].astype(lowp)

time: 853 us -> 861 us (level)
  waiting for transfers between devices: 209 us -> 218 us
    unnamed x316 -> x332, local copies, waits for them, and re-layouts: 34 us -> 31.6 us
  transfers between devices with their start and end apart: 74 -> 74, of which waited for: 43 -> 43; matrix products, arithmetic and copies ran while one was open for 20% -> 19% of each run, Pallas kernels for 28% -> 28%
where the time goes in v13:
time: 861 us; the launch traced here: 852 us
  Pallas kernels  256 us (30%)
  waiting for transfers between devices  218 us (25%)
  other arithmetic  155 us (18%)
  starting transfers between devices  80.4 us (9%)
  local copies, waits for them, and re-layouts  74.1 us (9%)
  matrix products  35.5 us (4%)
  between operations  26.3 us (3%)
    ppermute x70, waiting for transfers between devices, swap(): return lax.ppermute(value, axis, [(i, i ^ mask) for i in range(size)])  186 us
    ppermute x70, starting transfers between devices, swap(): return lax.ppermute(value, axis, [(i, i ^ mask) for i in range(size)])  61.1 us
    pallas_call x4, Pallas kernels, logits_part(): pl.pallas_call(functools.partial(logits_kernel, words), name='logits_part...  39 us
    pallas_call x4, Pallas kernels, logits_back(): pl.pallas_call(logits_back_kernel, name='logits_back', grid=(tiles,), out...  38.5 us
    dot_general x11, matrix products, mm(): return lax.dot_general(left, right, dims, preferred_element_type=single)  35.5 us
    unnamed x332, local copies, waits for them, and re-layouts  31.6 us
    pallas_call x1, Pallas kernels, table_grad_part(): pl.pallas_call(functools.partial(table_grad_kernel, len(grads)), name='ta...  24.3 us
    pallas_call x1, Pallas kernels, own_list(): pl.pallas_call(list_kernel, name='own_list', out_shape=(jax.ShapeDtypeStr...  21.4 us
  transfers between devices with their start and end apart: 74, of which 43 were waited for; matrix products, arithmetic and copies ran while one was open for 19% of the time, Pallas kernels for 28%

profile of v13, /device:TPU:0, one launch (start us, length us, event | category | flops | bytes accessed | tf_op | source)
XLA Modules:
  0.0 852.4 jit_solution(5455005737127828614)
XLA Ops:
  31.8 8.6 %lookup.2 = bf16[4096,128]{1,0:T(8,128)(2,1)} custom-call(s32[4096]{0:T(1024)} %get-tuple-element.495.row_ref, f32[8000,128]{1,0:T(8,128)} %table_ref.3), custom_call_target="tpu_custom_call" | custom-call | bytes 629145 | tf_op jit(solution)/shard_map/lookup/pallas_call | solution.py:178
  40.5 8.8 %lookup.3 = bf16[4096,128]{1,0:T(8,128)(2,1)} custom-call(s32[4096]{0:T(1024)} %get-tuple-element.494.row_ref, f32[8000,128]{1,0:T(8,128)} %table_ref.3), custom_call_target="tpu_custom_call" | custom-call | bytes 629145 | tf_op jit(solution)/shard_map/lookup/pallas_call | solution.py:178
  65.2 10.1 %state_norm.3.old_ref = bf16[3,1024,1024]{2,1,0:T(8,128)(2,1)} custom-call(s32[2]{0:T(128)} %pad_add_fusion.place_ref, f32[1,1024]{1,0:T(1,128)} %bitcast.346, bf16[2,1536,1024]{2,1,0:T(8,128)(2,1)} %in_ref.3), custom_call_target="tpu_custom_call" | custom-call | bytes 251658 | tf_op jit(solution)/shard_map/state_norm/pallas_call | solution.py:353
  96.4 17.0 %all-to-all-done.in_ref = bf16[8,256,128]{2,1,0:T(8,128)(2,1)S(1)} async-done(((bf16[8,256,128]{2,1,0:T(8,128)(2,1)}), bf16[8,256,128]{2,1,0:T(8,128)(2,1)S(1)}, u32[]{:S(2)}, u32[]{:S(2)}) %all-to-all-start) | async-done | bytes 524320 | tf_op jit(solution)/shard_map/all_to_all | solution.py:1006
  129.5 12.1 %compress.1 = (bf16[1024,512]{1,0:T(8,128)(2,1)}, bf16[3,1024,512]{2,1,0:T(8,128)(2,1)}) custom-call(bf16[3,1024,1024]{2,1,0:T(8,128)(2,1)} %state_norm.3.old_ref, bf16[1120,1024]{1,0:T(8,128)(2,1)} %copy-done.8, bf16[1120,1024]{1,0:T(8,128)(2,1)} %copy-done.8, bf16[2,384,128]{2,1,0:T(8,128)(2,1)} %bitcast.315), custom_call_target="tpu_custom_call" | custom-call | flops 64424508 | bytes 251658 | tf_op jit(solution)/shard_map/compress/pallas_call | solution.py:395
  154.2 10.9 %attend.1 = (bf16[2,2,256,256]{3,2,1,0:T(8,128)(2,1)}, f32[2,2,512,1]{3,2,1,0:T(8,128)}) custom-call(s32[8]{0:T(128)} %fusion.105.info_ref, bf16[2,2,256,768]{3,2,1,0:T(8,128)(2,1)} %bitcast.282, bf16[2,2,256,768]{3,2,1,0:T(8,128)(2,1)} %bitcast.283, bf16[2,2,256,768]{3,2,1,0:T(8,128)(2,1)} %bitcast.284, bf16[1024,512]{1,0:T(8,128)(2,1)} %get-tuple-element.186.kc_ref.vc_ref, ...), custom_call_target="tpu_custom_call" | custom-call | flops 146800640 | bytes 125829 | tf_op jit(solution)/shard_map/attend/pallas_call | solution.py:547
  183.8 20.2 %collective-permute-done.15 = bf16[1024,512]{1,0:T(8,128)(2,1)S(1)} collective-permute-done((bf16[1024,512]{1,0:T(8,128)(2,1)}, bf16[1024,512]{1,0:T(8,128)(2,1)S(1)}, u32[]{:S(2)}, u32[]{:S(2)}) %collective-permute-start.15) | collective-permute-done | bytes 1048608 | tf_op jit(solution)/shard_map/ppermute | solution.py:38
  207.1 11.5 %collective-permute-done.16 = bf16[256,1024]{1,0:T(8,128)(2,1)S(1)} collective-permute-done((bf16[256,1024]{1,0:T(8,128)(2,1)S(1)}, bf16[256,1024]{1,0:T(8,128)(2,1)S(1)}, u32[]{:S(2)}, u32[]{:S(2)}) %collective-permute-start.16) | collective-permute-done | bytes 524320 | tf_op jit(solution)/shard_map/ppermute | solution.py:38
  218.6 7.6 all-to-all-done.1
  250.7 9.5 %collective-permute-done.19 = bf16[256,1024]{1,0:T(8,128)(2,1)S(1)} collective-permute-done((bf16[256,1024]{1,0:T(8,128)(2,1)S(1)}, bf16[256,1024]{1,0:T(8,128)(2,1)S(1)}, u32[]{:S(2)}, u32[]{:S(2)}) %collective-permute-start.19) | collective-permute-done | bytes 524320 | tf_op jit(solution)/shard_map/ppermute | solution.py:38
  264.9 21.4 %own_list.1 = (s32[8200]{0:T(1024)}, s32[1]{0:T(128)}) custom-call(s32[8192]{0:T(1024)} %get-tuple-element.195.code_ref), custom_call_target="tpu_custom_call" | custom-call | bytes 1258291 | tf_op jit(solution)/shard_map/own_list/pallas_call | solution.py:209
  296.7 9.7 %logits_part.4 = (bf16[512,2048]{1,0:T(8,128)(2,1)}, bf16[512,2048]{1,0:T(8,128)(2,1)}, f32[8,1024]{1,0:T(8,128)}) custom-call(f32[4,8,1024]{2,1,0:T(8,128)} %bitcast.288, f32[4,8,1024]{2,1,0:T(8,128)} %bitcast.289, bf16[512,1024]{1,0:T(8,128)(2,1)} %pad_maximum_fusion.21.pair_ref.refs_8_, bf16[512,1024]{1,0:T(8,128)(2,1)} %collective-permute-done.24.near_ref.refs_9_, ...), custom_call_target="tpu_custom_call" | custom-call | flops 171798688 | bytes 209715 | tf_op jit(solution)/shard_map/logits_part/pallas_call | solution.py:640
  306.4 10.6 %collective-permute-done.22 = bf16[512,1024]{1,0:T(8,128)(2,1)} collective-permute-done((bf16[512,1024]{1,0:T(8,128)(2,1)}, bf16[512,1024]{1,0:T(8,128)(2,1)}, u32[]{:S(2)}, u32[]{:S(2)}) %collective-permute-start.22) | collective-permute-done | bytes 1048608 | tf_op jit(solution)/shard_map/ppermute | solution.py:38
  321.1 10.0 %logits_part.5 = (bf16[512,2048]{1,0:T(8,128)(2,1)}, bf16[512,2048]{1,0:T(8,128)(2,1)}, f32[8,1024]{1,0:T(8,128)}) custom-call(f32[4,8,1024]{2,1,0:T(8,128)} %bitcast.290, f32[4,8,1024]{2,1,0:T(8,128)} %bitcast.291, bf16[512,1024]{1,0:T(8,128)(2,1)} %copy-done.25, bf16[512,1024]{1,0:T(8,128)(2,1)} %copy-done.36, bf16[2048,512]{1,0:T(8,128)(2,1)} %copy-done, ...), custom_call_target="tpu_custom_call" | custom-call | flops 171798688 | bytes 209715 | tf_op jit(solution)/shard_map/logits_part/pallas_call | solution.py:640
  338.9 9.6 %logits_part.6 = (bf16[512,2048]{1,0:T(8,128)(2,1)}, bf16[512,2048]{1,0:T(8,128)(2,1)}, f32[8,1024]{1,0:T(8,128)}) custom-call(f32[4,8,1024]{2,1,0:T(8,128)} %bitcast.292, f32[4,8,1024]{2,1,0:T(8,128)} %bitcast.293, bf16[512,1024]{1,0:T(8,128)(2,1)} %copy-done.14, bf16[512,1024]{1,0:T(8,128)(2,1)} %copy-done.37, bf16[2048,512]{1,0:T(8,128)(2,1)} %copy-done, ...), custom_call_target="tpu_custom_call" | custom-call | flops 171798688 | bytes 209715 | tf_op jit(solution)/shard_map/logits_part/pallas_call | solution.py:640
  354.5 9.6 %logits_part.7 = (bf16[512,2048]{1,0:T(8,128)(2,1)}, bf16[512,2048]{1,0:T(8,128)(2,1)}, f32[8,1024]{1,0:T(8,128)}) custom-call(f32[4,8,1024]{2,1,0:T(8,128)} %bitcast.294, f32[4,8,1024]{2,1,0:T(8,128)} %bitcast.295, bf16[512,1024]{1,0:T(8,128)(2,1)} %copy-done.15, bf16[512,1024]{1,0:T(8,128)(2,1)} %copy-done.38, bf16[2048,512]{1,0:T(8,128)(2,1)} %copy-done, ...), custom_call_target="tpu_custom_call" | custom-call | flops 171798688 | bytes 209715 | tf_op jit(solution)/shard_map/logits_part/pallas_call | solution.py:640
  382.8 9.7 %logits_back.4 = (bf16[512,2048]{1,0:T(8,128)(2,1)}, bf16[512,2048]{1,0:T(8,128)(2,1)}, bf16[512,1024]{1,0:T(8,128)(2,1)}, bf16[512,1024]{1,0:T(8,128)(2,1)}) custom-call(f32[4,8,1024]{2,1,0:T(8,128)} %bitcast.297, f32[4,8,1024]{2,1,0:T(8,128)} %bitcast.298, f32[4,8,1024]{2,1,0:T(8,128)} %broadcast_in_dim.187.pair_factor_ref.near_factor_ref, ...), custom_call_target="tpu_custom_call" | custom-call | flops 171798688 | bytes 251658 | tf_op jit(solution)/shard_map/logits_back/pallas_call | solution.py:701
  398.5 9.5 %logits_back.5 = (bf16[512,2048]{1,0:T(8,128)(2,1)}, bf16[512,2048]{1,0:T(8,128)(2,1)}, bf16[512,1024]{1,0:T(8,128)(2,1)}, bf16[512,1024]{1,0:T(8,128)(2,1)}) custom-call(f32[4,8,1024]{2,1,0:T(8,128)} %bitcast.299, f32[4,8,1024]{2,1,0:T(8,128)} %bitcast.300, f32[4,8,1024]{2,1,0:T(8,128)} %broadcast_in_dim.187.pair_factor_ref.near_factor_ref, ...), custom_call_target="tpu_custom_call" | custom-call | flops 171798688 | bytes 251658 | tf_op jit(solution)/shard_map/logits_back/pallas_call | solution.py:701
  419.4 9.5 %logits_back.6 = (bf16[512,2048]{1,0:T(8,128)(2,1)}, bf16[512,2048]{1,0:T(8,128)(2,1)}, bf16[512,1024]{1,0:T(8,128)(2,1)}, bf16[512,1024]{1,0:T(8,128)(2,1)}) custom-call(f32[4,8,1024]{2,1,0:T(8,128)} %bitcast.301, f32[4,8,1024]{2,1,0:T(8,128)} %bitcast.302, f32[4,8,1024]{2,1,0:T(8,128)} %broadcast_in_dim.187.pair_factor_ref.near_factor_ref, ...), custom_call_target="tpu_custom_call" | custom-call | flops 171798688 | bytes 251658 | tf_op jit(solution)/shard_map/logits_back/pallas_call | solution.py:701
  444.4 9.9 %logits_back.7 = (bf16[512,2048]{1,0:T(8,128)(2,1)}, bf16[512,2048]{1,0:T(8,128)(2,1)}, bf16[512,1024]{1,0:T(8,128)(2,1)}, bf16[512,1024]{1,0:T(8,128)(2,1)}) custom-call(f32[4,8,1024]{2,1,0:T(8,128)} %bitcast.303, f32[4,8,1024]{2,1,0:T(8,128)} %bitcast.304, f32[4,8,1024]{2,1,0:T(8,128)} %broadcast_in_dim.187.pair_factor_ref.near_factor_ref, ...), custom_call_target="tpu_custom_call" | custom-call | flops 171798688 | bytes 251658 | tf_op jit(solution)/shard_map/logits_back/pallas_call | solution.py:701
  454.3 13.5 %collective-permute-done.43 = bf16[512,1024]{1,0:T(8,128)(2,1)} collective-permute-done((bf16[512,1024]{1,0:T(8,128)(2,1)}, bf16[512,1024]{1,0:T(8,128)(2,1)}, u32[]{:S(2)}, u32[]{:S(2)}) %collective-permute-start.43) | collective-permute-done | bytes 1048608 | tf_op jit(solution)/shard_map/ppermute | solution.py:38
  481.4 24.3 %table_grad_part.1 = (f32[2048,512]{1,0:T(8,128)}, bf16[2048,512]{1,0:T(8,128)(2,1)}) custom-call(bf16[512,2048]{1,0:T(8,128)(2,1)} %get-tuple-element.246.refs_0_, bf16[512,2048]{1,0:T(8,128)(2,1)} %get-tuple-element.247.refs_1_, bf16[512,2048]{1,0:T(8,128)(2,1)} %get-tuple-element.248.refs_2_, bf16[512,2048]{1,0:T(8,128)(2,1)} %get-tuple-element.249.refs_3_, ...), custom_call_target="tpu_custom_call" | custom-call | flops 515396064 | bytes 629145 | tf_op jit(solution)/shard_map/table_grad_part/pallas_call | solution.py:748
  559.7 11.6 %hidden_grads.1 = (f32[2048,512]{1,0:T(8,128)}, bf16[2048,512]{1,0:T(8,128)(2,1)}) custom-call(bf16[1024,1024]{1,0:T(8,128)(2,1)} %copy-done.55, bf16[1024,1024]{1,0:T(8,128)(2,1)} %copy-done.54, bf16[1024,1024]{1,0:T(8,128)(2,1)} %pad_maximum_fusion.2.in_ref, bf16[1024,1024]{1,0:T(8,128)(2,1)} %pad_maximum_fusion.5.down_ref), custom_call_target="tpu_custom_call" | custom-call | flops 128849016 | bytes 335544 | tf_op jit(solution)/shard_map/hidden_grads/pallas_call | solution.py:783
  571.3 10.8 %collective-permute-done.49 = bf16[2048,512]{1,0:T(8,128)(2,1)} collective-permute-done((bf16[2048,512]{1,0:T(8,128)(2,1)}, bf16[2048,512]{1,0:T(8,128)(2,1)}, u32[]{:S(2)}, u32[]{:S(2)}) %collective-permute-start.49) | collective-permute-done | bytes 2097184 | tf_op jit(solution)/shard_map/ppermute | solution.py:38
  611.2 15.3 %attend_back.1 = (bf16[2,2,256,768]{3,2,1,0:T(8,128)(2,1)}, bf16[1024,512]{1,0:T(8,128)(2,1)}, bf16[1024,512]{1,0:T(8,128)(2,1)}) custom-call(s32[8]{0:T(128)} %fusion.105.info_ref, bf16[2,2,256,768]{3,2,1,0:T(8,128)(2,1)} %bitcast.285, bf16[2,2,256,768]{3,2,1,0:T(8,128)(2,1)} %bitcast.286, bf16[2,2,256,768]{3,2,1,0:T(8,128)(2,1)} %bitcast.287, ...), custom_call_target="tpu_custom_call" | custom-call | flops 230686720 | bytes 188743 | tf_op jit(solution)/shard_map/attend_back/pallas_call | solution.py:570
  643.9 11.2 %collective-permute-done.50 = bf16[2048,512]{1,0:T(8,128)(2,1)} collective-permute-done((bf16[2048,512]{1,0:T(8,128)(2,1)}, bf16[2048,512]{1,0:T(8,128)(2,1)}, u32[]{:S(2)}, u32[]{:S(2)}) %collective-permute-start.50) | collective-permute-done | bytes 2097184 | tf_op jit(solution)/shard_map/ppermute | solution.py:38
  667.7 14.3 %attn_grads.1 = (f32[1024,512]{1,0:T(8,128)}, bf16[1024,512]{1,0:T(8,128)(2,1)}) custom-call(bf16[1024,768]{1,0:T(8,128)(2,1)} %bitcast.318, bf16[1024,256]{1,0:T(8,128)(2,1)} %bitcast.312, bf16[1024,512]{1,0:T(8,128)(2,1)} %get-tuple-element.287.mem_ref, bf16[3072,512]{1,0:T(8,128)(2,1)} %bitcast.313, bf16[1024,1024]{1,0:T(8,128)(2,1)} %pad_maximum_fusion.1.normed_ref, ...), custom_call_target="tpu_custom_call" | custom-call | flops 188743680 | bytes 503316 | tf_op jit(solution)/shard_map/attn_grads/pallas_call | solution.py:833
  698.4 8.0 all-to-all-done.3
  709.9 14.6 %collective-permute-done.57 = bf16[1120,512]{1,0:T(8,128)(2,1)} collective-permute-done((bf16[1120,512]{1,0:T(8,128)(2,1)}, bf16[1120,512]{1,0:T(8,128)(2,1)}, u32[]{:S(2)}, u32[]{:S(2)}) %collective-permute-start.57) | collective-permute-done | bytes 1146912 | tf_op jit(solution)/shard_map/ppermute | solution.py:38
  735.8 14.5 %scatter.1 = f32[8000,128]{1,0:T(8,128)} custom-call(s32[1]{0:T(128)} %get-tuple-element.299.count_ref, s32[8200]{0:T(1024)} %get-tuple-element.300.code_ref, f32[8000,128]{1,0:T(8,128)} %bitcast_convert_fusion.base_ref, bf16[8192,128]{1,0:T(8,128)(2,1)} %bitcast.307), custom_call_target="tpu_custom_call" | custom-call | bytes 629145 | tf_op jit(solution)/shard_map/scatter/pallas_call | solution.py:305
  757.1 8.9 %collective-permute-done.61 = bf16[1120,128]{1,0:T(8,128)(2,1)S(1)} collective-permute-done((bf16[1120,128]{1,0:T(8,128)(2,1)S(1)}, bf16[1120,128]{1,0:T(8,128)(2,1)S(1)}, u32[]{:S(2)}, u32[]{:S(2)}) %collective-permute-start.61) | collective-permute-done | bytes 286752 | tf_op jit(solution)/shard_map/ppermute | solution.py:38
  841.6 7.8 divide_subtract_fusion
  (756 shorter events, 445.5 us)
Async XLA Ops:
  17.5 31.7 %collective-permute-start.3 = (bf16[1120,128]{1,0:T(8,128)(2,1)S(1)}, bf16[1120,128]{1,0:T(8,128)(2,1)S(1)}, u32[]{:S(2)}, u32[]{:S(2)}) collective-permute-start(bf16[1120,128]{1,0:T(8,128)(2,1)S(1)} %pad_maximum_fusion.29), channel_id=1, source_target_pairs={{0,16},{4,20},{8,24},{12,28},{16,0},{20,4},{24,8},{28,12},{1,17},{... | collective-permute-start | bytes 860168 | tf_op jit(solution)/shard_map/ppermute | solution.py:38
  51.2 29.0 %collective-permute-start.5 = (bf16[1120,256]{1,0:T(8,128)(2,1)}, bf16[1120,256]{1,0:T(8,128)(2,1)}, u32[]{:S(2)}, u32[]{:S(2)}) collective-permute-start(bf16[1120,256]{1,0:T(8,128)(2,1)} %pad_maximum_fusion.27), channel_id=1, source_target_pairs={{0,8},{4,12},{8,0},{12,4},{16,24},{20,28},{24,16},{28,20},{1,9},{5... | collective-permute-start | bytes 1720328 | tf_op jit(solution)/shard_map/ppermute | solution.py:38
  53.2 26.2 %collective-permute-start.7 = (bf16[2048,128]{1,0:T(8,128)(2,1)S(1)}, bf16[2048,128]{1,0:T(8,128)(2,1)S(1)}, u32[]{:S(2)}, u32[]{:S(2)}) collective-permute-start(bf16[2048,128]{1,0:T(8,128)(2,1)S(1)} %pad_maximum_fusion.28), channel_id=1, source_target_pairs={{0,16},{4,20},{8,24},{12,28},{16,0},{20,4},{24,8},{28,12},{1,17},{... | collective-permute-start | bytes 1572872 | tf_op jit(solution)/shard_map/ppermute | solution.py:38
  56.3 23.9 %collective-permute-start.6 = (bf16[2048,128]{1,0:T(8,128)(2,1)}, bf16[2048,128]{1,0:T(8,128)(2,1)}, u32[]{:S(2)}, u32[]{:S(2)}) collective-permute-start(bf16[2048,128]{1,0:T(8,128)(2,1)} %slice.662), channel_id=1, source_target_pairs={{0,2},{1,3},{2,0},{3,1},{4,6},{5,7},{6,4},{7,5},{8,10},{9,11},{10,... | collective-permute-start | bytes 1572872 | tf_op jit(solution)/shard_map/ppermute | solution.py:38
  82.6 38.3 %collective-permute-start.10 = (bf16[1120,512]{1,0:T(8,128)(2,1)}, bf16[1120,512]{1,0:T(8,128)(2,1)}, u32[]{:S(2)}, u32[]{:S(2)}) collective-permute-start(bf16[1120,512]{1,0:T(8,128)(2,1)} %pad_maximum_fusion.16), channel_id=1, source_target_pairs={{0,4},{4,0},{8,12},{12,8},{16,20},{20,16},{24,28},{28,24},{1,5},{5... | collective-permute-start | bytes 3440648 | tf_op jit(solution)/shard_map/ppermute | solution.py:38
  85.0 28.4 %all-to-all-start = ((bf16[8,256,128]{2,1,0:T(8,128)(2,1)}), bf16[8,256,128]{2,1,0:T(8,128)(2,1)S(1)}, u32[]{:S(2)}, u32[]{:S(2)}) async-start(bf16[8,256,128]{2,1,0:T(8,128)(2,1)} %bitcast.20), calls=%async_computation | async-start | bytes 1048576 | tf_op jit(solution)/shard_map/all_to_all | solution.py:1006
  91.2 50.4 %collective-permute-start.11 = (bf16[2048,256]{1,0:T(8,128)(2,1)}, bf16[2048,256]{1,0:T(8,128)(2,1)}, u32[]{:S(2)}, u32[]{:S(2)}) collective-permute-start(bf16[2048,256]{1,0:T(8,128)(2,1)} %pad_maximum_fusion.19), channel_id=1, source_target_pairs={{0,8},{4,12},{8,0},{12,4},{16,24},{20,28},{24,16},{28,20},{1,9},{5... | collective-permute-start | bytes 3145736 | tf_op jit(solution)/shard_map/ppermute | solution.py:38
  128.5 21.5 %collective-permute-start.9 = (bf16[512,1024]{1,0:T(8,128)(2,1)}, bf16[512,1024]{1,0:T(8,128)(2,1)}, u32[]{:S(2)}, u32[]{:S(2)}) collective-permute-start(bf16[512,1024]{1,0:T(8,128)(2,1)} %pad_maximum_fusion.18), channel_id=1, source_target_pairs={{0,1},{1,0},{2,3},{3,2},{4,5},{5,4},{6,7},{7,6},{8,9},{9,8},{10,11... | collective-permute-start | bytes 3145736 | tf_op jit(solution)/shard_map/ppermute | solution.py:38
  147.3 33.0 %collective-permute-start.13 = (bf16[1024,512]{1,0:T(8,128)(2,1)}, bf16[1024,512]{1,0:T(8,128)(2,1)}, u32[]{:S(2)}, u32[]{:S(2)}) collective-permute-start(bf16[1024,512]{1,0:T(8,128)(2,1)} %get-tuple-element.434), channel_id=1, source_target_pairs={{0,4},{4,0},{8,12},{12,8},{16,20},{20,16},{24,28},{28,24},{1,5},{5... | collective-permute-start | bytes 3145736 | tf_op jit(solution)/shard_map/ppermute | solution.py:38
  171.9 54.4 %all-to-all-start.1 = ((bf16[4,2000,128]{2,1,0:T(8,128)(2,1)}), bf16[4,2000,128]{2,1,0:T(8,128)(2,1)S(1)}, u32[]{:S(2)}, u32[]{:S(2)}) async-start(bf16[4,2000,128]{2,1,0:T(8,128)(2,1)} %bitcast.308), calls=%async_computation.1 | async-start | bytes 4096000 | tf_op jit(solution)/shard_map/all_to_all | solution.py:1079
  178.7 25.4 %collective-permute-start.15 = (bf16[1024,512]{1,0:T(8,128)(2,1)}, bf16[1024,512]{1,0:T(8,128)(2,1)S(1)}, u32[]{:S(2)}, u32[]{:S(2)}) collective-permute-start(bf16[1024,512]{1,0:T(8,128)(2,1)} %get-tuple-element.433), channel_id=1, source_target_pairs={{0,4},{4,0},{8,12},{12,8},{16,20},{20,16},{24,28},{28,24},{1,5},{5... | collective-permute-start | bytes 3145736 | tf_op jit(solution)/shard_map/ppermute | solution.py:38
  182.2 21.8 %collective-permute-start.14 = (bf16[256,1024]{1,0:T(8,128)(2,1)S(1)}, bf16[256,1024]{1,0:T(8,128)(2,1)S(1)}, u32[]{:S(2)}, u32[]{:S(2)}) collective-permute-start(bf16[256,1024]{1,0:T(8,128)(2,1)S(1)} %slice.1035), channel_id=1, source_target_pairs={{0,2},{1,3},{2,0},{3,1},{4,6},{5,7},{6,4},{7,5},{8,10},{9,11},{10,... | collective-permute-start | bytes 1572872 | tf_op jit(solution)/shard_map/ppermute | solution.py:38
  249.1 47.6 %collective-permute-start.25 = (bf16[2048,512]{1,0:T(8,128)(2,1)S(1)}, bf16[2048,512]{1,0:T(8,128)(2,1)}, u32[]{:S(2)}, u32[]{:S(2)}) collective-permute-start(bf16[2048,512]{1,0:T(8,128)(2,1)S(1)} %fusion.13.left_ref), channel_id=1, source_target_pairs={{0,4},{4,0},{8,12},{12,8},{16,20},{20,16},{24,28},{28,24},{1,5},{5... | collective-permute-start | bytes 6291464 | tf_op jit(solution)/shard_map/ppermute | solution.py:38
  261.5 24.8 %collective-permute-start.23 = (bf16[256,1024]{1,0:T(8,128)(2,1)}, bf16[256,1024]{1,0:T(8,128)(2,1)}, u32[]{:S(2)}, u32[]{:S(2)}) collective-permute-start(bf16[256,1024]{1,0:T(8,128)(2,1)} %multiply_convert_fusion.1.refs_0_), channel_id=1, source_target_pairs={{0,2},{1,3},{2,0},{3,1},{4,6},{5,7},{6,4},{7,5},{8,10},{9,11},{10,... | collective-permute-start | bytes 1572872 | tf_op jit(solution)/shard_map/ppermute | solution.py:38
  264.9 24.2 %collective-permute-start.20 = (bf16[256,1024]{1,0:T(8,128)(2,1)}, bf16[256,1024]{1,0:T(8,128)(2,1)}, u32[]{:S(2)}, u32[]{:S(2)}) collective-permute-start(bf16[256,1024]{1,0:T(8,128)(2,1)} %reorder.4), channel_id=1, source_target_pairs={{0,16},{4,20},{8,24},{12,28},{16,0},{20,4},{24,8},{28,12},{1,17},{... | collective-permute-start | bytes 1572872 | tf_op jit(solution)/shard_map/ppermute | solution.py:38
  291.4 25.6 %collective-permute-start.22 = (bf16[512,1024]{1,0:T(8,128)(2,1)}, bf16[512,1024]{1,0:T(8,128)(2,1)}, u32[]{:S(2)}, u32[]{:S(2)}) collective-permute-start(bf16[512,1024]{1,0:T(8,128)(2,1)} %reorder.5), channel_id=1, source_target_pairs={{0,8},{4,12},{8,0},{12,4},{16,24},{20,28},{24,16},{28,20},{1,9},{5... | collective-permute-start | bytes 3145736 | tf_op jit(solution)/shard_map/ppermute | solution.py:38
  292.9 24.1 %collective-permute-start.21 = (bf16[256,1024]{1,0:T(8,128)(2,1)}, bf16[256,1024]{1,0:T(8,128)(2,1)S(1)}, u32[]{:S(2)}, u32[]{:S(2)}) collective-permute-start(bf16[256,1024]{1,0:T(8,128)(2,1)} %collective-permute-done.20.refs_1_), channel_id=1, source_target_pairs={{0,2},{1,3},{2,0},{3,1},{4,6},{5,7},{6,4},{7,5},{8,10},{9,11},{10,... | collective-permute-start | bytes 1572872 | tf_op jit(solution)/shard_map/ppermute | solution.py:38
  442.6 25.2 %collective-permute-start.43 = (bf16[512,1024]{1,0:T(8,128)(2,1)}, bf16[512,1024]{1,0:T(8,128)(2,1)}, u32[]{:S(2)}, u32[]{:S(2)}) collective-permute-start(bf16[512,1024]{1,0:T(8,128)(2,1)} %reorder.6), channel_id=1, source_target_pairs={{0,8},{4,12},{8,0},{12,4},{16,24},{20,28},{24,16},{28,20},{1,9},{5... | collective-permute-start | bytes 3145736 | tf_op jit(solution)/shard_map/ppermute | solution.py:38
  454.2 22.6 %collective-permute-start.41 = (bf16[512,1024]{1,0:T(8,128)(2,1)}, bf16[512,1024]{1,0:T(8,128)(2,1)}, u32[]{:S(2)}, u32[]{:S(2)}) collective-permute-start(bf16[512,1024]{1,0:T(8,128)(2,1)} %get-tuple-element.239), channel_id=1, source_target_pairs={{0,1},{1,0},{2,3},{3,2},{4,5},{5,4},{6,7},{7,6},{8,9},{9,8},{10,11... | collective-permute-start | bytes 3145736 | tf_op jit(solution)/shard_map/ppermute | solution.py:38
  474.1 31.6 %collective-permute-start.44 = (bf16[256,1024]{1,0:T(8,128)(2,1)}, bf16[256,1024]{1,0:T(8,128)(2,1)S(1)}, u32[]{:S(2)}, u32[]{:S(2)}) collective-permute-start(bf16[256,1024]{1,0:T(8,128)(2,1)} %reorder.7), channel_id=1, source_target_pairs={{0,16},{4,20},{8,24},{12,28},{16,0},{20,4},{24,8},{28,12},{1,17},{... | collective-permute-start | bytes 1572872 | tf_op jit(solution)/shard_map/ppermute | solution.py:38
  479.9 25.9 %collective-permute-start.42 = (bf16[256,1024]{1,0:T(8,128)(2,1)S(1)}, bf16[256,1024]{1,0:T(8,128)(2,1)S(1)}, u32[]{:S(2)}, u32[]{:S(2)}) collective-permute-start(bf16[256,1024]{1,0:T(8,128)(2,1)S(1)} %slice.1030), channel_id=1, source_target_pairs={{0,2},{1,3},{2,0},{3,1},{4,6},{5,7},{6,4},{7,5},{8,10},{9,11},{10,... | collective-permute-start | bytes 1572872 | tf_op jit(solution)/shard_map/ppermute | solution.py:38
  509.6 22.8 %collective-permute-start.45 = (bf16[256,1024]{1,0:T(8,128)(2,1)}, bf16[256,1024]{1,0:T(8,128)(2,1)}, u32[]{:S(2)}, u32[]{:S(2)}) collective-permute-start(bf16[256,1024]{1,0:T(8,128)(2,1)} %fusion.37), channel_id=1, source_target_pairs={{0,2},{1,3},{2,0},{3,1},{4,6},{5,7},{6,4},{7,5},{8,10},{9,11},{10,... | collective-permute-start | bytes 1572872 | tf_op jit(solution)/shard_map/ppermute | solution.py:38
  533.7 48.4 %collective-permute-start.49 = (bf16[2048,512]{1,0:T(8,128)(2,1)}, bf16[2048,512]{1,0:T(8,128)(2,1)}, u32[]{:S(2)}, u32[]{:S(2)}) collective-permute-start(bf16[2048,512]{1,0:T(8,128)(2,1)} %get-tuple-element.273), channel_id=1, source_target_pairs={{0,4},{4,0},{8,12},{12,8},{16,20},{20,16},{24,28},{28,24},{1,5},{5... | collective-permute-start | bytes 6291464 | tf_op jit(solution)/shard_map/ppermute | solution.py:38
  552.7 29.4 %collective-permute-start.48 = (bf16[256,1024]{1,0:T(8,128)(2,1)}, bf16[256,1024]{1,0:T(8,128)(2,1)}, u32[]{:S(2)}, u32[]{:S(2)}) collective-permute-start(bf16[256,1024]{1,0:T(8,128)(2,1)} %slice.1029), channel_id=1, source_target_pairs={{0,2},{1,3},{2,0},{3,1},{4,6},{5,7},{6,4},{7,5},{8,10},{9,11},{10,... | collective-permute-start | bytes 1572872 | tf_op jit(solution)/shard_map/ppermute | solution.py:38
  592.9 62.1 %all-to-all-start.2 = ((bf16[4,2000,128]{2,1,0:T(8,128)(2,1)}), bf16[4,2000,128]{2,1,0:T(8,128)(2,1)}, u32[]{:S(2)}, u32[]{:S(2)}) async-start(bf16[4,2000,128]{2,1,0:T(8,128)(2,1)} %pad_maximum_fusion.9), calls=%async_computation.2 | async-start | bytes 4096000 | tf_op jit(solution)/shard_map/all_to_all | solution.py:1201
  606.7 48.4 %collective-permute-start.50 = (bf16[2048,512]{1,0:T(8,128)(2,1)}, bf16[2048,512]{1,0:T(8,128)(2,1)}, u32[]{:S(2)}, u32[]{:S(2)}) collective-permute-start(bf16[2048,512]{1,0:T(8,128)(2,1)} %get-tuple-element.275), channel_id=1, source_target_pairs={{0,4},{4,0},{8,12},{12,8},{16,20},{20,16},{24,28},{28,24},{1,5},{5... | collective-permute-start | bytes 6291464 | tf_op jit(solution)/shard_map/ppermute | solution.py:38
  631.8 23.3 %collective-permute-start.53 = (bf16[512,1024]{1,0:T(8,128)(2,1)S(1)}, bf16[512,1024]{1,0:T(8,128)(2,1)S(1)}, u32[]{:S(2)}, u32[]{:S(2)}) collective-permute-start(bf16[512,1024]{1,0:T(8,128)(2,1)S(1)} %slice.1022), channel_id=1, source_target_pairs={{0,1},{1,0},{2,3},{3,2},{4,5},{5,4},{6,7},{7,6},{8,9},{9,8},{10,11... | collective-permute-start | bytes 3145736 | tf_op jit(solution)/shard_map/ppermute | solution.py:38
  663.7 34.7 %collective-permute-start.54 = (bf16[2048,256]{1,0:T(8,128)(2,1)}, bf16[2048,256]{1,0:T(8,128)(2,1)}, u32[]{:S(2)}, u32[]{:S(2)}) collective-permute-start(bf16[2048,256]{1,0:T(8,128)(2,1)} %slice.1021), channel_id=1, source_target_pairs={{0,8},{4,12},{8,0},{12,4},{16,24},{20,28},{24,16},{28,20},{1,9},{5... | collective-permute-start | bytes 3145736 | tf_op jit(solution)/shard_map/ppermute | solution.py:38
  664.0 20.6 %collective-permute-start.55 = (bf16[256,1024]{1,0:T(8,128)(2,1)S(1)}, bf16[256,1024]{1,0:T(8,128)(2,1)S(1)}, u32[]{:S(2)}, u32[]{:S(2)}) collective-permute-start(bf16[256,1024]{1,0:T(8,128)(2,1)S(1)} %slice.1028), channel_id=1, source_target_pairs={{0,2},{1,3},{2,0},{3,1},{4,6},{5,7},{6,4},{7,5},{8,10},{9,11},{10,... | collective-permute-start | bytes 1572872 | tf_op jit(solution)/shard_map/ppermute | solution.py:38
  692.5 32.0 %collective-permute-start.57 = (bf16[1120,512]{1,0:T(8,128)(2,1)}, bf16[1120,512]{1,0:T(8,128)(2,1)}, u32[]{:S(2)}, u32[]{:S(2)}) collective-permute-start(bf16[1120,512]{1,0:T(8,128)(2,1)} %pad_maximum_fusion.17), channel_id=1, source_target_pairs={{0,4},{4,0},{8,12},{12,8},{16,20},{20,16},{24,28},{28,24},{1,5},{5... | collective-permute-start | bytes 3440648 | tf_op jit(solution)/shard_map/ppermute | solution.py:38
  709.1 23.3 %collective-permute-start.56 = (bf16[2048,128]{1,0:T(8,128)(2,1)S(1)}, bf16[2048,128]{1,0:T(8,128)(2,1)S(1)}, u32[]{:S(2)}, u32[]{:S(2)}) collective-permute-start(bf16[2048,128]{1,0:T(8,128)(2,1)S(1)} %slice.1027), channel_id=1, source_target_pairs={{0,16},{4,20},{8,24},{12,28},{16,0},{20,4},{24,8},{28,12},{1,17},{... | collective-permute-start | bytes 1572872 | tf_op jit(solution)/shard_map/ppermute | solution.py:38
  727.3 23.0 %collective-permute-start.59 = (bf16[1120,256]{1,0:T(8,128)(2,1)}, bf16[1120,256]{1,0:T(8,128)(2,1)}, u32[]{:S(2)}, u32[]{:S(2)}) collective-permute-start(bf16[1120,256]{1,0:T(8,128)(2,1)} %slice.1026), channel_id=1, source_target_pairs={{0,8},{4,12},{8,0},{12,4},{16,24},{20,28},{24,16},{28,20},{1,9},{5... | collective-permute-start | bytes 1720328 | tf_op jit(solution)/shard_map/ppermute | solution.py:38
  (197 other events, 2508.6 us)
